TPU v7x, 32 devices: a whole 2x2x4 slice. The times are simulated.
32 devices in a mesh: groups: 2 (over x), tensor: 16 (over z, y, core).
Axes of the slice: x: 2, y: 2, z: 4, core: 2. Of those that a mesh axis runs over, the one named last changes fastest.
Arguments:
- queries: bfloat16 [256, 4096], P(('groups', 'tensor')), parts along dimension 0, may hold values from -6 to 6
- corpus: bfloat16 [2048, 4, 4096], P(('groups', 'tensor')), parts along dimension 0, may hold values from -6 to 6
- block_owner: int32 [48, 1], P('groups'), parts along dimension 0, may hold values from 0 to 15; in each aligned block of 24 rows (0 to 23, 24 to 47, ...) at most 3 rows name the same one
- slot_row: int32 [48], P('groups'), parts along dimension 0, may hold values from 0 to 63
- segment: int32 [48], P('groups'), parts along dimension 0, may hold values from 0 to 3, never falling along the last dimension, each value on 1 to 12 neighbouring positions
- query_weight: bfloat16 [1024, 4096], P('tensor'), may hold values from -3 to 3
- key_weight: bfloat16 [1024, 4096], P('tensor'), may hold values from -3 to 3
- value_weight: bfloat16 [1024, 4096], P('tensor'), may hold values from -0.09375 to 0.09375
- out_weight: bfloat16 [1024, 4096], P('tensor'), may hold values from -0.1875 to 0.1875
- gain_attn: float32 [4096], replicated, may hold values from 0.1 to 1.9
- gain_ffn: float32 [4096], replicated, may hold values from 0.1 to 1.9
- gate_weight: bfloat16 [2560, 4096], P('tensor'), may hold values from -0.09375 to 0.09375
- up_weight: bfloat16 [2560, 4096], P('tensor'), may hold values from -0.09375 to 0.09375
- down_weight: bfloat16 [2560, 4096], P('tensor'), may hold values from -0.125 to 0.125
Outputs:
- encoded: bfloat16 [448, 4096], P(('groups', 'tensor')), parts along dimension 0
There are 2 independent parts, one for each index of `groups`. A program takes and returns all parts, laid end to end along the dimension named above; an argument that names none is the same for every part. Nothing has to cross between parts.
Inputs may be any that keep to these rules, and one draw needn't show every extreme that they name: `block_owner`: every owner holds some block of the pack; no owner holds more than 3 of them, and some owner holds exactly 3. `segment`: never falls along the pack; each pair has 1 to 12 blocks, one exactly 12.
All inputs are finite; a program needn't handle non-finite values.
Results may differ from a plain program's by a relative error of at most 0.008.
Values may be sent and summed in bfloat16 or wider, within the bound.
No kernel may reach another device: no remote copies, remote signals or barrier semaphores. Data moves between devices by JAX's collectives and lax.ppermute only.
A program may use at most 64 MiB of HBM per device.

v0:
```python
import jax
import jax.numpy as jnp
from jax import lax
from jax.sharding import PartitionSpec as P

HDIM = 64
QLEN = 32
BLK = 4
CAP = 3


def normed(stream, gain):
    values = stream.astype(jnp.float32)
    mean_square = jnp.mean(values * values, axis=-1, keepdims=True)
    return (values * lax.rsqrt(mean_square + 1e-06) * gain).astype(jnp.bfloat16)


def by_rows(left, weight):
    return lax.dot_general(
        left, weight, (((1,), (1,)), ((), ())), preferred_element_type=jnp.float32
    )


def body(
    queries,
    corpus,
    block_owner,
    slot_row,
    segment,
    query_weight,
    key_weight,
    value_weight,
    out_weight,
    gain_attn,
    gain_ffn,
    gate_weight,
    up_weight,
    down_weight,
):
    devices = lax.axis_size("tensor")
    my_index = lax.axis_index("tensor")
    owners = block_owner[:, 0]
    blocks_total = owners.shape[0]
    features = queries.shape[1]
    positions = jnp.arange(blocks_total, dtype=jnp.int32)
    earlier = (owners[:, None] == owners[None, :]) & (positions[:, None] < positions[None, :])
    slot_rank = jnp.sum(earlier.astype(jnp.int32), axis=0)
    slot_ids = jnp.arange(CAP, dtype=jnp.int32)
    choose_slot = (owners[None, :] == my_index) & (slot_rank[None, :] == slot_ids[:, None])
    local_rows = jnp.sum(jnp.where(choose_slot, slot_row[None, :], 0), axis=1)
    present = jnp.any(choose_slot, axis=1)
    outgoing = jnp.take(corpus, local_rows, axis=0)
    outgoing = jnp.where(present[:, None, None], outgoing, jnp.zeros_like(outgoing)).reshape(
        CAP, -1
    )
    location = owners * CAP + slot_rank
    query_all, arrived = (
        lax.all_gather(queries, "tensor", axis=0, tiled=True),
        lax.all_gather(outgoing, "tensor", axis=0, tiled=True),
    )
    stream_in = jnp.concatenate(
        [query_all, jnp.take(arrived, location, axis=0).reshape(-1, features)], axis=0
    )
    normal_rows = normed(stream_in, gain_attn)
    projected = tuple(
        (
            by_rows(normal_rows, weight).astype(jnp.bfloat16)
            for weight in (query_weight, key_weight, value_weight)
        )
    )
    tokens = stream_in.shape[0]
    heads_here = query_weight.shape[0] // HDIM
    query_rows_total = query_all.shape[0]
    pair_ids = jnp.concatenate(
        [jnp.arange(query_rows_total, dtype=jnp.int32) // QLEN, jnp.repeat(segment, BLK)]
    )
    same_pair = pair_ids[:, None] == pair_ids[None, :]
    query_heads = projected[0].reshape(tokens, heads_here, HDIM)
    key_heads = projected[1].reshape(tokens, heads_here, HDIM)
    value_heads = projected[2].reshape(tokens, heads_here, HDIM)
    scores = jnp.einsum(
        "qhd,khd->hqk", query_heads, key_heads, preferred_element_type=jnp.float32
    ) * HDIM ** (-0.5)
    scores = jnp.where(same_pair[None, :, :], scores, -1e30)
    row_max = jnp.max(scores, axis=-1, keepdims=True)
    weights = jnp.exp(scores - row_max)
    probability = (weights / jnp.sum(weights, axis=-1, keepdims=True)).astype(jnp.bfloat16)
    context = (
        jnp.einsum("hqk,khd->qhd", probability, value_heads, preferred_element_type=jnp.float32)
        .astype(jnp.bfloat16)
        .reshape(tokens, heads_here * HDIM)
    )
    rows_here = tokens // devices
    first_mine = my_index * rows_here
    attended = lax.psum(jnp.dot(context, out_weight, preferred_element_type=jnp.float32), "tensor")
    stream_mid = (stream_in.astype(jnp.float32) + attended).astype(jnp.bfloat16)
    normal_mid = normed(stream_mid, gain_ffn)
    mid_mine = lax.dynamic_slice_in_dim(stream_mid, first_mine, rows_here, 0)
    gate_value = by_rows(normal_mid, gate_weight)
    up_value = by_rows(normal_mid, up_weight)
    hidden = (jax.nn.gelu(gate_value, approximate=True) * up_value).astype(jnp.bfloat16)
    ffn_result = lax.psum_scatter(
        jnp.dot(hidden, down_weight, preferred_element_type=jnp.float32),
        "tensor",
        scatter_dimension=0,
        tiled=True,
    )
    return (mid_mine.astype(jnp.float32) + ffn_result).astype(jnp.bfloat16)


def solution(mesh):
    placed = (
        P(("groups", "tensor"), None),
        P(("groups", "tensor"), None, None),
        P("groups", None),
        P("groups"),
        P("groups"),
        P("tensor", None),
        P("tensor", None),
        P("tensor", None),
        P("tensor", None),
        P(),
        P(),
        P("tensor", None),
        P("tensor", None),
        P("tensor", None),
    )
    return jax.shard_map(
        body, mesh=mesh, in_specs=placed, out_specs=P(("groups", "tensor"), None), check_vma=False
    )
```

profile of v0, /device:TPU:0, one launch (start us, length us, event | category | flops | bytes accessed | tf_op | source)
XLA Modules:
  0.0 298.2 jit_solution(11401972354691796657)
XLA Ops:
  6.5 0.0 copy-start
  6.5 0.0 all-gather.6.cloned.1.call-start
  6.5 0.8 broadcast_compare_fusion
  7.3 0.8 convert_reduce_fusion
  8.2 0.8 select_reduce_fusion
  9.0 0.1 fusion.31
  9.1 0.0 copy-done
  9.1 0.6 gather_fusion
  9.7 0.1 copy.15
  9.8 0.8 select_bitcast_fusion
  10.6 0.0 all-gather.6.cloned.1.call-update
  10.6 0.0 all-gather.4.cloned.1.call-start
  10.7 0.7 all-gather.4.cloned.1.call-update
  11.4 0.0 all-reduce.4.cloned.1.call-start
  11.4 0.7 and_bitcast_fusion
  12.1 0.1 broadcast_in_dim.69
  12.2 0.1 broadcast_in_dim.70
  12.3 0.7 broadcast_in_dim.79
  13.0 0.1 reshape.96
  13.2 41.7 %all-gather.6.cloned.1.call-done = bf16[16,3,16384]{2,1,0:T(4,128)(2,1)} async-done(((bf16[1,3,16384]{2,1,0:T(4,128)(2,1)}), bf16[16,3,16384]{2,1,0:T(4,128)(2,1)}) %all-gather.6.cloned.1.call-update) | async-done | bytes 1572880 | tf_op jit(solution)/shard_map/all_gather | solution.py:59
  54.9 3.4 %reshape.115 = bf16[48,16384]{1,0:T(8,128)(2,1)} reshape(bf16[16,3,16384]{2,1,0:T(4,128)(2,1)} %all-gather.6.cloned.1.call-done) | data formatting | bytes 3145728
  58.4 3.3 %gather_fusion.1 = bf16[24,16384]{1,0:T(8,128)(2,1)S(1)} fusion(bf16[48,16384]{1,0:T(8,128)(2,1)} %reshape.115, s32[1024]{0:T(1024)S(1)} %pad_clamp_fusion), kind=kCustom, calls=%fused_computation.1 | custom fusion | bytes 1572960 | tf_op jit(solution)/shard_map/jit(_take)/gather | solution.py:62
  61.7 1.5 gather.15
  63.2 0.0 copy-start.7
  63.2 1.3 broadcast_select_fusion
  64.5 29.3 %all-gather.4.cloned.1.call-done = bf16[128,4096]{1,0:T(8,128)(2,1)} async-done(((bf16[8,4096]{1,0:T(8,128)(2,1)}), bf16[128,4096]{1,0:T(8,128)(2,1)}) %all-gather.4.cloned.1.call-update) | async-done | bytes 1048592 | tf_op jit(solution)/shard_map/all_gather | solution.py:58
  93.8 0.0 copy-start.2
  93.8 1.8 fusion.4
  95.6 0.0 copy-done.7
  95.6 0.0 copy-done.2
  95.6 0.0 copy-start.5
  95.6 0.6 fusion.6
  96.2 0.0 copy-start.1
  96.2 1.2 copy-done.1
  97.4 0.0 copy-done.5
  97.4 0.7 convolution_convert_fusion.1
  98.1 2.5 fusion.34
  100.7 0.1 fusion.17
  100.7 2.4 fusion.11
  103.1 3.5 %fusion.35 = f32[224,4096]{1,0:T(8,128)} fusion(bf16[224,64]{0,1:T(8,128)(2,1)S(1)} %fusion.11, bf16[64,4096]{1,0:T(8,128)(2,1)} %param.22), kind=kOutput, calls=%fused_computation.68 | convolution fusion | flops 117440512 | bytes 4222976 | tf_op jit(solution)/shard_map/dot_general | solution.py:95
  106.7 0.0 all-reduce.4.cloned.1.call-update
  106.7 0.0 copy-start.8
  106.7 106.0 %all-reduce.4.cloned.1.call-done = f32[224,4096]{1,0:T(8,128)} async-done(((f32[224,4096]{1,0:T(8,128)}), f32[224,4096]{1,0:T(8,128)}) %all-reduce.4.cloned.1.call-update) | async-done | bytes 3670032 | tf_op jit(solution)/shard_map/psum | solution.py:95
  212.8 0.0 copy-start.10
  212.8 3.2 %fusion.1 = (f32[224]{0:T(256)S(1)}, bf16[224,4096]{1,0:T(8,128)(2,1)S(1)}) fusion(f32[224,4096]{1,0:T(8,128)} %all-reduce.4.cloned.1.call-done, bf16[96,4096]{1,0:T(8,128)(2,1)S(1)} %broadcast_select_fusion, bf16[128,4096]{1,0:T(8,128)(2,1)} %all-gather.4.cloned.1.call-done), kind=kLoop, calls=%fused_computation.7 | loop fusion | flops 8257312 | bytes 7340928 | tf_op jit(solution)/shard_map/reduce_sum | solution.py:14
  215.9 0.0 copy-start.3
  215.9 1.2 copy-done.3
  217.2 0.0 copy-done.8
  217.2 0.0 copy-done.10
  217.2 0.0 copy-start.4
  217.2 1.6 fusion.24
  218.8 0.0 copy-done.4
  218.8 6.0 %fusion.10 = f32[224,4096]{1,0:T(8,128)} fusion(bf16[160,4096]{1,0:T(8,128)(2,1)S(1)} %copy-done.4, f32[224,160]{0,1:T(8,128)} %fusion.24, bf16[160,4096]{1,0:T(8,128)(2,1)} %param.26, bf16[224,4096]{1,0:T(8,128)(2,1)} %copy-done.3, f32[4096]{0:T(1024)S(1)} %copy-done.8, f32[224]{0:T(256)S(1)} %add_rsqrt_fusion), kind=kOutput, calls=%fused_computation.19 | convolution fusion | flops 590944256 | bytes 8287104 | tf_op jit(solution)/shard_map/dot_general | solution.py:103
  224.8 0.0 copy-start.9
  224.8 49.4 %fusion = f32[16,4096]{1,0:T(8,128)S(1)} fusion(f32[224,4096]{1,0:T(8,128)} %fusion.10), kind=kCustom, calls=%all-reduce-scatter | all-reduce-scatter fusion | flops 1048577 | bytes 3932672
  274.2 2.6 collective-permute-start
  276.8 4.2 %collective-permute-start.1 = (f32[14,4096]{1,0:T(8,128)S(1)}, f32[14,4096]{1,0:T(8,128)S(1)}, u32[]{:S(2)}, u32[]{:S(2)}) collective-permute-start(f32[14,4096]{1,0:T(8,128)S(1)} %slice.4), channel_id=1, source_target_pairs={{0,2},{1,3},{2,4},{3,5},{4,6},{5,7},{6,8},{7,9},{8,10},{9,11},{10,... | collective-permute-start | bytes 688136
  281.0 0.0 copy-done.9
  281.0 0.6 dynamic-slice.4
  282.3 5.5 %collective-permute-done.1 = f32[14,4096]{1,0:T(8,128)S(1)} collective-permute-done((f32[14,4096]{1,0:T(8,128)S(1)}, f32[14,4096]{1,0:T(8,128)S(1)}, u32[]{:S(2)}, u32[]{:S(2)}) %collective-permute-start.1) | collective-permute-done | bytes 229408
  287.7 0.7 copy-done.6
  288.4 0.0 collective-permute-done
  288.4 1.6 concatenate.8
  290.0 1.7 fusion.16
  (10 shorter events, 0.1 us)
Async XLA Ops:
  6.5 2.6 copy-start
  6.5 48.4 %all-gather.6.cloned.1.call-start = ((), (), s32[]{:S(2)}) async-start(), calls=%async_computation.2 | async-start | bytes 2228224 | tf_op jit(solution)/shard_map/all_gather | solution.py:59
  10.6 83.2 %all-gather.4.cloned.1.call-start = ((), (), s32[]{:S(2)}) async-start(), calls=%async_computation | async-start | bytes 1114112 | tf_op jit(solution)/shard_map/all_gather | solution.py:58
  11.4 201.4 %all-reduce.4.cloned.1.call-start = ((), (), s32[]{:S(2)}) async-start(), calls=%async_computation.1 | async-start | bytes 7340032 | tf_op jit(solution)/shard_map/psum | solution.py:95
  63.2 32.4 %copy-start.7 = (f32[4096]{0:T(1024)S(1)}, f32[4096]{0:T(1024)}, u32[]{:S(2)}) copy-start(f32[4096]{0:T(1024)} %param.23) | copy-start | bytes 49156
  93.8 1.8 copy-start.2
  95.6 1.8 copy-start.5
  96.2 1.3 copy-start.1
  106.7 110.5 %copy-start.8 = (f32[4096]{0:T(1024)S(1)}, f32[4096]{0:T(1024)}, u32[]{:S(2)}) copy-start(f32[4096]{0:T(1024)} %param.24) | copy-start | bytes 49156
  212.8 4.4 %copy-start.10 = (bf16[160,4096]{1,0:T(8,128)(2,1)S(1)}, bf16[160,4096]{1,0:T(8,128)(2,1)}, u32[]{:S(2)}) copy-start(bf16[160,4096]{1,0:T(8,128)(2,1)} %param.25) | copy-start | bytes 3932164
  215.9 1.3 copy-start.3
  217.2 1.6 copy-start.4
  224.8 56.2 %copy-start.9 = (u32[32]{0:T(128)S(1)}, u32[32]{0:T(128)}, u32[]{:S(2)}) copy-start(u32[32]{0:T(128)} %constant.87) | copy-start | bytes 388
  274.2 14.3 %collective-permute-start = (f32[16,4096]{1,0:T(8,128)S(1)}, f32[16,4096]{1,0:T(8,128)S(1)}, u32[]{:S(2)}, u32[]{:S(2)}) collective-permute-start(f32[16,4096]{1,0:T(8,128)S(1)} %fusion), channel_id=1, source_target_pairs={{0,1},{1,2},{2,3},{3,4},{4,5},{5,6},{6,7},{7,8},{8,9},{9,10},{10,1... | collective-permute-start | bytes 786440
  276.8 10.9 %collective-permute-start.1 = (f32[14,4096]{1,0:T(8,128)S(1)}, f32[14,4096]{1,0:T(8,128)S(1)}, u32[]{:S(2)}, u32[]{:S(2)}) collective-permute-start(f32[14,4096]{1,0:T(8,128)S(1)} %slice.4), channel_id=1, source_target_pairs={{0,2},{1,3},{2,4},{3,5},{4,6},{5,7},{6,8},{7,9},{8,10},{9,11},{10,... | collective-permute-start | bytes 688136
  287.7 0.7 copy-start.6
Sparse Core Ops, SparseCore 0:
  10.8 44.0 all-gather.5
  57.1 36.7 all-gather.3
  106.8 105.8 all-reduce.3
where the time goes:
time: 299 us; the launch traced here: 298 us
  waiting for transfers between devices  183 us (61%)
  blocking collectives  49.4 us (17%)
  matrix products  16.8 us (6%)
  local copies, waits for them, and re-layouts  15.4 us (5%)
  between operations  14 us (5%)
  other arithmetic  12.5 us (4%)
  starting transfers between devices  6.87 us (2%)
    psum x1, waiting for transfers between devices, body(): lax.psum(jnp.dot(context, out_weight, preferred_element_type=jnp.float32)...  106 us
    unnamed x1, blocking collectives  49.4 us
    all_gather x1, waiting for transfers between devices, body(): lax.all_gather(outgoing, 'tensor', axis=0, tiled=True)  41.7 us
    all_gather x1, waiting for transfers between devices, body(): lax.all_gather(queries, 'tensor', axis=0, tiled=True)  29.3 us
    unnamed x27, local copies, waits for them, and re-layouts  8.93 us
    unnamed x2, starting transfers between devices  6.79 us
    unnamed x5, waiting for transfers between devices  6.21 us
    dot_general x1, matrix products, body(): jnp.dot(hidden, down_weight, preferred_element_type=jnp.float32)  6.04 us
  transfers between devices with their start and end apart: 5, of which 4 were waited for; matrix products, arithmetic and copies ran while one was open for 4% of the time, Pallas kernels for 0%

commit v1 on v0

v1 whole, which is shorter than its diff:
```python
import jax
import jax.numpy as jnp
from jax import lax
from jax.sharding import PartitionSpec as P

HDIM = 64
QLEN = 32
BLK = 4
CAP = 3
AXIS = "tensor"


def by_rows(left, weight):
    return lax.dot_general(
        left, weight, (((1,), (1,)), ((), ())), preferred_element_type=jnp.float32
    )


def dot(left, right):
    return jnp.dot(left, right, preferred_element_type=jnp.float32)


def body(
    queries,
    corpus,
    block_owner,
    slot_row,
    segment,
    query_weight,
    key_weight,
    value_weight,
    out_weight,
    gain_attn,
    gain_ffn,
    gate_weight,
    up_weight,
    down_weight,
):
    devices = lax.axis_size(AXIS)
    me = lax.axis_index(AXIS)
    nz = devices // 4
    zi, yi, ci = me // 4, (me // 2) % 2, me % 2
    z_order = sorted(range(1, nz), key=lambda k: -min(k, nz - k))

    def along_z(value, k):
        return lax.ppermute(value, AXIS, [(i, (i + 4 * k) % devices) for i in range(devices)])

    def across_y(value):
        return lax.ppermute(value, AXIS, [(i, i ^ 2) for i in range(devices)])

    def across_core(value):
        return lax.ppermute(value, AXIS, [(i, i ^ 1) for i in range(devices)])

    def plane_gather(value):
        near = {0: value}
        for k in z_order:
            near[k] = along_z(value, k)
        far = {k: across_y(near[k]) for k in [0] + z_order}
        return [piece for k in range(nz) for piece in (near[k], far[k])]

    owners = block_owner[:, 0]
    blocks_total = owners.shape[0]
    features = queries.shape[1]
    half = features // 2
    query_rows = queries.shape[0]
    query_total = query_rows * devices
    tokens = query_total + blocks_total * BLK
    width = features // devices
    heads_rows = query_weight.shape[0]
    hidden_here = gate_weight.shape[0]
    rows_here = tokens // devices
    chunk_rows = -(-rows_here // 16) * 16

    positions = jnp.arange(blocks_total, dtype=jnp.int32)
    earlier = (owners[:, None] == owners[None, :]) & (positions[:, None] < positions[None, :])
    slot_rank = jnp.sum(earlier.astype(jnp.int32), axis=0)
    slot_ids = jnp.arange(CAP, dtype=jnp.int32)
    choose_slot = (owners[None, :] == me) & (slot_rank[None, :] == slot_ids[:, None])
    local_rows = jnp.sum(jnp.where(choose_slot, slot_row[None, :], 0), axis=1)
    outgoing = jnp.take(corpus, local_rows, axis=0).reshape(CAP * BLK, features)
    piece_rows = -(-(query_rows + CAP * BLK) // 8) * 8
    piece = jnp.concatenate(
        [
            queries,
            outgoing,
            jnp.zeros((piece_rows - query_rows - CAP * BLK, features), jnp.bfloat16),
        ],
        axis=0,
    )

    row_ids = jnp.arange(query_total, dtype=jnp.int32)
    token_owner = jnp.concatenate([row_ids // query_rows, jnp.repeat(owners, BLK)])
    token_row = jnp.concatenate(
        [
            row_ids % query_rows,
            (query_rows + slot_rank[:, None] * BLK + jnp.arange(BLK)[None, :]).reshape(-1),
        ]
    )
    token_place = (
        ((token_owner % 2) ^ ci) * (2 * nz)
        + ((zi - token_owner // 4) % nz) * 2
        + ((token_owner // 2) % 2 ^ yi)
    ) * piece_rows + token_row
    pair_ids = jnp.concatenate([row_ids // QLEN, jnp.repeat(segment, BLK)])
    same_pair = pair_ids[:, None] == pair_ids[None, :]

    projection = jnp.concatenate([query_weight, key_weight, value_weight], axis=0)
    projection_other = across_core(projection)
    own_half = ci * half
    other_half = (1 - ci) * half
    gate_up = jnp.concatenate([gate_weight, up_weight], axis=0)
    gate_up_mine = lax.dynamic_slice_in_dim(gate_up, own_half, half, 1)
    gate_up_other = across_core(lax.dynamic_slice_in_dim(gate_up, other_half, half, 1))
    down_other = across_core(down_weight)

    def out_block(dz, dy):
        chip = 2 * ((zi + dz) % nz) + (yi ^ dy)
        return jnp.concatenate(
            [
                lax.dynamic_slice_in_dim(out_weight, chip * width, width, 1),
                lax.dynamic_slice_in_dim(out_weight, half + chip * width, width, 1),
            ],
            axis=1,
        )

    out_far = across_y(jnp.concatenate([out_block(dz, 1) for dz in range(nz)], axis=0))
    out_pairs = [
        jnp.concatenate(
            [out_block(dz, 0), out_far[dz * heads_rows : (dz + 1) * heads_rows]], axis=0
        )
        for dz in range(nz)
    ]
    out_columns = jnp.concatenate(
        [out_pairs[0]] + [along_z(out_pairs[k], k) for k in range(1, nz)], axis=0
    )

    stream = jnp.concatenate(plane_gather(piece), axis=0)
    values = stream.astype(jnp.float32)
    mean_square = jnp.mean(values * values, axis=-1, keepdims=True)
    normal = (values * lax.rsqrt(mean_square + 1e-06) * gain_attn).astype(jnp.bfloat16)
    projected = by_rows(normal, projection).astype(jnp.bfloat16)
    projected_other = by_rows(normal, projection_other).astype(jnp.bfloat16)
    chip = 2 * zi + yi
    columns = lax.dynamic_slice_in_dim(stream, own_half + chip * width, width, 1)
    columns_other = lax.dynamic_slice_in_dim(stream, other_half + chip * width, width, 1)
    arrived = across_core(jnp.concatenate([projected_other, columns_other], axis=1))
    both = jnp.concatenate([jnp.concatenate([projected, columns], axis=1), arrived], axis=0)
    packed = jnp.take(both, token_place, axis=0)

    query, key, value = (packed[:, i * HDIM : (i + 1) * HDIM] for i in range(3))
    scores = by_rows(query, key) * HDIM ** (-0.5)
    scores = jnp.where(same_pair, scores, -1e30)
    weights = jnp.exp(scores - jnp.max(scores, axis=-1, keepdims=True))
    probability = (weights / jnp.sum(weights, axis=-1, keepdims=True)).astype(jnp.bfloat16)
    context = dot(probability, value).astype(jnp.bfloat16)

    contexts = plane_gather(
        jnp.concatenate([context[: tokens // 2], context[tokens // 2 :]], axis=1)
    )
    context_all = jnp.concatenate(
        [jnp.concatenate([x[:, :HDIM], x[:, HDIM:]], axis=0) for x in contexts], axis=1
    )
    attended = dot(context_all, out_columns)
    attended_mine = lax.dynamic_slice_in_dim(attended, ci * width, width, 1)
    attended_other = across_core(lax.dynamic_slice_in_dim(attended, (1 - ci) * width, width, 1))
    middle = (
        packed[:, 3 * HDIM :].astype(jnp.float32) + attended_mine + attended_other
    ).astype(jnp.bfloat16)

    blocks = jnp.stack(plane_gather(middle), axis=0)
    chips = jnp.arange(2 * nz, dtype=jnp.int32)
    middle_half = (
        jnp.take(blocks, ((zi - chips // 2) % nz) * 2 + (chips % 2 ^ yi), axis=0)
        .transpose(1, 0, 2)
        .reshape(tokens, half)
    )
    middle_values = middle_half.astype(jnp.float32)
    squares = jnp.sum(middle_values * middle_values, axis=-1, keepdims=True)
    gained = (middle_values * lax.dynamic_slice_in_dim(gain_ffn, own_half, half, 0)).astype(
        jnp.bfloat16
    )
    gate_up_value = by_rows(gained, gate_up_mine)
    gate_up_value_other = by_rows(gained, gate_up_other)

    def rows_of(core):
        chunks = jnp.arange(2 * nz, dtype=jnp.int32)
        device = ((zi + chunks // 2) % nz) * 4 + ((chunks % 2) ^ yi) * 2 + core
        row = jnp.minimum(jnp.arange(chunk_rows, dtype=jnp.int32), rows_here - 1)
        return (device[:, None] * rows_here + row[None, :]).reshape(-1)

    rows_mine, rows_other = rows_of(ci), rows_of(1 - ci)
    received = across_core(
        jnp.take(
            jnp.concatenate([gate_up_value_other, gate_up_value, squares], axis=1),
            rows_other,
            axis=0,
        )
    )
    summed = (
        jnp.take(
            jnp.concatenate([gate_up_value, gate_up_value_other, squares], axis=1),
            rows_mine,
            axis=0,
        )
        + received
    )
    summed = summed[:, :-1] * lax.rsqrt(summed[:, -1:] / features + 1e-06)
    parts = [summed[:, i * hidden_here : (i + 1) * hidden_here] for i in range(4)]
    gate_value = jnp.concatenate([parts[0], parts[2]], axis=1)
    up_value = jnp.concatenate([parts[1], parts[3]], axis=1)
    hidden = (jax.nn.gelu(gate_value, approximate=True) * up_value).astype(jnp.bfloat16)

    first_mine = me * rows_here
    kept = lax.dynamic_slice_in_dim(middle_half, first_mine, rows_here, 0)
    kept_other = across_core(
        lax.dynamic_slice_in_dim(middle_half, (me ^ 1) * rows_here, rows_here, 0)
    )
    kept_all = jnp.where(
        ci == 0,
        jnp.concatenate([kept, kept_other], axis=1),
        jnp.concatenate([kept_other, kept], axis=1),
    )

    result = dot(hidden, jnp.concatenate([down_weight, down_other], axis=0)).astype(jnp.bfloat16)
    result = result.reshape(nz, 2, chunk_rows, features)
    sums = {}
    for k in z_order + [0]:
        sums[k] = result[k, 0].astype(jnp.float32) + across_y(result[k, 1]).astype(jnp.float32)
    total = sums[0]
    for k in z_order:
        total = total + along_z(sums[k].astype(jnp.bfloat16), k).astype(jnp.float32)
    return (kept_all.astype(jnp.float32) + total[:rows_here]).astype(jnp.bfloat16)


def solution(mesh):
    placed = (
        P(("groups", "tensor"), None),
        P(("groups", "tensor"), None, None),
        P("groups", None),
        P("groups"),
        P("groups"),
        P("tensor", None),
        P("tensor", None),
        P("tensor", None),
        P("tensor", None),
        P(),
        P(),
        P("tensor", None),
        P("tensor", None),
        P("tensor", None),
    )
    return jax.shard_map(
        body, mesh=mesh, in_specs=placed, out_specs=P(("groups", "tensor"), None), check_vma=False
    )
```

time: 299 us -> 171 us (0.57)
  waiting for transfers between devices: 183 us -> 43.6 us
  blocking collectives: 49.4 us -> 0 us
  local copies, waits for them, and re-layouts: 15.4 us -> 53.5 us
  starting transfers between devices: 6.87 us -> 39.2 us
  between operations: 14 us -> 0.71 us
  other arithmetic: 12.5 us -> 23.4 us
  matrix products: 16.8 us -> 9.39 us
    psum x1 -> x0, waiting for transfers between devices: 106 us -> none  [body(): lax.psum(jnp.dot(context, out_weight, preferred_element_type=jnp.float32)...]
    all_gather x2 -> x0, waiting for transfers between devices: 71.1 us -> none  [the longest x1 41.7 us: body(): lax.all_gather(outgoing, 'tensor', axis=0, tiled=True)]
    unnamed x1 -> x0, blocking collectives: 49.4 us -> none
    ppermute x0 -> x39, waiting for transfers between devices: none -> 43.6 us  [the longest x17 20.9 us: across_y(): return lax.ppermute(value, AXIS, [(i, i ^ 2) for i in range(devices)])]
    ppermute x0 -> x39, starting transfers between devices: none -> 39.2 us  [the longest x15 21 us: along_z(): lax.ppermute(value, AXIS, [(i, (i + 4 * k) % devices) for i in range(devi...]
    concatenate x0 -> x9, local copies, waits for them, and re-layouts: none -> 23.4 us  [the longest x1 16 us: body(): stream = jnp.concatenate(plane_gather(piece), axis=0)]
    dot_general x4 -> x3, matrix products: 14.5 us -> 2.62 us  [dot(): return jnp.dot(left, right, preferred_element_type=jnp.float32)]
    unnamed x2 -> x0, starting transfers between devices: 6.79 us -> none
  transfers between devices with their start and end apart: 5 -> 39, of which waited for: 4 -> 21; matrix products, arithmetic and copies ran while one was open for 4% -> 45% of each run, Pallas kernels for 0% -> 0%
where the time goes in v1:
time: 171 us; the launch traced here: 170 us
  local copies, waits for them, and re-layouts  53.5 us (31%)
  waiting for transfers between devices  43.6 us (25%)
  starting transfers between devices  39.2 us (23%)
  other arithmetic  23.4 us (14%)
  matrix products  9.39 us (5%)
    ppermute x15, starting transfers between devices, along_z(): lax.ppermute(value, AXIS, [(i, (i + 4 * k) % devices) for i in range(devi...  21 us
    ppermute x17, waiting for transfers between devices, across_y(): return lax.ppermute(value, AXIS, [(i, i ^ 2) for i in range(devices)])  20.9 us
    ppermute x15, waiting for transfers between devices, along_z(): lax.ppermute(value, AXIS, [(i, (i + 4 * k) % devices) for i in range(devi...  19.1 us
    ppermute x17, starting transfers between devices, across_y(): return lax.ppermute(value, AXIS, [(i, i ^ 2) for i in range(devices)])  17.4 us
    concatenate x1, local copies, waits for them, and re-layouts, body(): stream = jnp.concatenate(plane_gather(piece), axis=0)  16 us
    unnamed x75, local copies, waits for them, and re-layouts  11.3 us
    dot_general x5, matrix products, by_rows(): lax.dot_general(left, weight, (((1,), (1,)), ((), ())), preferred_element...  6.78 us
    ppermute x7, waiting for transfers between devices, across_core(): return lax.ppermute(value, AXIS, [(i, i ^ 1) for i in range(devices)])  3.55 us
  transfers between devices with their start and end apart: 39, of which 21 were waited for; matrix products, arithmetic and copies ran while one was open for 45% of the time, Pallas kernels for 0%

profile of v1, /device:TPU:0, one launch (start us, length us, event | category | flops | bytes accessed | tf_op | source)
XLA Modules:
  0.0 169.8 jit_solution(6530999236501996711)
XLA Ops:
  3.4 1.6 pad_maximum_fusion.3
  5.0 3.0 %collective-permute-start.1 = (bf16[24,4096]{1,0:T(8,128)(2,1)}, bf16[24,4096]{1,0:T(8,128)(2,1)}, u32[]{:S(2)}, u32[]{:S(2)}) collective-permute-start(bf16[24,4096]{1,0:T(8,128)(2,1)} %pad_maximum_fusion.3), channel_id=1, source_target_pairs={{0,4},{1,5},{2,6},{3,7},{4,8},{5,9},{6,10},{7,11},{8,12},{9,13},{1... | collective-permute-start | bytes 589832 | tf_op jit(solution)/shard_map/ppermute | solution.py:46
  8.0 2.6 %collective-permute-start.3 = (bf16[24,4096]{1,0:T(8,128)(2,1)}, bf16[24,4096]{1,0:T(8,128)(2,1)}, u32[]{:S(2)}, u32[]{:S(2)}) collective-permute-start(bf16[24,4096]{1,0:T(8,128)(2,1)} %pad_maximum_fusion.3), channel_id=1, source_target_pairs={{0,8},{1,9},{2,10},{3,11},{4,12},{5,13},{6,14},{7,15},{8,0},{9,1},... | collective-permute-start | bytes 589832 | tf_op jit(solution)/shard_map/ppermute | solution.py:46
  10.6 1.3 collective-permute-start.5
  13.4 1.5 collective-permute-start.16
  15.8 1.9 %constant_dynamic-update-slice_fusion.1 = bf16[192,4096]{1,0:T(8,128)(2,1)} fusion(bf16[192,4096]{1,0:T(8,128)(2,1)} %constant_dynamic-update-slice_fusion.2, bf16[64,4096]{1,0:T(8,128)(2,1)} %param.22), kind=kLoop, calls=%fused_computation.97 | loop fusion | bytes 1048576
  21.4 1.3 broadcast_in_dim.90
  22.7 1.3 concatenate.185
  25.3 1.3 broadcast_in_dim.100
  26.6 1.4 reshape.562
  28.0 1.2 constant_dynamic-update-slice_fusion.15
  29.8 1.2 pad_add_fusion.2
  31.1 2.5 %constant_dynamic-update-slice_fusion.14 = bf16[320,4096]{1,0:T(8,128)(2,1)} fusion(bf16[320,4096]{1,0:T(8,128)(2,1)} %constant_dynamic-update-slice_fusion.15, bf16[160,4096]{1,0:T(8,128)(2,1)} %param.28), kind=kLoop, calls=%fused_computation.110 | loop fusion | bytes 2621440 | tf_op jit(solution)/shard_map/concatenate | solution.py:111
  33.7 2.7 %constant_dynamic-slice_fusion = bf16[320,2048]{1,0:T(8,128)(2,1)} fusion(bf16[320,4096]{1,0:T(8,128)(2,1)} %constant_dynamic-update-slice_fusion.14, s32[]{:T(128)S(6)} %select_n.464), kind=kLoop, calls=%fused_computation.117 | loop fusion | bytes 2621444 | tf_op jit(solution)/shard_map/dynamic_slice | solution.py:113
  37.2 1.0 fusion.83
  41.2 1.5 collective-permute-start.2
  42.7 8.1 %collective-permute-done.18 = bf16[128,512]{1,0:T(8,128)(2,1)} collective-permute-done((bf16[128,512]{1,0:T(8,128)(2,1)S(1)}, bf16[128,512]{1,0:T(8,128)(2,1)}, u32[]{:S(2)}, u32[]{:S(2)}) %collective-permute-start.18) | collective-permute-done | bytes 131104 | tf_op jit(solution)/shard_map/ppermute | solution.py:46
  51.3 1.5 collective-permute-start.6
  53.7 0.9 constant_dynamic-update-slice_fusion.12
  55.2 3.5 %collective-permute-done.4 = bf16[24,4096]{1,0:T(8,128)(2,1)S(1)} collective-permute-done((bf16[24,4096]{1,0:T(8,128)(2,1)}, bf16[24,4096]{1,0:T(8,128)(2,1)S(1)}, u32[]{:S(2)}, u32[]{:S(2)}) %collective-permute-start.4) | collective-permute-done | bytes 196640 | tf_op jit(solution)/shard_map/ppermute | solution.py:49
  58.7 1.5 collective-permute-start.19
  60.2 1.8 %collective-permute-done.6 = bf16[24,4096]{1,0:T(8,128)(2,1)} collective-permute-done((bf16[24,4096]{1,0:T(8,128)(2,1)}, bf16[24,4096]{1,0:T(8,128)(2,1)}, u32[]{:S(2)}, u32[]{:S(2)}) %collective-permute-start.6) | collective-permute-done | bytes 196640 | tf_op jit(solution)/shard_map/ppermute | solution.py:49
  62.0 16.0 %concatenate.179 = bf16[192,4096]{1,0:T(8,128)(2,1)} concatenate(bf16[8,4096]{1,0:T(8,128)(2,1)S(1)} %copy-done.10, bf16[12,4096]{1,0:T(8,128)(2,1)S(1)} %broadcast_select_fusion.3, bf16[4,4096]{1,0:T(4,128)(2,1)S(1)} %copy-done.9, bf16[24,4096]{1,0:T(8,128)(2,1)S(1)} %collective-permute-done, bf16[24,4096]{1,0:T(8,128)(2,1)} %collective-permute-done.1, ...), dimensions={0} | concatenate | bytes 3145728 | tf_op jit(solution)/shard_map/concatenate | solution.py:137
  78.0 1.1 constant_dynamic-slice_fusion.21
  79.1 1.8 %fusion = f32[192]{0:T(256)S(1)} fusion(bf16[192,4096]{1,0:T(8,128)(2,1)} %concatenate.179), kind=kLoop, calls=%fused_computation.8 | loop fusion | flops 2359104 | bytes 1573632 | tf_op jit(solution)/shard_map/reduce_sum | solution.py:139
  81.0 2.1 %convolution_convert_fusion.1 = bf16[192,192]{1,0:T(8,128)(2,1)S(1)} fusion(bf16[192,4096]{1,0:T(8,128)(2,1)} %collective-permute-done.7, bf16[192,4096]{1,0:T(8,128)(2,1)S(1)} %copy-done.1, f32[4096]{0:T(1024)S(1)} %copy-done.31, f32[192]{0:T(256)S(1)} %add_rsqrt_fusion), kind=kOutput, calls=%fused_computation.20 | convolution fusion | flops 305172480 | bytes 3236608 | tf_op jit(solution)/shard_map/dot_general | solution.py:14
  83.2 2.1 %convolution_convert_fusion.2 = bf16[192,192]{1,0:T(8,128)(2,1)S(1)} fusion(bf16[192,4096]{1,0:T(8,128)(2,1)} %constant_dynamic-update-slice_fusion, bf16[192,4096]{1,0:T(8,128)(2,1)S(1)} %copy-done.1, f32[4096]{0:T(1024)S(1)} %copy-done.31, f32[192]{0:T(256)S(1)} %add_rsqrt_fusion), kind=kOutput, calls=%fused_computation.21 | convolution fusion | flops 305172480 | bytes 3236608 | tf_op jit(solution)/shard_map/dot_general | solution.py:14
  85.4 1.2 gather_fusion.1
  89.8 1.2 collective-permute-start.12
  91.1 2.1 %collective-permute-done.10 = bf16[112,128]{0,1:T(8,128)(2,1)S(1)} collective-permute-done((bf16[112,128]{0,1:T(8,128)(2,1)S(1)}, bf16[112,128]{0,1:T(8,128)(2,1)S(1)}, u32[]{:S(2)}, u32[]{:S(2)}) %collective-permute-start.10) | collective-permute-done | bytes 28704 | tf_op jit(solution)/shard_map/ppermute | solution.py:46
  93.2 1.2 collective-permute-start.11
  95.0 1.5 collective-permute-start.13
  97.9 1.1 collective-permute-done.13
  99.1 2.0 %collective-permute-done.15 = bf16[112,128]{0,1:T(8,128)(2,1)S(1)} collective-permute-done((bf16[112,128]{0,1:T(8,128)(2,1)S(1)}, bf16[112,128]{0,1:T(8,128)(2,1)S(1)}, u32[]{:S(2)}, u32[]{:S(2)}) %collective-permute-start.15) | collective-permute-done | bytes 28704 | tf_op jit(solution)/shard_map/ppermute | solution.py:49
  101.8 1.4 collective-permute-done.20
  104.4 1.2 collective-permute-start.22
  105.6 1.9 %collective-permute-start.24 = (bf16[224,256]{1,0:T(8,128)(2,1)S(1)}, bf16[224,256]{1,0:T(8,128)(2,1)S(1)}, u32[]{:S(2)}, u32[]{:S(2)}) collective-permute-start(bf16[224,256]{1,0:T(8,128)(2,1)S(1)} %get-tuple-element.7), channel_id=1, source_target_pairs={{0,8},{1,9},{2,10},{3,11},{4,12},{5,13},{6,14},{7,15},{8,0},{9,1},... | collective-permute-start | bytes 344072 | tf_op jit(solution)/shard_map/ppermute | solution.py:46
  107.6 1.5 collective-permute-done.21
  109.1 2.4 %collective-permute-start.26 = (bf16[224,256]{1,0:T(8,128)(2,1)S(1)}, bf16[224,256]{1,0:T(8,128)(2,1)S(1)}, u32[]{:S(2)}, u32[]{:S(2)}) collective-permute-start(bf16[224,256]{1,0:T(8,128)(2,1)S(1)} %get-tuple-element.7), channel_id=1, source_target_pairs={{0,12},{1,13},{2,14},{3,15},{4,0},{5,1},{6,2},{7,3},{8,4},{9,5},{1... | collective-permute-start | bytes 344072 | tf_op jit(solution)/shard_map/ppermute | solution.py:46
  112.3 1.5 collective-permute-start.23
  115.1 1.1 collective-permute-done.24
  116.1 1.5 collective-permute-start.25
  119.5 2.7 %collective-permute-done.25 = bf16[224,256]{1,0:T(8,128)(2,1)S(1)} collective-permute-done((bf16[224,256]{1,0:T(8,128)(2,1)S(1)}, bf16[224,256]{1,0:T(8,128)(2,1)S(1)}, u32[]{:S(2)}, u32[]{:S(2)}) %collective-permute-start.25) | collective-permute-done | bytes 114720 | tf_op jit(solution)/shard_map/ppermute | solution.py:49
  124.2 1.8 %gather_fusion.2 = bf16[8,224,256]{2,1,0:T(8,128)(2,1)S(1)} fusion(bf16[8,224,256]{2,1,0:T(8,128)(2,1)} %bitcast_dynamic-update-slice_fusion, s32[1024]{0:T(1024)S(1)} %pad_clamp_fusion.2), kind=kCustom, calls=%fused_computation.4 | custom fusion | bytes 1835040 | tf_op jit(solution)/shard_map/jit(_take)/gather | solution.py:173
  126.7 1.6 copy-done.2
  128.8 1.8 %fusion.9 = f32[224,320]{0,1:T(8,128)S(1)} fusion(bf16[320,2048]{1,0:T(8,128)(2,1)} %collective-permute-done.29, bf16[224,2048]{1,0:T(8,128)(2,1)S(1)} %bitcast.68, f32[2048]{0:T(1024)S(1)} %dynamic_slice.97), kind=kOutput, calls=%fused_computation.26 | convolution fusion | flops 294977536 | bytes 2523136 | tf_op jit(solution)/shard_map/dot_general | solution.py:14
  130.7 1.0 pad_maximum_fusion.1
  131.6 1.3 copy.22
  133.0 1.6 gather_fusion.4
  134.6 1.9 %broadcast_select_fusion.2 = f32[128,641]{1,0:T(8,128)} fusion(f32[128,641]{1,0:T(8,128)} %gather_fusion.4, pred[128]{0:T(512)(128)(4,1)S(1)} %copy-done.29), kind=kLoop, calls=%fused_computation.61 | loop fusion | flops 82048 | bytes 656512 | tf_op jit(solution)/shard_map/jit(_take)/select_n | solution.py:193
  137.6 0.9 collective-permute-done.30
  138.5 1.1 select_add_fusion
  140.0 2.1 %convolution_convert_fusion = bf16[128,4096]{1,0:T(8,128)(2,1)S(1)} fusion(bf16[160,4096]{1,0:T(8,128)(2,1)} %collective-permute-done.31, bf16[160,4096]{1,0:T(8,128)(2,1)S(1)} %copy-done.30, f32[128,160]{1,0:T(8,128)S(1)} %get-tuple-element.40, f32[128,160]{1,0:T(8,128)S(1)} %get-tuple-element.41, f32[128,160]{1,0:T(8,128)S(1)} %get-tuple-element.39, ...), kind=kOutput, calls=%fused_computation.5 | convolution fusion | flops 341803008 | bytes 3997696 | tf_op jit(solution)/shard_map/dot_general | solution.py:20
  143.5 1.4 collective-permute-start.35
  145.5 1.4 collective-permute-start.32
  146.9 2.6 %collective-permute-done.33 = bf16[16,4096]{1,0:T(8,128)(2,1)} collective-permute-done((bf16[16,4096]{1,0:T(8,128)(2,1)}, bf16[16,4096]{1,0:T(8,128)(2,1)}, u32[]{:S(2)}, u32[]{:S(2)}) %collective-permute-start.33) | collective-permute-done | bytes 131104 | tf_op jit(solution)/shard_map/ppermute | solution.py:49
  149.5 2.8 %collective-permute-done.35 = bf16[16,4096]{1,0:T(8,128)(2,1)} collective-permute-done((bf16[16,4096]{1,0:T(8,128)(2,1)}, bf16[16,4096]{1,0:T(8,128)(2,1)}, u32[]{:S(2)}, u32[]{:S(2)}) %collective-permute-start.35) | collective-permute-done | bytes 131104 | tf_op jit(solution)/shard_map/ppermute | solution.py:49
  152.4 2.8 %collective-permute-done.37 = bf16[16,4096]{1,0:T(8,128)(2,1)} collective-permute-done((bf16[16,4096]{1,0:T(8,128)(2,1)}, bf16[16,4096]{1,0:T(8,128)(2,1)}, u32[]{:S(2)}, u32[]{:S(2)}) %collective-permute-start.37) | collective-permute-done | bytes 131104 | tf_op jit(solution)/shard_map/ppermute | solution.py:49
  155.2 1.8 %fusion.15 = (bf16[16,4096]{1,0:T(8,128)(2,1)}, bf16[16,4096]{1,0:T(8,128)(2,1)}, bf16[16,4096]{1,0:T(8,128)(2,1)}) fusion(bf16[16,4096]{1,0:T(8,128)(2,1)} %collective-permute-done.33, bf16[4,2,16,4096]{3,2,1,0:T(8,128)(2,1)S(1)} %bitcast.71, bf16[16,4096]{1,0:T(8,128)(2,1)} %collective-permute-done.37, bf16[16,4096]{1,0:T(8,128)(2,1)} %collective-permute-done.35), kind=kLoop, calls=%fused_computation.38 | loop fusion | flops 786432 | bytes 1179648 | tf_op jit(solution)/shard_map/convert_element_type | solution.py:231
  157.0 3.0 %collective-permute-start.36 = (bf16[16,4096]{1,0:T(8,128)(2,1)}, bf16[16,4096]{1,0:T(8,128)(2,1)S(1)}, u32[]{:S(2)}, u32[]{:S(2)}) collective-permute-start(bf16[16,4096]{1,0:T(8,128)(2,1)} %get-tuple-element.17), channel_id=1, source_target_pairs={{0,4},{1,5},{2,6},{3,7},{4,8},{5,9},{6,10},{7,11},{8,12},{9,13},{1... | collective-permute-start | bytes 393224 | tf_op jit(solution)/shard_map/ppermute | solution.py:46
  160.8 1.0 constant_dynamic-slice_fusion.2
  161.9 1.2 collective-permute-done.28
  163.1 4.6 %collective-permute-done.34 = bf16[16,4096]{1,0:T(8,128)(2,1)S(1)} collective-permute-done((bf16[16,4096]{1,0:T(8,128)(2,1)}, bf16[16,4096]{1,0:T(8,128)(2,1)S(1)}, u32[]{:S(2)}, u32[]{:S(2)}) %collective-permute-start.34) | collective-permute-done | bytes 131104 | tf_op jit(solution)/shard_map/ppermute | solution.py:46
  167.7 1.3 collective-permute-done.38
  (198 shorter events, 36.9 us)
Async XLA Ops:
  0.0 2.4 %copy-start = (bf16[64,4,4096]{2,1,0:T(4,128)(2,1)S(1)}, bf16[64,4,4096]{2,1,0:T(4,128)(2,1)}, u32[]{:S(2)}) copy-start(bf16[64,4,4096]{2,1,0:T(4,128)(2,1)} %param.17) | copy-start | bytes 6291460
  0.0 11.9 %copy-start.5 = (bf16[64,4096]{1,0:T(8,128)(2,1)S(1)}, bf16[64,4096]{1,0:T(8,128)(2,1)}, u32[]{:S(2)}) copy-start(bf16[64,4096]{1,0:T(8,128)(2,1)} %param.24) | copy-start | bytes 1572868
  3.4 9.3 %copy-start.8 = (bf16[4,4096]{1,0:T(4,128)(2,1)}, bf16[4,4096]{1,0:T(4,128)(2,1)S(1)}, u32[]{:S(2)}) copy-start(bf16[4,4096]{1,0:T(4,128)(2,1)S(1)} %broadcast_in_dim.98) | copy-start | bytes 98308
  5.0 34.3 %collective-permute-start.1 = (bf16[24,4096]{1,0:T(8,128)(2,1)}, bf16[24,4096]{1,0:T(8,128)(2,1)}, u32[]{:S(2)}, u32[]{:S(2)}) collective-permute-start(bf16[24,4096]{1,0:T(8,128)(2,1)} %pad_maximum_fusion.3), channel_id=1, source_target_pairs={{0,4},{1,5},{2,6},{3,7},{4,8},{5,9},{6,10},{7,11},{8,12},{9,13},{1... | collective-permute-start | bytes 589832 | tf_op jit(solution)/shard_map/ppermute | solution.py:46
  8.0 32.7 %collective-permute-start.3 = (bf16[24,4096]{1,0:T(8,128)(2,1)}, bf16[24,4096]{1,0:T(8,128)(2,1)}, u32[]{:S(2)}, u32[]{:S(2)}) collective-permute-start(bf16[24,4096]{1,0:T(8,128)(2,1)} %pad_maximum_fusion.3), channel_id=1, source_target_pairs={{0,8},{1,9},{2,10},{3,11},{4,12},{5,13},{6,14},{7,15},{8,0},{9,1},... | collective-permute-start | bytes 589832 | tf_op jit(solution)/shard_map/ppermute | solution.py:46
  10.6 30.6 %collective-permute-start.5 = (bf16[24,4096]{1,0:T(8,128)(2,1)}, bf16[24,4096]{1,0:T(8,128)(2,1)}, u32[]{:S(2)}, u32[]{:S(2)}) collective-permute-start(bf16[24,4096]{1,0:T(8,128)(2,1)} %pad_maximum_fusion.3), channel_id=1, source_target_pairs={{0,12},{1,13},{2,14},{3,15},{4,0},{5,1},{6,2},{7,3},{8,4},{9,5},{1... | collective-permute-start | bytes 589832 | tf_op jit(solution)/shard_map/ppermute | solution.py:46
  11.9 3.0 %copy-start.6 = (bf16[64,4096]{1,0:T(8,128)(2,1)S(1)}, bf16[64,4096]{1,0:T(8,128)(2,1)}, u32[]{:S(2)}) copy-start(bf16[64,4096]{1,0:T(8,128)(2,1)} %param.21) | copy-start | bytes 1572868
  12.6 5.0 %copy-start.7 = (bf16[64,4096]{1,0:T(8,128)(2,1)S(1)}, bf16[64,4096]{1,0:T(8,128)(2,1)}, u32[]{:S(2)}) copy-start(bf16[64,4096]{1,0:T(8,128)(2,1)} %param.23) | copy-start | bytes 1572868
  13.4 14.6 %copy-start.3 = (bf16[160,4096]{1,0:T(8,128)(2,1)S(1)}, bf16[160,4096]{1,0:T(8,128)(2,1)}, u32[]{:S(2)}) copy-start(bf16[160,4096]{1,0:T(8,128)(2,1)} %param.27) | copy-start | bytes 3932164
  13.4 23.8 %collective-permute-start.16 = (bf16[256,512]{1,0:T(8,128)(2,1)}, bf16[256,512]{1,0:T(8,128)(2,1)}, u32[]{:S(2)}, u32[]{:S(2)}) collective-permute-start(bf16[256,512]{1,0:T(8,128)(2,1)} %maximum_maximum_fusion), channel_id=1, source_target_pairs={{0,2},{1,3},{2,0},{3,1},{4,6},{5,7},{6,4},{7,5},{8,10},{9,11},{10,... | collective-permute-start | bytes 786440 | tf_op jit(solution)/shard_map/ppermute | solution.py:49
  18.5 62.4 %collective-permute-start.7 = (bf16[192,4096]{1,0:T(8,128)(2,1)}, bf16[192,4096]{1,0:T(8,128)(2,1)}, u32[]{:S(2)}, u32[]{:S(2)}) collective-permute-start(bf16[192,4096]{1,0:T(8,128)(2,1)} %constant_dynamic-update-slice_fusion), channel_id=1, source_target_pairs={{0,1},{1,0},{2,3},{3,2},{4,5},{5,4},{6,7},{7,6},{8,9},{9,8},{10,11... | collective-permute-start | bytes 4718600 | tf_op jit(solution)/shard_map/ppermute | solution.py:52
  33.6 2.9 %copy-start.19 = (s32[24,4]{1,0:T(8,128)S(1)}, s32[24,4]{1,0:T(8,128)}, u32[]{:S(2)}) copy-start(s32[24,4]{1,0:T(8,128)} %broadcast_in_dim.90) | copy-start | bytes 1156
  33.6 3.0 %copy-start.11 = (bf16[64,256]{1,0:T(8,128)(2,1)S(1)}, bf16[64,256]{1,0:T(8,128)(2,1)}, u32[]{:S(2)}) copy-start(bf16[64,256]{1,0:T(8,128)(2,1)} %get-tuple-element.35) | copy-start | bytes 98308
  33.6 3.0 %copy-start.12 = (bf16[64,256]{1,0:T(8,128)(2,1)S(1)}, bf16[64,256]{1,0:T(8,128)(2,1)}, u32[]{:S(2)}) copy-start(bf16[64,256]{1,0:T(8,128)(2,1)} %get-tuple-element.36) | copy-start | bytes 98308
  33.6 4.5 %copy-start.17 = (bf16[64,256]{1,0:T(8,128)(2,1)S(1)}, bf16[64,256]{1,0:T(8,128)(2,1)}, u32[]{:S(2)}) copy-start(bf16[64,256]{1,0:T(8,128)(2,1)} %get-tuple-element.23) | copy-start | bytes 98308
  33.6 4.5 %copy-start.18 = (bf16[64,256]{1,0:T(8,128)(2,1)S(1)}, bf16[64,256]{1,0:T(8,128)(2,1)}, u32[]{:S(2)}) copy-start(bf16[64,256]{1,0:T(8,128)(2,1)} %get-tuple-element.24) | copy-start | bytes 98308
  33.6 4.9 %copy-start.15 = (bf16[64,256]{1,0:T(8,128)(2,1)S(1)}, bf16[64,256]{1,0:T(8,128)(2,1)}, u32[]{:S(2)}) copy-start(bf16[64,256]{1,0:T(8,128)(2,1)} %get-tuple-element.25) | copy-start | bytes 98308
  33.6 4.9 %copy-start.16 = (bf16[64,256]{1,0:T(8,128)(2,1)S(1)}, bf16[64,256]{1,0:T(8,128)(2,1)}, u32[]{:S(2)}) copy-start(bf16[64,256]{1,0:T(8,128)(2,1)} %get-tuple-element.26) | copy-start | bytes 98308
  33.6 6.3 %copy-start.28 = (s32[128]{0:T(128)S(1)}, s32[128]{0:T(128)}, u32[]{:S(2)}) copy-start(s32[128]{0:T(128)} %get-tuple-element.71) | copy-start | bytes 1540
  33.7 6.3 %copy-start.13 = (bf16[64,256]{1,0:T(8,128)(2,1)S(1)}, bf16[64,256]{1,0:T(8,128)(2,1)}, u32[]{:S(2)}) copy-start(bf16[64,256]{1,0:T(8,128)(2,1)} %get-tuple-element.22) | copy-start | bytes 98308
  33.7 6.3 %copy-start.14 = (bf16[64,256]{1,0:T(8,128)(2,1)S(1)}, bf16[64,256]{1,0:T(8,128)(2,1)}, u32[]{:S(2)}) copy-start(bf16[64,256]{1,0:T(8,128)(2,1)} %get-tuple-element.37) | copy-start | bytes 98308
  36.4 25.6 %copy-start.9 = (bf16[4,4096]{1,0:T(4,128)(2,1)S(1)}, bf16[4,4096]{1,0:T(4,128)(2,1)}, u32[]{:S(2)}) copy-start(bf16[4,4096]{1,0:T(4,128)(2,1)} %copy-done.8) | copy-start | bytes 98308
  36.4 25.6 %copy-start.10 = (bf16[8,4096]{1,0:T(8,128)(2,1)S(1)}, bf16[8,4096]{1,0:T(8,128)(2,1)}, u32[]{:S(2)}) copy-start(bf16[8,4096]{1,0:T(8,128)(2,1)} %param.16) | copy-start | bytes 196612
  38.2 12.6 %collective-permute-start.18 = (bf16[128,512]{1,0:T(8,128)(2,1)S(1)}, bf16[128,512]{1,0:T(8,128)(2,1)}, u32[]{:S(2)}, u32[]{:S(2)}) collective-permute-start(bf16[128,512]{1,0:T(8,128)(2,1)S(1)} %pad_maximum_fusion.6), channel_id=1, source_target_pairs={{0,8},{1,9},{2,10},{3,11},{4,12},{5,13},{6,14},{7,15},{8,0},{9,1},... | collective-permute-start | bytes 393224 | tf_op jit(solution)/shard_map/ppermute | solution.py:46
  39.2 12.0 %collective-permute-start.17 = (bf16[128,512]{1,0:T(8,128)(2,1)}, bf16[128,512]{1,0:T(8,128)(2,1)}, u32[]{:S(2)}, u32[]{:S(2)}) collective-permute-start(bf16[128,512]{1,0:T(8,128)(2,1)} %pad_maximum_fusion.5), channel_id=1, source_target_pairs={{0,4},{1,5},{2,6},{3,7},{4,8},{5,9},{6,10},{7,11},{8,12},{9,13},{1... | collective-permute-start | bytes 393224 | tf_op jit(solution)/shard_map/ppermute | solution.py:46
  40.7 14.0 %collective-permute-start = (bf16[24,4096]{1,0:T(8,128)(2,1)}, bf16[24,4096]{1,0:T(8,128)(2,1)S(1)}, u32[]{:S(2)}, u32[]{:S(2)}) collective-permute-start(bf16[24,4096]{1,0:T(8,128)(2,1)} %pad_maximum_fusion.3), channel_id=1, source_target_pairs={{0,2},{1,3},{2,0},{3,1},{4,6},{5,7},{6,4},{7,5},{8,10},{9,11},{10,... | collective-permute-start | bytes 589832 | tf_op jit(solution)/shard_map/ppermute | solution.py:49
  41.2 13.5 %collective-permute-start.2 = (bf16[24,4096]{1,0:T(8,128)(2,1)}, bf16[24,4096]{1,0:T(8,128)(2,1)S(1)}, u32[]{:S(2)}, u32[]{:S(2)}) collective-permute-start(bf16[24,4096]{1,0:T(8,128)(2,1)} %collective-permute-done.1), channel_id=1, source_target_pairs={{0,2},{1,3},{2,0},{3,1},{4,6},{5,7},{6,4},{7,5},{8,10},{9,11},{10,... | collective-permute-start | bytes 589832 | tf_op jit(solution)/shard_map/ppermute | solution.py:49
  50.8 8.0 %collective-permute-start.4 = (bf16[24,4096]{1,0:T(8,128)(2,1)}, bf16[24,4096]{1,0:T(8,128)(2,1)S(1)}, u32[]{:S(2)}, u32[]{:S(2)}) collective-permute-start(bf16[24,4096]{1,0:T(8,128)(2,1)} %collective-permute-done.3), channel_id=1, source_target_pairs={{0,2},{1,3},{2,0},{3,1},{4,6},{5,7},{6,4},{7,5},{8,10},{9,11},{10,... | collective-permute-start | bytes 589832 | tf_op jit(solution)/shard_map/ppermute | solution.py:49
  51.3 10.7 %collective-permute-start.6 = (bf16[24,4096]{1,0:T(8,128)(2,1)}, bf16[24,4096]{1,0:T(8,128)(2,1)}, u32[]{:S(2)}, u32[]{:S(2)}) collective-permute-start(bf16[24,4096]{1,0:T(8,128)(2,1)} %collective-permute-done.5), channel_id=1, source_target_pairs={{0,2},{1,3},{2,0},{3,1},{4,6},{5,7},{6,4},{7,5},{8,10},{9,11},{10,... | collective-permute-start | bytes 589832 | tf_op jit(solution)/shard_map/ppermute | solution.py:49
  54.6 74.2 %collective-permute-start.29 = (bf16[320,2048]{1,0:T(8,128)(2,1)}, bf16[320,2048]{1,0:T(8,128)(2,1)}, u32[]{:S(2)}, u32[]{:S(2)}) collective-permute-start(bf16[320,2048]{1,0:T(8,128)(2,1)} %constant_dynamic-slice_fusion), channel_id=1, source_target_pairs={{0,1},{1,0},{2,3},{3,2},{4,5},{5,4},{6,7},{7,6},{8,9},{9,8},{10,11... | collective-permute-start | bytes 3932168 | tf_op jit(solution)/shard_map/ppermute | solution.py:52
  54.7 85.3 %collective-permute-start.31 = (bf16[160,4096]{1,0:T(8,128)(2,1)}, bf16[160,4096]{1,0:T(8,128)(2,1)}, u32[]{:S(2)}, u32[]{:S(2)}) collective-permute-start(bf16[160,4096]{1,0:T(8,128)(2,1)} %param.29), channel_id=1, source_target_pairs={{0,1},{1,0},{2,3},{3,2},{4,5},{5,4},{6,7},{7,6},{8,9},{9,8},{10,11... | collective-permute-start | bytes 3932168 | tf_op jit(solution)/shard_map/ppermute | solution.py:52
  58.7 29.6 %collective-permute-start.19 = (bf16[128,512]{1,0:T(8,128)(2,1)}, bf16[128,512]{1,0:T(8,128)(2,1)}, u32[]{:S(2)}, u32[]{:S(2)}) collective-permute-start(bf16[128,512]{1,0:T(8,128)(2,1)} %pad_maximum_fusion.7), channel_id=1, source_target_pairs={{0,12},{1,13},{2,14},{3,15},{4,0},{5,1},{6,2},{7,3},{8,4},{9,5},{1... | collective-permute-start | bytes 393224 | tf_op jit(solution)/shard_map/ppermute | solution.py:46
  78.0 2.9 %copy-start.1 = (bf16[192,4096]{1,0:T(8,128)(2,1)S(1)}, bf16[192,4096]{1,0:T(8,128)(2,1)}, u32[]{:S(2)}) copy-start(bf16[192,4096]{1,0:T(8,128)(2,1)} %concatenate.179) | copy-start | bytes 4718596
  78.0 2.9 %copy-start.31 = (f32[4096]{0:T(1024)S(1)}, f32[4096]{0:T(1024)}, u32[]{:S(2)}) copy-start(f32[4096]{0:T(1024)} %param.25) | copy-start | bytes 49156
  83.1 2.2 %collective-permute-start.8 = (bf16[192,448]{1,0:T(8,128)(2,1)S(1)}, bf16[192,448]{1,0:T(8,128)(2,1)S(1)}, u32[]{:S(2)}, u32[]{:S(2)}) collective-permute-start(bf16[192,448]{1,0:T(8,128)(2,1)S(1)} %pad_maximum_fusion.4), channel_id=1, source_target_pairs={{0,1},{1,0},{2,3},{3,2},{4,5},{5,4},{6,7},{7,6},{8,9},{9,8},{10,11... | collective-permute-start | bytes 516104 | tf_op jit(solution)/shard_map/ppermute | solution.py:52
  87.3 14.3 %copy-start.26 = (s32[8]{0:T(128)S(1)}, s32[8]{0:T(128)}, u32[]{:S(2)}) copy-start(s32[8]{0:T(128)} %fusion.71) | copy-start | bytes 100
  87.3 14.4 %copy-start.22 = (s32[128]{0:T(128)S(1)}, s32[128]{0:T(128)}, u32[]{:S(2)}) copy-start(s32[128]{0:T(128)} %copy-done.21) | copy-start | bytes 1540
  87.4 5.8 %collective-permute-start.10 = (bf16[112,128]{0,1:T(8,128)(2,1)S(1)}, bf16[112,128]{0,1:T(8,128)(2,1)S(1)}, u32[]{:S(2)}, u32[]{:S(2)}) collective-permute-start(bf16[112,128]{0,1:T(8,128)(2,1)S(1)} %pad_maximum_fusion.8), channel_id=1, source_target_pairs={{0,4},{1,5},{2,6},{3,7},{4,8},{5,9},{6,10},{7,11},{8,12},{9,13},{1... | collective-permute-start | bytes 86024 | tf_op jit(solution)/shard_map/ppermute | solution.py:46
  89.3 4.0 %collective-permute-start.9 = (bf16[112,128]{0,1:T(8,128)(2,1)S(1)}, bf16[112,128]{0,1:T(8,128)(2,1)S(1)}, u32[]{:S(2)}, u32[]{:S(2)}) collective-permute-start(bf16[112,128]{0,1:T(8,128)(2,1)S(1)} %pad_maximum_fusion.8), channel_id=1, source_target_pairs={{0,2},{1,3},{2,0},{3,1},{4,6},{5,7},{6,4},{7,5},{8,10},{9,11},{10,... | collective-permute-start | bytes 86024 | tf_op jit(solution)/shard_map/ppermute | solution.py:49
  89.8 5.1 %collective-permute-start.12 = (bf16[112,128]{0,1:T(8,128)(2,1)S(1)}, bf16[112,128]{0,1:T(8,128)(2,1)S(1)}, u32[]{:S(2)}, u32[]{:S(2)}) collective-permute-start(bf16[112,128]{0,1:T(8,128)(2,1)S(1)} %pad_maximum_fusion.8), channel_id=1, source_target_pairs={{0,8},{1,9},{2,10},{3,11},{4,12},{5,13},{6,14},{7,15},{8,0},{9,1},... | collective-permute-start | bytes 86024 | tf_op jit(solution)/shard_map/ppermute | solution.py:46
  93.2 3.9 %collective-permute-start.14 = (bf16[112,128]{0,1:T(8,128)(2,1)S(1)}, bf16[112,128]{0,1:T(8,128)(2,1)S(1)}, u32[]{:S(2)}, u32[]{:S(2)}) collective-permute-start(bf16[112,128]{0,1:T(8,128)(2,1)S(1)} %pad_maximum_fusion.8), channel_id=1, source_target_pairs={{0,12},{1,13},{2,14},{3,15},{4,0},{5,1},{6,2},{7,3},{8,4},{9,5},{1... | collective-permute-start | bytes 86024 | tf_op jit(solution)/shard_map/ppermute | solution.py:46
  93.2 4.5 %collective-permute-start.11 = (bf16[112,128]{0,1:T(8,128)(2,1)S(1)}, bf16[112,128]{0,1:T(8,128)(2,1)S(1)}, u32[]{:S(2)}, u32[]{:S(2)}) collective-permute-start(bf16[112,128]{0,1:T(8,128)(2,1)S(1)} %collective-permute-done.10), channel_id=1, source_target_pairs={{0,2},{1,3},{2,0},{3,1},{4,6},{5,7},{6,4},{7,5},{8,10},{9,11},{10,... | collective-permute-start | bytes 86024 | tf_op jit(solution)/shard_map/ppermute | solution.py:49
  95.0 4.0 %collective-permute-start.13 = (bf16[112,128]{0,1:T(8,128)(2,1)S(1)}, bf16[112,128]{0,1:T(8,128)(2,1)S(1)}, u32[]{:S(2)}, u32[]{:S(2)}) collective-permute-start(bf16[112,128]{0,1:T(8,128)(2,1)S(1)} %collective-permute-done.12), channel_id=1, source_target_pairs={{0,2},{1,3},{2,0},{3,1},{4,6},{5,7},{6,4},{7,5},{8,10},{9,11},{10,... | collective-permute-start | bytes 86024 | tf_op jit(solution)/shard_map/ppermute | solution.py:49
  97.1 8.5 %copy-start.20 = (f32[4096]{0:T(1024)S(1)}, f32[4096]{0:T(1024)}, u32[]{:S(2)}) copy-start(f32[4096]{0:T(1024)} %param.26) | copy-start | bytes 49156
  97.2 3.9 %collective-permute-start.15 = (bf16[112,128]{0,1:T(8,128)(2,1)S(1)}, bf16[112,128]{0,1:T(8,128)(2,1)S(1)}, u32[]{:S(2)}, u32[]{:S(2)}) collective-permute-start(bf16[112,128]{0,1:T(8,128)(2,1)S(1)} %collective-permute-done.14), channel_id=1, source_target_pairs={{0,2},{1,3},{2,0},{3,1},{4,6},{5,7},{6,4},{7,5},{8,10},{9,11},{10,... | collective-permute-start | bytes 86024 | tf_op jit(solution)/shard_map/ppermute | solution.py:49
  101.6 1.6 collective-permute-start.20
  103.9 5.2 %collective-permute-start.21 = (bf16[224,256]{1,0:T(8,128)(2,1)S(1)}, bf16[224,256]{1,0:T(8,128)(2,1)S(1)}, u32[]{:S(2)}, u32[]{:S(2)}) collective-permute-start(bf16[224,256]{1,0:T(8,128)(2,1)S(1)} %get-tuple-element.7), channel_id=1, source_target_pairs={{0,2},{1,3},{2,0},{3,1},{4,6},{5,7},{6,4},{7,5},{8,10},{9,11},{10,... | collective-permute-start | bytes 344072 | tf_op jit(solution)/shard_map/ppermute | solution.py:49
  104.4 7.9 %collective-permute-start.22 = (bf16[224,256]{1,0:T(8,128)(2,1)S(1)}, bf16[224,256]{1,0:T(8,128)(2,1)S(1)}, u32[]{:S(2)}, u32[]{:S(2)}) collective-permute-start(bf16[224,256]{1,0:T(8,128)(2,1)S(1)} %get-tuple-element.7), channel_id=1, source_target_pairs={{0,4},{1,5},{2,6},{3,7},{4,8},{5,9},{6,10},{7,11},{8,12},{9,13},{1... | collective-permute-start | bytes 344072 | tf_op jit(solution)/shard_map/ppermute | solution.py:46
  105.6 10.5 %collective-permute-start.24 = (bf16[224,256]{1,0:T(8,128)(2,1)S(1)}, bf16[224,256]{1,0:T(8,128)(2,1)S(1)}, u32[]{:S(2)}, u32[]{:S(2)}) collective-permute-start(bf16[224,256]{1,0:T(8,128)(2,1)S(1)} %get-tuple-element.7), channel_id=1, source_target_pairs={{0,8},{1,9},{2,10},{3,11},{4,12},{5,13},{6,14},{7,15},{8,0},{9,1},... | collective-permute-start | bytes 344072 | tf_op jit(solution)/shard_map/ppermute | solution.py:46
  109.1 8.6 %collective-permute-start.26 = (bf16[224,256]{1,0:T(8,128)(2,1)S(1)}, bf16[224,256]{1,0:T(8,128)(2,1)S(1)}, u32[]{:S(2)}, u32[]{:S(2)}) collective-permute-start(bf16[224,256]{1,0:T(8,128)(2,1)S(1)} %get-tuple-element.7), channel_id=1, source_target_pairs={{0,12},{1,13},{2,14},{3,15},{4,0},{5,1},{6,2},{7,3},{8,4},{9,5},{1... | collective-permute-start | bytes 344072 | tf_op jit(solution)/shard_map/ppermute | solution.py:46
  112.3 5.9 %collective-permute-start.23 = (bf16[224,256]{1,0:T(8,128)(2,1)S(1)}, bf16[224,256]{1,0:T(8,128)(2,1)S(1)}, u32[]{:S(2)}, u32[]{:S(2)}) collective-permute-start(bf16[224,256]{1,0:T(8,128)(2,1)S(1)} %collective-permute-done.22), channel_id=1, source_target_pairs={{0,2},{1,3},{2,0},{3,1},{4,6},{5,7},{6,4},{7,5},{8,10},{9,11},{10,... | collective-permute-start | bytes 344072 | tf_op jit(solution)/shard_map/ppermute | solution.py:49
  116.1 6.0 %collective-permute-start.25 = (bf16[224,256]{1,0:T(8,128)(2,1)S(1)}, bf16[224,256]{1,0:T(8,128)(2,1)S(1)}, u32[]{:S(2)}, u32[]{:S(2)}) collective-permute-start(bf16[224,256]{1,0:T(8,128)(2,1)S(1)} %collective-permute-done.24), channel_id=1, source_target_pairs={{0,2},{1,3},{2,0},{3,1},{4,6},{5,7},{6,4},{7,5},{8,10},{9,11},{10,... | collective-permute-start | bytes 344072 | tf_op jit(solution)/shard_map/ppermute | solution.py:49
  117.7 5.9 %collective-permute-start.27 = (bf16[224,256]{1,0:T(8,128)(2,1)S(1)}, bf16[224,256]{1,0:T(8,128)(2,1)S(1)}, u32[]{:S(2)}, u32[]{:S(2)}) collective-permute-start(bf16[224,256]{1,0:T(8,128)(2,1)S(1)} %collective-permute-done.26), channel_id=1, source_target_pairs={{0,2},{1,3},{2,0},{3,1},{4,6},{5,7},{6,4},{7,5},{8,10},{9,11},{10,... | collective-permute-start | bytes 344072 | tf_op jit(solution)/shard_map/ppermute | solution.py:49
  126.3 2.5 %copy-start.4 = (bf16[8,28,8,256]{3,2,0,1:T(8,128)(2,1)}, bf16[8,28,8,256]{3,2,0,1:T(8,128)(2,1)S(1)}, u32[]{:S(2)}) copy-start(bf16[8,28,8,256]{3,2,0,1:T(8,128)(2,1)S(1)} %copy.23) | copy-start | bytes 2752516
  136.4 2.1 %collective-permute-start.30 = (f32[128,641]{1,0:T(8,128)}, f32[128,641]{1,0:T(8,128)}, u32[]{:S(2)}, u32[]{:S(2)}) collective-permute-start(f32[128,641]{1,0:T(8,128)} %broadcast_select_fusion.2), channel_id=1, source_target_pairs={{0,1},{1,0},{2,3},{3,2},{4,5},{5,4},{6,7},{7,6},{8,9},{9,8},{10,11... | collective-permute-start | bytes 984584 | tf_op jit(solution)/shard_map/ppermute | solution.py:52
  137.5 2.5 %copy-start.30 = (bf16[160,4096]{1,0:T(8,128)(2,1)S(1)}, bf16[160,4096]{1,0:T(8,128)(2,1)}, u32[]{:S(2)}) copy-start(bf16[160,4096]{1,0:T(8,128)(2,1)} %param.29) | copy-start | bytes 3932164
  142.9 6.7 %collective-permute-start.33 = (bf16[16,4096]{1,0:T(8,128)(2,1)}, bf16[16,4096]{1,0:T(8,128)(2,1)}, u32[]{:S(2)}, u32[]{:S(2)}) collective-permute-start(bf16[16,4096]{1,0:T(8,128)(2,1)} %get-tuple-element.13), channel_id=1, source_target_pairs={{0,2},{1,3},{2,0},{3,1},{4,6},{5,7},{6,4},{7,5},{8,10},{9,11},{10,... | collective-permute-start | bytes 393224 | tf_op jit(solution)/shard_map/ppermute | solution.py:49
  143.5 8.9 %collective-permute-start.35 = (bf16[16,4096]{1,0:T(8,128)(2,1)}, bf16[16,4096]{1,0:T(8,128)(2,1)}, u32[]{:S(2)}, u32[]{:S(2)}) collective-permute-start(bf16[16,4096]{1,0:T(8,128)(2,1)} %get-tuple-element.12), channel_id=1, source_target_pairs={{0,2},{1,3},{2,0},{3,1},{4,6},{5,7},{6,4},{7,5},{8,10},{9,11},{10,... | collective-permute-start | bytes 393224 | tf_op jit(solution)/shard_map/ppermute | solution.py:49
  144.9 10.3 %collective-permute-start.37 = (bf16[16,4096]{1,0:T(8,128)(2,1)}, bf16[16,4096]{1,0:T(8,128)(2,1)}, u32[]{:S(2)}, u32[]{:S(2)}) collective-permute-start(bf16[16,4096]{1,0:T(8,128)(2,1)} %get-tuple-element.11), channel_id=1, source_target_pairs={{0,2},{1,3},{2,0},{3,1},{4,6},{5,7},{6,4},{7,5},{8,10},{9,11},{10,... | collective-permute-start | bytes 393224 | tf_op jit(solution)/shard_map/ppermute | solution.py:49
  145.5 17.6 %collective-permute-start.32 = (bf16[16,4096]{1,0:T(8,128)(2,1)S(1)}, bf16[16,4096]{1,0:T(8,128)(2,1)S(1)}, u32[]{:S(2)}, u32[]{:S(2)}) collective-permute-start(bf16[16,4096]{1,0:T(8,128)(2,1)S(1)} %get-tuple-element.10), channel_id=1, source_target_pairs={{0,2},{1,3},{2,0},{3,1},{4,6},{5,7},{6,4},{7,5},{8,10},{9,11},{10,... | collective-permute-start | bytes 393224 | tf_op jit(solution)/shard_map/ppermute | solution.py:49
  157.0 10.7 %collective-permute-start.34 = (bf16[16,4096]{1,0:T(8,128)(2,1)}, bf16[16,4096]{1,0:T(8,128)(2,1)S(1)}, u32[]{:S(2)}, u32[]{:S(2)}) collective-permute-start(bf16[16,4096]{1,0:T(8,128)(2,1)} %get-tuple-element.15), channel_id=1, source_target_pairs={{0,8},{1,9},{2,10},{3,11},{4,12},{5,13},{6,14},{7,15},{8,0},{9,1},... | collective-permute-start | bytes 393224 | tf_op jit(solution)/shard_map/ppermute | solution.py:46
  157.0 10.7 %collective-permute-start.36 = (bf16[16,4096]{1,0:T(8,128)(2,1)}, bf16[16,4096]{1,0:T(8,128)(2,1)S(1)}, u32[]{:S(2)}, u32[]{:S(2)}) collective-permute-start(bf16[16,4096]{1,0:T(8,128)(2,1)} %get-tuple-element.17), channel_id=1, source_target_pairs={{0,4},{1,5},{2,6},{3,7},{4,8},{5,9},{6,10},{7,11},{8,12},{9,13},{1... | collective-permute-start | bytes 393224 | tf_op jit(solution)/shard_map/ppermute | solution.py:46
  160.0 9.0 %collective-permute-start.38 = (bf16[16,4096]{1,0:T(8,128)(2,1)}, bf16[16,4096]{1,0:T(8,128)(2,1)S(1)}, u32[]{:S(2)}, u32[]{:S(2)}) collective-permute-start(bf16[16,4096]{1,0:T(8,128)(2,1)} %get-tuple-element.16), channel_id=1, source_target_pairs={{0,12},{1,13},{2,14},{3,15},{4,0},{5,1},{6,2},{7,3},{8,4},{9,5},{1... | collective-permute-start | bytes 393224 | tf_op jit(solution)/shard_map/ppermute | solution.py:46
  161.8 1.3 collective-permute-start.28
  (7 other events, 10.5 us)

commit v2 on v0

v2 whole, which is shorter than its diff:
```python
import functools

import jax
import jax.numpy as jnp
from jax import lax
from jax.experimental import pallas as pl
from jax.experimental.pallas import tpu as pltpu
from jax.sharding import PartitionSpec as P

HDIM = 64
QLEN = 32
BLK = 4
CAP = 3
AXIS = "tensor"
VMEM_LIMIT = 60 * 1024 * 1024


def by_rows(left, weight):
    return lax.dot_general(
        left, weight, (((1,), (1,)), ((), ())), preferred_element_type=jnp.float32
    )


def dot(left, right):
    return jnp.dot(left, right, preferred_element_type=jnp.float32)


def place():
    me = lax.axis_index(AXIS)
    return me, me // 4, (me // 2) % 2, me % 2


def kernel_call(kernel, out_shape, in_specs, scratch=(), name=None):
    return pl.pallas_call(
        kernel,
        out_shape=out_shape,
        in_specs=in_specs,
        out_specs=jax.tree.map(lambda _: pl.BlockSpec(memory_space=pltpu.VMEM), out_shape),
        scratch_shapes=scratch,
        compiler_params=pltpu.CompilerParams(vmem_limit_bytes=VMEM_LIMIT),
        name=name,
    )


SMEM = pl.BlockSpec(memory_space=pltpu.SMEM)
VMEM = pl.BlockSpec(memory_space=pltpu.VMEM)
ANY = pl.BlockSpec(memory_space=pl.ANY)


def piece_layout(rows):
    full, rest = divmod(rows, 8)
    if 0 < rest <= 4:
        return full, True
    return full + (rest > 0), False


def fetch_kernel(owner_ref, row_ref, corpus_ref, query_ref, piece_ref, blocks, rows, sems):
    me = place()[0]
    features = query_ref.shape[1]
    query_rows = query_ref.shape[0]

    def look(b, carry):
        count, found = carry[0], carry[1:]
        mine = owner_ref[b] == me
        found = tuple(
            jnp.where(mine & (count == k), row_ref[b], found[k]) for k in range(CAP)
        )
        return (count + mine.astype(jnp.int32),) + found

    zero = jnp.int32(0)
    found = lax.fori_loop(0, owner_ref.shape[0], look, (zero,) * (CAP + 1))[1:]
    copies = [
        pltpu.make_async_copy(corpus_ref.at[found[k]], blocks.at[k], sems.at[k])
        for k in range(CAP)
    ]
    for copy in copies:
        copy.start()
    total = query_rows + CAP * BLK
    full, halved = piece_layout(total)
    rows[0:query_rows, :] = query_ref[...].astype(jnp.float32)
    for k in range(CAP):
        copies[k].wait()
        first = query_rows + k * BLK
        rows[first : first + BLK, :] = blocks[k].astype(jnp.float32)
    if not halved and total < full * 8:
        rows[total : full * 8, :] = jnp.zeros((full * 8 - total, features), jnp.float32)
    for i in range(full):
        piece_ref[:, i * features : (i + 1) * features] = rows[i * 8 : i * 8 + 8, :].astype(
            jnp.bfloat16
        )
    if halved:
        half = features // 2
        last = rows[full * 8 : full * 8 + 4, :]
        if total % 8 < 4:
            last = jnp.where(
                lax.broadcasted_iota(jnp.int32, last.shape, 0) < total % 8, last, 0.0
            )
        piece_ref[:, full * features :] = jnp.concatenate(
            [last[:, :half], last[:, half:]], axis=0
        ).astype(jnp.bfloat16)


def columns_at(ref, start, width):
    if width % 128 == 0:
        return ref[:, pl.ds(pl.multiple_of(start, 128), width)].astype(jnp.float32)
    base = pl.multiple_of(start // 128 * 128, 128)
    window = ref[:, pl.ds(base, 128)].astype(jnp.float32)
    return pltpu.roll(window, (128 - start % 128) % 128, 1)[:, :width]


def projection_kernel(piece_rows, *refs):
    count = len(refs) - 10
    pieces, rest = refs[:count], refs[count:]
    gain_ref, mine, other, out_ref, out_other_ref, normal = (
        rest[0],
        rest[1:4],
        rest[4:7],
        rest[7],
        rest[8],
        rest[9],
    )
    _, zi, yi, ci = place()
    features = gain_ref.shape[1]
    half = features // 2
    full, halved = piece_layout(piece_rows)
    width = features // lax.axis_size(AXIS)
    chip = 2 * zi + yi
    gain = gain_ref[...]
    spot = 256
    own_column = ci * half + chip * width
    other_column = (1 - ci) * half + chip * width

    def scaled(values, squares):
        return values * lax.rsqrt(squares / features + 1e-06)

    def put(row, groups):
        normal[row : row + 16, :] = jnp.concatenate(groups, axis=0).astype(jnp.bfloat16)

    chunks = [(p, i) for p in range(count) for i in range(full)]
    for first in range(0, len(chunks), 2):
        groups, own, away = [], [], []
        for p, i in chunks[first : first + 2]:
            values = pieces[p][:, i * features : (i + 1) * features].astype(jnp.float32)
            squares = jnp.sum(values * values, axis=-1, keepdims=True)
            groups.append(scaled(values, squares) * gain)
            own.append(columns_at(pieces[p], i * features + own_column, width))
            away.append(columns_at(pieces[p], i * features + other_column, width))
        row = first * 8
        put(row, groups)
        out_ref[row : row + 16, spot : spot + width] = jnp.concatenate(own, axis=0).astype(
            jnp.bfloat16
        )
        out_other_ref[row : row + 16, spot : spot + width] = jnp.concatenate(
            away, axis=0
        ).astype(jnp.bfloat16)
    if halved:
        for first in range(0, count, 4):
            groups, own, away = [], [], []
            for p in range(first, first + 4, 2):
                a, b = (
                    pieces[q][:, full * features :].astype(jnp.float32) for q in (p, p + 1)
                )
                low = jnp.concatenate([a[0:4], b[0:4]], axis=0)
                high = jnp.concatenate([a[4:8], b[4:8]], axis=0)
                squares = jnp.sum(low * low, axis=-1, keepdims=True) + jnp.sum(
                    high * high, axis=-1, keepdims=True
                )
                groups.append(
                    jnp.concatenate([scaled(low, squares), scaled(high, squares)], axis=1)
                    * gain
                )
                a, b = (
                    columns_at(pieces[q], full * features + chip * width, width)
                    for q in (p, p + 1)
                )
                low = jnp.concatenate([a[0:4], b[0:4]], axis=0)
                high = jnp.concatenate([a[4:8], b[4:8]], axis=0)
                own.append(jnp.where(ci == 0, low, high))
                away.append(jnp.where(ci == 0, high, low))
            row = len(chunks) * 8 + first * 4
            put(row, groups)
            out_ref[row : row + 16, spot : spot + width] = jnp.concatenate(
                own, axis=0
            ).astype(jnp.bfloat16)
            out_other_ref[row : row + 16, spot : spot + width] = jnp.concatenate(
                away, axis=0
            ).astype(jnp.bfloat16)
    rows = normal[...]
    for target, weights in ((out_other_ref, other), (out_ref, mine)):
        value = jnp.concatenate([by_rows(rows, w[...]) for w in weights], axis=1)
        target[:, 0 : value.shape[1]] = value.astype(jnp.bfloat16)


def attention_kernel(query_rows, width, owner_ref, segment_ref, own_ref, away_ref, ctx_ref, col_ref):
    _, zi, yi, ci = place()
    nz = lax.axis_size(AXIS) // 4
    query_total = query_rows * 4 * nz
    blocks_total = owner_ref.shape[0]
    tokens = query_total + blocks_total * BLK
    piece_rows = query_rows + CAP * BLK
    full, halved = piece_layout(piece_rows)
    plane_rows = own_ref.shape[0]

    def lay(shape, axis):
        token = lax.broadcasted_iota(jnp.int32, shape, axis)
        block = (token - query_total) // BLK
        is_query = token < query_total
        owner = jnp.where(is_query, token // query_rows, 0)
        pair = jnp.where(is_query, token // QLEN, 0)

        def fill(b, carry):
            here = (block == b) & (token >= query_total)
            return (
                jnp.where(here, owner_ref[b], carry[0]),
                jnp.where(here, segment_ref[b], carry[1]),
            )

        owner, pair = lax.fori_loop(0, blocks_total, fill, (owner, pair))
        return token, block, owner, pair

    token, block, owner, pair = lay((tokens, 1), 0)
    token_row, block_row, owner_row, pair_row = lay((1, tokens), 1)
    ahead = (
        (owner == owner_row)
        & (block_row < block)
        & (token_row >= query_total)
        & (token >= query_total)
    )
    before = jnp.sum(ahead.astype(jnp.float32), axis=-1, keepdims=True).astype(jnp.int32)
    local = jnp.where(
        token < query_total,
        token % query_rows,
        query_rows + before + (token - query_total) % BLK,
    )
    source = ((zi - owner // 4 + 4 * nz) % nz) * 2 + (((owner // 2) % 2) ^ yi)
    pieces = 2 * nz
    spot = source * (full * 8) + local
    if halved:
        spot = jnp.where(
            local < full * 8, spot, pieces * full * 8 + source * 4 + local - full * 8
        )
    spot = spot + ((owner % 2) ^ ci) * plane_rows
    lanes = lax.broadcasted_iota(jnp.int32, (tokens, plane_rows), 1)
    pick_own = (lanes == spot).astype(jnp.bfloat16)
    pick_away = (lanes == spot - plane_rows).astype(jnp.bfloat16)
    packed = dot(pick_own, own_ref[...]) + dot(pick_away, away_ref[...])
    col_ref[...] = packed[:, 256 : 256 + width].astype(jnp.bfloat16)
    query, key, value = (
        packed[:, i * HDIM : (i + 1) * HDIM].astype(jnp.bfloat16) for i in range(3)
    )
    scores = by_rows(query, key) * HDIM ** (-0.5)
    scores = jnp.where(pair == pair_row, scores, -1e30)
    weights = jnp.exp(scores - jnp.max(scores, axis=-1, keepdims=True))
    probability = (weights / jnp.sum(weights, axis=-1, keepdims=True)).astype(jnp.bfloat16)
    context = dot(probability, value)
    ctx_ref[...] = jnp.concatenate(
        [context[: tokens // 2], context[tokens // 2 :]], axis=1
    ).astype(jnp.bfloat16)


def gate_kernel(rows_here, chunk_rows, *refs):
    count = len(refs) - 11
    pieces = refs[:count]
    (
        gain_ref,
        gate_ref,
        up_ref,
        gate_other_ref,
        up_other_ref,
        keep_ref,
        send_ref,
        kept_ref,
        kept_send_ref,
        order_ref,
        rows_ref,
    ) = refs[count:]
    _, zi, yi, ci = place()
    nz = lax.axis_size(AXIS) // 4
    tokens, width = pieces[0].shape
    half = 2 * nz * width
    total = order_ref.shape[0]
    slots = total // 2
    row = lax.broadcasted_iota(jnp.int32, (total, 1), 0)
    core = jnp.where(row < slots, ci, 1 - ci)
    chunk = (row % slots) // chunk_rows
    device = ((zi + chunk // 2) % nz) * 4 + ((chunk % 2) ^ yi) * 2 + core
    wanted = device * rows_here + jnp.minimum(row % chunk_rows, rows_here - 1)
    lanes = lax.broadcasted_iota(jnp.int32, (total, tokens), 1)
    order_ref[...] = (lanes == wanted).astype(jnp.bfloat16)
    squares = jnp.zeros((total, 1), jnp.float32)
    for dz in range(nz):
        near, far = pieces[2 * dz][...], pieces[2 * dz + 1][...]
        pair = jnp.where(
            yi == 0,
            jnp.concatenate([near, far], axis=1),
            jnp.concatenate([far, near], axis=1),
        )
        start = pl.multiple_of(((zi - dz + nz) % nz) * (2 * width), 128)
        values = dot(order_ref[...], pair)
        squares = squares + jnp.sum(values * values, axis=-1, keepdims=True)
        kept_ref[:, pl.ds(start, 2 * width)] = values[0:chunk_rows].astype(jnp.bfloat16)
        kept_send_ref[:, pl.ds(start, 2 * width)] = values[slots : slots + chunk_rows].astype(
            jnp.bfloat16
        )
        gain = gain_ref[:, pl.ds(pl.multiple_of(ci * half + start, 128), 2 * width)]
        rows_ref[:, pl.ds(start, 2 * width)] = (values * gain).astype(jnp.bfloat16)
    mine = pl.ds(pl.multiple_of(ci * half, 128), half)
    rows = rows_ref[...]
    units = gate_ref.shape[0]
    gate = by_rows(rows, gate_ref[:, mine])
    up = by_rows(rows, up_ref[:, mine])
    gate_other = by_rows(rows, gate_other_ref[...])
    up_other = by_rows(rows, up_other_ref[...])
    wide = keep_ref.shape[1] - 4 * units
    spread = jnp.broadcast_to(squares, (total, wide))
    keep_ref[...] = jnp.concatenate(
        [gate[:slots], gate_other[:slots], up[:slots], up_other[:slots], spread[:slots]], axis=1
    )
    send_ref[...] = jnp.concatenate(
        [gate_other[slots:], gate[slots:], up_other[slots:], up[slots:], spread[slots:]], axis=1
    )


def hidden_kernel(features, keep_ref, came_ref, down_ref, down_other_ref, *refs):
    chunk_rows = refs[0].shape[0]
    hidden_ref = refs[-1]
    units = down_ref.shape[0]
    summed = keep_ref[...] + came_ref[...]
    scale = lax.rsqrt(summed[:, 4 * units : 4 * units + 1] / features + 1e-06)
    gate = summed[:, 0 : 2 * units] * scale
    up = summed[:, 2 * units : 4 * units] * scale
    hidden = (jax.nn.gelu(gate, approximate=True) * up).astype(jnp.bfloat16)
    hidden_ref[...] = hidden
    far = jnp.concatenate(
        [
            hidden[(2 * dz + 1) * chunk_rows : (2 * dz + 2) * chunk_rows]
            for dz in range(len(refs) - 1)
        ],
        axis=0,
    )
    result = dot(far[:, :units], down_ref[...]) + dot(far[:, units:], down_other_ref[...])
    for dz in range(len(refs) - 1):
        refs[dz][...] = result[dz * chunk_rows : (dz + 1) * chunk_rows].astype(jnp.bfloat16)


def down_kernel(chunk_rows, hidden_ref, down_ref, down_other_ref, out_ref):
    units = down_ref.shape[0]
    hidden = hidden_ref[...]
    near = jnp.concatenate(
        [
            hidden[2 * dz * chunk_rows : (2 * dz + 1) * chunk_rows]
            for dz in range(hidden.shape[0] // chunk_rows // 2)
        ],
        axis=0,
    )
    out_ref[...] = dot(near[:, :units], down_ref[...]) + dot(near[:, units:], down_other_ref[...])


def add_kernel(first_row, near_ref, far_ref, out_ref):
    rows = out_ref.shape[0]
    out_ref[...] = (
        near_ref[first_row : first_row + rows, :] + far_ref[...].astype(jnp.float32)
    ).astype(jnp.bfloat16)


def last_kernel(count, *refs):
    near_ref, far_ref = refs[0], refs[1]
    arrived = refs[2 : 2 + count]
    kept_ref, kept_other_ref, out_ref = refs[2 + count :]
    ci = place()[3]
    rows = out_ref.shape[0]
    half = kept_ref.shape[1]
    kept, other = kept_ref[...].astype(jnp.float32), kept_other_ref[...].astype(jnp.float32)
    total = near_ref[0 : far_ref.shape[0], :] + far_ref[...].astype(jnp.float32)
    for ref in arrived:
        total = total + ref[...].astype(jnp.float32)
    low, high = jnp.where(ci == 0, kept, other), jnp.where(ci == 0, other, kept)
    out_ref[:, :half] = (low + total[:, :half])[:rows].astype(jnp.bfloat16)
    out_ref[:, half:] = (high + total[:, half:])[:rows].astype(jnp.bfloat16)


def body(
    queries,
    corpus,
    block_owner,
    slot_row,
    segment,
    query_weight,
    key_weight,
    value_weight,
    out_weight,
    gain_attn,
    gain_ffn,
    gate_weight,
    up_weight,
    down_weight,
):
    devices = lax.axis_size(AXIS)
    nz = devices // 4
    _, zi, yi, ci = place()
    z_order = sorted(range(1, nz), key=lambda k: -min(k, nz - k))

    def along_z(value, k):
        return lax.ppermute(value, AXIS, [(i, (i + 4 * k) % devices) for i in range(devices)])

    def across_y(value):
        return lax.ppermute(value, AXIS, [(i, i ^ 2) for i in range(devices)])

    def across_core(value):
        return lax.ppermute(value, AXIS, [(i, i ^ 1) for i in range(devices)])

    def plane_gather(value):
        near = {0: value}
        for k in z_order:
            near[k] = along_z(value, k)
        far = {k: across_y(near[k]) for k in [0] + z_order}
        return [piece for k in range(nz) for piece in (near[k], far[k])]

    owners = block_owner[:, 0]
    features = queries.shape[1]
    half = features // 2
    query_rows = queries.shape[0]
    tokens = query_rows * devices + owners.shape[0] * BLK
    width = features // devices
    heads_rows = query_weight.shape[0]
    units = gate_weight.shape[0]
    rows_here = tokens // devices
    chunk_rows = -(-rows_here // 16) * 16
    bf16, f32 = jnp.bfloat16, jnp.float32
    shape = jax.ShapeDtypeStruct

    full, halved = piece_layout(query_rows + CAP * BLK)
    piece = kernel_call(
        fetch_kernel,
        shape((8, full * features + halved * half), bf16),
        [SMEM, SMEM, ANY, VMEM],
        [
            pltpu.VMEM((CAP, BLK, features), bf16),
            pltpu.VMEM((full * 8 + halved * 8, features), f32),
            pltpu.SemaphoreType.DMA((CAP,)),
        ],
        name="fetch",
    )(owners, slot_row, corpus, queries)

    projections = [query_weight, key_weight, value_weight]
    projections_other = [across_core(w) for w in projections]
    other_half = (1 - ci) * half
    gate_other = across_core(lax.dynamic_slice_in_dim(gate_weight, other_half, half, 1))
    up_other = across_core(lax.dynamic_slice_in_dim(up_weight, other_half, half, 1))
    down_other = across_core(down_weight)

    def out_block(dz, dy):
        chip = 2 * ((zi + dz) % nz) + (yi ^ dy)
        return jnp.concatenate(
            [
                lax.dynamic_slice_in_dim(out_weight, chip * width, width, 1),
                lax.dynamic_slice_in_dim(out_weight, half + chip * width, width, 1),
            ],
            axis=1,
        )

    out_far = across_y(jnp.concatenate([out_block(dz, 1) for dz in range(nz)], axis=0))
    out_pairs = [
        jnp.concatenate(
            [out_block(dz, 0), out_far[dz * heads_rows : (dz + 1) * heads_rows]], axis=0
        )
        for dz in range(nz)
    ]
    out_columns = jnp.concatenate(
        [out_pairs[0]] + [along_z(out_pairs[k], k) for k in range(1, nz)], axis=0
    )

    plane_rows = 2 * nz * (full * 8 + halved * 4)
    wide = 256 + -(-width // 128) * 128
    own, away = kernel_call(
        functools.partial(projection_kernel, query_rows + CAP * BLK),
        (shape((plane_rows, wide), bf16), shape((plane_rows, wide), bf16)),
        [VMEM] * (2 * nz + 7),
        [pltpu.VMEM((plane_rows, features), bf16)],
        name="project",
    )(*plane_gather(piece), gain_attn[None, :], *projections, *projections_other)

    context, columns = kernel_call(
        functools.partial(attention_kernel, query_rows, width),
        (shape((tokens // 2, 2 * HDIM), bf16), shape((tokens, width), bf16)),
        [SMEM, SMEM, VMEM, VMEM],
        name="attend",
    )(owners, segment, own, across_core(away))

    contexts = plane_gather(context)
    context_all = jnp.concatenate(
        [jnp.concatenate([x[:, :HDIM], x[:, HDIM:]], axis=0) for x in contexts], axis=1
    )
    attended = dot(context_all, out_columns)
    attended_mine = lax.dynamic_slice_in_dim(attended, ci * width, width, 1)
    attended_other = across_core(lax.dynamic_slice_in_dim(attended, (1 - ci) * width, width, 1))
    middle = (columns.astype(f32) + attended_mine + attended_other).astype(bf16)

    slots = 2 * nz * chunk_rows
    lanes = -(-(4 * units + 1) // 128) * 128
    keep, send, kept, kept_send = kernel_call(
        functools.partial(gate_kernel, rows_here, chunk_rows),
        (
            shape((slots, lanes), f32),
            shape((slots, lanes), f32),
            shape((chunk_rows, half), bf16),
            shape((chunk_rows, half), bf16),
        ),
        [VMEM] * (2 * nz + 5),
        [pltpu.VMEM((2 * slots, tokens), bf16), pltpu.VMEM((2 * slots, half), bf16)],
        name="gate_up",
    )(*plane_gather(middle), gain_ffn[None, :], gate_weight, up_weight, gate_other, up_other)
    came = across_core(send)
    kept_other = across_core(kept_send)

    chunk = shape((chunk_rows, features), bf16)
    *far, hidden = kernel_call(
        functools.partial(hidden_kernel, features),
        (chunk,) * nz + (shape((slots, 2 * units), bf16),),
        [VMEM] * 4,
        name="hidden",
    )(keep, came, down_weight, down_other)
    moved = {k: across_y(far[k]) for k in z_order + [0]}
    near = kernel_call(
        functools.partial(down_kernel, chunk_rows),
        shape((nz * chunk_rows, features), f32),
        [VMEM] * 3,
        name="down",
    )(hidden, down_weight, down_other)
    arrived = []
    for k in z_order:
        part = kernel_call(
            functools.partial(add_kernel, k * chunk_rows), chunk, [VMEM, VMEM], name="add"
        )(near, moved[k])
        arrived.append(along_z(part, k))
    return kernel_call(
        functools.partial(last_kernel, len(arrived)),
        shape((rows_here, features), bf16),
        [VMEM] * (len(arrived) + 4),
        name="last",
    )(near, moved[0], *arrived, kept, kept_other)


def solution(mesh):
    placed = (
        P(("groups", "tensor"), None),
        P(("groups", "tensor"), None, None),
        P("groups", None),
        P("groups"),
        P("groups"),
        P("tensor", None),
        P("tensor", None),
        P("tensor", None),
        P("tensor", None),
        P(),
        P(),
        P("tensor", None),
        P("tensor", None),
        P("tensor", None),
    )
    return jax.shard_map(
        body, mesh=mesh, in_specs=placed, out_specs=P(("groups", "tensor"), None), check_vma=False
    )
```

time: 299 us -> 135 us (0.45)
  waiting for transfers between devices: 183 us -> 42.8 us
  blocking collectives: 49.4 us -> 0 us
  starting transfers between devices: 6.87 us -> 43.1 us
  Pallas kernels: 0 us -> 31.5 us
  matrix products: 16.8 us -> 1.32 us
  between operations: 14 us -> 0.39 us
  other arithmetic: 12.5 us -> 4 us
  local copies, waits for them, and re-layouts: 15.4 us -> 11.4 us
    psum x1 -> x0, waiting for transfers between devices: 106 us -> none  [body(): lax.psum(jnp.dot(context, out_weight, preferred_element_type=jnp.float32)...]
    all_gather x2 -> x0, waiting for transfers between devices: 71.1 us -> none  [the longest x1 41.7 us: body(): lax.all_gather(outgoing, 'tensor', axis=0, tiled=True)]
    unnamed x1 -> x0, blocking collectives: 49.4 us -> none
    ppermute x0 -> x42, starting transfers between devices: none -> 43.1 us  [the longest x15 24.3 us: along_z(): lax.ppermute(value, AXIS, [(i, (i + 4 * k) % devices) for i in range(devi...]
    ppermute x0 -> x42, waiting for transfers between devices: none -> 42.8 us  [the longest x15 20.6 us: along_z(): lax.ppermute(value, AXIS, [(i, (i + 4 * k) % devices) for i in range(devi...]
    pallas_call x0 -> x10, Pallas kernels: none -> 31.5 us  [the longest x3 5.7 us: body(): kernel_call(functools.partial(add_kernel, k * chunk_rows), chunk, [VMEM,...]
    dot_general x6 -> x1, matrix products: 16.8 us -> 1.32 us  [dot(): return jnp.dot(left, right, preferred_element_type=jnp.float32)]
    unnamed x2 -> x0, starting transfers between devices: 6.79 us -> none
  transfers between devices with their start and end apart: 5 -> 42, of which waited for: 4 -> 20; matrix products, arithmetic and copies ran while one was open for 4% -> 8% of each run, Pallas kernels for 0% -> 17%
where the time goes in v2:
time: 135 us; the launch traced here: 134 us
  starting transfers between devices  43.1 us (32%)
  waiting for transfers between devices  42.8 us (32%)
  Pallas kernels  31.5 us (23%)
  local copies, waits for them, and re-layouts  11.4 us (8%)
  other arithmetic  4 us (3%)
    ppermute x15, starting transfers between devices, along_z(): lax.ppermute(value, AXIS, [(i, (i + 4 * k) % devices) for i in range(devi...  24.3 us
    ppermute x15, waiting for transfers between devices, along_z(): lax.ppermute(value, AXIS, [(i, (i + 4 * k) % devices) for i in range(devi...  20.6 us
    ppermute x17, waiting for transfers between devices, across_y(): return lax.ppermute(value, AXIS, [(i, i ^ 2) for i in range(devices)])  17.6 us
    ppermute x17, starting transfers between devices, across_y(): return lax.ppermute(value, AXIS, [(i, i ^ 2) for i in range(devices)])  16.6 us
    unnamed x66, local copies, waits for them, and re-layouts  6.32 us
    pallas_call x3, Pallas kernels, body(): kernel_call(functools.partial(add_kernel, k * chunk_rows), chunk, [VMEM,...  5.7 us
    pallas_call x1, Pallas kernels, body(): kernel_call(functools.partial(projection_kernel, query_rows + CAP * BLK),...  5.68 us
    pallas_call x1, Pallas kernels, body(): kernel_call(functools.partial(gate_kernel, rows_here, chunk_rows), (shape...  5.24 us
  transfers between devices with their start and end apart: 42, of which 20 were waited for; matrix products, arithmetic and copies ran while one was open for 8% of the time, Pallas kernels for 17%

profile of v2, /device:TPU:0, one launch (start us, length us, event | category | flops | bytes accessed | tf_op | source)
XLA Modules:
  0.0 134.5 jit_solution(3893713625340181521)
XLA Ops:
  0.0 2.6 %fetch.1.refs_0_ = bf16[8,10240]{1,0:T(8,128)(2,1)} custom-call(s32[24]{0:T(128)} %bitcast.7, s32[24]{0:T(128)} %row_ref.1, bf16[64,4,4096]{2,1,0:T(4,128)(2,1)} %corpus_ref.1, bf16[8,4096]{1,0:T(8,128)(2,1)} %query_ref.1), custom_call_target="tpu_custom_call" | custom-call | tf_op jit(solution)/shard_map/fetch/pallas_call | solution.py:433
  2.7 3.1 %collective-permute-start = (bf16[8,10240]{1,0:T(8,128)(2,1)}, bf16[8,10240]{1,0:T(8,128)(2,1)}, u32[]{:S(2)}, u32[]{:S(2)}) collective-permute-start(bf16[8,10240]{1,0:T(8,128)(2,1)} %fetch.1.refs_0_), channel_id=1, source_target_pairs={{0,2},{1,3},{2,0},{3,1},{4,6},{5,7},{6,4},{7,5},{8,10},{9,11},{10,... | collective-permute-start | bytes 491528 | tf_op jit(solution)/shard_map/ppermute | solution.py:407
  5.7 1.6 %collective-permute-start.1 = (bf16[8,10240]{1,0:T(8,128)(2,1)}, bf16[8,10240]{1,0:T(8,128)(2,1)}, u32[]{:S(2)}, u32[]{:S(2)}) collective-permute-start(bf16[8,10240]{1,0:T(8,128)(2,1)} %fetch.1.refs_0_), channel_id=1, source_target_pairs={{0,4},{1,5},{2,6},{3,7},{4,8},{5,9},{6,10},{7,11},{8,12},{9,13},{1... | collective-permute-start | bytes 491528 | tf_op jit(solution)/shard_map/ppermute | solution.py:404
  7.3 2.5 %collective-permute-start.3 = (bf16[8,10240]{1,0:T(8,128)(2,1)}, bf16[8,10240]{1,0:T(8,128)(2,1)}, u32[]{:S(2)}, u32[]{:S(2)}) collective-permute-start(bf16[8,10240]{1,0:T(8,128)(2,1)} %fetch.1.refs_0_), channel_id=1, source_target_pairs={{0,8},{1,9},{2,10},{3,11},{4,12},{5,13},{6,14},{7,15},{8,0},{9,1},... | collective-permute-start | bytes 491528 | tf_op jit(solution)/shard_map/ppermute | solution.py:404
  9.9 1.4 %collective-permute-start.5 = (bf16[8,10240]{1,0:T(8,128)(2,1)}, bf16[8,10240]{1,0:T(8,128)(2,1)}, u32[]{:S(2)}, u32[]{:S(2)}) collective-permute-start(bf16[8,10240]{1,0:T(8,128)(2,1)} %fetch.1.refs_0_), channel_id=1, source_target_pairs={{0,12},{1,13},{2,14},{3,15},{4,0},{5,1},{6,2},{7,3},{8,4},{9,5},{1... | collective-permute-start | bytes 491528 | tf_op jit(solution)/shard_map/ppermute | solution.py:404
  11.3 0.7 constant_dynamic-slice_fusion.4
  11.9 0.7 maximum_maximum_fusion
  13.2 0.9 constant_dynamic-slice_fusion.1
  14.1 0.9 constant_dynamic-slice_fusion
  15.6 5.1 %collective-permute-done.3.refs_4_ = bf16[8,10240]{1,0:T(8,128)(2,1)} collective-permute-done((bf16[8,10240]{1,0:T(8,128)(2,1)}, bf16[8,10240]{1,0:T(8,128)(2,1)}, u32[]{:S(2)}, u32[]{:S(2)}) %collective-permute-start.3) | collective-permute-done | bytes 163872 | tf_op jit(solution)/shard_map/ppermute | solution.py:404
  21.2 1.6 %collective-permute-start.4 = (bf16[8,10240]{1,0:T(8,128)(2,1)}, bf16[8,10240]{1,0:T(8,128)(2,1)S(1)}, u32[]{:S(2)}, u32[]{:S(2)}) collective-permute-start(bf16[8,10240]{1,0:T(8,128)(2,1)} %collective-permute-done.3.refs_4_), channel_id=1, source_target_pairs={{0,2},{1,3},{2,0},{3,1},{4,6},{5,7},{6,4},{7,5},{8,10},{9,11},{10,... | collective-permute-start | bytes 491528 | tf_op jit(solution)/shard_map/ppermute | solution.py:407
  22.8 5.2 %collective-permute-done.2.refs_3_ = bf16[8,10240]{1,0:T(8,128)(2,1)S(1)} collective-permute-done((bf16[8,10240]{1,0:T(8,128)(2,1)}, bf16[8,10240]{1,0:T(8,128)(2,1)S(1)}, u32[]{:S(2)}, u32[]{:S(2)}) %collective-permute-start.2) | collective-permute-done | bytes 163872 | tf_op jit(solution)/shard_map/ppermute | solution.py:407
  28.4 0.8 pad_maximum_fusion
  29.2 2.3 %collective-permute-done.4.refs_5_ = bf16[8,10240]{1,0:T(8,128)(2,1)S(1)} collective-permute-done((bf16[8,10240]{1,0:T(8,128)(2,1)}, bf16[8,10240]{1,0:T(8,128)(2,1)S(1)}, u32[]{:S(2)}, u32[]{:S(2)}) %collective-permute-start.4) | collective-permute-done | bytes 163872 | tf_op jit(solution)/shard_map/ppermute | solution.py:407
  31.4 4.0 %collective-permute-start.19 = (bf16[128,512]{1,0:T(8,128)(2,1)S(1)}, bf16[128,512]{1,0:T(8,128)(2,1)S(1)}, u32[]{:S(2)}, u32[]{:S(2)}) collective-permute-start(bf16[128,512]{1,0:T(8,128)(2,1)S(1)} %pad_maximum_fusion), channel_id=1, source_target_pairs={{0,4},{1,5},{2,6},{3,7},{4,8},{5,9},{6,10},{7,11},{8,12},{9,13},{1... | collective-permute-start | bytes 393224 | tf_op jit(solution)/shard_map/ppermute | solution.py:404
  35.5 0.8 pad_maximum_fusion.1
  36.3 1.6 %collective-permute-start.20 = (bf16[128,512]{1,0:T(8,128)(2,1)S(1)}, bf16[128,512]{1,0:T(8,128)(2,1)}, u32[]{:S(2)}, u32[]{:S(2)}) collective-permute-start(bf16[128,512]{1,0:T(8,128)(2,1)S(1)} %pad_maximum_fusion.1), channel_id=1, source_target_pairs={{0,8},{1,9},{2,10},{3,11},{4,12},{5,13},{6,14},{7,15},{8,0},{9,1},... | collective-permute-start | bytes 393224 | tf_op jit(solution)/shard_map/ppermute | solution.py:404
  37.9 0.7 pad_maximum_fusion.2
  38.6 1.0 collective-permute-done.19
  39.6 1.9 %collective-permute-start.21 = (bf16[128,512]{1,0:T(8,128)(2,1)}, bf16[128,512]{1,0:T(8,128)(2,1)}, u32[]{:S(2)}, u32[]{:S(2)}) collective-permute-start(bf16[128,512]{1,0:T(8,128)(2,1)} %pad_maximum_fusion.2), channel_id=1, source_target_pairs={{0,12},{1,13},{2,14},{3,15},{4,0},{5,1},{6,2},{7,3},{8,4},{9,5},{1... | collective-permute-start | bytes 393224 | tf_op jit(solution)/shard_map/ppermute | solution.py:404
  43.2 5.7 %project.1 = (bf16[160,512]{1,0:T(8,128)(2,1)}, bf16[160,512]{1,0:T(8,128)(2,1)}) custom-call(bf16[8,10240]{1,0:T(8,128)(2,1)} %fetch.1.refs_0_, bf16[8,10240]{1,0:T(8,128)(2,1)} %collective-permute-done.refs_1_, bf16[8,10240]{1,0:T(8,128)(2,1)} %collective-permute-done.1.refs_2_, bf16[8,10240]{1,0:T(8,128)(2,1)} %copy-done.12, ...), custom_call_target="tpu_custom_call" | custom-call | tf_op jit(solution)/shard_map/project/pallas_call | solution.py:475
  49.4 0.9 constant_dynamic-update-slice_fusion.1
  50.3 0.9 constant_dynamic-update-slice_fusion
  51.3 0.7 copy-done.15
  52.0 3.2 %attend.1 = (bf16[112,128]{1,0:T(8,128)(2,1)}, bf16[224,256]{1,0:T(8,128)(2,1)}) custom-call(s32[24]{0:T(128)} %bitcast.8, s32[24]{0:T(128)} %segment_ref.1, bf16[160,512]{1,0:T(8,128)(2,1)} %get-tuple-element.18.own_ref, bf16[160,512]{1,0:T(8,128)(2,1)} %copy-done.15), custom_call_target="tpu_custom_call" | custom-call | tf_op jit(solution)/shard_map/attend/pallas_call | solution.py:483
  55.7 0.9 fusion.8
  56.7 2.5 %collective-permute-done.11 = bf16[112,128]{1,0:T(8,128)(2,1)S(1)} collective-permute-done((bf16[112,128]{1,0:T(8,128)(2,1)}, bf16[112,128]{1,0:T(8,128)(2,1)S(1)}, u32[]{:S(2)}, u32[]{:S(2)}) %collective-permute-start.11) | collective-permute-done | bytes 28704 | tf_op jit(solution)/shard_map/ppermute | solution.py:407
  59.3 1.4 %collective-permute-start.14 = (bf16[112,128]{1,0:T(8,128)(2,1)}, bf16[112,128]{1,0:T(8,128)(2,1)S(1)}, u32[]{:S(2)}, u32[]{:S(2)}) collective-permute-start(bf16[112,128]{1,0:T(8,128)(2,1)} %get-tuple-element.21), channel_id=1, source_target_pairs={{0,8},{1,9},{2,10},{3,11},{4,12},{5,13},{6,14},{7,15},{8,0},{9,1},... | collective-permute-start | bytes 86024 | tf_op jit(solution)/shard_map/ppermute | solution.py:404
  60.8 1.7 %collective-permute-done.12 = bf16[112,128]{1,0:T(8,128)(2,1)S(1)} collective-permute-done((bf16[112,128]{1,0:T(8,128)(2,1)}, bf16[112,128]{1,0:T(8,128)(2,1)S(1)}, u32[]{:S(2)}, u32[]{:S(2)}) %collective-permute-start.12) | collective-permute-done | bytes 28704 | tf_op jit(solution)/shard_map/ppermute | solution.py:404
  62.6 1.8 %collective-permute-done.14 = bf16[112,128]{1,0:T(8,128)(2,1)S(1)} collective-permute-done((bf16[112,128]{1,0:T(8,128)(2,1)}, bf16[112,128]{1,0:T(8,128)(2,1)S(1)}, u32[]{:S(2)}, u32[]{:S(2)}) %collective-permute-start.14) | collective-permute-done | bytes 28704 | tf_op jit(solution)/shard_map/ppermute | solution.py:404
  64.5 0.7 collective-permute-start.13
  65.2 1.4 %collective-permute-done.16 = bf16[112,128]{1,0:T(8,128)(2,1)S(1)} collective-permute-done((bf16[112,128]{1,0:T(8,128)(2,1)}, bf16[112,128]{1,0:T(8,128)(2,1)S(1)}, u32[]{:S(2)}, u32[]{:S(2)}) %collective-permute-start.16) | collective-permute-done | bytes 28704 | tf_op jit(solution)/shard_map/ppermute | solution.py:404
  66.6 1.5 %collective-permute-start.15 = (bf16[112,128]{1,0:T(8,128)(2,1)S(1)}, bf16[112,128]{1,0:T(8,128)(2,1)S(1)}, u32[]{:S(2)}, u32[]{:S(2)}) collective-permute-start(bf16[112,128]{1,0:T(8,128)(2,1)S(1)} %collective-permute-done.14), channel_id=1, source_target_pairs={{0,2},{1,3},{2,0},{3,1},{4,6},{5,7},{6,4},{7,5},{8,10},{9,11},{10,... | collective-permute-start | bytes 86024 | tf_op jit(solution)/shard_map/ppermute | solution.py:407
  69.4 1.0 collective-permute-done.15
  70.6 2.0 %collective-permute-done.17 = bf16[112,128]{1,0:T(8,128)(2,1)S(1)} collective-permute-done((bf16[112,128]{1,0:T(8,128)(2,1)S(1)}, bf16[112,128]{1,0:T(8,128)(2,1)S(1)}, u32[]{:S(2)}, u32[]{:S(2)}) %collective-permute-start.17) | collective-permute-done | bytes 28704 | tf_op jit(solution)/shard_map/ppermute | solution.py:407
  72.9 1.3 fusion.9
  74.3 1.5 %collective-permute-done.22 = f32[224,256]{1,0:T(8,128)S(1)} collective-permute-done((f32[224,256]{1,0:T(8,128)S(1)}, f32[224,256]{1,0:T(8,128)S(1)}, u32[]{:S(2)}, u32[]{:S(2)}) %collective-permute-start.22) | collective-permute-done | bytes 229408 | tf_op jit(solution)/shard_map/ppermute | solution.py:410
  75.8 0.9 add_convert_fusion.refs_0_
  77.0 1.7 %collective-permute-start.26 = (bf16[224,256]{1,0:T(8,128)(2,1)S(1)}, bf16[224,256]{1,0:T(8,128)(2,1)S(1)}, u32[]{:S(2)}, u32[]{:S(2)}) collective-permute-start(bf16[224,256]{1,0:T(8,128)(2,1)S(1)} %add_convert_fusion.refs_0_), channel_id=1, source_target_pairs={{0,8},{1,9},{2,10},{3,11},{4,12},{5,13},{6,14},{7,15},{8,0},{9,1},... | collective-permute-start | bytes 344072 | tf_op jit(solution)/shard_map/ppermute | solution.py:404
  78.7 2.1 %collective-permute-start.28 = (bf16[224,256]{1,0:T(8,128)(2,1)S(1)}, bf16[224,256]{1,0:T(8,128)(2,1)S(1)}, u32[]{:S(2)}, u32[]{:S(2)}) collective-permute-start(bf16[224,256]{1,0:T(8,128)(2,1)S(1)} %add_convert_fusion.refs_0_), channel_id=1, source_target_pairs={{0,12},{1,13},{2,14},{3,15},{4,0},{5,1},{6,2},{7,3},{8,4},{9,5},{1... | collective-permute-start | bytes 344072 | tf_op jit(solution)/shard_map/ppermute | solution.py:404
  81.3 3.4 %collective-permute-done.24.refs_2_ = bf16[224,256]{1,0:T(8,128)(2,1)S(1)} collective-permute-done((bf16[224,256]{1,0:T(8,128)(2,1)S(1)}, bf16[224,256]{1,0:T(8,128)(2,1)S(1)}, u32[]{:S(2)}, u32[]{:S(2)}) %collective-permute-start.24) | collective-permute-done | bytes 114720 | tf_op jit(solution)/shard_map/ppermute | solution.py:404
  85.3 3.5 %collective-permute-done.26.refs_4_ = bf16[224,256]{1,0:T(8,128)(2,1)S(1)} collective-permute-done((bf16[224,256]{1,0:T(8,128)(2,1)S(1)}, bf16[224,256]{1,0:T(8,128)(2,1)S(1)}, u32[]{:S(2)}, u32[]{:S(2)}) %collective-permute-start.26) | collective-permute-done | bytes 114720 | tf_op jit(solution)/shard_map/ppermute | solution.py:404
  89.4 1.4 %collective-permute-start.29 = (bf16[224,256]{1,0:T(8,128)(2,1)S(1)}, bf16[224,256]{1,0:T(8,128)(2,1)S(1)}, u32[]{:S(2)}, u32[]{:S(2)}) collective-permute-start(bf16[224,256]{1,0:T(8,128)(2,1)S(1)} %collective-permute-done.28.refs_6_), channel_id=1, source_target_pairs={{0,2},{1,3},{2,0},{3,1},{4,6},{5,7},{6,4},{7,5},{8,10},{9,11},{10,... | collective-permute-start | bytes 344072 | tf_op jit(solution)/shard_map/ppermute | solution.py:407
  90.9 2.8 %collective-permute-done.27.refs_5_ = bf16[224,256]{1,0:T(8,128)(2,1)S(1)} collective-permute-done((bf16[224,256]{1,0:T(8,128)(2,1)S(1)}, bf16[224,256]{1,0:T(8,128)(2,1)S(1)}, u32[]{:S(2)}, u32[]{:S(2)}) %collective-permute-start.27) | collective-permute-done | bytes 114720 | tf_op jit(solution)/shard_map/ppermute | solution.py:407
  93.7 1.2 collective-permute-done.29.refs_7_
  95.6 5.2 %gate_up.1 = (f32[128,768]{1,0:T(8,128)}, f32[128,768]{1,0:T(8,128)}, bf16[16,2048]{1,0:T(8,128)(2,1)}, bf16[16,2048]{1,0:T(8,128)(2,1)}) custom-call(bf16[224,256]{1,0:T(8,128)(2,1)} %copy-done.10, bf16[224,256]{1,0:T(8,128)(2,1)} %copy-done.26, bf16[224,256]{1,0:T(8,128)(2,1)} %copy-done.23, bf16[224,256]{1,0:T(8,128)(2,1)} %copy-done.27, ...), custom_call_target="tpu_custom_call" | custom-call | tf_op jit(solution)/shard_map/gate_up/pallas_call | solution.py:501
  100.8 1.9 %collective-permute-done.32.came_ref = f32[128,768]{1,0:T(8,128)S(1)} collective-permute-done((f32[128,768]{1,0:T(8,128)}, f32[128,768]{1,0:T(8,128)S(1)}, u32[]{:S(2)}, u32[]{:S(2)}) %collective-permute-start.32) | collective-permute-done | bytes 393248 | tf_op jit(solution)/shard_map/ppermute | solution.py:410
  102.7 0.7 copy-done.11
  103.5 3.5 %hidden.1 = (bf16[16,4096]{1,0:T(8,128)(2,1)}, bf16[16,4096]{1,0:T(8,128)(2,1)}, bf16[16,4096]{1,0:T(8,128)(2,1)}, bf16[16,4096]{1,0:T(8,128)(2,1)}, bf16[128,320]{1,0:T(8,128)(2,1)}) custom-call(f32[128,768]{1,0:T(8,128)} %get-tuple-element.22.keep_ref, f32[128,768]{1,0:T(8,128)} %copy-done.11, bf16[160,4096]{1,0:T(8,128)(2,1)} %down_ref.3, ...), custom_call_target="tpu_custom_call" | custom-call | tf_op jit(solution)/shard_map/hidden/pallas_call | solution.py:517
  107.0 1.5 %collective-permute-start.35 = (bf16[16,4096]{1,0:T(8,128)(2,1)}, bf16[16,4096]{1,0:T(8,128)(2,1)S(1)}, u32[]{:S(2)}, u32[]{:S(2)}) collective-permute-start(bf16[16,4096]{1,0:T(8,128)(2,1)} %get-tuple-element.26), channel_id=1, source_target_pairs={{0,2},{1,3},{2,0},{3,1},{4,6},{5,7},{6,4},{7,5},{8,10},{9,11},{10,... | collective-permute-start | bytes 393224 | tf_op jit(solution)/shard_map/ppermute | solution.py:407
  109.0 1.5 %collective-permute-start.39 = (bf16[16,4096]{1,0:T(8,128)(2,1)}, bf16[16,4096]{1,0:T(8,128)(2,1)S(1)}, u32[]{:S(2)}, u32[]{:S(2)}) collective-permute-start(bf16[16,4096]{1,0:T(8,128)(2,1)} %get-tuple-element.28), channel_id=1, source_target_pairs={{0,2},{1,3},{2,0},{3,1},{4,6},{5,7},{6,4},{7,5},{8,10},{9,11},{10,... | collective-permute-start | bytes 393224 | tf_op jit(solution)/shard_map/ppermute | solution.py:407
  111.1 3.3 %down.1.near_ref.refs_0_ = f32[64,4096]{1,0:T(8,128)} custom-call(bf16[128,320]{1,0:T(8,128)(2,1)} %get-tuple-element.24.hidden_ref, bf16[160,4096]{1,0:T(8,128)(2,1)} %down_ref.3, bf16[160,4096]{1,0:T(8,128)(2,1)} %copy-done.1), custom_call_target="tpu_custom_call" | custom-call | tf_op jit(solution)/shard_map/down/pallas_call | solution.py:524
  114.4 0.6 copy-done.22
  115.0 1.9 %add.216 = bf16[16,4096]{1,0:T(8,128)(2,1)} custom-call(f32[64,4096]{1,0:T(8,128)} %down.1.near_ref.refs_0_, bf16[16,4096]{1,0:T(8,128)(2,1)} %copy-done.22), custom_call_target="tpu_custom_call" | custom-call | tf_op jit(solution)/shard_map/add/pallas_call | solution.py:532
  116.9 1.8 %collective-permute-start.36 = (bf16[16,4096]{1,0:T(8,128)(2,1)}, bf16[16,4096]{1,0:T(8,128)(2,1)S(1)}, u32[]{:S(2)}, u32[]{:S(2)}) collective-permute-start(bf16[16,4096]{1,0:T(8,128)(2,1)} %add.216), channel_id=1, source_target_pairs={{0,8},{1,9},{2,10},{3,11},{4,12},{5,13},{6,14},{7,15},{8,0},{9,1},... | collective-permute-start | bytes 393224 | tf_op jit(solution)/shard_map/ppermute | solution.py:404
  118.7 0.7 copy-done.21
  119.4 1.9 %add.217 = bf16[16,4096]{1,0:T(8,128)(2,1)} custom-call(f32[64,4096]{1,0:T(8,128)} %down.1.near_ref.refs_0_, bf16[16,4096]{1,0:T(8,128)(2,1)} %copy-done.21), custom_call_target="tpu_custom_call" | custom-call | tf_op jit(solution)/shard_map/add/pallas_call | solution.py:532
  121.3 2.6 %collective-permute-start.38 = (bf16[16,4096]{1,0:T(8,128)(2,1)}, bf16[16,4096]{1,0:T(8,128)(2,1)S(1)}, u32[]{:S(2)}, u32[]{:S(2)}) collective-permute-start(bf16[16,4096]{1,0:T(8,128)(2,1)} %add.217), channel_id=1, source_target_pairs={{0,4},{1,5},{2,6},{3,7},{4,8},{5,9},{6,10},{7,11},{8,12},{9,13},{1... | collective-permute-start | bytes 393224 | tf_op jit(solution)/shard_map/ppermute | solution.py:404
  123.9 0.7 copy-done.20
  124.6 1.9 %add.218 = bf16[16,4096]{1,0:T(8,128)(2,1)} custom-call(f32[64,4096]{1,0:T(8,128)} %down.1.near_ref.refs_0_, bf16[16,4096]{1,0:T(8,128)(2,1)} %copy-done.20), custom_call_target="tpu_custom_call" | custom-call | tf_op jit(solution)/shard_map/add/pallas_call | solution.py:532
  126.5 1.2 collective-permute-start.40
  127.7 1.3 collective-permute-done.41.refs_6_
  129.1 2.5 %collective-permute-done.40.refs_4_ = bf16[16,4096]{1,0:T(8,128)(2,1)S(1)} collective-permute-done((bf16[16,4096]{1,0:T(8,128)(2,1)}, bf16[16,4096]{1,0:T(8,128)(2,1)S(1)}, u32[]{:S(2)}, u32[]{:S(2)}) %collective-permute-start.40) | collective-permute-done | bytes 131104 | tf_op jit(solution)/shard_map/ppermute | solution.py:404
  132.3 2.2 %last.1 = bf16[14,4096]{1,0:T(8,128)(2,1)} custom-call(f32[64,4096]{1,0:T(8,128)} %down.1.near_ref.refs_0_, bf16[16,4096]{1,0:T(8,128)(2,1)} %copy-done.16, bf16[16,4096]{1,0:T(8,128)(2,1)} %copy-done.17, bf16[16,4096]{1,0:T(8,128)(2,1)} %copy-done.18, bf16[16,4096]{1,0:T(8,128)(2,1)} %copy-done.19, bf16[16,2048]{1,0:T(8,128)(2,1)} %get-tuple-element.29.refs_5_, ...), custom_call_target="tpu_custom_call" | custom-call | tf_op jit(solution)/shard_map/last/pallas_call | solution.py:536
  (122 shorter events, 11.6 us)
Async XLA Ops:
  0.0 11.2 %copy-start.9 = (bf16[64,4096]{1,0:T(8,128)(2,1)S(1)}, bf16[64,4096]{1,0:T(8,128)(2,1)}, u32[]{:S(2)}) copy-start(bf16[64,4096]{1,0:T(8,128)(2,1)} %param.22) | copy-start | bytes 1572868
  2.6 10.6 %copy-start.2 = (bf16[160,4096]{1,0:T(8,128)(2,1)S(1)}, bf16[160,4096]{1,0:T(8,128)(2,1)}, u32[]{:S(2)}) copy-start(bf16[160,4096]{1,0:T(8,128)(2,1)} %refs_9_.3) | copy-start | bytes 3932164
  2.7 12.3 %collective-permute-start = (bf16[8,10240]{1,0:T(8,128)(2,1)}, bf16[8,10240]{1,0:T(8,128)(2,1)}, u32[]{:S(2)}, u32[]{:S(2)}) collective-permute-start(bf16[8,10240]{1,0:T(8,128)(2,1)} %fetch.1.refs_0_), channel_id=1, source_target_pairs={{0,2},{1,3},{2,0},{3,1},{4,6},{5,7},{6,4},{7,5},{8,10},{9,11},{10,... | collective-permute-start | bytes 491528 | tf_op jit(solution)/shard_map/ppermute | solution.py:407
  5.7 9.3 %collective-permute-start.1 = (bf16[8,10240]{1,0:T(8,128)(2,1)}, bf16[8,10240]{1,0:T(8,128)(2,1)}, u32[]{:S(2)}, u32[]{:S(2)}) collective-permute-start(bf16[8,10240]{1,0:T(8,128)(2,1)} %fetch.1.refs_0_), channel_id=1, source_target_pairs={{0,4},{1,5},{2,6},{3,7},{4,8},{5,9},{6,10},{7,11},{8,12},{9,13},{1... | collective-permute-start | bytes 491528 | tf_op jit(solution)/shard_map/ppermute | solution.py:404
  7.3 13.4 %collective-permute-start.3 = (bf16[8,10240]{1,0:T(8,128)(2,1)}, bf16[8,10240]{1,0:T(8,128)(2,1)}, u32[]{:S(2)}, u32[]{:S(2)}) collective-permute-start(bf16[8,10240]{1,0:T(8,128)(2,1)} %fetch.1.refs_0_), channel_id=1, source_target_pairs={{0,8},{1,9},{2,10},{3,11},{4,12},{5,13},{6,14},{7,15},{8,0},{9,1},... | collective-permute-start | bytes 491528 | tf_op jit(solution)/shard_map/ppermute | solution.py:404
  9.9 10.9 %collective-permute-start.5 = (bf16[8,10240]{1,0:T(8,128)(2,1)}, bf16[8,10240]{1,0:T(8,128)(2,1)}, u32[]{:S(2)}, u32[]{:S(2)}) collective-permute-start(bf16[8,10240]{1,0:T(8,128)(2,1)} %fetch.1.refs_0_), channel_id=1, source_target_pairs={{0,12},{1,13},{2,14},{3,15},{4,0},{5,1},{6,2},{7,3},{8,4},{9,5},{1... | collective-permute-start | bytes 491528 | tf_op jit(solution)/shard_map/ppermute | solution.py:404
  11.2 2.8 %copy-start.3 = (bf16[160,4096]{1,0:T(8,128)(2,1)S(1)}, bf16[160,4096]{1,0:T(8,128)(2,1)}, u32[]{:S(2)}) copy-start(bf16[160,4096]{1,0:T(8,128)(2,1)} %refs_10_.3) | copy-start | bytes 3932164
  12.7 8.5 %collective-permute-start.18 = (bf16[256,512]{1,0:T(8,128)(2,1)}, bf16[256,512]{1,0:T(8,128)(2,1)S(1)}, u32[]{:S(2)}, u32[]{:S(2)}) collective-permute-start(bf16[256,512]{1,0:T(8,128)(2,1)} %maximum_maximum_fusion), channel_id=1, source_target_pairs={{0,2},{1,3},{2,0},{3,1},{4,6},{5,7},{6,4},{7,5},{8,10},{9,11},{10,... | collective-permute-start | bytes 786440 | tf_op jit(solution)/shard_map/ppermute | solution.py:407
  13.2 1.8 %copy-start.5 = (bf16[64,4096]{1,0:T(8,128)(2,1)S(1)}, bf16[64,4096]{1,0:T(8,128)(2,1)}, u32[]{:S(2)}) copy-start(bf16[64,4096]{1,0:T(8,128)(2,1)} %refs_9_.2) | copy-start | bytes 1572868
  14.1 28.3 %copy-start = (bf16[160,4096]{1,0:T(8,128)(2,1)S(1)}, bf16[160,4096]{1,0:T(8,128)(2,1)}, u32[]{:S(2)}) copy-start(bf16[160,4096]{1,0:T(8,128)(2,1)} %down_ref.3) | copy-start | bytes 3932164
  15.0 26.4 %collective-permute-start.7 = (bf16[64,4096]{1,0:T(8,128)(2,1)S(1)}, bf16[64,4096]{1,0:T(8,128)(2,1)S(1)}, u32[]{:S(2)}, u32[]{:S(2)}) collective-permute-start(bf16[64,4096]{1,0:T(8,128)(2,1)S(1)} %copy-done.5), channel_id=1, source_target_pairs={{0,1},{1,0},{2,3},{3,2},{4,5},{5,4},{6,7},{7,6},{8,9},{9,8},{10,11... | collective-permute-start | bytes 1572872 | tf_op jit(solution)/shard_map/ppermute | solution.py:410
  15.1 26.5 %collective-permute-start.8 = (bf16[64,4096]{1,0:T(8,128)(2,1)}, bf16[64,4096]{1,0:T(8,128)(2,1)S(1)}, u32[]{:S(2)}, u32[]{:S(2)}) collective-permute-start(bf16[64,4096]{1,0:T(8,128)(2,1)} %refs_10_.2), channel_id=1, source_target_pairs={{0,1},{1,0},{2,3},{3,2},{4,5},{5,4},{6,7},{7,6},{8,9},{9,8},{10,11... | collective-permute-start | bytes 1572872 | tf_op jit(solution)/shard_map/ppermute | solution.py:410
  20.7 21.7 %collective-permute-start.9 = (bf16[64,4096]{1,0:T(8,128)(2,1)}, bf16[64,4096]{1,0:T(8,128)(2,1)S(1)}, u32[]{:S(2)}, u32[]{:S(2)}) collective-permute-start(bf16[64,4096]{1,0:T(8,128)(2,1)} %refs_11_.1), channel_id=1, source_target_pairs={{0,1},{1,0},{2,3},{3,2},{4,5},{5,4},{6,7},{7,6},{8,9},{9,8},{10,11... | collective-permute-start | bytes 1572872 | tf_op jit(solution)/shard_map/ppermute | solution.py:410
  20.7 7.2 %collective-permute-start.2 = (bf16[8,10240]{1,0:T(8,128)(2,1)}, bf16[8,10240]{1,0:T(8,128)(2,1)S(1)}, u32[]{:S(2)}, u32[]{:S(2)}) collective-permute-start(bf16[8,10240]{1,0:T(8,128)(2,1)} %collective-permute-done.1.refs_2_), channel_id=1, source_target_pairs={{0,2},{1,3},{2,0},{3,1},{4,6},{5,7},{6,4},{7,5},{8,10},{9,11},{10,... | collective-permute-start | bytes 491528 | tf_op jit(solution)/shard_map/ppermute | solution.py:407
  21.2 10.2 %collective-permute-start.4 = (bf16[8,10240]{1,0:T(8,128)(2,1)}, bf16[8,10240]{1,0:T(8,128)(2,1)S(1)}, u32[]{:S(2)}, u32[]{:S(2)}) collective-permute-start(bf16[8,10240]{1,0:T(8,128)(2,1)} %collective-permute-done.3.refs_4_), channel_id=1, source_target_pairs={{0,2},{1,3},{2,0},{3,1},{4,6},{5,7},{6,4},{7,5},{8,10},{9,11},{10,... | collective-permute-start | bytes 491528 | tf_op jit(solution)/shard_map/ppermute | solution.py:407
  27.9 15.0 %copy-start.12 = (bf16[8,10240]{1,0:T(8,128)(2,1)}, bf16[8,10240]{1,0:T(8,128)(2,1)S(1)}, u32[]{:S(2)}) copy-start(bf16[8,10240]{1,0:T(8,128)(2,1)S(1)} %collective-permute-done.2.refs_3_) | copy-start | bytes 491524
  27.9 8.3 %collective-permute-start.6 = (bf16[8,10240]{1,0:T(8,128)(2,1)}, bf16[8,10240]{1,0:T(8,128)(2,1)S(1)}, u32[]{:S(2)}, u32[]{:S(2)}) collective-permute-start(bf16[8,10240]{1,0:T(8,128)(2,1)} %collective-permute-done.5.refs_6_), channel_id=1, source_target_pairs={{0,2},{1,3},{2,0},{3,1},{4,6},{5,7},{6,4},{7,5},{8,10},{9,11},{10,... | collective-permute-start | bytes 491528 | tf_op jit(solution)/shard_map/ppermute | solution.py:407
  31.4 11.5 %copy-start.13 = (bf16[8,10240]{1,0:T(8,128)(2,1)}, bf16[8,10240]{1,0:T(8,128)(2,1)S(1)}, u32[]{:S(2)}) copy-start(bf16[8,10240]{1,0:T(8,128)(2,1)S(1)} %collective-permute-done.4.refs_5_) | copy-start | bytes 491524
  31.4 8.1 %collective-permute-start.19 = (bf16[128,512]{1,0:T(8,128)(2,1)S(1)}, bf16[128,512]{1,0:T(8,128)(2,1)S(1)}, u32[]{:S(2)}, u32[]{:S(2)}) collective-permute-start(bf16[128,512]{1,0:T(8,128)(2,1)S(1)} %pad_maximum_fusion), channel_id=1, source_target_pairs={{0,4},{1,5},{2,6},{3,7},{4,8},{5,9},{6,10},{7,11},{8,12},{9,13},{1... | collective-permute-start | bytes 393224 | tf_op jit(solution)/shard_map/ppermute | solution.py:404
  36.3 6.9 %copy-start.14 = (bf16[8,10240]{1,0:T(8,128)(2,1)}, bf16[8,10240]{1,0:T(8,128)(2,1)S(1)}, u32[]{:S(2)}) copy-start(bf16[8,10240]{1,0:T(8,128)(2,1)S(1)} %collective-permute-done.6.refs_7_) | copy-start | bytes 491524
  36.3 12.6 %collective-permute-start.20 = (bf16[128,512]{1,0:T(8,128)(2,1)S(1)}, bf16[128,512]{1,0:T(8,128)(2,1)}, u32[]{:S(2)}, u32[]{:S(2)}) collective-permute-start(bf16[128,512]{1,0:T(8,128)(2,1)S(1)} %pad_maximum_fusion.1), channel_id=1, source_target_pairs={{0,8},{1,9},{2,10},{3,11},{4,12},{5,13},{6,14},{7,15},{8,0},{9,1},... | collective-permute-start | bytes 393224 | tf_op jit(solution)/shard_map/ppermute | solution.py:404
  39.6 10.8 %collective-permute-start.21 = (bf16[128,512]{1,0:T(8,128)(2,1)}, bf16[128,512]{1,0:T(8,128)(2,1)}, u32[]{:S(2)}, u32[]{:S(2)}) collective-permute-start(bf16[128,512]{1,0:T(8,128)(2,1)} %pad_maximum_fusion.2), channel_id=1, source_target_pairs={{0,12},{1,13},{2,14},{3,15},{4,0},{5,1},{6,2},{7,3},{8,4},{9,5},{1... | collective-permute-start | bytes 393224 | tf_op jit(solution)/shard_map/ppermute | solution.py:404
  41.4 1.8 %copy-start.6 = (bf16[64,4096]{1,0:T(8,128)(2,1)}, bf16[64,4096]{1,0:T(8,128)(2,1)S(1)}, u32[]{:S(2)}) copy-start(bf16[64,4096]{1,0:T(8,128)(2,1)S(1)} %collective-permute-done.7.refs_12_) | copy-start | bytes 1572868
  41.5 37.3 %collective-permute-start.30 = (bf16[160,2048]{1,0:T(8,128)(2,1)}, bf16[160,2048]{1,0:T(8,128)(2,1)}, u32[]{:S(2)}, u32[]{:S(2)}) collective-permute-start(bf16[160,2048]{1,0:T(8,128)(2,1)} %constant_dynamic-slice_fusion.1), channel_id=1, source_target_pairs={{0,1},{1,0},{2,3},{3,2},{4,5},{5,4},{6,7},{7,6},{8,9},{9,8},{10,11... | collective-permute-start | bytes 1966088 | tf_op jit(solution)/shard_map/ppermute | solution.py:410
  41.6 39.3 %collective-permute-start.31 = (bf16[160,2048]{1,0:T(8,128)(2,1)}, bf16[160,2048]{1,0:T(8,128)(2,1)}, u32[]{:S(2)}, u32[]{:S(2)}) collective-permute-start(bf16[160,2048]{1,0:T(8,128)(2,1)} %constant_dynamic-slice_fusion), channel_id=1, source_target_pairs={{0,1},{1,0},{2,3},{3,2},{4,5},{5,4},{6,7},{7,6},{8,9},{9,8},{10,11... | collective-permute-start | bytes 1966088 | tf_op jit(solution)/shard_map/ppermute | solution.py:410
  42.4 58.4 %collective-permute-start.33 = (bf16[160,4096]{1,0:T(8,128)(2,1)S(1)}, bf16[160,4096]{1,0:T(8,128)(2,1)S(1)}, u32[]{:S(2)}, u32[]{:S(2)}) collective-permute-start(bf16[160,4096]{1,0:T(8,128)(2,1)S(1)} %copy-done), channel_id=1, source_target_pairs={{0,1},{1,0},{2,3},{3,2},{4,5},{5,4},{6,7},{7,6},{8,9},{9,8},{10,11... | collective-permute-start | bytes 3932168 | tf_op jit(solution)/shard_map/ppermute | solution.py:410
  48.9 2.4 %collective-permute-start.10 = (bf16[160,512]{1,0:T(8,128)(2,1)}, bf16[160,512]{1,0:T(8,128)(2,1)S(1)}, u32[]{:S(2)}, u32[]{:S(2)}) collective-permute-start(bf16[160,512]{1,0:T(8,128)(2,1)} %get-tuple-element.19), channel_id=1, source_target_pairs={{0,1},{1,0},{2,3},{3,2},{4,5},{5,4},{6,7},{7,6},{8,9},{9,8},{10,11... | collective-permute-start | bytes 491528 | tf_op jit(solution)/shard_map/ppermute | solution.py:410
  51.3 21.4 %copy-start.4 = (bf16[512,512]{1,0:T(8,128)(2,1)}, bf16[512,512]{1,0:T(8,128)(2,1)S(1)}, u32[]{:S(2)}) copy-start(bf16[512,512]{1,0:T(8,128)(2,1)S(1)} %constant_dynamic-update-slice_fusion) | copy-start | bytes 1572868
  55.2 4.1 %collective-permute-start.11 = (bf16[112,128]{1,0:T(8,128)(2,1)}, bf16[112,128]{1,0:T(8,128)(2,1)S(1)}, u32[]{:S(2)}, u32[]{:S(2)}) collective-permute-start(bf16[112,128]{1,0:T(8,128)(2,1)} %get-tuple-element.21), channel_id=1, source_target_pairs={{0,2},{1,3},{2,0},{3,1},{4,6},{5,7},{6,4},{7,5},{8,10},{9,11},{10,... | collective-permute-start | bytes 86024 | tf_op jit(solution)/shard_map/ppermute | solution.py:407
  56.6 5.9 %collective-permute-start.12 = (bf16[112,128]{1,0:T(8,128)(2,1)}, bf16[112,128]{1,0:T(8,128)(2,1)S(1)}, u32[]{:S(2)}, u32[]{:S(2)}) collective-permute-start(bf16[112,128]{1,0:T(8,128)(2,1)} %get-tuple-element.21), channel_id=1, source_target_pairs={{0,4},{1,5},{2,6},{3,7},{4,8},{5,9},{6,10},{7,11},{8,12},{9,13},{1... | collective-permute-start | bytes 86024 | tf_op jit(solution)/shard_map/ppermute | solution.py:404
  59.3 5.1 %collective-permute-start.14 = (bf16[112,128]{1,0:T(8,128)(2,1)}, bf16[112,128]{1,0:T(8,128)(2,1)S(1)}, u32[]{:S(2)}, u32[]{:S(2)}) collective-permute-start(bf16[112,128]{1,0:T(8,128)(2,1)} %get-tuple-element.21), channel_id=1, source_target_pairs={{0,8},{1,9},{2,10},{3,11},{4,12},{5,13},{6,14},{7,15},{8,0},{9,1},... | collective-permute-start | bytes 86024 | tf_op jit(solution)/shard_map/ppermute | solution.py:404
  62.5 4.1 %collective-permute-start.16 = (bf16[112,128]{1,0:T(8,128)(2,1)}, bf16[112,128]{1,0:T(8,128)(2,1)S(1)}, u32[]{:S(2)}, u32[]{:S(2)}) collective-permute-start(bf16[112,128]{1,0:T(8,128)(2,1)} %get-tuple-element.21), channel_id=1, source_target_pairs={{0,12},{1,13},{2,14},{3,15},{4,0},{5,1},{6,2},{7,3},{8,4},{9,5},{1... | collective-permute-start | bytes 86024 | tf_op jit(solution)/shard_map/ppermute | solution.py:404
  64.5 4.2 %collective-permute-start.13 = (bf16[112,128]{1,0:T(8,128)(2,1)S(1)}, bf16[112,128]{1,0:T(8,128)(2,1)S(1)}, u32[]{:S(2)}, u32[]{:S(2)}) collective-permute-start(bf16[112,128]{1,0:T(8,128)(2,1)S(1)} %collective-permute-done.12), channel_id=1, source_target_pairs={{0,2},{1,3},{2,0},{3,1},{4,6},{5,7},{6,4},{7,5},{8,10},{9,11},{10,... | collective-permute-start | bytes 86024 | tf_op jit(solution)/shard_map/ppermute | solution.py:407
  66.6 3.9 %collective-permute-start.15 = (bf16[112,128]{1,0:T(8,128)(2,1)S(1)}, bf16[112,128]{1,0:T(8,128)(2,1)S(1)}, u32[]{:S(2)}, u32[]{:S(2)}) collective-permute-start(bf16[112,128]{1,0:T(8,128)(2,1)S(1)} %collective-permute-done.14), channel_id=1, source_target_pairs={{0,2},{1,3},{2,0},{3,1},{4,6},{5,7},{6,4},{7,5},{8,10},{9,11},{10,... | collective-permute-start | bytes 86024 | tf_op jit(solution)/shard_map/ppermute | solution.py:407
  68.7 3.9 %collective-permute-start.17 = (bf16[112,128]{1,0:T(8,128)(2,1)S(1)}, bf16[112,128]{1,0:T(8,128)(2,1)S(1)}, u32[]{:S(2)}, u32[]{:S(2)}) collective-permute-start(bf16[112,128]{1,0:T(8,128)(2,1)S(1)} %collective-permute-done.16), channel_id=1, source_target_pairs={{0,2},{1,3},{2,0},{3,1},{4,6},{5,7},{6,4},{7,5},{8,10},{9,11},{10,... | collective-permute-start | bytes 86024 | tf_op jit(solution)/shard_map/ppermute | solution.py:407
  74.2 1.6 %collective-permute-start.22 = (f32[224,256]{1,0:T(8,128)S(1)}, f32[224,256]{1,0:T(8,128)S(1)}, u32[]{:S(2)}, u32[]{:S(2)}) collective-permute-start(f32[224,256]{1,0:T(8,128)S(1)} %constant_dynamic-slice_fusion.2), channel_id=1, source_target_pairs={{0,1},{1,0},{2,3},{3,2},{4,5},{5,4},{6,7},{7,6},{8,9},{9,8},{10,11... | collective-permute-start | bytes 688136 | tf_op jit(solution)/shard_map/ppermute | solution.py:410
  76.7 18.2 %copy-start.10 = (bf16[224,256]{1,0:T(8,128)(2,1)}, bf16[224,256]{1,0:T(8,128)(2,1)S(1)}, u32[]{:S(2)}) copy-start(bf16[224,256]{1,0:T(8,128)(2,1)S(1)} %add_convert_fusion.refs_0_) | copy-start | bytes 344068
  76.8 7.9 %collective-permute-start.24 = (bf16[224,256]{1,0:T(8,128)(2,1)S(1)}, bf16[224,256]{1,0:T(8,128)(2,1)S(1)}, u32[]{:S(2)}, u32[]{:S(2)}) collective-permute-start(bf16[224,256]{1,0:T(8,128)(2,1)S(1)} %add_convert_fusion.refs_0_), channel_id=1, source_target_pairs={{0,4},{1,5},{2,6},{3,7},{4,8},{5,9},{6,10},{7,11},{8,12},{9,13},{1... | collective-permute-start | bytes 344072 | tf_op jit(solution)/shard_map/ppermute | solution.py:404
  77.0 11.8 %collective-permute-start.26 = (bf16[224,256]{1,0:T(8,128)(2,1)S(1)}, bf16[224,256]{1,0:T(8,128)(2,1)S(1)}, u32[]{:S(2)}, u32[]{:S(2)}) collective-permute-start(bf16[224,256]{1,0:T(8,128)(2,1)S(1)} %add_convert_fusion.refs_0_), channel_id=1, source_target_pairs={{0,8},{1,9},{2,10},{3,11},{4,12},{5,13},{6,14},{7,15},{8,0},{9,1},... | collective-permute-start | bytes 344072 | tf_op jit(solution)/shard_map/ppermute | solution.py:404
  78.7 10.7 %collective-permute-start.28 = (bf16[224,256]{1,0:T(8,128)(2,1)S(1)}, bf16[224,256]{1,0:T(8,128)(2,1)S(1)}, u32[]{:S(2)}, u32[]{:S(2)}) collective-permute-start(bf16[224,256]{1,0:T(8,128)(2,1)S(1)} %add_convert_fusion.refs_0_), channel_id=1, source_target_pairs={{0,12},{1,13},{2,14},{3,15},{4,0},{5,1},{6,2},{7,3},{8,4},{9,5},{1... | collective-permute-start | bytes 344072 | tf_op jit(solution)/shard_map/ppermute | solution.py:404
  80.8 10.0 %collective-permute-start.23 = (bf16[224,256]{1,0:T(8,128)(2,1)S(1)}, bf16[224,256]{1,0:T(8,128)(2,1)S(1)}, u32[]{:S(2)}, u32[]{:S(2)}) collective-permute-start(bf16[224,256]{1,0:T(8,128)(2,1)S(1)} %add_convert_fusion.refs_0_), channel_id=1, source_target_pairs={{0,2},{1,3},{2,0},{3,1},{4,6},{5,7},{6,4},{7,5},{8,10},{9,11},{10,... | collective-permute-start | bytes 344072 | tf_op jit(solution)/shard_map/ppermute | solution.py:407
  84.7 10.2 %copy-start.23 = (bf16[224,256]{1,0:T(8,128)(2,1)}, bf16[224,256]{1,0:T(8,128)(2,1)S(1)}, u32[]{:S(2)}) copy-start(bf16[224,256]{1,0:T(8,128)(2,1)S(1)} %collective-permute-done.24.refs_2_) | copy-start | bytes 344068
  84.7 6.1 %collective-permute-start.25 = (bf16[224,256]{1,0:T(8,128)(2,1)S(1)}, bf16[224,256]{1,0:T(8,128)(2,1)S(1)}, u32[]{:S(2)}, u32[]{:S(2)}) collective-permute-start(bf16[224,256]{1,0:T(8,128)(2,1)S(1)} %collective-permute-done.24.refs_2_), channel_id=1, source_target_pairs={{0,2},{1,3},{2,0},{3,1},{4,6},{5,7},{6,4},{7,5},{8,10},{9,11},{10,... | collective-permute-start | bytes 344072 | tf_op jit(solution)/shard_map/ppermute | solution.py:407
  88.8 6.1 %copy-start.24 = (bf16[224,256]{1,0:T(8,128)(2,1)}, bf16[224,256]{1,0:T(8,128)(2,1)S(1)}, u32[]{:S(2)}) copy-start(bf16[224,256]{1,0:T(8,128)(2,1)S(1)} %collective-permute-done.26.refs_4_) | copy-start | bytes 344068
  88.8 4.9 %collective-permute-start.27 = (bf16[224,256]{1,0:T(8,128)(2,1)S(1)}, bf16[224,256]{1,0:T(8,128)(2,1)S(1)}, u32[]{:S(2)}, u32[]{:S(2)}) collective-permute-start(bf16[224,256]{1,0:T(8,128)(2,1)S(1)} %collective-permute-done.26.refs_4_), channel_id=1, source_target_pairs={{0,2},{1,3},{2,0},{3,1},{4,6},{5,7},{6,4},{7,5},{8,10},{9,11},{10,... | collective-permute-start | bytes 344072 | tf_op jit(solution)/shard_map/ppermute | solution.py:407
  89.4 5.5 %copy-start.25 = (bf16[224,256]{1,0:T(8,128)(2,1)}, bf16[224,256]{1,0:T(8,128)(2,1)S(1)}, u32[]{:S(2)}) copy-start(bf16[224,256]{1,0:T(8,128)(2,1)S(1)} %collective-permute-done.28.refs_6_) | copy-start | bytes 344068
  89.4 5.5 %collective-permute-start.29 = (bf16[224,256]{1,0:T(8,128)(2,1)S(1)}, bf16[224,256]{1,0:T(8,128)(2,1)S(1)}, u32[]{:S(2)}, u32[]{:S(2)}) collective-permute-start(bf16[224,256]{1,0:T(8,128)(2,1)S(1)} %collective-permute-done.28.refs_6_), channel_id=1, source_target_pairs={{0,2},{1,3},{2,0},{3,1},{4,6},{5,7},{6,4},{7,5},{8,10},{9,11},{10,... | collective-permute-start | bytes 344072 | tf_op jit(solution)/shard_map/ppermute | solution.py:407
  90.8 4.1 %copy-start.26 = (bf16[224,256]{1,0:T(8,128)(2,1)}, bf16[224,256]{1,0:T(8,128)(2,1)S(1)}, u32[]{:S(2)}) copy-start(bf16[224,256]{1,0:T(8,128)(2,1)S(1)} %collective-permute-done.23.refs_1_) | copy-start | bytes 344068
  90.8 4.1 %copy-start.27 = (bf16[224,256]{1,0:T(8,128)(2,1)}, bf16[224,256]{1,0:T(8,128)(2,1)S(1)}, u32[]{:S(2)}) copy-start(bf16[224,256]{1,0:T(8,128)(2,1)S(1)} %collective-permute-done.25.refs_3_) | copy-start | bytes 344068
  100.8 1.9 %collective-permute-start.32 = (f32[128,768]{1,0:T(8,128)}, f32[128,768]{1,0:T(8,128)S(1)}, u32[]{:S(2)}, u32[]{:S(2)}) collective-permute-start(f32[128,768]{1,0:T(8,128)} %get-tuple-element.23), channel_id=1, source_target_pairs={{0,1},{1,0},{2,3},{3,2},{4,5},{5,4},{6,7},{7,6},{8,9},{9,8},{10,11... | collective-permute-start | bytes 1179656 | tf_op jit(solution)/shard_map/ppermute | solution.py:410
  100.8 1.9 %copy-start.1 = (bf16[160,4096]{1,0:T(8,128)(2,1)}, bf16[160,4096]{1,0:T(8,128)(2,1)S(1)}, u32[]{:S(2)}) copy-start(bf16[160,4096]{1,0:T(8,128)(2,1)S(1)} %collective-permute-done.33.down_other_ref) | copy-start | bytes 3932164
  107.0 7.4 %collective-permute-start.35 = (bf16[16,4096]{1,0:T(8,128)(2,1)}, bf16[16,4096]{1,0:T(8,128)(2,1)S(1)}, u32[]{:S(2)}, u32[]{:S(2)}) collective-permute-start(bf16[16,4096]{1,0:T(8,128)(2,1)} %get-tuple-element.26), channel_id=1, source_target_pairs={{0,2},{1,3},{2,0},{3,1},{4,6},{5,7},{6,4},{7,5},{8,10},{9,11},{10,... | collective-permute-start | bytes 393224 | tf_op jit(solution)/shard_map/ppermute | solution.py:407
  108.5 10.2 %collective-permute-start.37 = (bf16[16,4096]{1,0:T(8,128)(2,1)}, bf16[16,4096]{1,0:T(8,128)(2,1)S(1)}, u32[]{:S(2)}, u32[]{:S(2)}) collective-permute-start(bf16[16,4096]{1,0:T(8,128)(2,1)} %get-tuple-element.27), channel_id=1, source_target_pairs={{0,2},{1,3},{2,0},{3,1},{4,6},{5,7},{6,4},{7,5},{8,10},{9,11},{10,... | collective-permute-start | bytes 393224 | tf_op jit(solution)/shard_map/ppermute | solution.py:407
  109.0 14.9 %collective-permute-start.39 = (bf16[16,4096]{1,0:T(8,128)(2,1)}, bf16[16,4096]{1,0:T(8,128)(2,1)S(1)}, u32[]{:S(2)}, u32[]{:S(2)}) collective-permute-start(bf16[16,4096]{1,0:T(8,128)(2,1)} %get-tuple-element.28), channel_id=1, source_target_pairs={{0,2},{1,3},{2,0},{3,1},{4,6},{5,7},{6,4},{7,5},{8,10},{9,11},{10,... | collective-permute-start | bytes 393224 | tf_op jit(solution)/shard_map/ppermute | solution.py:407
  110.5 18.4 %collective-permute-start.34 = (bf16[16,4096]{1,0:T(8,128)(2,1)}, bf16[16,4096]{1,0:T(8,128)(2,1)S(1)}, u32[]{:S(2)}, u32[]{:S(2)}) collective-permute-start(bf16[16,4096]{1,0:T(8,128)(2,1)} %get-tuple-element.25), channel_id=1, source_target_pairs={{0,2},{1,3},{2,0},{3,1},{4,6},{5,7},{6,4},{7,5},{8,10},{9,11},{10,... | collective-permute-start | bytes 393224 | tf_op jit(solution)/shard_map/ppermute | solution.py:407
  116.9 10.7 %copy-start.31 = (bf16[16,2048]{1,0:T(8,128)(2,1)S(1)}, bf16[16,2048]{1,0:T(8,128)(2,1)}, u32[]{:S(2)}) copy-start(bf16[16,2048]{1,0:T(8,128)(2,1)} %get-tuple-element.30) | copy-start | bytes 196612
  116.9 12.0 %collective-permute-start.36 = (bf16[16,4096]{1,0:T(8,128)(2,1)}, bf16[16,4096]{1,0:T(8,128)(2,1)S(1)}, u32[]{:S(2)}, u32[]{:S(2)}) collective-permute-start(bf16[16,4096]{1,0:T(8,128)(2,1)} %add.216), channel_id=1, source_target_pairs={{0,8},{1,9},{2,10},{3,11},{4,12},{5,13},{6,14},{7,15},{8,0},{9,1},... | collective-permute-start | bytes 393224 | tf_op jit(solution)/shard_map/ppermute | solution.py:404
  121.3 7.9 %collective-permute-start.38 = (bf16[16,4096]{1,0:T(8,128)(2,1)}, bf16[16,4096]{1,0:T(8,128)(2,1)S(1)}, u32[]{:S(2)}, u32[]{:S(2)}) collective-permute-start(bf16[16,4096]{1,0:T(8,128)(2,1)} %add.217), channel_id=1, source_target_pairs={{0,4},{1,5},{2,6},{3,7},{4,8},{5,9},{6,10},{7,11},{8,12},{9,13},{1... | collective-permute-start | bytes 393224 | tf_op jit(solution)/shard_map/ppermute | solution.py:404
  126.5 5.2 %collective-permute-start.40 = (bf16[16,4096]{1,0:T(8,128)(2,1)}, bf16[16,4096]{1,0:T(8,128)(2,1)S(1)}, u32[]{:S(2)}, u32[]{:S(2)}) collective-permute-start(bf16[16,4096]{1,0:T(8,128)(2,1)} %add.218), channel_id=1, source_target_pairs={{0,12},{1,13},{2,14},{3,15},{4,0},{5,1},{6,2},{7,3},{8,4},{9,5},{1... | collective-permute-start | bytes 393224 | tf_op jit(solution)/shard_map/ppermute | solution.py:404
  127.7 1.3 collective-permute-start.41
  128.9 2.7 %copy-start.30 = (bf16[16,2048]{1,0:T(8,128)(2,1)}, bf16[16,2048]{1,0:T(8,128)(2,1)S(1)}, u32[]{:S(2)}) copy-start(bf16[16,2048]{1,0:T(8,128)(2,1)S(1)} %collective-permute-done.41.refs_6_) | copy-start | bytes 196612
  128.9 2.7 %copy-start.16 = (bf16[16,4096]{1,0:T(8,128)(2,1)}, bf16[16,4096]{1,0:T(8,128)(2,1)S(1)}, u32[]{:S(2)}) copy-start(bf16[16,4096]{1,0:T(8,128)(2,1)S(1)} %collective-permute-done.34.refs_1_) | copy-start | bytes 393220
  128.9 2.7 %copy-start.17 = (bf16[16,4096]{1,0:T(8,128)(2,1)}, bf16[16,4096]{1,0:T(8,128)(2,1)S(1)}, u32[]{:S(2)}) copy-start(bf16[16,4096]{1,0:T(8,128)(2,1)S(1)} %collective-permute-done.36.refs_2_) | copy-start | bytes 393220
  129.1 2.5 %copy-start.18 = (bf16[16,4096]{1,0:T(8,128)(2,1)}, bf16[16,4096]{1,0:T(8,128)(2,1)S(1)}, u32[]{:S(2)}) copy-start(bf16[16,4096]{1,0:T(8,128)(2,1)S(1)} %collective-permute-done.38.refs_3_) | copy-start | bytes 393220
  (10 other events, 7.7 us)

commit v3 on v2

--- a/solution.py
+++ b/solution.py
@@ -12,7 +12,7 @@
 BLK = 4
 CAP = 3
 AXIS = "tensor"
-VMEM_LIMIT = 60 * 1024 * 1024
+VMEM_LIMIT = 28 * 1024 * 1024
 
 
 def by_rows(left, weight):
@@ -106,6 +106,58 @@
     base = pl.multiple_of(start // 128 * 128, 128)
     window = ref[:, pl.ds(base, 128)].astype(jnp.float32)
     return pltpu.roll(window, (128 - start % 128) % 128, 1)[:, :width]
+
+
+def slab_kernel(weight_ref, *out_refs):
+    zi = place()[1]
+    features = weight_ref.shape[1]
+    wide = out_refs[0].shape[1] // 2
+    for d, out_ref in enumerate(out_refs):
+        for core in range(2):
+            start = pl.multiple_of(core * (features // 2) + (zi ^ d) * wide, 128)
+            out_ref[:, core * wide : (core + 1) * wide] = weight_ref[:, pl.ds(start, wide)]
+
+
+def half_kernel(gate_ref, up_ref, gate_out_ref, up_out_ref):
+    half = gate_out_ref.shape[1]
+    other = pl.ds(pl.multiple_of((1 - place()[3]) * half, 128), half)
+    gate_out_ref[...] = gate_ref[:, other]
+    up_out_ref[...] = up_ref[:, other]
+
+
+def strip_kernel(*refs):
+    slabs, (keep_ref, send_ref) = refs[:-2], refs[-2:]
+    yi = place()[2]
+    rows, wide = slabs[0].shape
+    width = wide // 4
+    for d, slab in enumerate(slabs):
+        parts = [slab[:, i * width : (i + 1) * width] for i in range(4)]
+        low = jnp.concatenate([parts[0], parts[2]], axis=1)
+        high = jnp.concatenate([parts[1], parts[3]], axis=1)
+        keep_ref[d * rows : (d + 1) * rows, :] = jnp.where(yi == 0, low, high)
+        send_ref[d * rows : (d + 1) * rows, :] = jnp.where(yi == 0, high, low)
+
+
+def out_kernel(*refs):
+    contexts, (near_ref, far_ref, mine_ref, other_ref) = refs[:-4], refs[-4:]
+    width = mine_ref.shape[1]
+    ci = place()[3]
+    half = contexts[0].shape[0] // 2
+
+    def heads(first):
+        values = [ref[first : first + half, :] for ref in contexts]
+        return jnp.concatenate(
+            [
+                jnp.concatenate([v[:, :HDIM] for v in values], axis=1),
+                jnp.concatenate([v[:, HDIM:] for v in values], axis=1),
+            ],
+            axis=0,
+        )
+
+    attended = dot(heads(0), near_ref[...]) + dot(heads(half), far_ref[...])
+    low, high = attended[:, :width], attended[:, width:]
+    mine_ref[...] = jnp.where(ci == 0, low, high)
+    other_ref[...] = jnp.where(ci == 0, high, low)
 
 
 def projection_kernel(piece_rows, *refs):
@@ -232,7 +284,7 @@
         token % query_rows,
         query_rows + before + (token - query_total) % BLK,
     )
-    source = ((zi - owner // 4 + 4 * nz) % nz) * 2 + (((owner // 2) % 2) ^ yi)
+    source = (zi ^ (owner // 4)) * 2 + (((owner // 2) % 2) ^ yi)
     pieces = 2 * nz
     spot = source * (full * 8) + local
     if halved:
@@ -283,7 +335,7 @@
     row = lax.broadcasted_iota(jnp.int32, (total, 1), 0)
     core = jnp.where(row < slots, ci, 1 - ci)
     chunk = (row % slots) // chunk_rows
-    device = ((zi + chunk // 2) % nz) * 4 + ((chunk % 2) ^ yi) * 2 + core
+    device = (zi ^ (chunk // 2)) * 4 + ((chunk % 2) ^ yi) * 2 + core
     wanted = device * rows_here + jnp.minimum(row % chunk_rows, rows_here - 1)
     lanes = lax.broadcasted_iota(jnp.int32, (total, tokens), 1)
     order_ref[...] = (lanes == wanted).astype(jnp.bfloat16)
@@ -295,7 +347,7 @@
             jnp.concatenate([near, far], axis=1),
             jnp.concatenate([far, near], axis=1),
         )
-        start = pl.multiple_of(((zi - dz + nz) % nz) * (2 * width), 128)
+        start = pl.multiple_of((zi ^ dz) * (2 * width), 128)
         values = dot(order_ref[...], pair)
         squares = squares + jnp.sum(values * values, axis=-1, keepdims=True)
         kept_ref[:, pl.ds(start, 2 * width)] = values[0:chunk_rows].astype(jnp.bfloat16)
@@ -343,24 +395,24 @@
         refs[dz][...] = result[dz * chunk_rows : (dz + 1) * chunk_rows].astype(jnp.bfloat16)
 
 
-def down_kernel(chunk_rows, hidden_ref, down_ref, down_other_ref, out_ref):
+def down_kernel(hidden_ref, down_ref, down_other_ref, *out_refs):
+    chunk_rows = out_refs[0].shape[0]
     units = down_ref.shape[0]
     hidden = hidden_ref[...]
     near = jnp.concatenate(
         [
             hidden[2 * dz * chunk_rows : (2 * dz + 1) * chunk_rows]
-            for dz in range(hidden.shape[0] // chunk_rows // 2)
+            for dz in range(len(out_refs))
         ],
         axis=0,
     )
-    out_ref[...] = dot(near[:, :units], down_ref[...]) + dot(near[:, units:], down_other_ref[...])
-
-
-def add_kernel(first_row, near_ref, far_ref, out_ref):
-    rows = out_ref.shape[0]
-    out_ref[...] = (
-        near_ref[first_row : first_row + rows, :] + far_ref[...].astype(jnp.float32)
-    ).astype(jnp.bfloat16)
+    result = dot(near[:, :units], down_ref[...]) + dot(near[:, units:], down_other_ref[...])
+    for dz in range(len(out_refs)):
+        out_refs[dz][...] = result[dz * chunk_rows : (dz + 1) * chunk_rows]
+
+
+def add_kernel(near_ref, far_ref, out_ref):
+    out_ref[...] = (near_ref[...] + far_ref[...].astype(jnp.float32)).astype(jnp.bfloat16)
 
 
 def last_kernel(count, *refs):
@@ -371,7 +423,7 @@
     rows = out_ref.shape[0]
     half = kept_ref.shape[1]
     kept, other = kept_ref[...].astype(jnp.float32), kept_other_ref[...].astype(jnp.float32)
-    total = near_ref[0 : far_ref.shape[0], :] + far_ref[...].astype(jnp.float32)
+    total = near_ref[...] + far_ref[...].astype(jnp.float32)
     for ref in arrived:
         total = total + ref[...].astype(jnp.float32)
     low, high = jnp.where(ci == 0, kept, other), jnp.where(ci == 0, other, kept)
@@ -398,10 +450,10 @@
     devices = lax.axis_size(AXIS)
     nz = devices // 4
     _, zi, yi, ci = place()
-    z_order = sorted(range(1, nz), key=lambda k: -min(k, nz - k))
+    z_order = [k for k in (2, 1) if k < nz] + list(range(3, nz))
 
     def along_z(value, k):
-        return lax.ppermute(value, AXIS, [(i, (i + 4 * k) % devices) for i in range(devices)])
+        return lax.ppermute(value, AXIS, [(i, i ^ (4 * k)) for i in range(devices)])
 
     def across_y(value):
         return lax.ppermute(value, AXIS, [(i, i ^ 2) for i in range(devices)])
@@ -413,7 +465,9 @@
         near = {0: value}
         for k in z_order:
             near[k] = along_z(value, k)
-        far = {k: across_y(near[k]) for k in [0] + z_order}
+        return near, {k: across_y(near[k]) for k in [0] + z_order}
+
+    def paired(near, far):
         return [piece for k in range(nz) for piece in (near[k], far[k])]
 
     owners = block_owner[:, 0]
@@ -444,41 +498,38 @@
 
     projections = [query_weight, key_weight, value_weight]
     projections_other = [across_core(w) for w in projections]
-    other_half = (1 - ci) * half
-    gate_other = across_core(lax.dynamic_slice_in_dim(gate_weight, other_half, half, 1))
-    up_other = across_core(lax.dynamic_slice_in_dim(up_weight, other_half, half, 1))
     down_other = across_core(down_weight)
-
-    def out_block(dz, dy):
-        chip = 2 * ((zi + dz) % nz) + (yi ^ dy)
-        return jnp.concatenate(
-            [
-                lax.dynamic_slice_in_dim(out_weight, chip * width, width, 1),
-                lax.dynamic_slice_in_dim(out_weight, half + chip * width, width, 1),
-            ],
-            axis=1,
-        )
-
-    out_far = across_y(jnp.concatenate([out_block(dz, 1) for dz in range(nz)], axis=0))
-    out_pairs = [
-        jnp.concatenate(
-            [out_block(dz, 0), out_far[dz * heads_rows : (dz + 1) * heads_rows]], axis=0
-        )
-        for dz in range(nz)
-    ]
-    out_columns = jnp.concatenate(
-        [out_pairs[0]] + [along_z(out_pairs[k], k) for k in range(1, nz)], axis=0
-    )
+    slab = shape((heads_rows, 4 * width), bf16)
+    slabs = kernel_call(
+        slab_kernel, (slab,) * nz, [VMEM], name="slabs"
+    )(out_weight)
+    gate_half, up_half = kernel_call(
+        half_kernel,
+        (shape((units, half), bf16),) * 2,
+        [VMEM, VMEM],
+        name="halves",
+    )(gate_weight, up_weight)
+    gate_other, up_other = across_core(gate_half), across_core(up_half)
 
     plane_rows = 2 * nz * (full * 8 + halved * 4)
     wide = 256 + -(-width // 128) * 128
+    near, far = plane_gather(piece)
     own, away = kernel_call(
         functools.partial(projection_kernel, query_rows + CAP * BLK),
         (shape((plane_rows, wide), bf16), shape((plane_rows, wide), bf16)),
         [VMEM] * (2 * nz + 7),
         [pltpu.VMEM((plane_rows, features), bf16)],
         name="project",
-    )(*plane_gather(piece), gain_attn[None, :], *projections, *projections_other)
+    )(*paired(near, far), gain_attn[None, :], *projections, *projections_other)
+
+    slabs = list(slabs)
+    slabs[1:], _ = lax.optimization_barrier((slabs[1:], near[z_order[0]]))
+    slabs = [slabs[0]] + [along_z(slabs[k], k) for k in range(1, nz)]
+    strip = shape((nz * heads_rows, 2 * width), bf16)
+    strip_near, strip_send = kernel_call(
+        strip_kernel, (strip, strip), [VMEM] * nz, name="strips"
+    )(*slabs)
+    strip_far = across_y(strip_send)
 
     context, columns = kernel_call(
         functools.partial(attention_kernel, query_rows, width),
@@ -487,14 +538,15 @@
         name="attend",
     )(owners, segment, own, across_core(away))
 
-    contexts = plane_gather(context)
-    context_all = jnp.concatenate(
-        [jnp.concatenate([x[:, :HDIM], x[:, HDIM:]], axis=0) for x in contexts], axis=1
-    )
-    attended = dot(context_all, out_columns)
-    attended_mine = lax.dynamic_slice_in_dim(attended, ci * width, width, 1)
-    attended_other = across_core(lax.dynamic_slice_in_dim(attended, (1 - ci) * width, width, 1))
-    middle = (columns.astype(f32) + attended_mine + attended_other).astype(bf16)
+    contexts = jnp.concatenate([context, across_y(context)], axis=0)
+    contexts = [contexts] + [along_z(contexts, k) for k in range(1, nz)]
+    attended_mine, attended_other = kernel_call(
+        out_kernel,
+        (shape((tokens, width), f32),) * 2,
+        [VMEM] * (nz + 2),
+        name="out",
+    )(*contexts, strip_near, strip_far)
+    middle = (columns.astype(f32) + attended_mine + across_core(attended_other)).astype(bf16)
 
     slots = 2 * nz * chunk_rows
     lanes = -(-(4 * units + 1) // 128) * 128
@@ -509,7 +561,7 @@
         [VMEM] * (2 * nz + 5),
         [pltpu.VMEM((2 * slots, tokens), bf16), pltpu.VMEM((2 * slots, half), bf16)],
         name="gate_up",
-    )(*plane_gather(middle), gain_ffn[None, :], gate_weight, up_weight, gate_other, up_other)
+    )(*paired(*plane_gather(middle)), gain_ffn[None, :], gate_weight, up_weight, gate_other, up_other)
     came = across_core(send)
     kept_other = across_core(kept_send)
 
@@ -522,23 +574,21 @@
     )(keep, came, down_weight, down_other)
     moved = {k: across_y(far[k]) for k in z_order + [0]}
     near = kernel_call(
-        functools.partial(down_kernel, chunk_rows),
-        shape((nz * chunk_rows, features), f32),
+        down_kernel,
+        (shape((chunk_rows, features), f32),) * nz,
         [VMEM] * 3,
         name="down",
     )(hidden, down_weight, down_other)
     arrived = []
     for k in z_order:
-        part = kernel_call(
-            functools.partial(add_kernel, k * chunk_rows), chunk, [VMEM, VMEM], name="add"
-        )(near, moved[k])
+        part = kernel_call(add_kernel, chunk, [VMEM, VMEM], name="add")(near[k], moved[k])
         arrived.append(along_z(part, k))
     return kernel_call(
         functools.partial(last_kernel, len(arrived)),
         shape((rows_here, features), bf16),
         [VMEM] * (len(arrived) + 4),
         name="last",
-    )(near, moved[0], *arrived, kept, kept_other)
+    )(near[0], moved[0], *arrived, kept, kept_other)
 
 
 def solution(mesh):

time: 135 us -> 121 us (0.90)
  Pallas kernels: 31.5 us -> 10.2 us
  waiting for transfers between devices: 42.8 us -> 60.7 us
  local copies, waits for them, and re-layouts: 11.4 us -> 3.81 us
  other arithmetic: 4 us -> 0.04 us
  starting transfers between devices: 43.1 us -> 45.5 us
    ppermute x15, waiting for transfers between devices: 20.6 us -> 35.8 us  [along_z(): return lax.ppermute(value, AXIS, [(i, i ^ 4 * k) for i in range(devices)])]
    pallas_call x4 -> x8, Pallas kernels: 9 us -> 1.16 us  [the longest x1 0.55 us: body(): kernel_call(down_kernel, (shape((chunk_rows, features), f32),) * nz, [VME...]
    pallas_call x1, Pallas kernels: 5.24 us -> 1.86 us  [body(): kernel_call(functools.partial(gate_kernel, rows_here, chunk_rows), (shape...]
    ppermute x15, starting transfers between devices: 24.3 us -> 27.4 us  [along_z(): return lax.ppermute(value, AXIS, [(i, i ^ 4 * k) for i in range(devices)])]
    pallas_call x1, Pallas kernels: 5.68 us -> 2.59 us  [body(): kernel_call(functools.partial(projection_kernel, query_rows + CAP * BLK),...]
    concatenate x8 -> x0, other arithmetic: 3.04 us -> none  [the longest x3 2.23 us: body(): jnp.concatenate([out_block(dz, 0), out_far[dz * heads_rows:(dz + 1) * hea...]
    ppermute x17 -> x14, waiting for transfers between devices: 17.6 us -> 20.4 us  [across_y(): return lax.ppermute(value, AXIS, [(i, i ^ 2) for i in range(devices)])]
    pallas_call x1, Pallas kernels: 3.51 us -> 0.8 us  [body(): kernel_call(functools.partial(hidden_kernel, features), (chunk,) * nz + (...]
  transfers between devices with their start and end apart: 42 -> 39, of which waited for: 20 -> 23; matrix products, arithmetic and copies ran while one was open for 8% -> 0% of each run, Pallas kernels for 17% -> 4%
where the time goes in v3:
time: 121 us
  waiting for transfers between devices  60.7 us (50%)
  starting transfers between devices  45.5 us (38%)
  Pallas kernels  10.2 us (8%)
  local copies, waits for them, and re-layouts  3.81 us (3%)
    ppermute x15, waiting for transfers between devices, along_z(): return lax.ppermute(value, AXIS, [(i, i ^ 4 * k) for i in range(devices)])  35.8 us
    ppermute x15, starting transfers between devices, along_z(): return lax.ppermute(value, AXIS, [(i, i ^ 4 * k) for i in range(devices)])  27.4 us
    ppermute x14, waiting for transfers between devices, across_y(): return lax.ppermute(value, AXIS, [(i, i ^ 2) for i in range(devices)])  20.4 us
    ppermute x14, starting transfers between devices, across_y(): return lax.ppermute(value, AXIS, [(i, i ^ 2) for i in range(devices)])  17.3 us
    ppermute x10, waiting for transfers between devices, across_core(): return lax.ppermute(value, AXIS, [(i, i ^ 1) for i in range(devices)])  4.44 us
    unnamed x31, local copies, waits for them, and re-layouts  3.8 us
    pallas_call x1, Pallas kernels, body(): kernel_call(functools.partial(projection_kernel, query_rows + CAP * BLK),...  2.59 us
  transfers between devices with their start and end apart: 39, of which 23 were waited for; matrix products, arithmetic and copies ran while one was open for 0% of the time, Pallas kernels for 4%

profile of v3, /device:TPU:0, one launch (start us, length us, event | category | flops | bytes accessed | tf_op | source)
XLA Modules:
  0.0 120.5 jit_solution(9147199587524657756)
XLA Ops:
  0.0 1.6 %copy-done.3 = bf16[64,4,4096]{2,1,0:T(4,128)(2,1)S(1)} copy-done((bf16[64,4,4096]{2,1,0:T(4,128)(2,1)S(1)}, bf16[64,4,4096]{2,1,0:T(4,128)(2,1)}, u32[]{:S(2)}) %copy-start.3) | copy-done | bytes 2097176
  1.6 0.8 copy-done.8
  2.4 0.7 copy-done.11
  3.1 0.7 copy-done.14
  3.8 1.0 fetch.1.refs_0_
  4.7 4.1 %collective-permute-start.3 = (bf16[8,10240]{1,0:T(8,128)(2,1)S(1)}, bf16[8,10240]{1,0:T(8,128)(2,1)S(1)}, u32[]{:S(2)}, u32[]{:S(2)}) collective-permute-start(bf16[8,10240]{1,0:T(8,128)(2,1)S(1)} %fetch.1.refs_0_), channel_id=1, source_target_pairs={{0,8},{1,9},{2,10},{3,11},{4,12},{5,13},{6,14},{7,15},{8,0},{9,1},... | collective-permute-start | bytes 491528 | tf_op jit(solution)/shard_map/ppermute | solution.py:456
  8.8 0.5 collective-permute-start.8
  9.4 1.6 %collective-permute-start.1 = (bf16[8,10240]{1,0:T(8,128)(2,1)S(1)}, bf16[8,10240]{1,0:T(8,128)(2,1)S(1)}, u32[]{:S(2)}, u32[]{:S(2)}) collective-permute-start(bf16[8,10240]{1,0:T(8,128)(2,1)S(1)} %fetch.1.refs_0_), channel_id=1, source_target_pairs={{0,4},{1,5},{2,6},{3,7},{4,0},{5,1},{6,2},{7,3},{8,12},{9,13},{10,... | collective-permute-start | bytes 491528 | tf_op jit(solution)/shard_map/ppermute | solution.py:456
  11.0 5.6 %collective-permute-done.3.refs_4_ = bf16[8,10240]{1,0:T(8,128)(2,1)S(1)} collective-permute-done((bf16[8,10240]{1,0:T(8,128)(2,1)S(1)}, bf16[8,10240]{1,0:T(8,128)(2,1)S(1)}, u32[]{:S(2)}, u32[]{:S(2)}) %collective-permute-start.3) | collective-permute-done | bytes 163872 | tf_op jit(solution)/shard_map/ppermute | solution.py:456
  16.6 3.5 %collective-permute-start.5 = (bf16[8,10240]{1,0:T(8,128)(2,1)S(1)}, bf16[8,10240]{1,0:T(8,128)(2,1)S(1)}, u32[]{:S(2)}, u32[]{:S(2)}) collective-permute-start(bf16[8,10240]{1,0:T(8,128)(2,1)S(1)} %fetch.1.refs_0_), channel_id=1, source_target_pairs={{0,12},{1,13},{2,14},{3,15},{4,8},{5,9},{6,10},{7,11},{8,4},{9,5},... | collective-permute-start | bytes 491528 | tf_op jit(solution)/shard_map/ppermute | solution.py:456
  20.2 1.5 %collective-permute-start = (bf16[8,10240]{1,0:T(8,128)(2,1)S(1)}, bf16[8,10240]{1,0:T(8,128)(2,1)S(1)}, u32[]{:S(2)}, u32[]{:S(2)}) collective-permute-start(bf16[8,10240]{1,0:T(8,128)(2,1)S(1)} %fetch.1.refs_0_), channel_id=1, source_target_pairs={{0,2},{1,3},{2,0},{3,1},{4,6},{5,7},{6,4},{7,5},{8,10},{9,11},{10,... | collective-permute-start | bytes 491528 | tf_op jit(solution)/shard_map/ppermute | solution.py:459
  21.7 2.9 %collective-permute-done.5.refs_6_ = bf16[8,10240]{1,0:T(8,128)(2,1)S(1)} collective-permute-done((bf16[8,10240]{1,0:T(8,128)(2,1)S(1)}, bf16[8,10240]{1,0:T(8,128)(2,1)S(1)}, u32[]{:S(2)}, u32[]{:S(2)}) %collective-permute-start.5) | collective-permute-done | bytes 163872 | tf_op jit(solution)/shard_map/ppermute | solution.py:456
  24.6 1.5 %collective-permute-start.4 = (bf16[8,10240]{1,0:T(8,128)(2,1)S(1)}, bf16[8,10240]{1,0:T(8,128)(2,1)S(1)}, u32[]{:S(2)}, u32[]{:S(2)}) collective-permute-start(bf16[8,10240]{1,0:T(8,128)(2,1)S(1)} %collective-permute-done.3.refs_4_), channel_id=1, source_target_pairs={{0,2},{1,3},{2,0},{3,1},{4,6},{5,7},{6,4},{7,5},{8,10},{9,11},{10,... | collective-permute-start | bytes 491528 | tf_op jit(solution)/shard_map/ppermute | solution.py:459
  26.1 1.4 %collective-permute-start.2 = (bf16[8,10240]{1,0:T(8,128)(2,1)S(1)}, bf16[8,10240]{1,0:T(8,128)(2,1)S(1)}, u32[]{:S(2)}, u32[]{:S(2)}) collective-permute-start(bf16[8,10240]{1,0:T(8,128)(2,1)S(1)} %collective-permute-done.1.refs_2_), channel_id=1, source_target_pairs={{0,2},{1,3},{2,0},{3,1},{4,6},{5,7},{6,4},{7,5},{8,10},{9,11},{10,... | collective-permute-start | bytes 491528 | tf_op jit(solution)/shard_map/ppermute | solution.py:459
  27.5 4.3 %collective-permute-done.4.refs_5_ = bf16[8,10240]{1,0:T(8,128)(2,1)S(1)} collective-permute-done((bf16[8,10240]{1,0:T(8,128)(2,1)S(1)}, bf16[8,10240]{1,0:T(8,128)(2,1)S(1)}, u32[]{:S(2)}, u32[]{:S(2)}) %collective-permute-start.4) | collective-permute-done | bytes 163872 | tf_op jit(solution)/shard_map/ppermute | solution.py:459
  31.8 1.5 %collective-permute-start.6 = (bf16[8,10240]{1,0:T(8,128)(2,1)S(1)}, bf16[8,10240]{1,0:T(8,128)(2,1)S(1)}, u32[]{:S(2)}, u32[]{:S(2)}) collective-permute-start(bf16[8,10240]{1,0:T(8,128)(2,1)S(1)} %collective-permute-done.5.refs_6_), channel_id=1, source_target_pairs={{0,2},{1,3},{2,0},{3,1},{4,6},{5,7},{6,4},{7,5},{8,10},{9,11},{10,... | collective-permute-start | bytes 491528 | tf_op jit(solution)/shard_map/ppermute | solution.py:459
  33.3 1.8 %collective-permute-done.2.refs_3_ = bf16[8,10240]{1,0:T(8,128)(2,1)S(1)} collective-permute-done((bf16[8,10240]{1,0:T(8,128)(2,1)S(1)}, bf16[8,10240]{1,0:T(8,128)(2,1)S(1)}, u32[]{:S(2)}, u32[]{:S(2)}) %collective-permute-start.2) | collective-permute-done | bytes 163872 | tf_op jit(solution)/shard_map/ppermute | solution.py:459
  35.1 2.0 %collective-permute-done.6.refs_7_ = bf16[8,10240]{1,0:T(8,128)(2,1)S(1)} collective-permute-done((bf16[8,10240]{1,0:T(8,128)(2,1)S(1)}, bf16[8,10240]{1,0:T(8,128)(2,1)S(1)}, u32[]{:S(2)}, u32[]{:S(2)}) %collective-permute-start.6) | collective-permute-done | bytes 163872 | tf_op jit(solution)/shard_map/ppermute | solution.py:459
  37.1 2.6 %project.1 = (bf16[160,512]{1,0:T(8,128)(2,1)S(1)}, bf16[160,512]{1,0:T(8,128)(2,1)S(1)}) custom-call(bf16[8,10240]{1,0:T(8,128)(2,1)S(1)} %fetch.1.refs_0_, bf16[8,10240]{1,0:T(8,128)(2,1)S(1)} %collective-permute-done.refs_1_, bf16[8,10240]{1,0:T(8,128)(2,1)S(1)} %collective-permute-done.1.refs_2_, bf16[8,10240]{1,0:T(8,128)(2,1)S(1)} %collective-permute-done.2.refs_3_, ...), custom_call_target="tpu_custom_call" | custom-call | tf_op jit(solution)/shard_map/project/pallas_call | solution.py:517
  39.9 2.4 %collective-permute-start.15 = (bf16[64,1024]{1,0:T(8,128)(2,1)S(1)}, bf16[64,1024]{1,0:T(8,128)(2,1)S(1)}, u32[]{:S(2)}, u32[]{:S(2)}) collective-permute-start(bf16[64,1024]{1,0:T(8,128)(2,1)S(1)} %get-tuple-element.43), channel_id=1, source_target_pairs={{0,4},{1,5},{2,6},{3,7},{4,0},{5,1},{6,2},{7,3},{8,12},{9,13},{10,... | collective-permute-start | bytes 393224 | tf_op jit(solution)/shard_map/ppermute | solution.py:456
  42.3 1.7 %collective-permute-start.16 = (bf16[64,1024]{1,0:T(8,128)(2,1)S(1)}, bf16[64,1024]{1,0:T(8,128)(2,1)S(1)}, u32[]{:S(2)}, u32[]{:S(2)}) collective-permute-start(bf16[64,1024]{1,0:T(8,128)(2,1)S(1)} %get-tuple-element.44), channel_id=1, source_target_pairs={{0,8},{1,9},{2,10},{3,11},{4,12},{5,13},{6,14},{7,15},{8,0},{9,1},... | collective-permute-start | bytes 393224 | tf_op jit(solution)/shard_map/ppermute | solution.py:456
  44.0 0.8 collective-permute-start.17
  44.9 3.1 %collective-permute-done.15.refs_1_ = bf16[64,1024]{1,0:T(8,128)(2,1)S(1)} collective-permute-done((bf16[64,1024]{1,0:T(8,128)(2,1)S(1)}, bf16[64,1024]{1,0:T(8,128)(2,1)S(1)}, u32[]{:S(2)}, u32[]{:S(2)}) %collective-permute-start.15) | collective-permute-done | bytes 131104 | tf_op jit(solution)/shard_map/ppermute | solution.py:456
  48.1 7.2 %collective-permute-done.16.refs_2_ = bf16[64,1024]{1,0:T(8,128)(2,1)S(1)} collective-permute-done((bf16[64,1024]{1,0:T(8,128)(2,1)S(1)}, bf16[64,1024]{1,0:T(8,128)(2,1)S(1)}, u32[]{:S(2)}, u32[]{:S(2)}) %collective-permute-start.16) | collective-permute-done | bytes 131104 | tf_op jit(solution)/shard_map/ppermute | solution.py:456
  55.3 1.6 %collective-permute-start.18 = (bf16[256,512]{1,0:T(8,128)(2,1)S(1)}, bf16[256,512]{1,0:T(8,128)(2,1)S(1)}, u32[]{:S(2)}, u32[]{:S(2)}) collective-permute-start(bf16[256,512]{1,0:T(8,128)(2,1)S(1)} %get-tuple-element.47), channel_id=1, source_target_pairs={{0,2},{1,3},{2,0},{3,1},{4,6},{5,7},{6,4},{7,5},{8,10},{9,11},{10,... | collective-permute-start | bytes 786440 | tf_op jit(solution)/shard_map/ppermute | solution.py:459
  56.9 2.1 %attend.1 = (bf16[112,128]{1,0:T(8,128)(2,1)S(1)}, bf16[224,256]{1,0:T(8,128)(2,1)S(1)}) custom-call(s32[24]{0:T(128)S(1)} %bitcast.6, s32[24]{0:T(128)S(1)} %copy-done.13, bf16[160,512]{1,0:T(8,128)(2,1)S(1)} %get-tuple-element.35.own_ref, bf16[160,512]{1,0:T(8,128)(2,1)S(1)} %collective-permute-done.10.away_ref), custom_call_target="tpu_custom_call" | custom-call | tf_op jit(solution)/shard_map/attend/pallas_call | solution.py:534
  59.0 0.6 collective-permute-start.11
  59.6 3.4 %collective-permute-done.11 = bf16[112,128]{1,0:T(8,128)(2,1)S(1)} collective-permute-done((bf16[112,128]{1,0:T(8,128)(2,1)S(1)}, bf16[112,128]{1,0:T(8,128)(2,1)S(1)}, u32[]{:S(2)}, u32[]{:S(2)}) %collective-permute-start.11) | collective-permute-done | bytes 28704 | tf_op jit(solution)/shard_map/ppermute | solution.py:459
  62.9 3.3 %collective-permute-start.12 = (bf16[224,128]{1,0:T(8,128)(2,1)S(1)}, bf16[224,128]{1,0:T(8,128)(2,1)S(1)}, u32[]{:S(2)}, u32[]{:S(2)}) collective-permute-start(bf16[224,128]{1,0:T(8,128)(2,1)S(1)} %constant_dynamic-update-slice_fusion.refs_0_), channel_id=1, source_target_pairs={{0,4},{1,5},{2,6},{3,7},{4,0},{5,1},{6,2},{7,3},{8,12},{9,13},{10,... | collective-permute-start | bytes 172040 | tf_op jit(solution)/shard_map/ppermute | solution.py:456
  66.2 0.5 collective-permute-start.13
  66.7 1.8 %collective-permute-done.12.refs_1_ = bf16[224,128]{1,0:T(8,128)(2,1)S(1)} collective-permute-done((bf16[224,128]{1,0:T(8,128)(2,1)S(1)}, bf16[224,128]{1,0:T(8,128)(2,1)S(1)}, u32[]{:S(2)}, u32[]{:S(2)}) %collective-permute-start.12) | collective-permute-done | bytes 57376 | tf_op jit(solution)/shard_map/ppermute | solution.py:456
  68.5 1.7 %collective-permute-start.14 = (bf16[224,128]{1,0:T(8,128)(2,1)S(1)}, bf16[224,128]{1,0:T(8,128)(2,1)S(1)}, u32[]{:S(2)}, u32[]{:S(2)}) collective-permute-start(bf16[224,128]{1,0:T(8,128)(2,1)S(1)} %constant_dynamic-update-slice_fusion.refs_0_), channel_id=1, source_target_pairs={{0,12},{1,13},{2,14},{3,15},{4,8},{5,9},{6,10},{7,11},{8,4},{9,5},... | collective-permute-start | bytes 172040 | tf_op jit(solution)/shard_map/ppermute | solution.py:456
  70.1 3.2 %collective-permute-done.13.refs_2_ = bf16[224,128]{1,0:T(8,128)(2,1)S(1)} collective-permute-done((bf16[224,128]{1,0:T(8,128)(2,1)S(1)}, bf16[224,128]{1,0:T(8,128)(2,1)S(1)}, u32[]{:S(2)}, u32[]{:S(2)}) %collective-permute-start.13) | collective-permute-done | bytes 57376 | tf_op jit(solution)/shard_map/ppermute | solution.py:456
  73.3 1.2 %collective-permute-done.14.refs_3_ = bf16[224,128]{1,0:T(8,128)(2,1)S(1)} collective-permute-done((bf16[224,128]{1,0:T(8,128)(2,1)S(1)}, bf16[224,128]{1,0:T(8,128)(2,1)S(1)}, u32[]{:S(2)}, u32[]{:S(2)}) %collective-permute-start.14) | collective-permute-done | bytes 57376 | tf_op jit(solution)/shard_map/ppermute | solution.py:456
  74.9 1.5 %collective-permute-done.19 = f32[224,256]{1,0:T(8,128)S(1)} collective-permute-done((f32[224,256]{1,0:T(8,128)S(1)}, f32[224,256]{1,0:T(8,128)S(1)}, u32[]{:S(2)}, u32[]{:S(2)}) %collective-permute-start.19) | collective-permute-done | bytes 229408 | tf_op jit(solution)/shard_map/ppermute | solution.py:462
  76.4 1.2 collective-permute-start.21
  77.6 1.1 collective-permute-start.23
  78.7 2.2 %collective-permute-start.25 = (bf16[224,256]{1,0:T(8,128)(2,1)S(1)}, bf16[224,256]{1,0:T(8,128)(2,1)S(1)}, u32[]{:S(2)}, u32[]{:S(2)}) collective-permute-start(bf16[224,256]{1,0:T(8,128)(2,1)S(1)} %add_convert_fusion.refs_0_), channel_id=1, source_target_pairs={{0,12},{1,13},{2,14},{3,15},{4,8},{5,9},{6,10},{7,11},{8,4},{9,5},... | collective-permute-start | bytes 344072 | tf_op jit(solution)/shard_map/ppermute | solution.py:456
  80.9 1.5 %collective-permute-start.20 = (bf16[224,256]{1,0:T(8,128)(2,1)S(1)}, bf16[224,256]{1,0:T(8,128)(2,1)S(1)}, u32[]{:S(2)}, u32[]{:S(2)}) collective-permute-start(bf16[224,256]{1,0:T(8,128)(2,1)S(1)} %add_convert_fusion.refs_0_), channel_id=1, source_target_pairs={{0,2},{1,3},{2,0},{3,1},{4,6},{5,7},{6,4},{7,5},{8,10},{9,11},{10,... | collective-permute-start | bytes 344072 | tf_op jit(solution)/shard_map/ppermute | solution.py:459
  82.4 0.7 collective-permute-done.21.refs_2_
  83.1 1.5 %collective-permute-start.22 = (bf16[224,256]{1,0:T(8,128)(2,1)S(1)}, bf16[224,256]{1,0:T(8,128)(2,1)S(1)}, u32[]{:S(2)}, u32[]{:S(2)}) collective-permute-start(bf16[224,256]{1,0:T(8,128)(2,1)S(1)} %collective-permute-done.21.refs_2_), channel_id=1, source_target_pairs={{0,2},{1,3},{2,0},{3,1},{4,6},{5,7},{6,4},{7,5},{8,10},{9,11},{10,... | collective-permute-start | bytes 344072 | tf_op jit(solution)/shard_map/ppermute | solution.py:459
  84.6 4.6 %collective-permute-done.23.refs_4_ = bf16[224,256]{1,0:T(8,128)(2,1)S(1)} collective-permute-done((bf16[224,256]{1,0:T(8,128)(2,1)S(1)}, bf16[224,256]{1,0:T(8,128)(2,1)S(1)}, u32[]{:S(2)}, u32[]{:S(2)}) %collective-permute-start.23) | collective-permute-done | bytes 114720 | tf_op jit(solution)/shard_map/ppermute | solution.py:456
  89.2 1.5 %collective-permute-start.24 = (bf16[224,256]{1,0:T(8,128)(2,1)S(1)}, bf16[224,256]{1,0:T(8,128)(2,1)S(1)}, u32[]{:S(2)}, u32[]{:S(2)}) collective-permute-start(bf16[224,256]{1,0:T(8,128)(2,1)S(1)} %collective-permute-done.23.refs_4_), channel_id=1, source_target_pairs={{0,2},{1,3},{2,0},{3,1},{4,6},{5,7},{6,4},{7,5},{8,10},{9,11},{10,... | collective-permute-start | bytes 344072 | tf_op jit(solution)/shard_map/ppermute | solution.py:459
  90.8 0.5 collective-permute-start.26
  91.3 2.8 %collective-permute-done.24.refs_5_ = bf16[224,256]{1,0:T(8,128)(2,1)S(1)} collective-permute-done((bf16[224,256]{1,0:T(8,128)(2,1)S(1)}, bf16[224,256]{1,0:T(8,128)(2,1)S(1)}, u32[]{:S(2)}, u32[]{:S(2)}) %collective-permute-start.24) | collective-permute-done | bytes 114720 | tf_op jit(solution)/shard_map/ppermute | solution.py:459
  94.0 1.5 %collective-permute-done.26.refs_7_ = bf16[224,256]{1,0:T(8,128)(2,1)S(1)} collective-permute-done((bf16[224,256]{1,0:T(8,128)(2,1)S(1)}, bf16[224,256]{1,0:T(8,128)(2,1)S(1)}, u32[]{:S(2)}, u32[]{:S(2)}) %collective-permute-start.26) | collective-permute-done | bytes 114720 | tf_op jit(solution)/shard_map/ppermute | solution.py:459
  95.6 1.9 %gate_up.1 = (f32[128,768]{1,0:T(8,128)S(1)}, f32[128,768]{1,0:T(8,128)S(1)}, bf16[16,2048]{1,0:T(8,128)(2,1)S(1)}, bf16[16,2048]{1,0:T(8,128)(2,1)S(1)}) custom-call(bf16[224,256]{1,0:T(8,128)(2,1)S(1)} %add_convert_fusion.refs_0_, bf16[224,256]{1,0:T(8,128)(2,1)S(1)} %collective-permute-done.20.refs_1_, ...), custom_call_target="tpu_custom_call" | custom-call | tf_op jit(solution)/shard_map/gate_up/pallas_call | solution.py:553
  97.5 1.7 %collective-permute-done.29.came_ref = f32[128,768]{1,0:T(8,128)S(1)} collective-permute-done((f32[128,768]{1,0:T(8,128)S(1)}, f32[128,768]{1,0:T(8,128)S(1)}, u32[]{:S(2)}, u32[]{:S(2)}) %collective-permute-start.29) | collective-permute-done | bytes 393248 | tf_op jit(solution)/shard_map/ppermute | solution.py:462
  99.2 0.8 hidden.1
  100.0 1.3 %collective-permute-start.36 = (bf16[16,4096]{1,0:T(8,128)(2,1)S(1)}, bf16[16,4096]{1,0:T(8,128)(2,1)S(1)}, u32[]{:S(2)}, u32[]{:S(2)}) collective-permute-start(bf16[16,4096]{1,0:T(8,128)(2,1)S(1)} %get-tuple-element.62), channel_id=1, source_target_pairs={{0,2},{1,3},{2,0},{3,1},{4,6},{5,7},{6,4},{7,5},{8,10},{9,11},{10,... | collective-permute-start | bytes 393224 | tf_op jit(solution)/shard_map/ppermute | solution.py:459
  101.3 0.8 collective-permute-start.34
  102.1 1.3 %collective-permute-start.32 = (bf16[16,4096]{1,0:T(8,128)(2,1)S(1)}, bf16[16,4096]{1,0:T(8,128)(2,1)S(1)}, u32[]{:S(2)}, u32[]{:S(2)}) collective-permute-start(bf16[16,4096]{1,0:T(8,128)(2,1)S(1)} %get-tuple-element.58), channel_id=1, source_target_pairs={{0,2},{1,3},{2,0},{3,1},{4,6},{5,7},{6,4},{7,5},{8,10},{9,11},{10,... | collective-permute-start | bytes 393224 | tf_op jit(solution)/shard_map/ppermute | solution.py:459
  103.4 0.8 collective-permute-start.31
  104.1 0.6 down.1
  104.7 1.7 %collective-permute-done.36.far_ref = bf16[16,4096]{1,0:T(8,128)(2,1)S(1)} collective-permute-done((bf16[16,4096]{1,0:T(8,128)(2,1)S(1)}, bf16[16,4096]{1,0:T(8,128)(2,1)S(1)}, u32[]{:S(2)}, u32[]{:S(2)}) %collective-permute-start.36) | collective-permute-done | bytes 131104 | tf_op jit(solution)/shard_map/ppermute | solution.py:459
  106.5 1.9 %collective-permute-start.37 = (bf16[16,4096]{1,0:T(8,128)(2,1)S(1)}, bf16[16,4096]{1,0:T(8,128)(2,1)S(1)}, u32[]{:S(2)}, u32[]{:S(2)}) collective-permute-start(bf16[16,4096]{1,0:T(8,128)(2,1)S(1)} %add.15), channel_id=1, source_target_pairs={{0,12},{1,13},{2,14},{3,15},{4,8},{5,9},{6,10},{7,11},{8,4},{9,5},... | collective-permute-start | bytes 393224 | tf_op jit(solution)/shard_map/ppermute | solution.py:456
  108.4 0.9 collective-permute-done.34.far_ref
  109.3 0.7 collective-permute-start.35
  109.9 2.1 %collective-permute-done.32.far_ref = bf16[16,4096]{1,0:T(8,128)(2,1)S(1)} collective-permute-done((bf16[16,4096]{1,0:T(8,128)(2,1)S(1)}, bf16[16,4096]{1,0:T(8,128)(2,1)S(1)}, u32[]{:S(2)}, u32[]{:S(2)}) %collective-permute-start.32) | collective-permute-done | bytes 131104 | tf_op jit(solution)/shard_map/ppermute | solution.py:459
  112.1 0.9 collective-permute-start.33
  113.0 1.3 %collective-permute-done.38.refs_6_ = bf16[16,2048]{1,0:T(8,128)(2,1)S(1)} collective-permute-done((bf16[16,2048]{1,0:T(8,128)(2,1)S(1)}, bf16[16,2048]{1,0:T(8,128)(2,1)S(1)}, u32[]{:S(2)}, u32[]{:S(2)}) %collective-permute-start.38) | collective-permute-done | bytes 65568 | tf_op jit(solution)/shard_map/ppermute | solution.py:462
  114.2 1.8 %collective-permute-done.35.refs_3_ = bf16[16,4096]{1,0:T(8,128)(2,1)S(1)} collective-permute-done((bf16[16,4096]{1,0:T(8,128)(2,1)S(1)}, bf16[16,4096]{1,0:T(8,128)(2,1)S(1)}, u32[]{:S(2)}, u32[]{:S(2)}) %collective-permute-start.35) | collective-permute-done | bytes 131104 | tf_op jit(solution)/shard_map/ppermute | solution.py:456
  116.1 3.7 %collective-permute-done.33.refs_2_ = bf16[16,4096]{1,0:T(8,128)(2,1)S(1)} collective-permute-done((bf16[16,4096]{1,0:T(8,128)(2,1)S(1)}, bf16[16,4096]{1,0:T(8,128)(2,1)S(1)}, u32[]{:S(2)}, u32[]{:S(2)}) %collective-permute-start.33) | collective-permute-done | bytes 131104 | tf_op jit(solution)/shard_map/ppermute | solution.py:456
  119.8 0.8 last.1
  (61 shorter events, 1.1 us)
Async XLA Ops:
  0.0 1.6 %copy-start.3 = (bf16[64,4,4096]{2,1,0:T(4,128)(2,1)S(1)}, bf16[64,4,4096]{2,1,0:T(4,128)(2,1)}, u32[]{:S(2)}) copy-start(bf16[64,4,4096]{2,1,0:T(4,128)(2,1)} %corpus_ref.1) | copy-start | bytes 6291460
  1.6 0.8 copy-start.8
  2.4 0.7 copy-start.11
  3.1 0.7 copy-start.14
  3.7 5.1 %copy-start.4 = (bf16[64,4096]{1,0:T(8,128)(2,1)S(1)}, bf16[64,4096]{1,0:T(8,128)(2,1)}, u32[]{:S(2)}) copy-start(bf16[64,4096]{1,0:T(8,128)(2,1)} %refs_9_.2) | copy-start | bytes 1572868
  3.7 5.1 %copy-start.5 = (bf16[64,4096]{1,0:T(8,128)(2,1)S(1)}, bf16[64,4096]{1,0:T(8,128)(2,1)}, u32[]{:S(2)}) copy-start(bf16[64,4096]{1,0:T(8,128)(2,1)} %refs_10_.2) | copy-start | bytes 1572868
  3.7 5.6 %copy-start.6 = (bf16[64,4096]{1,0:T(8,128)(2,1)S(1)}, bf16[64,4096]{1,0:T(8,128)(2,1)}, u32[]{:S(2)}) copy-start(bf16[64,4096]{1,0:T(8,128)(2,1)} %refs_11_.1) | copy-start | bytes 1572868
  3.8 33.3 %copy-start.9 = (f32[4096]{0:T(1024)S(1)}, f32[4096]{0:T(1024)}, u32[]{:S(2)}) copy-start(f32[4096]{0:T(1024)} %param.23) | copy-start | bytes 49156
  4.7 11.9 %collective-permute-start.3 = (bf16[8,10240]{1,0:T(8,128)(2,1)S(1)}, bf16[8,10240]{1,0:T(8,128)(2,1)S(1)}, u32[]{:S(2)}, u32[]{:S(2)}) collective-permute-start(bf16[8,10240]{1,0:T(8,128)(2,1)S(1)} %fetch.1.refs_0_), channel_id=1, source_target_pairs={{0,8},{1,9},{2,10},{3,11},{4,12},{5,13},{6,14},{7,15},{8,0},{9,1},... | collective-permute-start | bytes 491528 | tf_op jit(solution)/shard_map/ppermute | solution.py:456
  8.8 28.2 %collective-permute-start.7 = (bf16[64,4096]{1,0:T(8,128)(2,1)S(1)}, bf16[64,4096]{1,0:T(8,128)(2,1)S(1)}, u32[]{:S(2)}, u32[]{:S(2)}) collective-permute-start(bf16[64,4096]{1,0:T(8,128)(2,1)S(1)} %copy-done.4), channel_id=1, source_target_pairs={{0,1},{1,0},{2,3},{3,2},{4,5},{5,4},{6,7},{7,6},{8,9},{9,8},{10,11... | collective-permute-start | bytes 1572872 | tf_op jit(solution)/shard_map/ppermute | solution.py:462
  8.8 28.2 %collective-permute-start.8 = (bf16[64,4096]{1,0:T(8,128)(2,1)S(1)}, bf16[64,4096]{1,0:T(8,128)(2,1)S(1)}, u32[]{:S(2)}, u32[]{:S(2)}) collective-permute-start(bf16[64,4096]{1,0:T(8,128)(2,1)S(1)} %copy-done.5), channel_id=1, source_target_pairs={{0,1},{1,0},{2,3},{3,2},{4,5},{5,4},{6,7},{7,6},{8,9},{9,8},{10,11... | collective-permute-start | bytes 1572872 | tf_op jit(solution)/shard_map/ppermute | solution.py:462
  9.4 27.7 %collective-permute-start.9 = (bf16[64,4096]{1,0:T(8,128)(2,1)S(1)}, bf16[64,4096]{1,0:T(8,128)(2,1)S(1)}, u32[]{:S(2)}, u32[]{:S(2)}) collective-permute-start(bf16[64,4096]{1,0:T(8,128)(2,1)S(1)} %copy-done.6), channel_id=1, source_target_pairs={{0,1},{1,0},{2,3},{3,2},{4,5},{5,4},{6,7},{7,6},{8,9},{9,8},{10,11... | collective-permute-start | bytes 1572872 | tf_op jit(solution)/shard_map/ppermute | solution.py:462
  9.4 10.8 %collective-permute-start.1 = (bf16[8,10240]{1,0:T(8,128)(2,1)S(1)}, bf16[8,10240]{1,0:T(8,128)(2,1)S(1)}, u32[]{:S(2)}, u32[]{:S(2)}) collective-permute-start(bf16[8,10240]{1,0:T(8,128)(2,1)S(1)} %fetch.1.refs_0_), channel_id=1, source_target_pairs={{0,4},{1,5},{2,6},{3,7},{4,0},{5,1},{6,2},{7,3},{8,12},{9,13},{10,... | collective-permute-start | bytes 491528 | tf_op jit(solution)/shard_map/ppermute | solution.py:456
  16.6 8.0 %collective-permute-start.5 = (bf16[8,10240]{1,0:T(8,128)(2,1)S(1)}, bf16[8,10240]{1,0:T(8,128)(2,1)S(1)}, u32[]{:S(2)}, u32[]{:S(2)}) collective-permute-start(bf16[8,10240]{1,0:T(8,128)(2,1)S(1)} %fetch.1.refs_0_), channel_id=1, source_target_pairs={{0,12},{1,13},{2,14},{3,15},{4,8},{5,9},{6,10},{7,11},{8,4},{9,5},... | collective-permute-start | bytes 491528 | tf_op jit(solution)/shard_map/ppermute | solution.py:456
  20.2 5.9 %collective-permute-start = (bf16[8,10240]{1,0:T(8,128)(2,1)S(1)}, bf16[8,10240]{1,0:T(8,128)(2,1)S(1)}, u32[]{:S(2)}, u32[]{:S(2)}) collective-permute-start(bf16[8,10240]{1,0:T(8,128)(2,1)S(1)} %fetch.1.refs_0_), channel_id=1, source_target_pairs={{0,2},{1,3},{2,0},{3,1},{4,6},{5,7},{6,4},{7,5},{8,10},{9,11},{10,... | collective-permute-start | bytes 491528 | tf_op jit(solution)/shard_map/ppermute | solution.py:459
  24.6 7.1 %collective-permute-start.4 = (bf16[8,10240]{1,0:T(8,128)(2,1)S(1)}, bf16[8,10240]{1,0:T(8,128)(2,1)S(1)}, u32[]{:S(2)}, u32[]{:S(2)}) collective-permute-start(bf16[8,10240]{1,0:T(8,128)(2,1)S(1)} %collective-permute-done.3.refs_4_), channel_id=1, source_target_pairs={{0,2},{1,3},{2,0},{3,1},{4,6},{5,7},{6,4},{7,5},{8,10},{9,11},{10,... | collective-permute-start | bytes 491528 | tf_op jit(solution)/shard_map/ppermute | solution.py:459
  26.1 8.9 %collective-permute-start.2 = (bf16[8,10240]{1,0:T(8,128)(2,1)S(1)}, bf16[8,10240]{1,0:T(8,128)(2,1)S(1)}, u32[]{:S(2)}, u32[]{:S(2)}) collective-permute-start(bf16[8,10240]{1,0:T(8,128)(2,1)S(1)} %collective-permute-done.1.refs_2_), channel_id=1, source_target_pairs={{0,2},{1,3},{2,0},{3,1},{4,6},{5,7},{6,4},{7,5},{8,10},{9,11},{10,... | collective-permute-start | bytes 491528 | tf_op jit(solution)/shard_map/ppermute | solution.py:459
  31.8 5.3 %collective-permute-start.6 = (bf16[8,10240]{1,0:T(8,128)(2,1)S(1)}, bf16[8,10240]{1,0:T(8,128)(2,1)S(1)}, u32[]{:S(2)}, u32[]{:S(2)}) collective-permute-start(bf16[8,10240]{1,0:T(8,128)(2,1)S(1)} %collective-permute-done.5.refs_6_), channel_id=1, source_target_pairs={{0,2},{1,3},{2,0},{3,1},{4,6},{5,7},{6,4},{7,5},{8,10},{9,11},{10,... | collective-permute-start | bytes 491528 | tf_op jit(solution)/shard_map/ppermute | solution.py:459
  37.1 2.7 %copy-start.7 = (bf16[64,4096]{1,0:T(8,128)(2,1)S(1)}, bf16[64,4096]{1,0:T(8,128)(2,1)}, u32[]{:S(2)}) copy-start(bf16[64,4096]{1,0:T(8,128)(2,1)} %weight_ref.1) | copy-start | bytes 1572868
  37.1 7.7 %copy-start.1 = (bf16[160,4096]{1,0:T(8,128)(2,1)S(1)}, bf16[160,4096]{1,0:T(8,128)(2,1)}, u32[]{:S(2)}) copy-start(bf16[160,4096]{1,0:T(8,128)(2,1)} %refs_9_.3) | copy-start | bytes 3932164
  37.1 7.6 %copy-start.2 = (bf16[160,4096]{1,0:T(8,128)(2,1)S(1)}, bf16[160,4096]{1,0:T(8,128)(2,1)}, u32[]{:S(2)}) copy-start(bf16[160,4096]{1,0:T(8,128)(2,1)} %refs_10_.3) | copy-start | bytes 3932164
  39.7 17.2 %collective-permute-start.10 = (bf16[160,512]{1,0:T(8,128)(2,1)S(1)}, bf16[160,512]{1,0:T(8,128)(2,1)S(1)}, u32[]{:S(2)}, u32[]{:S(2)}) collective-permute-start(bf16[160,512]{1,0:T(8,128)(2,1)S(1)} %get-tuple-element.36), channel_id=1, source_target_pairs={{0,1},{1,0},{2,3},{3,2},{4,5},{5,4},{6,7},{7,6},{8,9},{9,8},{10,11... | collective-permute-start | bytes 491528 | tf_op jit(solution)/shard_map/ppermute | solution.py:462
  39.9 8.2 %copy-start = (bf16[160,4096]{1,0:T(8,128)(2,1)S(1)}, bf16[160,4096]{1,0:T(8,128)(2,1)}, u32[]{:S(2)}) copy-start(bf16[160,4096]{1,0:T(8,128)(2,1)} %down_ref.3) | copy-start | bytes 3932164
  39.9 17.0 %copy-start.12 = (s32[24,1]{0,1:T(1,128)S(1)}, s32[24,1]{0,1:T(1,128)}, u32[]{:S(2)}) copy-start(s32[24,1]{0,1:T(1,128)} %param.16) | copy-start | bytes 292
  39.9 17.0 %copy-start.13 = (s32[24]{0:T(128)S(1)}, s32[24]{0:T(128)}, u32[]{:S(2)}) copy-start(s32[24]{0:T(128)} %segment_ref.1) | copy-start | bytes 292
  39.9 8.1 %collective-permute-start.15 = (bf16[64,1024]{1,0:T(8,128)(2,1)S(1)}, bf16[64,1024]{1,0:T(8,128)(2,1)S(1)}, u32[]{:S(2)}, u32[]{:S(2)}) collective-permute-start(bf16[64,1024]{1,0:T(8,128)(2,1)S(1)} %get-tuple-element.43), channel_id=1, source_target_pairs={{0,4},{1,5},{2,6},{3,7},{4,0},{5,1},{6,2},{7,3},{8,12},{9,13},{10,... | collective-permute-start | bytes 393224 | tf_op jit(solution)/shard_map/ppermute | solution.py:456
  42.3 12.9 %collective-permute-start.16 = (bf16[64,1024]{1,0:T(8,128)(2,1)S(1)}, bf16[64,1024]{1,0:T(8,128)(2,1)S(1)}, u32[]{:S(2)}, u32[]{:S(2)}) collective-permute-start(bf16[64,1024]{1,0:T(8,128)(2,1)S(1)} %get-tuple-element.44), channel_id=1, source_target_pairs={{0,8},{1,9},{2,10},{3,11},{4,12},{5,13},{6,14},{7,15},{8,0},{9,1},... | collective-permute-start | bytes 393224 | tf_op jit(solution)/shard_map/ppermute | solution.py:456
  44.0 11.2 %collective-permute-start.17 = (bf16[64,1024]{1,0:T(8,128)(2,1)S(1)}, bf16[64,1024]{1,0:T(8,128)(2,1)S(1)}, u32[]{:S(2)}, u32[]{:S(2)}) collective-permute-start(bf16[64,1024]{1,0:T(8,128)(2,1)S(1)} %get-tuple-element.45), channel_id=1, source_target_pairs={{0,12},{1,13},{2,14},{3,15},{4,8},{5,9},{6,10},{7,11},{8,4},{9,5},... | collective-permute-start | bytes 393224 | tf_op jit(solution)/shard_map/ppermute | solution.py:456
  44.9 50.7 %copy-start.10 = (f32[4096]{0:T(1024)S(1)}, f32[4096]{0:T(1024)}, u32[]{:S(2)}) copy-start(f32[4096]{0:T(1024)} %param.24) | copy-start | bytes 49156
  44.9 33.9 %collective-permute-start.27 = (bf16[160,2048]{1,0:T(8,128)(2,1)S(1)}, bf16[160,2048]{1,0:T(8,128)(2,1)S(1)}, u32[]{:S(2)}, u32[]{:S(2)}) collective-permute-start(bf16[160,2048]{1,0:T(8,128)(2,1)S(1)} %get-tuple-element.50), channel_id=1, source_target_pairs={{0,1},{1,0},{2,3},{3,2},{4,5},{5,4},{6,7},{7,6},{8,9},{9,8},{10,11... | collective-permute-start | bytes 1966088 | tf_op jit(solution)/shard_map/ppermute | solution.py:462
  48.1 49.5 %collective-permute-start.30 = (bf16[160,4096]{1,0:T(8,128)(2,1)S(1)}, bf16[160,4096]{1,0:T(8,128)(2,1)S(1)}, u32[]{:S(2)}, u32[]{:S(2)}) collective-permute-start(bf16[160,4096]{1,0:T(8,128)(2,1)S(1)} %copy-done), channel_id=1, source_target_pairs={{0,1},{1,0},{2,3},{3,2},{4,5},{5,4},{6,7},{7,6},{8,9},{9,8},{10,11... | collective-permute-start | bytes 3932168 | tf_op jit(solution)/shard_map/ppermute | solution.py:462
  55.3 10.9 %collective-permute-start.18 = (bf16[256,512]{1,0:T(8,128)(2,1)S(1)}, bf16[256,512]{1,0:T(8,128)(2,1)S(1)}, u32[]{:S(2)}, u32[]{:S(2)}) collective-permute-start(bf16[256,512]{1,0:T(8,128)(2,1)S(1)} %get-tuple-element.47), channel_id=1, source_target_pairs={{0,2},{1,3},{2,0},{3,1},{4,6},{5,7},{6,4},{7,5},{8,10},{9,11},{10,... | collective-permute-start | bytes 786440 | tf_op jit(solution)/shard_map/ppermute | solution.py:459
  59.0 3.9 %collective-permute-start.11 = (bf16[112,128]{1,0:T(8,128)(2,1)S(1)}, bf16[112,128]{1,0:T(8,128)(2,1)S(1)}, u32[]{:S(2)}, u32[]{:S(2)}) collective-permute-start(bf16[112,128]{1,0:T(8,128)(2,1)S(1)} %get-tuple-element.38), channel_id=1, source_target_pairs={{0,2},{1,3},{2,0},{3,1},{4,6},{5,7},{6,4},{7,5},{8,10},{9,11},{10,... | collective-permute-start | bytes 86024 | tf_op jit(solution)/shard_map/ppermute | solution.py:459
  62.9 5.5 %collective-permute-start.12 = (bf16[224,128]{1,0:T(8,128)(2,1)S(1)}, bf16[224,128]{1,0:T(8,128)(2,1)S(1)}, u32[]{:S(2)}, u32[]{:S(2)}) collective-permute-start(bf16[224,128]{1,0:T(8,128)(2,1)S(1)} %constant_dynamic-update-slice_fusion.refs_0_), channel_id=1, source_target_pairs={{0,4},{1,5},{2,6},{3,7},{4,0},{5,1},{6,2},{7,3},{8,12},{9,13},{10,... | collective-permute-start | bytes 172040 | tf_op jit(solution)/shard_map/ppermute | solution.py:456
  66.2 14.7 %collective-permute-start.28 = (bf16[160,2048]{1,0:T(8,128)(2,1)S(1)}, bf16[160,2048]{1,0:T(8,128)(2,1)S(1)}, u32[]{:S(2)}, u32[]{:S(2)}) collective-permute-start(bf16[160,2048]{1,0:T(8,128)(2,1)S(1)} %get-tuple-element.51), channel_id=1, source_target_pairs={{0,1},{1,0},{2,3},{3,2},{4,5},{5,4},{6,7},{7,6},{8,9},{9,8},{10,11... | collective-permute-start | bytes 1966088 | tf_op jit(solution)/shard_map/ppermute | solution.py:462
  66.2 7.1 %collective-permute-start.13 = (bf16[224,128]{1,0:T(8,128)(2,1)S(1)}, bf16[224,128]{1,0:T(8,128)(2,1)S(1)}, u32[]{:S(2)}, u32[]{:S(2)}) collective-permute-start(bf16[224,128]{1,0:T(8,128)(2,1)S(1)} %constant_dynamic-update-slice_fusion.refs_0_), channel_id=1, source_target_pairs={{0,8},{1,9},{2,10},{3,11},{4,12},{5,13},{6,14},{7,15},{8,0},{9,1},... | collective-permute-start | bytes 172040 | tf_op jit(solution)/shard_map/ppermute | solution.py:456
  68.5 6.0 %collective-permute-start.14 = (bf16[224,128]{1,0:T(8,128)(2,1)S(1)}, bf16[224,128]{1,0:T(8,128)(2,1)S(1)}, u32[]{:S(2)}, u32[]{:S(2)}) collective-permute-start(bf16[224,128]{1,0:T(8,128)(2,1)S(1)} %constant_dynamic-update-slice_fusion.refs_0_), channel_id=1, source_target_pairs={{0,12},{1,13},{2,14},{3,15},{4,8},{5,9},{6,10},{7,11},{8,4},{9,5},... | collective-permute-start | bytes 172040 | tf_op jit(solution)/shard_map/ppermute | solution.py:456
  74.8 1.6 %collective-permute-start.19 = (f32[224,256]{1,0:T(8,128)S(1)}, f32[224,256]{1,0:T(8,128)S(1)}, u32[]{:S(2)}, u32[]{:S(2)}) collective-permute-start(f32[224,256]{1,0:T(8,128)S(1)} %get-tuple-element.49), channel_id=1, source_target_pairs={{0,1},{1,0},{2,3},{3,2},{4,5},{5,4},{6,7},{7,6},{8,9},{9,8},{10,11... | collective-permute-start | bytes 688136 | tf_op jit(solution)/shard_map/ppermute | solution.py:462
  76.4 6.6 %collective-permute-start.21 = (bf16[224,256]{1,0:T(8,128)(2,1)S(1)}, bf16[224,256]{1,0:T(8,128)(2,1)S(1)}, u32[]{:S(2)}, u32[]{:S(2)}) collective-permute-start(bf16[224,256]{1,0:T(8,128)(2,1)S(1)} %add_convert_fusion.refs_0_), channel_id=1, source_target_pairs={{0,4},{1,5},{2,6},{3,7},{4,0},{5,1},{6,2},{7,3},{8,12},{9,13},{10,... | collective-permute-start | bytes 344072 | tf_op jit(solution)/shard_map/ppermute | solution.py:456
  77.6 11.6 %collective-permute-start.23 = (bf16[224,256]{1,0:T(8,128)(2,1)S(1)}, bf16[224,256]{1,0:T(8,128)(2,1)S(1)}, u32[]{:S(2)}, u32[]{:S(2)}) collective-permute-start(bf16[224,256]{1,0:T(8,128)(2,1)S(1)} %add_convert_fusion.refs_0_), channel_id=1, source_target_pairs={{0,8},{1,9},{2,10},{3,11},{4,12},{5,13},{6,14},{7,15},{8,0},{9,1},... | collective-permute-start | bytes 344072 | tf_op jit(solution)/shard_map/ppermute | solution.py:456
  78.7 12.0 %collective-permute-start.25 = (bf16[224,256]{1,0:T(8,128)(2,1)S(1)}, bf16[224,256]{1,0:T(8,128)(2,1)S(1)}, u32[]{:S(2)}, u32[]{:S(2)}) collective-permute-start(bf16[224,256]{1,0:T(8,128)(2,1)S(1)} %add_convert_fusion.refs_0_), channel_id=1, source_target_pairs={{0,12},{1,13},{2,14},{3,15},{4,8},{5,9},{6,10},{7,11},{8,4},{9,5},... | collective-permute-start | bytes 344072 | tf_op jit(solution)/shard_map/ppermute | solution.py:456
  80.9 10.4 %collective-permute-start.20 = (bf16[224,256]{1,0:T(8,128)(2,1)S(1)}, bf16[224,256]{1,0:T(8,128)(2,1)S(1)}, u32[]{:S(2)}, u32[]{:S(2)}) collective-permute-start(bf16[224,256]{1,0:T(8,128)(2,1)S(1)} %add_convert_fusion.refs_0_), channel_id=1, source_target_pairs={{0,2},{1,3},{2,0},{3,1},{4,6},{5,7},{6,4},{7,5},{8,10},{9,11},{10,... | collective-permute-start | bytes 344072 | tf_op jit(solution)/shard_map/ppermute | solution.py:459
  83.1 8.2 %collective-permute-start.22 = (bf16[224,256]{1,0:T(8,128)(2,1)S(1)}, bf16[224,256]{1,0:T(8,128)(2,1)S(1)}, u32[]{:S(2)}, u32[]{:S(2)}) collective-permute-start(bf16[224,256]{1,0:T(8,128)(2,1)S(1)} %collective-permute-done.21.refs_2_), channel_id=1, source_target_pairs={{0,2},{1,3},{2,0},{3,1},{4,6},{5,7},{6,4},{7,5},{8,10},{9,11},{10,... | collective-permute-start | bytes 344072 | tf_op jit(solution)/shard_map/ppermute | solution.py:459
  89.2 4.8 %collective-permute-start.24 = (bf16[224,256]{1,0:T(8,128)(2,1)S(1)}, bf16[224,256]{1,0:T(8,128)(2,1)S(1)}, u32[]{:S(2)}, u32[]{:S(2)}) collective-permute-start(bf16[224,256]{1,0:T(8,128)(2,1)S(1)} %collective-permute-done.23.refs_4_), channel_id=1, source_target_pairs={{0,2},{1,3},{2,0},{3,1},{4,6},{5,7},{6,4},{7,5},{8,10},{9,11},{10,... | collective-permute-start | bytes 344072 | tf_op jit(solution)/shard_map/ppermute | solution.py:459
  90.8 4.8 %collective-permute-start.26 = (bf16[224,256]{1,0:T(8,128)(2,1)S(1)}, bf16[224,256]{1,0:T(8,128)(2,1)S(1)}, u32[]{:S(2)}, u32[]{:S(2)}) collective-permute-start(bf16[224,256]{1,0:T(8,128)(2,1)S(1)} %collective-permute-done.25.refs_6_), channel_id=1, source_target_pairs={{0,2},{1,3},{2,0},{3,1},{4,6},{5,7},{6,4},{7,5},{8,10},{9,11},{10,... | collective-permute-start | bytes 344072 | tf_op jit(solution)/shard_map/ppermute | solution.py:459
  97.4 1.8 %collective-permute-start.29 = (f32[128,768]{1,0:T(8,128)S(1)}, f32[128,768]{1,0:T(8,128)S(1)}, u32[]{:S(2)}, u32[]{:S(2)}) collective-permute-start(f32[128,768]{1,0:T(8,128)S(1)} %get-tuple-element.53), channel_id=1, source_target_pairs={{0,1},{1,0},{2,3},{3,2},{4,5},{5,4},{6,7},{7,6},{8,9},{9,8},{10,11... | collective-permute-start | bytes 1179656 | tf_op jit(solution)/shard_map/ppermute | solution.py:462
  100.0 6.4 %collective-permute-start.36 = (bf16[16,4096]{1,0:T(8,128)(2,1)S(1)}, bf16[16,4096]{1,0:T(8,128)(2,1)S(1)}, u32[]{:S(2)}, u32[]{:S(2)}) collective-permute-start(bf16[16,4096]{1,0:T(8,128)(2,1)S(1)} %get-tuple-element.62), channel_id=1, source_target_pairs={{0,2},{1,3},{2,0},{3,1},{4,6},{5,7},{6,4},{7,5},{8,10},{9,11},{10,... | collective-permute-start | bytes 393224 | tf_op jit(solution)/shard_map/ppermute | solution.py:459
  101.3 7.9 %collective-permute-start.34 = (bf16[16,4096]{1,0:T(8,128)(2,1)S(1)}, bf16[16,4096]{1,0:T(8,128)(2,1)S(1)}, u32[]{:S(2)}, u32[]{:S(2)}) collective-permute-start(bf16[16,4096]{1,0:T(8,128)(2,1)S(1)} %get-tuple-element.60), channel_id=1, source_target_pairs={{0,2},{1,3},{2,0},{3,1},{4,6},{5,7},{6,4},{7,5},{8,10},{9,11},{10,... | collective-permute-start | bytes 393224 | tf_op jit(solution)/shard_map/ppermute | solution.py:459
  102.1 9.9 %collective-permute-start.32 = (bf16[16,4096]{1,0:T(8,128)(2,1)S(1)}, bf16[16,4096]{1,0:T(8,128)(2,1)S(1)}, u32[]{:S(2)}, u32[]{:S(2)}) collective-permute-start(bf16[16,4096]{1,0:T(8,128)(2,1)S(1)} %get-tuple-element.58), channel_id=1, source_target_pairs={{0,2},{1,3},{2,0},{3,1},{4,6},{5,7},{6,4},{7,5},{8,10},{9,11},{10,... | collective-permute-start | bytes 393224 | tf_op jit(solution)/shard_map/ppermute | solution.py:459
  103.4 10.9 %collective-permute-start.31 = (bf16[16,4096]{1,0:T(8,128)(2,1)S(1)}, bf16[16,4096]{1,0:T(8,128)(2,1)S(1)}, u32[]{:S(2)}, u32[]{:S(2)}) collective-permute-start(bf16[16,4096]{1,0:T(8,128)(2,1)S(1)} %get-tuple-element.56), channel_id=1, source_target_pairs={{0,2},{1,3},{2,0},{3,1},{4,6},{5,7},{6,4},{7,5},{8,10},{9,11},{10,... | collective-permute-start | bytes 393224 | tf_op jit(solution)/shard_map/ppermute | solution.py:459
  106.5 7.8 %collective-permute-start.37 = (bf16[16,4096]{1,0:T(8,128)(2,1)S(1)}, bf16[16,4096]{1,0:T(8,128)(2,1)S(1)}, u32[]{:S(2)}, u32[]{:S(2)}) collective-permute-start(bf16[16,4096]{1,0:T(8,128)(2,1)S(1)} %add.15), channel_id=1, source_target_pairs={{0,12},{1,13},{2,14},{3,15},{4,8},{5,9},{6,10},{7,11},{8,4},{9,5},... | collective-permute-start | bytes 393224 | tf_op jit(solution)/shard_map/ppermute | solution.py:456
  109.3 6.8 %collective-permute-start.35 = (bf16[16,4096]{1,0:T(8,128)(2,1)S(1)}, bf16[16,4096]{1,0:T(8,128)(2,1)S(1)}, u32[]{:S(2)}, u32[]{:S(2)}) collective-permute-start(bf16[16,4096]{1,0:T(8,128)(2,1)S(1)} %add.14), channel_id=1, source_target_pairs={{0,4},{1,5},{2,6},{3,7},{4,0},{5,1},{6,2},{7,3},{8,12},{9,13},{10,... | collective-permute-start | bytes 393224 | tf_op jit(solution)/shard_map/ppermute | solution.py:456
  112.1 7.7 %collective-permute-start.33 = (bf16[16,4096]{1,0:T(8,128)(2,1)S(1)}, bf16[16,4096]{1,0:T(8,128)(2,1)S(1)}, u32[]{:S(2)}, u32[]{:S(2)}) collective-permute-start(bf16[16,4096]{1,0:T(8,128)(2,1)S(1)} %add.13), channel_id=1, source_target_pairs={{0,8},{1,9},{2,10},{3,11},{4,12},{5,13},{6,14},{7,15},{8,0},{9,1},... | collective-permute-start | bytes 393224 | tf_op jit(solution)/shard_map/ppermute | solution.py:456
  113.0 1.3 %collective-permute-start.38 = (bf16[16,2048]{1,0:T(8,128)(2,1)S(1)}, bf16[16,2048]{1,0:T(8,128)(2,1)S(1)}, u32[]{:S(2)}, u32[]{:S(2)}) collective-permute-start(bf16[16,2048]{1,0:T(8,128)(2,1)S(1)} %get-tuple-element.64), channel_id=1, source_target_pairs={{0,1},{1,0},{2,3},{3,2},{4,5},{5,4},{6,7},{7,6},{8,9},{9,8},{10,11... | collective-permute-start | bytes 196616 | tf_op jit(solution)/shard_map/ppermute | solution.py:462

commit v4 on v3

--- a/solution.py
+++ b/solution.py
@@ -30,14 +30,17 @@
     return me, me // 4, (me // 2) % 2, me % 2
 
 
-def kernel_call(kernel, out_shape, in_specs, scratch=(), name=None):
+def kernel_call(kernel, out_shape, in_specs, scratch=(), name=None, limit=VMEM_LIMIT, micros=1):
     return pl.pallas_call(
         kernel,
         out_shape=out_shape,
+        cost_estimate=pl.CostEstimate(
+            flops=micros * 1_000_000_000, bytes_accessed=micros * 3_000_000, transcendentals=0
+        ),
         in_specs=in_specs,
         out_specs=jax.tree.map(lambda _: pl.BlockSpec(memory_space=pltpu.VMEM), out_shape),
         scratch_shapes=scratch,
-        compiler_params=pltpu.CompilerParams(vmem_limit_bytes=VMEM_LIMIT),
+        compiler_params=pltpu.CompilerParams(vmem_limit_bytes=limit),
         name=name,
     )
 
@@ -108,69 +111,94 @@
     return pltpu.roll(window, (128 - start % 128) % 128, 1)[:, :width]
 
 
-def slab_kernel(weight_ref, *out_refs):
-    zi = place()[1]
-    features = weight_ref.shape[1]
-    wide = out_refs[0].shape[1] // 2
-    for d, out_ref in enumerate(out_refs):
-        for core in range(2):
-            start = pl.multiple_of(core * (features // 2) + (zi ^ d) * wide, 128)
-            out_ref[:, core * wide : (core + 1) * wide] = weight_ref[:, pl.ds(start, wide)]
-
-
-def half_kernel(gate_ref, up_ref, gate_out_ref, up_out_ref):
-    half = gate_out_ref.shape[1]
+def across_kernel(piece_ref, weight_ref, out_ref):
+    _, zi, yi, _ = place()
+    nz = lax.axis_size(AXIS) // 4
+    rows, features = weight_ref.shape
+    width = features // (4 * nz)
+    first = piece_ref.shape[1]
+    wide = 2 * nz * width
+    out_ref[:, :first] = piece_ref[...]
+    columns = jnp.concatenate(
+        [
+            columns_at(
+                weight_ref, core * (features // 2) + (2 * (zi ^ d) + 1 - yi) * width, width
+            )
+            for d in range(nz)
+            for core in range(2)
+        ],
+        axis=1,
+    )
+    for g in range(rows // 8):
+        out_ref[:, first + g * wide : first + (g + 1) * wide] = columns[
+            g * 8 : g * 8 + 8
+        ].astype(jnp.bfloat16)
+
+
+def pair_kernel(first, weight_ref, far_ref, keep_ref, send_ref):
+    _, zi, yi, ci = place()
+    rows, features = weight_ref.shape
+    nz = lax.axis_size(AXIS) // 4
+    width = features // (4 * nz)
+    wide = 2 * nz * width
+    for core, out_ref in ((ci, keep_ref), (1 - ci, send_ref)):
+        own = [
+            columns_at(
+                weight_ref, core * (features // 2) + (2 * (zi ^ d) + yi) * width, width
+            )
+            for d in range(nz)
+        ]
+        out_ref[:rows, :] = jnp.concatenate(own, axis=1).astype(jnp.bfloat16)
+        groups = []
+        for g in range(rows // 8):
+            parts = []
+            for d in range(nz):
+                start = first + g * wide + 2 * d * width
+                both = far_ref[:, start : start + 2 * width].astype(jnp.float32)
+                parts.append(jnp.where(core == 0, both[:, :width], both[:, width:]))
+            groups.append(jnp.concatenate(parts, axis=1))
+        out_ref[rows:, :] = jnp.concatenate(groups, axis=0).astype(jnp.bfloat16)
+
+
+def stack_kernel(*refs):
+    rows = refs[0].shape[0]
+    for i, ref in enumerate(refs[:-1]):
+        refs[-1][i * rows : (i + 1) * rows, :] = ref[...]
+
+
+def share_kernel(gate_ref, up_ref, down_ref, out_ref):
+    units, features = down_ref.shape
+    half = features // 2
     other = pl.ds(pl.multiple_of((1 - place()[3]) * half, 128), half)
-    gate_out_ref[...] = gate_ref[:, other]
-    up_out_ref[...] = up_ref[:, other]
-
-
-def strip_kernel(*refs):
-    slabs, (keep_ref, send_ref) = refs[:-2], refs[-2:]
-    yi = place()[2]
-    rows, wide = slabs[0].shape
-    width = wide // 4
-    for d, slab in enumerate(slabs):
-        parts = [slab[:, i * width : (i + 1) * width] for i in range(4)]
-        low = jnp.concatenate([parts[0], parts[2]], axis=1)
-        high = jnp.concatenate([parts[1], parts[3]], axis=1)
-        keep_ref[d * rows : (d + 1) * rows, :] = jnp.where(yi == 0, low, high)
-        send_ref[d * rows : (d + 1) * rows, :] = jnp.where(yi == 0, high, low)
-
-
-def out_kernel(*refs):
-    contexts, (near_ref, far_ref, mine_ref, other_ref) = refs[:-4], refs[-4:]
+    out_ref[:units, :half] = gate_ref[:, other]
+    out_ref[:units, half:] = up_ref[:, other]
+    out_ref[units:, :] = down_ref[...]
+
+
+def out_kernel(own_ref, other_ref, weight_ref, weight_other_ref, mine_ref, *send_refs):
     width = mine_ref.shape[1]
-    ci = place()[3]
-    half = contexts[0].shape[0] // 2
-
-    def heads(first):
-        values = [ref[first : first + half, :] for ref in contexts]
+    half = own_ref.shape[0] // 2
+
+    def heads(ref):
+        near, far = ref[:half, :], ref[half:, :]
         return jnp.concatenate(
             [
-                jnp.concatenate([v[:, :HDIM] for v in values], axis=1),
-                jnp.concatenate([v[:, HDIM:] for v in values], axis=1),
+                jnp.concatenate([near[:, :HDIM], far[:, :HDIM]], axis=1),
+                jnp.concatenate([near[:, HDIM:], far[:, HDIM:]], axis=1),
             ],
             axis=0,
         )
 
-    attended = dot(heads(0), near_ref[...]) + dot(heads(half), far_ref[...])
-    low, high = attended[:, :width], attended[:, width:]
-    mine_ref[...] = jnp.where(ci == 0, low, high)
-    other_ref[...] = jnp.where(ci == 0, high, low)
+    attended = dot(heads(own_ref), weight_ref[...]) + dot(heads(other_ref), weight_other_ref[...])
+    mine_ref[...] = attended[:, :width]
+    for d, ref in enumerate(send_refs, 1):
+        ref[...] = attended[:, d * width : (d + 1) * width].astype(jnp.bfloat16)
 
 
 def projection_kernel(piece_rows, *refs):
-    count = len(refs) - 10
+    count = len(refs) - 8
     pieces, rest = refs[:count], refs[count:]
-    gain_ref, mine, other, out_ref, out_other_ref, normal = (
-        rest[0],
-        rest[1:4],
-        rest[4:7],
-        rest[7],
-        rest[8],
-        rest[9],
-    )
+    gain_ref, *mine, other_ref, out_ref, out_other_ref, normal = rest
     _, zi, yi, ci = place()
     features = gain_ref.shape[1]
     half = features // 2
@@ -210,7 +238,8 @@
             groups, own, away = [], [], []
             for p in range(first, first + 4, 2):
                 a, b = (
-                    pieces[q][:, full * features :].astype(jnp.float32) for q in (p, p + 1)
+                    pieces[q][:, full * features : full * features + half].astype(jnp.float32)
+                    for q in (p, p + 1)
                 )
                 low = jnp.concatenate([a[0:4], b[0:4]], axis=0)
                 high = jnp.concatenate([a[4:8], b[4:8]], axis=0)
@@ -238,7 +267,7 @@
                 away, axis=0
             ).astype(jnp.bfloat16)
     rows = normal[...]
-    for target, weights in ((out_other_ref, other), (out_ref, mine)):
+    for target, weights in ((out_other_ref, [other_ref]), (out_ref, mine)):
         value = jnp.concatenate([by_rows(rows, w[...]) for w in weights], axis=1)
         target[:, 0 : value.shape[1]] = value.astype(jnp.bfloat16)
 
@@ -311,14 +340,13 @@
 
 
 def gate_kernel(rows_here, chunk_rows, *refs):
-    count = len(refs) - 11
+    count = len(refs) - 10
     pieces = refs[:count]
     (
         gain_ref,
         gate_ref,
         up_ref,
-        gate_other_ref,
-        up_other_ref,
+        share_ref,
         keep_ref,
         send_ref,
         kept_ref,
@@ -361,8 +389,8 @@
     units = gate_ref.shape[0]
     gate = by_rows(rows, gate_ref[:, mine])
     up = by_rows(rows, up_ref[:, mine])
-    gate_other = by_rows(rows, gate_other_ref[...])
-    up_other = by_rows(rows, up_other_ref[...])
+    gate_other = by_rows(rows, share_ref[:units, :half])
+    up_other = by_rows(rows, share_ref[:units, half:])
     wide = keep_ref.shape[1] - 4 * units
     spread = jnp.broadcast_to(squares, (total, wide))
     keep_ref[...] = jnp.concatenate(
@@ -373,7 +401,7 @@
     )
 
 
-def hidden_kernel(features, keep_ref, came_ref, down_ref, down_other_ref, *refs):
+def hidden_kernel(features, keep_ref, came_ref, down_ref, share_ref, *refs):
     chunk_rows = refs[0].shape[0]
     hidden_ref = refs[-1]
     units = down_ref.shape[0]
@@ -390,12 +418,12 @@
         ],
         axis=0,
     )
-    result = dot(far[:, :units], down_ref[...]) + dot(far[:, units:], down_other_ref[...])
+    result = dot(far[:, :units], down_ref[...]) + dot(far[:, units:], share_ref[units:, :])
     for dz in range(len(refs) - 1):
         refs[dz][...] = result[dz * chunk_rows : (dz + 1) * chunk_rows].astype(jnp.bfloat16)
 
 
-def down_kernel(hidden_ref, down_ref, down_other_ref, *out_refs):
+def down_kernel(hidden_ref, down_ref, share_ref, *out_refs):
     chunk_rows = out_refs[0].shape[0]
     units = down_ref.shape[0]
     hidden = hidden_ref[...]
@@ -406,7 +434,7 @@
         ],
         axis=0,
     )
-    result = dot(near[:, :units], down_ref[...]) + dot(near[:, units:], down_other_ref[...])
+    result = dot(near[:, :units], down_ref[...]) + dot(near[:, units:], share_ref[units:, :])
     for dz in range(len(out_refs)):
         out_refs[dz][...] = result[dz * chunk_rows : (dz + 1) * chunk_rows]
 
@@ -461,11 +489,18 @@
     def across_core(value):
         return lax.ppermute(value, AXIS, [(i, i ^ 1) for i in range(devices)])
 
-    def plane_gather(value):
+    def plane_gather(value, value_across=None, fence=None):
         near = {0: value}
         for k in z_order:
             near[k] = along_z(value, k)
-        return near, {k: across_y(near[k]) for k in [0] + z_order}
+        if fence is not None:
+            for k in near:
+                near[k], fence = lax.optimization_barrier((near[k], fence))
+        if value_across is None:
+            value_across = near[0]
+        return near, {
+            k: across_y(near[k] if k else value_across) for k in [0] + z_order
+        }
 
     def paired(near, far):
         return [piece for k in range(nz) for piece in (near[k], far[k])]
@@ -494,42 +529,45 @@
             pltpu.SemaphoreType.DMA((CAP,)),
         ],
         name="fetch",
+        limit=60 * 1024 * 1024,
     )(owners, slot_row, corpus, queries)
 
     projections = [query_weight, key_weight, value_weight]
-    projections_other = [across_core(w) for w in projections]
-    down_other = across_core(down_weight)
-    slab = shape((heads_rows, 4 * width), bf16)
-    slabs = kernel_call(
-        slab_kernel, (slab,) * nz, [VMEM], name="slabs"
-    )(out_weight)
-    gate_half, up_half = kernel_call(
-        half_kernel,
-        (shape((units, half), bf16),) * 2,
-        [VMEM, VMEM],
-        name="halves",
-    )(gate_weight, up_weight)
-    gate_other, up_other = across_core(gate_half), across_core(up_half)
-
     plane_rows = 2 * nz * (full * 8 + halved * 4)
     wide = 256 + -(-width // 128) * 128
-    near, far = plane_gather(piece)
+    *tied, _ = lax.optimization_barrier((*projections, piece))
+    stacked = kernel_call(
+        stack_kernel,
+        shape((3 * heads_rows, features), bf16),
+        [VMEM] * 3,
+        name="stack",
+        micros=20,
+    )(*tied)
+    piece_wide = piece.shape[1]
+    value_across = kernel_call(
+        across_kernel,
+        shape((8, piece_wide + heads_rows // 8 * 2 * nz * width), bf16),
+        [VMEM] * 2,
+        name="across",
+    )(piece, out_weight)
+    near, far = plane_gather(piece, value_across, stacked)
+    projections_other = across_core(stacked)
     own, away = kernel_call(
         functools.partial(projection_kernel, query_rows + CAP * BLK),
         (shape((plane_rows, wide), bf16), shape((plane_rows, wide), bf16)),
-        [VMEM] * (2 * nz + 7),
+        [VMEM] * (2 * nz + 5),
         [pltpu.VMEM((plane_rows, features), bf16)],
         name="project",
-    )(*paired(near, far), gain_attn[None, :], *projections, *projections_other)
-
-    slabs = list(slabs)
-    slabs[1:], _ = lax.optimization_barrier((slabs[1:], near[z_order[0]]))
-    slabs = [slabs[0]] + [along_z(slabs[k], k) for k in range(1, nz)]
-    strip = shape((nz * heads_rows, 2 * width), bf16)
-    strip_near, strip_send = kernel_call(
-        strip_kernel, (strip, strip), [VMEM] * nz, name="strips"
-    )(*slabs)
-    strip_far = across_y(strip_send)
+        micros=10,
+    )(*paired(near, far), gain_attn[None, :], *projections, projections_other)
+
+    out_keep, out_send = kernel_call(
+        functools.partial(pair_kernel, piece_wide),
+        (shape((2 * heads_rows, nz * width), bf16),) * 2,
+        [VMEM] * 2,
+        name="pairs",
+    )(out_weight, far[0])
+    out_came = across_core(out_send)
 
     context, columns = kernel_call(
         functools.partial(attention_kernel, query_rows, width),
@@ -537,16 +575,26 @@
         [SMEM, SMEM, VMEM, VMEM],
         name="attend",
     )(owners, segment, own, across_core(away))
+    share_gate, share_up, share_down, _ = lax.optimization_barrier(
+        (gate_weight, up_weight, down_weight, context)
+    )
+    share = across_core(
+        kernel_call(
+            share_kernel, shape((2 * units, features), bf16), [VMEM] * 3, name="share"
+        )(share_gate, share_up, share_down)
+    )
 
     contexts = jnp.concatenate([context, across_y(context)], axis=0)
-    contexts = [contexts] + [along_z(contexts, k) for k in range(1, nz)]
-    attended_mine, attended_other = kernel_call(
+    attended, *parts = kernel_call(
         out_kernel,
-        (shape((tokens, width), f32),) * 2,
-        [VMEM] * (nz + 2),
+        (shape((tokens, width), f32),) + (shape((tokens, width), bf16),) * (nz - 1),
+        [VMEM] * 4,
         name="out",
-    )(*contexts, strip_near, strip_far)
-    middle = (columns.astype(f32) + attended_mine + across_core(attended_other)).astype(bf16)
+    )(contexts, across_core(contexts), out_keep, out_came)
+    middle = columns.astype(f32) + attended
+    for d in z_order:
+        middle = middle + along_z(parts[d - 1], d).astype(f32)
+    middle = middle.astype(bf16)
 
     slots = 2 * nz * chunk_rows
     lanes = -(-(4 * units + 1) // 128) * 128
@@ -558,10 +606,10 @@
             shape((chunk_rows, half), bf16),
             shape((chunk_rows, half), bf16),
         ),
-        [VMEM] * (2 * nz + 5),
+        [VMEM] * (2 * nz + 4),
         [pltpu.VMEM((2 * slots, tokens), bf16), pltpu.VMEM((2 * slots, half), bf16)],
         name="gate_up",
-    )(*paired(*plane_gather(middle)), gain_ffn[None, :], gate_weight, up_weight, gate_other, up_other)
+    )(*paired(*plane_gather(middle)), gain_ffn[None, :], gate_weight, up_weight, share)
     came = across_core(send)
     kept_other = across_core(kept_send)
 
@@ -571,14 +619,14 @@
         (chunk,) * nz + (shape((slots, 2 * units), bf16),),
         [VMEM] * 4,
         name="hidden",
-    )(keep, came, down_weight, down_other)
+    )(keep, came, down_weight, share)
     moved = {k: across_y(far[k]) for k in z_order + [0]}
     near = kernel_call(
         down_kernel,
         (shape((chunk_rows, features), f32),) * nz,
         [VMEM] * 3,
         name="down",
-    )(hidden, down_weight, down_other)
+    )(hidden, down_weight, share)
     arrived = []
     for k in z_order:
         part = kernel_call(add_kernel, chunk, [VMEM, VMEM], name="add")(near[k], moved[k])

time: 121 us -> 99.6 us (0.82)
  starting transfers between devices: 45.5 us -> 32.6 us
  waiting for transfers between devices: 60.7 us -> 54.3 us
  local copies, waits for them, and re-layouts: 3.81 us -> 0.4 us
  Pallas kernels: 10.2 us -> 11.7 us
    ppermute x15 -> x12, starting transfers between devices: 27.4 us -> 17.7 us  [along_z(): return lax.ppermute(value, AXIS, [(i, i ^ 4 * k) for i in range(devices)])]
    ppermute x15 -> x12, waiting for transfers between devices: 35.8 us -> 31.6 us  [along_z(): return lax.ppermute(value, AXIS, [(i, i ^ 4 * k) for i in range(devices)])]
    ppermute x14 -> x13, starting transfers between devices: 17.3 us -> 13.5 us  [across_y(): return lax.ppermute(value, AXIS, [(i, i ^ 2) for i in range(devices)])]
    unnamed x31 -> x25, local copies, waits for them, and re-layouts: 3.8 us -> 0.39 us
    ppermute x14 -> x13, waiting for transfers between devices: 20.4 us -> 17.1 us  [across_y(): return lax.ppermute(value, AXIS, [(i, i ^ 2) for i in range(devices)])]
    pallas_call x1, Pallas kernels: 0.97 us -> 2.7 us  [body(): kernel_call(fetch_kernel, shape((8, full * features + halved * half), bf1...]
    ppermute x10 -> x7, waiting for transfers between devices: 4.44 us -> 5.58 us  [across_core(): return lax.ppermute(value, AXIS, [(i, i ^ 1) for i in range(devices)])]
  transfers between devices with their start and end apart: 39 -> 32, of which waited for: 23 -> 21; matrix products, arithmetic and copies ran while one was open for 0% -> 0% of each run, Pallas kernels for 4% -> 1%
where the time goes in v4:
time: 99.6 us; the launch traced here: 99.3 us
  waiting for transfers between devices  54.3 us (55%)
  starting transfers between devices  32.6 us (33%)
  Pallas kernels  11.7 us (12%)
    ppermute x12, waiting for transfers between devices, along_z(): return lax.ppermute(value, AXIS, [(i, i ^ 4 * k) for i in range(devices)])  31.6 us
    ppermute x12, starting transfers between devices, along_z(): return lax.ppermute(value, AXIS, [(i, i ^ 4 * k) for i in range(devices)])  17.7 us
    ppermute x13, waiting for transfers between devices, across_y(): return lax.ppermute(value, AXIS, [(i, i ^ 2) for i in range(devices)])  17.1 us
    ppermute x13, starting transfers between devices, across_y(): return lax.ppermute(value, AXIS, [(i, i ^ 2) for i in range(devices)])  13.5 us
    ppermute x7, waiting for transfers between devices, across_core(): return lax.ppermute(value, AXIS, [(i, i ^ 1) for i in range(devices)])  5.58 us
    pallas_call x1, Pallas kernels, body(): kernel_call(fetch_kernel, shape((8, full * features + halved * half), bf1...  2.7 us
    pallas_call x1, Pallas kernels, body(): kernel_call(functools.partial(attention_kernel, query_rows, width), (shap...  2.11 us
  transfers between devices with their start and end apart: 32, of which 21 were waited for; matrix products, arithmetic and copies ran while one was open for 0% of the time, Pallas kernels for 1%

profile of v4, /device:TPU:0, one launch (start us, length us, event | category | flops | bytes accessed | tf_op | source)
XLA Modules:
  0.0 99.3 jit_solution(10092276633523386202)
XLA Ops:
  0.0 2.7 %fetch.1.piece_ref.refs_0_ = bf16[8,10240]{1,0:T(8,128)(2,1)} custom-call(s32[24]{0:T(128)} %bitcast.5, s32[24]{0:T(128)} %row_ref.1, bf16[64,4,4096]{2,1,0:T(4,128)(2,1)} %corpus_ref.1, bf16[8,4096]{1,0:T(8,128)(2,1)} %query_ref.1), custom_call_target="tpu_custom_call" | custom-call | flops 1000000000 | bytes 3000000 | tf_op jit(solution)/shard_map/fetch/pallas_call | solution.py:522
  2.8 0.1 stack.1
  2.9 0.6 collective-permute-start.7
  3.5 0.3 copy-done.7
  3.9 3.1 %collective-permute-start = (bf16[8,26624]{1,0:T(8,128)(2,1)S(1)}, bf16[8,26624]{1,0:T(8,128)(2,1)S(1)}, u32[]{:S(2)}, u32[]{:S(2)}) collective-permute-start(bf16[8,26624]{1,0:T(8,128)(2,1)S(1)} %across.1), channel_id=1, source_target_pairs={{0,2},{1,3},{2,0},{3,1},{4,6},{5,7},{6,4},{7,5},{8,10},{9,11},{10,... | collective-permute-start | bytes 1277960 | tf_op jit(solution)/shard_map/ppermute | solution.py:487
  7.0 1.5 %collective-permute-start.1 = (bf16[8,10240]{1,0:T(8,128)(2,1)S(1)}, bf16[8,10240]{1,0:T(8,128)(2,1)S(1)}, u32[]{:S(2)}, u32[]{:S(2)}) collective-permute-start(bf16[8,10240]{1,0:T(8,128)(2,1)S(1)} %copy-done.8), channel_id=1, source_target_pairs={{0,4},{1,5},{2,6},{3,7},{4,0},{5,1},{6,2},{7,3},{8,12},{9,13},{10,... | collective-permute-start | bytes 491528 | tf_op jit(solution)/shard_map/ppermute | solution.py:484
  8.5 2.6 %collective-permute-start.3 = (bf16[8,10240]{1,0:T(8,128)(2,1)S(1)}, bf16[8,10240]{1,0:T(8,128)(2,1)S(1)}, u32[]{:S(2)}, u32[]{:S(2)}) collective-permute-start(bf16[8,10240]{1,0:T(8,128)(2,1)S(1)} %copy-done.8), channel_id=1, source_target_pairs={{0,8},{1,9},{2,10},{3,11},{4,12},{5,13},{6,14},{7,15},{8,0},{9,1},... | collective-permute-start | bytes 491528 | tf_op jit(solution)/shard_map/ppermute | solution.py:484
  11.1 0.2 collective-permute-start.5
  11.3 3.5 %collective-permute-done.1.refs_2_ = bf16[8,10240]{1,0:T(8,128)(2,1)S(1)} collective-permute-done((bf16[8,10240]{1,0:T(8,128)(2,1)S(1)}, bf16[8,10240]{1,0:T(8,128)(2,1)S(1)}, u32[]{:S(2)}, u32[]{:S(2)}) %collective-permute-start.1) | collective-permute-done | bytes 163872 | tf_op jit(solution)/shard_map/ppermute | solution.py:484
  14.8 0.3 collective-permute-start.2
  15.2 8.4 %collective-permute-done.3.refs_4_ = bf16[8,10240]{1,0:T(8,128)(2,1)S(1)} collective-permute-done((bf16[8,10240]{1,0:T(8,128)(2,1)S(1)}, bf16[8,10240]{1,0:T(8,128)(2,1)S(1)}, u32[]{:S(2)}, u32[]{:S(2)}) %collective-permute-start.3) | collective-permute-done | bytes 163872 | tf_op jit(solution)/shard_map/ppermute | solution.py:484
  23.6 0.6 collective-permute-start.4
  24.1 1.5 %collective-permute-start.6 = (bf16[8,10240]{1,0:T(8,128)(2,1)S(1)}, bf16[8,10240]{1,0:T(8,128)(2,1)S(1)}, u32[]{:S(2)}, u32[]{:S(2)}) collective-permute-start(bf16[8,10240]{1,0:T(8,128)(2,1)S(1)} %collective-permute-done.5.refs_6_), channel_id=1, source_target_pairs={{0,2},{1,3},{2,0},{3,1},{4,6},{5,7},{6,4},{7,5},{8,10},{9,11},{10,... | collective-permute-start | bytes 491528 | tf_op jit(solution)/shard_map/ppermute | solution.py:487
  25.6 3.3 %collective-permute-done.4.refs_5_ = bf16[8,10240]{1,0:T(8,128)(2,1)S(1)} collective-permute-done((bf16[8,10240]{1,0:T(8,128)(2,1)S(1)}, bf16[8,10240]{1,0:T(8,128)(2,1)S(1)}, u32[]{:S(2)}, u32[]{:S(2)}) %collective-permute-start.4) | collective-permute-done | bytes 163872 | tf_op jit(solution)/shard_map/ppermute | solution.py:487
  28.9 1.8 %collective-permute-done.6.refs_7_ = bf16[8,10240]{1,0:T(8,128)(2,1)S(1)} collective-permute-done((bf16[8,10240]{1,0:T(8,128)(2,1)S(1)}, bf16[8,10240]{1,0:T(8,128)(2,1)S(1)}, u32[]{:S(2)}, u32[]{:S(2)}) %collective-permute-start.6) | collective-permute-done | bytes 163872 | tf_op jit(solution)/shard_map/ppermute | solution.py:487
  30.7 2.0 %project.1 = (bf16[160,512]{1,0:T(8,128)(2,1)S(1)}, bf16[160,512]{1,0:T(8,128)(2,1)S(1)}) custom-call(bf16[8,10240]{1,0:T(8,128)(2,1)S(1)} %copy-done.8, bf16[8,26624]{1,0:T(8,128)(2,1)S(1)} %collective-permute-done.refs_1_.far_ref, bf16[8,10240]{1,0:T(8,128)(2,1)S(1)} %collective-permute-done.1.refs_2_, ...), custom_call_target="tpu_custom_call" | custom-call | flops 10000000000 | bytes 30000000 | tf_op jit(solution)/shard_map/project/pallas_call | solution.py:555
  32.7 0.1 collective-permute-start.8
  32.7 1.4 %collective-permute-done.8.away_ref = bf16[160,512]{1,0:T(8,128)(2,1)S(1)} collective-permute-done((bf16[160,512]{1,0:T(8,128)(2,1)S(1)}, bf16[160,512]{1,0:T(8,128)(2,1)S(1)}, u32[]{:S(2)}, u32[]{:S(2)}) %collective-permute-start.8) | collective-permute-done | bytes 163872 | tf_op jit(solution)/shard_map/ppermute | solution.py:490
  34.1 2.1 %attend.1 = (bf16[112,128]{1,0:T(8,128)(2,1)S(1)}, bf16[224,256]{1,0:T(8,128)(2,1)S(1)}) custom-call(s32[24]{0:T(128)S(1)} %bitcast.6, s32[24]{0:T(128)S(1)} %copy-done.11, bf16[160,512]{1,0:T(8,128)(2,1)S(1)} %get-tuple-element.39.own_ref, bf16[160,512]{1,0:T(8,128)(2,1)S(1)} %collective-permute-done.8.away_ref), custom_call_target="tpu_custom_call" | custom-call | flops 1000000000 | bytes 3000000 | tf_op jit(solution)/shard_map/attend/pallas_call | solution.py:572
  36.3 0.2 share.1
  36.4 0.2 collective-permute-start.22
  36.6 0.1 pairs.1
  36.7 0.4 collective-permute-start.11
  37.2 0.5 collective-permute-start.9
  37.7 3.3 %collective-permute-done.9 = bf16[112,128]{1,0:T(8,128)(2,1)S(1)} collective-permute-done((bf16[112,128]{1,0:T(8,128)(2,1)S(1)}, bf16[112,128]{1,0:T(8,128)(2,1)S(1)}, u32[]{:S(2)}, u32[]{:S(2)}) %collective-permute-start.9) | collective-permute-done | bytes 28704 | tf_op jit(solution)/shard_map/ppermute | solution.py:487
  41.1 0.7 collective-permute-done.11.weight_other_ref
  41.8 0.5 collective-permute-done.10.other_ref
  42.3 0.4 out.1
  42.7 1.7 %collective-permute-start.12 = (bf16[224,256]{1,0:T(8,128)(2,1)S(1)}, bf16[224,256]{1,0:T(8,128)(2,1)S(1)}, u32[]{:S(2)}, u32[]{:S(2)}) collective-permute-start(bf16[224,256]{1,0:T(8,128)(2,1)S(1)} %get-tuple-element.46), channel_id=1, source_target_pairs={{0,8},{1,9},{2,10},{3,11},{4,12},{5,13},{6,14},{7,15},{8,0},{9,1},... | collective-permute-start | bytes 344072 | tf_op jit(solution)/shard_map/ppermute | solution.py:484
  44.4 1.1 %collective-permute-start.13 = (bf16[224,256]{1,0:T(8,128)(2,1)S(1)}, bf16[224,256]{1,0:T(8,128)(2,1)S(1)}, u32[]{:S(2)}, u32[]{:S(2)}) collective-permute-start(bf16[224,256]{1,0:T(8,128)(2,1)S(1)} %get-tuple-element.47), channel_id=1, source_target_pairs={{0,4},{1,5},{2,6},{3,7},{4,0},{5,1},{6,2},{7,3},{8,12},{9,13},{10,... | collective-permute-start | bytes 344072 | tf_op jit(solution)/shard_map/ppermute | solution.py:484
  45.5 1.7 %collective-permute-start.14 = (bf16[224,256]{1,0:T(8,128)(2,1)S(1)}, bf16[224,256]{1,0:T(8,128)(2,1)S(1)}, u32[]{:S(2)}, u32[]{:S(2)}) collective-permute-start(bf16[224,256]{1,0:T(8,128)(2,1)S(1)} %get-tuple-element.48), channel_id=1, source_target_pairs={{0,12},{1,13},{2,14},{3,15},{4,8},{5,9},{6,10},{7,11},{8,4},{9,5},... | collective-permute-start | bytes 344072 | tf_op jit(solution)/shard_map/ppermute | solution.py:484
  47.2 5.5 %collective-permute-done.12 = bf16[224,256]{1,0:T(8,128)(2,1)S(1)} collective-permute-done((bf16[224,256]{1,0:T(8,128)(2,1)S(1)}, bf16[224,256]{1,0:T(8,128)(2,1)S(1)}, u32[]{:S(2)}, u32[]{:S(2)}) %collective-permute-start.12) | collective-permute-done | bytes 114720 | tf_op jit(solution)/shard_map/ppermute | solution.py:484
  52.7 1.8 %collective-permute-done.14 = bf16[224,256]{1,0:T(8,128)(2,1)S(1)} collective-permute-done((bf16[224,256]{1,0:T(8,128)(2,1)S(1)}, bf16[224,256]{1,0:T(8,128)(2,1)S(1)}, u32[]{:S(2)}, u32[]{:S(2)}) %collective-permute-start.14) | collective-permute-done | bytes 114720 | tf_op jit(solution)/shard_map/ppermute | solution.py:484
  54.5 0.1 add_convert_fusion.refs_0_
  54.6 2.4 %collective-permute-start.16 = (bf16[224,256]{1,0:T(8,128)(2,1)S(1)}, bf16[224,256]{1,0:T(8,128)(2,1)S(1)}, u32[]{:S(2)}, u32[]{:S(2)}) collective-permute-start(bf16[224,256]{1,0:T(8,128)(2,1)S(1)} %add_convert_fusion.refs_0_), channel_id=1, source_target_pairs={{0,4},{1,5},{2,6},{3,7},{4,0},{5,1},{6,2},{7,3},{8,12},{9,13},{10,... | collective-permute-start | bytes 344072 | tf_op jit(solution)/shard_map/ppermute | solution.py:484
  57.0 0.8 collective-permute-start.18
  57.7 1.7 %collective-permute-start.20 = (bf16[224,256]{1,0:T(8,128)(2,1)S(1)}, bf16[224,256]{1,0:T(8,128)(2,1)S(1)}, u32[]{:S(2)}, u32[]{:S(2)}) collective-permute-start(bf16[224,256]{1,0:T(8,128)(2,1)S(1)} %add_convert_fusion.refs_0_), channel_id=1, source_target_pairs={{0,12},{1,13},{2,14},{3,15},{4,8},{5,9},{6,10},{7,11},{8,4},{9,5},... | collective-permute-start | bytes 344072 | tf_op jit(solution)/shard_map/ppermute | solution.py:484
  59.4 0.6 collective-permute-start.15
  60.0 0.6 collective-permute-done.16.refs_2_
  60.6 0.9 collective-permute-start.17
  61.5 6.9 %collective-permute-done.18.refs_4_ = bf16[224,256]{1,0:T(8,128)(2,1)S(1)} collective-permute-done((bf16[224,256]{1,0:T(8,128)(2,1)S(1)}, bf16[224,256]{1,0:T(8,128)(2,1)S(1)}, u32[]{:S(2)}, u32[]{:S(2)}) %collective-permute-start.18) | collective-permute-done | bytes 114720 | tf_op jit(solution)/shard_map/ppermute | solution.py:484
  68.3 0.6 collective-permute-start.19
  68.9 1.4 %collective-permute-start.21 = (bf16[224,256]{1,0:T(8,128)(2,1)S(1)}, bf16[224,256]{1,0:T(8,128)(2,1)S(1)}, u32[]{:S(2)}, u32[]{:S(2)}) collective-permute-start(bf16[224,256]{1,0:T(8,128)(2,1)S(1)} %collective-permute-done.20.refs_6_), channel_id=1, source_target_pairs={{0,2},{1,3},{2,0},{3,1},{4,6},{5,7},{6,4},{7,5},{8,10},{9,11},{10,... | collective-permute-start | bytes 344072 | tf_op jit(solution)/shard_map/ppermute | solution.py:487
  70.4 2.8 %collective-permute-done.19.refs_5_ = bf16[224,256]{1,0:T(8,128)(2,1)S(1)} collective-permute-done((bf16[224,256]{1,0:T(8,128)(2,1)S(1)}, bf16[224,256]{1,0:T(8,128)(2,1)S(1)}, u32[]{:S(2)}, u32[]{:S(2)}) %collective-permute-start.19) | collective-permute-done | bytes 114720 | tf_op jit(solution)/shard_map/ppermute | solution.py:487
  73.1 1.2 %collective-permute-done.21.refs_7_ = bf16[224,256]{1,0:T(8,128)(2,1)S(1)} collective-permute-done((bf16[224,256]{1,0:T(8,128)(2,1)S(1)}, bf16[224,256]{1,0:T(8,128)(2,1)S(1)}, u32[]{:S(2)}, u32[]{:S(2)}) %collective-permute-start.21) | collective-permute-done | bytes 114720 | tf_op jit(solution)/shard_map/ppermute | solution.py:487
  74.4 1.9 %gate_up.1 = (f32[128,768]{1,0:T(8,128)S(1)}, f32[128,768]{1,0:T(8,128)S(1)}, bf16[16,2048]{1,0:T(8,128)(2,1)S(1)}, bf16[16,2048]{1,0:T(8,128)(2,1)S(1)}) custom-call(bf16[224,256]{1,0:T(8,128)(2,1)S(1)} %add_convert_fusion.refs_0_, bf16[224,256]{1,0:T(8,128)(2,1)S(1)} %collective-permute-done.15.refs_1_, ...), custom_call_target="tpu_custom_call" | custom-call | flops 1000000000 | bytes 3000000 | tf_op jit(solution)/shard_map/gate_up/pallas_call | solution.py:601
  76.2 0.1 collective-permute-start.23
  76.3 1.7 %collective-permute-done.23.came_ref = f32[128,768]{1,0:T(8,128)S(1)} collective-permute-done((f32[128,768]{1,0:T(8,128)S(1)}, f32[128,768]{1,0:T(8,128)S(1)}, u32[]{:S(2)}, u32[]{:S(2)}) %collective-permute-start.23) | collective-permute-done | bytes 393248 | tf_op jit(solution)/shard_map/ppermute | solution.py:490
  78.0 0.8 hidden.1
  78.8 0.8 collective-permute-start.29
  79.7 1.3 %collective-permute-start.27 = (bf16[16,4096]{1,0:T(8,128)(2,1)S(1)}, bf16[16,4096]{1,0:T(8,128)(2,1)S(1)}, u32[]{:S(2)}, u32[]{:S(2)}) collective-permute-start(bf16[16,4096]{1,0:T(8,128)(2,1)S(1)} %get-tuple-element.60), channel_id=1, source_target_pairs={{0,2},{1,3},{2,0},{3,1},{4,6},{5,7},{6,4},{7,5},{8,10},{9,11},{10,... | collective-permute-start | bytes 393224 | tf_op jit(solution)/shard_map/ppermute | solution.py:487
  80.9 0.8 collective-permute-start.25
  81.7 1.3 %collective-permute-start.24 = (bf16[16,4096]{1,0:T(8,128)(2,1)S(1)}, bf16[16,4096]{1,0:T(8,128)(2,1)S(1)}, u32[]{:S(2)}, u32[]{:S(2)}) collective-permute-start(bf16[16,4096]{1,0:T(8,128)(2,1)S(1)} %get-tuple-element.56), channel_id=1, source_target_pairs={{0,2},{1,3},{2,0},{3,1},{4,6},{5,7},{6,4},{7,5},{8,10},{9,11},{10,... | collective-permute-start | bytes 393224 | tf_op jit(solution)/shard_map/ppermute | solution.py:487
  83.0 0.5 down.1
  83.5 1.7 %collective-permute-done.29.far_ref = bf16[16,4096]{1,0:T(8,128)(2,1)S(1)} collective-permute-done((bf16[16,4096]{1,0:T(8,128)(2,1)S(1)}, bf16[16,4096]{1,0:T(8,128)(2,1)S(1)}, u32[]{:S(2)}, u32[]{:S(2)}) %collective-permute-start.29) | collective-permute-done | bytes 131104 | tf_op jit(solution)/shard_map/ppermute | solution.py:487
  85.3 1.9 %collective-permute-start.30 = (bf16[16,4096]{1,0:T(8,128)(2,1)S(1)}, bf16[16,4096]{1,0:T(8,128)(2,1)S(1)}, u32[]{:S(2)}, u32[]{:S(2)}) collective-permute-start(bf16[16,4096]{1,0:T(8,128)(2,1)S(1)} %add.25), channel_id=1, source_target_pairs={{0,12},{1,13},{2,14},{3,15},{4,8},{5,9},{6,10},{7,11},{8,4},{9,5},... | collective-permute-start | bytes 393224 | tf_op jit(solution)/shard_map/ppermute | solution.py:484
  87.2 0.8 collective-permute-done.27.far_ref
  88.1 0.6 collective-permute-start.28
  88.7 2.1 %collective-permute-done.25.far_ref = bf16[16,4096]{1,0:T(8,128)(2,1)S(1)} collective-permute-done((bf16[16,4096]{1,0:T(8,128)(2,1)S(1)}, bf16[16,4096]{1,0:T(8,128)(2,1)S(1)}, u32[]{:S(2)}, u32[]{:S(2)}) %collective-permute-start.25) | collective-permute-done | bytes 131104 | tf_op jit(solution)/shard_map/ppermute | solution.py:487
  90.9 1.5 %collective-permute-start.26 = (bf16[16,4096]{1,0:T(8,128)(2,1)S(1)}, bf16[16,4096]{1,0:T(8,128)(2,1)S(1)}, u32[]{:S(2)}, u32[]{:S(2)}) collective-permute-start(bf16[16,4096]{1,0:T(8,128)(2,1)S(1)} %add.23), channel_id=1, source_target_pairs={{0,8},{1,9},{2,10},{3,11},{4,12},{5,13},{6,14},{7,15},{8,0},{9,1},... | collective-permute-start | bytes 393224 | tf_op jit(solution)/shard_map/ppermute | solution.py:484
  92.3 1.3 %collective-permute-done.31.refs_6_ = bf16[16,2048]{1,0:T(8,128)(2,1)S(1)} collective-permute-done((bf16[16,2048]{1,0:T(8,128)(2,1)S(1)}, bf16[16,2048]{1,0:T(8,128)(2,1)S(1)}, u32[]{:S(2)}, u32[]{:S(2)}) %collective-permute-start.31) | collective-permute-done | bytes 65568 | tf_op jit(solution)/shard_map/ppermute | solution.py:490
  93.6 1.4 %collective-permute-done.28.refs_3_ = bf16[16,4096]{1,0:T(8,128)(2,1)S(1)} collective-permute-done((bf16[16,4096]{1,0:T(8,128)(2,1)S(1)}, bf16[16,4096]{1,0:T(8,128)(2,1)S(1)}, u32[]{:S(2)}, u32[]{:S(2)}) %collective-permute-start.28) | collective-permute-done | bytes 131104 | tf_op jit(solution)/shard_map/ppermute | solution.py:484
  95.0 3.6 %collective-permute-done.26.refs_2_ = bf16[16,4096]{1,0:T(8,128)(2,1)S(1)} collective-permute-done((bf16[16,4096]{1,0:T(8,128)(2,1)S(1)}, bf16[16,4096]{1,0:T(8,128)(2,1)S(1)}, u32[]{:S(2)}, u32[]{:S(2)}) %collective-permute-start.26) | collective-permute-done | bytes 131104 | tf_op jit(solution)/shard_map/ppermute | solution.py:484
  98.6 0.8 last.1
  (42 shorter events, 0.3 us)
Async XLA Ops:
  0.0 2.7 %copy-start.4 = (bf16[64,4096]{1,0:T(8,128)(2,1)S(1)}, bf16[64,4096]{1,0:T(8,128)(2,1)}, u32[]{:S(2)}) copy-start(bf16[64,4096]{1,0:T(8,128)(2,1)} %refs_9_.2) | copy-start | bytes 1572868
  0.0 2.7 %copy-start.5 = (bf16[64,4096]{1,0:T(8,128)(2,1)S(1)}, bf16[64,4096]{1,0:T(8,128)(2,1)}, u32[]{:S(2)}) copy-start(bf16[64,4096]{1,0:T(8,128)(2,1)} %refs_10_.2) | copy-start | bytes 1572868
  0.0 2.7 %copy-start.6 = (bf16[64,4096]{1,0:T(8,128)(2,1)S(1)}, bf16[64,4096]{1,0:T(8,128)(2,1)}, u32[]{:S(2)}) copy-start(bf16[64,4096]{1,0:T(8,128)(2,1)} %refs_11_.1) | copy-start | bytes 1572868
  2.7 1.0 %copy-start.7 = (bf16[64,4096]{1,0:T(8,128)(2,1)S(1)}, bf16[64,4096]{1,0:T(8,128)(2,1)}, u32[]{:S(2)}) copy-start(bf16[64,4096]{1,0:T(8,128)(2,1)} %weight_ref.3) | copy-start | bytes 1572868
  2.8 1.1 %copy-start.8 = (bf16[8,10240]{1,0:T(8,128)(2,1)S(1)}, bf16[8,10240]{1,0:T(8,128)(2,1)}, u32[]{:S(2)}) copy-start(bf16[8,10240]{1,0:T(8,128)(2,1)} %fetch.1.piece_ref.refs_0_) | copy-start | bytes 491524
  2.9 27.8 %copy-start.9 = (f32[4096]{0:T(1024)S(1)}, f32[4096]{0:T(1024)}, u32[]{:S(2)}) copy-start(f32[4096]{0:T(1024)} %param.23) | copy-start | bytes 49156
  2.9 27.7 %collective-permute-start.7 = (bf16[192,4096]{1,0:T(8,128)(2,1)S(1)}, bf16[192,4096]{1,0:T(8,128)(2,1)S(1)}, u32[]{:S(2)}, u32[]{:S(2)}) collective-permute-start(bf16[192,4096]{1,0:T(8,128)(2,1)S(1)} %stack.1), channel_id=1, source_target_pairs={{0,1},{1,0},{2,3},{3,2},{4,5},{5,4},{6,7},{7,6},{8,9},{9,8},{10,11... | collective-permute-start | bytes 4718600 | tf_op jit(solution)/shard_map/ppermute | solution.py:490
  3.9 26.8 %collective-permute-start = (bf16[8,26624]{1,0:T(8,128)(2,1)S(1)}, bf16[8,26624]{1,0:T(8,128)(2,1)S(1)}, u32[]{:S(2)}, u32[]{:S(2)}) collective-permute-start(bf16[8,26624]{1,0:T(8,128)(2,1)S(1)} %across.1), channel_id=1, source_target_pairs={{0,2},{1,3},{2,0},{3,1},{4,6},{5,7},{6,4},{7,5},{8,10},{9,11},{10,... | collective-permute-start | bytes 1277960 | tf_op jit(solution)/shard_map/ppermute | solution.py:487
  7.0 7.9 %collective-permute-start.1 = (bf16[8,10240]{1,0:T(8,128)(2,1)S(1)}, bf16[8,10240]{1,0:T(8,128)(2,1)S(1)}, u32[]{:S(2)}, u32[]{:S(2)}) collective-permute-start(bf16[8,10240]{1,0:T(8,128)(2,1)S(1)} %copy-done.8), channel_id=1, source_target_pairs={{0,4},{1,5},{2,6},{3,7},{4,0},{5,1},{6,2},{7,3},{8,12},{9,13},{10,... | collective-permute-start | bytes 491528 | tf_op jit(solution)/shard_map/ppermute | solution.py:484
  8.5 15.1 %collective-permute-start.3 = (bf16[8,10240]{1,0:T(8,128)(2,1)S(1)}, bf16[8,10240]{1,0:T(8,128)(2,1)S(1)}, u32[]{:S(2)}, u32[]{:S(2)}) collective-permute-start(bf16[8,10240]{1,0:T(8,128)(2,1)S(1)} %copy-done.8), channel_id=1, source_target_pairs={{0,8},{1,9},{2,10},{3,11},{4,12},{5,13},{6,14},{7,15},{8,0},{9,1},... | collective-permute-start | bytes 491528 | tf_op jit(solution)/shard_map/ppermute | solution.py:484
  11.1 13.0 %collective-permute-start.5 = (bf16[8,10240]{1,0:T(8,128)(2,1)S(1)}, bf16[8,10240]{1,0:T(8,128)(2,1)S(1)}, u32[]{:S(2)}, u32[]{:S(2)}) collective-permute-start(bf16[8,10240]{1,0:T(8,128)(2,1)S(1)} %copy-done.8), channel_id=1, source_target_pairs={{0,12},{1,13},{2,14},{3,15},{4,8},{5,9},{6,10},{7,11},{8,4},{9,5},... | collective-permute-start | bytes 491528 | tf_op jit(solution)/shard_map/ppermute | solution.py:484
  14.8 10.7 %collective-permute-start.2 = (bf16[8,10240]{1,0:T(8,128)(2,1)S(1)}, bf16[8,10240]{1,0:T(8,128)(2,1)S(1)}, u32[]{:S(2)}, u32[]{:S(2)}) collective-permute-start(bf16[8,10240]{1,0:T(8,128)(2,1)S(1)} %collective-permute-done.1.refs_2_), channel_id=1, source_target_pairs={{0,2},{1,3},{2,0},{3,1},{4,6},{5,7},{6,4},{7,5},{8,10},{9,11},{10,... | collective-permute-start | bytes 491528 | tf_op jit(solution)/shard_map/ppermute | solution.py:487
  23.6 5.3 %collective-permute-start.4 = (bf16[8,10240]{1,0:T(8,128)(2,1)S(1)}, bf16[8,10240]{1,0:T(8,128)(2,1)S(1)}, u32[]{:S(2)}, u32[]{:S(2)}) collective-permute-start(bf16[8,10240]{1,0:T(8,128)(2,1)S(1)} %collective-permute-done.3.refs_4_), channel_id=1, source_target_pairs={{0,2},{1,3},{2,0},{3,1},{4,6},{5,7},{6,4},{7,5},{8,10},{9,11},{10,... | collective-permute-start | bytes 491528 | tf_op jit(solution)/shard_map/ppermute | solution.py:487
  24.1 6.5 %collective-permute-start.6 = (bf16[8,10240]{1,0:T(8,128)(2,1)S(1)}, bf16[8,10240]{1,0:T(8,128)(2,1)S(1)}, u32[]{:S(2)}, u32[]{:S(2)}) collective-permute-start(bf16[8,10240]{1,0:T(8,128)(2,1)S(1)} %collective-permute-done.5.refs_6_), channel_id=1, source_target_pairs={{0,2},{1,3},{2,0},{3,1},{4,6},{5,7},{6,4},{7,5},{8,10},{9,11},{10,... | collective-permute-start | bytes 491528 | tf_op jit(solution)/shard_map/ppermute | solution.py:487
  30.6 3.5 %copy-start.10 = (s32[24,1]{0,1:T(1,128)S(1)}, s32[24,1]{0,1:T(1,128)}, u32[]{:S(2)}) copy-start(s32[24,1]{0,1:T(1,128)} %param.16) | copy-start | bytes 292
  30.6 3.5 %copy-start.11 = (s32[24]{0:T(128)S(1)}, s32[24]{0:T(128)}, u32[]{:S(2)}) copy-start(s32[24]{0:T(128)} %segment_ref.1) | copy-start | bytes 292
  30.7 5.6 %copy-start.2 = (bf16[160,4096]{1,0:T(8,128)(2,1)S(1)}, bf16[160,4096]{1,0:T(8,128)(2,1)}, u32[]{:S(2)}) copy-start(bf16[160,4096]{1,0:T(8,128)(2,1)} %refs_10_.3) | copy-start | bytes 3932164
  32.7 1.5 %collective-permute-start.8 = (bf16[160,512]{1,0:T(8,128)(2,1)S(1)}, bf16[160,512]{1,0:T(8,128)(2,1)S(1)}, u32[]{:S(2)}, u32[]{:S(2)}) collective-permute-start(bf16[160,512]{1,0:T(8,128)(2,1)S(1)} %get-tuple-element.40), channel_id=1, source_target_pairs={{0,1},{1,0},{2,3},{3,2},{4,5},{5,4},{6,7},{7,6},{8,9},{9,8},{10,11... | collective-permute-start | bytes 491528 | tf_op jit(solution)/shard_map/ppermute | solution.py:490
  34.1 2.1 %copy-start = (bf16[160,4096]{1,0:T(8,128)(2,1)S(1)}, bf16[160,4096]{1,0:T(8,128)(2,1)}, u32[]{:S(2)}) copy-start(bf16[160,4096]{1,0:T(8,128)(2,1)} %down_ref.4) | copy-start | bytes 3932164
  34.1 2.1 %copy-start.1 = (bf16[160,4096]{1,0:T(8,128)(2,1)S(1)}, bf16[160,4096]{1,0:T(8,128)(2,1)}, u32[]{:S(2)}) copy-start(bf16[160,4096]{1,0:T(8,128)(2,1)} %refs_9_.3) | copy-start | bytes 3932164
  36.4 37.9 %collective-permute-start.22 = (bf16[320,4096]{1,0:T(8,128)(2,1)S(1)}, bf16[320,4096]{1,0:T(8,128)(2,1)S(1)}, u32[]{:S(2)}, u32[]{:S(2)}) collective-permute-start(bf16[320,4096]{1,0:T(8,128)(2,1)S(1)} %share.1), channel_id=1, source_target_pairs={{0,1},{1,0},{2,3},{3,2},{4,5},{5,4},{6,7},{7,6},{8,9},{9,8},{10,11... | collective-permute-start | bytes 7864328 | tf_op jit(solution)/shard_map/ppermute | solution.py:490
  36.7 5.1 %collective-permute-start.11 = (bf16[128,1024]{1,0:T(8,128)(2,1)S(1)}, bf16[128,1024]{1,0:T(8,128)(2,1)S(1)}, u32[]{:S(2)}, u32[]{:S(2)}) collective-permute-start(bf16[128,1024]{1,0:T(8,128)(2,1)S(1)} %get-tuple-element.44), channel_id=1, source_target_pairs={{0,1},{1,0},{2,3},{3,2},{4,5},{5,4},{6,7},{7,6},{8,9},{9,8},{10,11... | collective-permute-start | bytes 786440 | tf_op jit(solution)/shard_map/ppermute | solution.py:490
  37.2 3.9 %collective-permute-start.9 = (bf16[112,128]{1,0:T(8,128)(2,1)S(1)}, bf16[112,128]{1,0:T(8,128)(2,1)S(1)}, u32[]{:S(2)}, u32[]{:S(2)}) collective-permute-start(bf16[112,128]{1,0:T(8,128)(2,1)S(1)} %get-tuple-element.42), channel_id=1, source_target_pairs={{0,2},{1,3},{2,0},{3,1},{4,6},{5,7},{6,4},{7,5},{8,10},{9,11},{10,... | collective-permute-start | bytes 86024 | tf_op jit(solution)/shard_map/ppermute | solution.py:487
  41.1 1.2 %collective-permute-start.10 = (bf16[224,128]{1,0:T(8,128)(2,1)S(1)}, bf16[224,128]{1,0:T(8,128)(2,1)S(1)}, u32[]{:S(2)}, u32[]{:S(2)}) collective-permute-start(bf16[224,128]{1,0:T(8,128)(2,1)S(1)} %constant_dynamic-update-slice_fusion.own_ref), channel_id=1, source_target_pairs={{0,1},{1,0},{2,3},{3,2},{4,5},{5,4},{6,7},{7,6},{8,9},{9,8},{10,11... | collective-permute-start | bytes 172040 | tf_op jit(solution)/shard_map/ppermute | solution.py:490
  42.3 32.1 %copy-start.3 = (f32[4096]{0:T(1024)S(1)}, f32[4096]{0:T(1024)}, u32[]{:S(2)}) copy-start(f32[4096]{0:T(1024)} %param.24) | copy-start | bytes 49156
  42.7 10.0 %collective-permute-start.12 = (bf16[224,256]{1,0:T(8,128)(2,1)S(1)}, bf16[224,256]{1,0:T(8,128)(2,1)S(1)}, u32[]{:S(2)}, u32[]{:S(2)}) collective-permute-start(bf16[224,256]{1,0:T(8,128)(2,1)S(1)} %get-tuple-element.46), channel_id=1, source_target_pairs={{0,8},{1,9},{2,10},{3,11},{4,12},{5,13},{6,14},{7,15},{8,0},{9,1},... | collective-permute-start | bytes 344072 | tf_op jit(solution)/shard_map/ppermute | solution.py:484
  44.4 8.3 %collective-permute-start.13 = (bf16[224,256]{1,0:T(8,128)(2,1)S(1)}, bf16[224,256]{1,0:T(8,128)(2,1)S(1)}, u32[]{:S(2)}, u32[]{:S(2)}) collective-permute-start(bf16[224,256]{1,0:T(8,128)(2,1)S(1)} %get-tuple-element.47), channel_id=1, source_target_pairs={{0,4},{1,5},{2,6},{3,7},{4,0},{5,1},{6,2},{7,3},{8,12},{9,13},{10,... | collective-permute-start | bytes 344072 | tf_op jit(solution)/shard_map/ppermute | solution.py:484
  45.5 9.0 %collective-permute-start.14 = (bf16[224,256]{1,0:T(8,128)(2,1)S(1)}, bf16[224,256]{1,0:T(8,128)(2,1)S(1)}, u32[]{:S(2)}, u32[]{:S(2)}) collective-permute-start(bf16[224,256]{1,0:T(8,128)(2,1)S(1)} %get-tuple-element.48), channel_id=1, source_target_pairs={{0,12},{1,13},{2,14},{3,15},{4,8},{5,9},{6,10},{7,11},{8,4},{9,5},... | collective-permute-start | bytes 344072 | tf_op jit(solution)/shard_map/ppermute | solution.py:484
  54.6 6.0 %collective-permute-start.16 = (bf16[224,256]{1,0:T(8,128)(2,1)S(1)}, bf16[224,256]{1,0:T(8,128)(2,1)S(1)}, u32[]{:S(2)}, u32[]{:S(2)}) collective-permute-start(bf16[224,256]{1,0:T(8,128)(2,1)S(1)} %add_convert_fusion.refs_0_), channel_id=1, source_target_pairs={{0,4},{1,5},{2,6},{3,7},{4,0},{5,1},{6,2},{7,3},{8,12},{9,13},{10,... | collective-permute-start | bytes 344072 | tf_op jit(solution)/shard_map/ppermute | solution.py:484
  57.0 11.3 %collective-permute-start.18 = (bf16[224,256]{1,0:T(8,128)(2,1)S(1)}, bf16[224,256]{1,0:T(8,128)(2,1)S(1)}, u32[]{:S(2)}, u32[]{:S(2)}) collective-permute-start(bf16[224,256]{1,0:T(8,128)(2,1)S(1)} %add_convert_fusion.refs_0_), channel_id=1, source_target_pairs={{0,8},{1,9},{2,10},{3,11},{4,12},{5,13},{6,14},{7,15},{8,0},{9,1},... | collective-permute-start | bytes 344072 | tf_op jit(solution)/shard_map/ppermute | solution.py:484
  57.7 11.2 %collective-permute-start.20 = (bf16[224,256]{1,0:T(8,128)(2,1)S(1)}, bf16[224,256]{1,0:T(8,128)(2,1)S(1)}, u32[]{:S(2)}, u32[]{:S(2)}) collective-permute-start(bf16[224,256]{1,0:T(8,128)(2,1)S(1)} %add_convert_fusion.refs_0_), channel_id=1, source_target_pairs={{0,12},{1,13},{2,14},{3,15},{4,8},{5,9},{6,10},{7,11},{8,4},{9,5},... | collective-permute-start | bytes 344072 | tf_op jit(solution)/shard_map/ppermute | solution.py:484
  59.4 10.9 %collective-permute-start.15 = (bf16[224,256]{1,0:T(8,128)(2,1)S(1)}, bf16[224,256]{1,0:T(8,128)(2,1)S(1)}, u32[]{:S(2)}, u32[]{:S(2)}) collective-permute-start(bf16[224,256]{1,0:T(8,128)(2,1)S(1)} %add_convert_fusion.refs_0_), channel_id=1, source_target_pairs={{0,2},{1,3},{2,0},{3,1},{4,6},{5,7},{6,4},{7,5},{8,10},{9,11},{10,... | collective-permute-start | bytes 344072 | tf_op jit(solution)/shard_map/ppermute | solution.py:487
  60.6 9.8 %collective-permute-start.17 = (bf16[224,256]{1,0:T(8,128)(2,1)S(1)}, bf16[224,256]{1,0:T(8,128)(2,1)S(1)}, u32[]{:S(2)}, u32[]{:S(2)}) collective-permute-start(bf16[224,256]{1,0:T(8,128)(2,1)S(1)} %collective-permute-done.16.refs_2_), channel_id=1, source_target_pairs={{0,2},{1,3},{2,0},{3,1},{4,6},{5,7},{6,4},{7,5},{8,10},{9,11},{10,... | collective-permute-start | bytes 344072 | tf_op jit(solution)/shard_map/ppermute | solution.py:487
  68.3 4.8 %collective-permute-start.19 = (bf16[224,256]{1,0:T(8,128)(2,1)S(1)}, bf16[224,256]{1,0:T(8,128)(2,1)S(1)}, u32[]{:S(2)}, u32[]{:S(2)}) collective-permute-start(bf16[224,256]{1,0:T(8,128)(2,1)S(1)} %collective-permute-done.18.refs_4_), channel_id=1, source_target_pairs={{0,2},{1,3},{2,0},{3,1},{4,6},{5,7},{6,4},{7,5},{8,10},{9,11},{10,... | collective-permute-start | bytes 344072 | tf_op jit(solution)/shard_map/ppermute | solution.py:487
  68.9 5.4 %collective-permute-start.21 = (bf16[224,256]{1,0:T(8,128)(2,1)S(1)}, bf16[224,256]{1,0:T(8,128)(2,1)S(1)}, u32[]{:S(2)}, u32[]{:S(2)}) collective-permute-start(bf16[224,256]{1,0:T(8,128)(2,1)S(1)} %collective-permute-done.20.refs_6_), channel_id=1, source_target_pairs={{0,2},{1,3},{2,0},{3,1},{4,6},{5,7},{6,4},{7,5},{8,10},{9,11},{10,... | collective-permute-start | bytes 344072 | tf_op jit(solution)/shard_map/ppermute | solution.py:487
  76.2 1.8 %collective-permute-start.23 = (f32[128,768]{1,0:T(8,128)S(1)}, f32[128,768]{1,0:T(8,128)S(1)}, u32[]{:S(2)}, u32[]{:S(2)}) collective-permute-start(f32[128,768]{1,0:T(8,128)S(1)} %get-tuple-element.53), channel_id=1, source_target_pairs={{0,1},{1,0},{2,3},{3,2},{4,5},{5,4},{6,7},{7,6},{8,9},{9,8},{10,11... | collective-permute-start | bytes 1179656 | tf_op jit(solution)/shard_map/ppermute | solution.py:490
  78.8 6.4 %collective-permute-start.29 = (bf16[16,4096]{1,0:T(8,128)(2,1)S(1)}, bf16[16,4096]{1,0:T(8,128)(2,1)S(1)}, u32[]{:S(2)}, u32[]{:S(2)}) collective-permute-start(bf16[16,4096]{1,0:T(8,128)(2,1)S(1)} %get-tuple-element.62), channel_id=1, source_target_pairs={{0,2},{1,3},{2,0},{3,1},{4,6},{5,7},{6,4},{7,5},{8,10},{9,11},{10,... | collective-permute-start | bytes 393224 | tf_op jit(solution)/shard_map/ppermute | solution.py:487
  79.7 8.4 %collective-permute-start.27 = (bf16[16,4096]{1,0:T(8,128)(2,1)S(1)}, bf16[16,4096]{1,0:T(8,128)(2,1)S(1)}, u32[]{:S(2)}, u32[]{:S(2)}) collective-permute-start(bf16[16,4096]{1,0:T(8,128)(2,1)S(1)} %get-tuple-element.60), channel_id=1, source_target_pairs={{0,2},{1,3},{2,0},{3,1},{4,6},{5,7},{6,4},{7,5},{8,10},{9,11},{10,... | collective-permute-start | bytes 393224 | tf_op jit(solution)/shard_map/ppermute | solution.py:487
  80.9 9.9 %collective-permute-start.25 = (bf16[16,4096]{1,0:T(8,128)(2,1)S(1)}, bf16[16,4096]{1,0:T(8,128)(2,1)S(1)}, u32[]{:S(2)}, u32[]{:S(2)}) collective-permute-start(bf16[16,4096]{1,0:T(8,128)(2,1)S(1)} %get-tuple-element.58), channel_id=1, source_target_pairs={{0,2},{1,3},{2,0},{3,1},{4,6},{5,7},{6,4},{7,5},{8,10},{9,11},{10,... | collective-permute-start | bytes 393224 | tf_op jit(solution)/shard_map/ppermute | solution.py:487
  81.7 11.9 %collective-permute-start.24 = (bf16[16,4096]{1,0:T(8,128)(2,1)S(1)}, bf16[16,4096]{1,0:T(8,128)(2,1)S(1)}, u32[]{:S(2)}, u32[]{:S(2)}) collective-permute-start(bf16[16,4096]{1,0:T(8,128)(2,1)S(1)} %get-tuple-element.56), channel_id=1, source_target_pairs={{0,2},{1,3},{2,0},{3,1},{4,6},{5,7},{6,4},{7,5},{8,10},{9,11},{10,... | collective-permute-start | bytes 393224 | tf_op jit(solution)/shard_map/ppermute | solution.py:487
  85.3 8.3 %collective-permute-start.30 = (bf16[16,4096]{1,0:T(8,128)(2,1)S(1)}, bf16[16,4096]{1,0:T(8,128)(2,1)S(1)}, u32[]{:S(2)}, u32[]{:S(2)}) collective-permute-start(bf16[16,4096]{1,0:T(8,128)(2,1)S(1)} %add.25), channel_id=1, source_target_pairs={{0,12},{1,13},{2,14},{3,15},{4,8},{5,9},{6,10},{7,11},{8,4},{9,5},... | collective-permute-start | bytes 393224 | tf_op jit(solution)/shard_map/ppermute | solution.py:484
  88.1 6.9 %collective-permute-start.28 = (bf16[16,4096]{1,0:T(8,128)(2,1)S(1)}, bf16[16,4096]{1,0:T(8,128)(2,1)S(1)}, u32[]{:S(2)}, u32[]{:S(2)}) collective-permute-start(bf16[16,4096]{1,0:T(8,128)(2,1)S(1)} %add.24), channel_id=1, source_target_pairs={{0,4},{1,5},{2,6},{3,7},{4,0},{5,1},{6,2},{7,3},{8,12},{9,13},{10,... | collective-permute-start | bytes 393224 | tf_op jit(solution)/shard_map/ppermute | solution.py:484
  90.9 7.7 %collective-permute-start.26 = (bf16[16,4096]{1,0:T(8,128)(2,1)S(1)}, bf16[16,4096]{1,0:T(8,128)(2,1)S(1)}, u32[]{:S(2)}, u32[]{:S(2)}) collective-permute-start(bf16[16,4096]{1,0:T(8,128)(2,1)S(1)} %add.23), channel_id=1, source_target_pairs={{0,8},{1,9},{2,10},{3,11},{4,12},{5,13},{6,14},{7,15},{8,0},{9,1},... | collective-permute-start | bytes 393224 | tf_op jit(solution)/shard_map/ppermute | solution.py:484
  92.3 1.3 %collective-permute-start.31 = (bf16[16,2048]{1,0:T(8,128)(2,1)S(1)}, bf16[16,2048]{1,0:T(8,128)(2,1)S(1)}, u32[]{:S(2)}, u32[]{:S(2)}) collective-permute-start(bf16[16,2048]{1,0:T(8,128)(2,1)S(1)} %get-tuple-element.64), channel_id=1, source_target_pairs={{0,1},{1,0},{2,3},{3,2},{4,5},{5,4},{6,7},{7,6},{8,9},{9,8},{10,11... | collective-permute-start | bytes 196616 | tf_op jit(solution)/shard_map/ppermute | solution.py:490

commit v5 on v4

--- a/solution.py
+++ b/solution.py
@@ -401,8 +401,42 @@
     )
 
 
-def hidden_kernel(features, keep_ref, came_ref, down_ref, share_ref, *refs):
-    chunk_rows = refs[0].shape[0]
+def packed(rows):
+    count, features = rows.shape
+    groups = [rows[i : i + 8] for i in range(0, count // 8 * 8, 8)]
+    first = count // 8 * 8
+    for size in (4, 2, 1):
+        if (count - first) & size:
+            step = features * size // 8
+            groups.append(
+                jnp.concatenate(
+                    [
+                        rows[first : first + size, j * step : (j + 1) * step]
+                        for j in range(8 // size)
+                    ],
+                    axis=0,
+                )
+            )
+            first += size
+    return jnp.concatenate(groups, axis=1) if len(groups) > 1 else groups[0]
+
+
+def unpack(value, target):
+    count, features = target.shape
+    for i in range(count // 8):
+        target[i * 8 : i * 8 + 8, :] = value[:, i * features : (i + 1) * features]
+    first, lane = count // 8 * 8, count // 8 * features
+    for size in (4, 2, 1):
+        if (count - first) & size:
+            step = features * size // 8
+            for j in range(8 // size):
+                target[first : first + size, j * step : (j + 1) * step] = value[
+                    j * size : (j + 1) * size, lane : lane + step
+                ]
+            first, lane = first + size, lane + step
+
+
+def hidden_kernel(features, chunk_rows, rows_here, keep_ref, came_ref, down_ref, share_ref, *refs):
     hidden_ref = refs[-1]
     units = down_ref.shape[0]
     summed = keep_ref[...] + came_ref[...]
@@ -420,11 +454,11 @@
     )
     result = dot(far[:, :units], down_ref[...]) + dot(far[:, units:], share_ref[units:, :])
     for dz in range(len(refs) - 1):
-        refs[dz][...] = result[dz * chunk_rows : (dz + 1) * chunk_rows].astype(jnp.bfloat16)
-
-
-def down_kernel(hidden_ref, down_ref, share_ref, *out_refs):
-    chunk_rows = out_refs[0].shape[0]
+        first = dz * chunk_rows
+        refs[dz][...] = packed(result[first : first + rows_here]).astype(jnp.bfloat16)
+
+
+def down_kernel(chunk_rows, rows_here, hidden_ref, down_ref, share_ref, *out_refs):
     units = down_ref.shape[0]
     hidden = hidden_ref[...]
     near = jnp.concatenate(
@@ -436,7 +470,8 @@
     )
     result = dot(near[:, :units], down_ref[...]) + dot(near[:, units:], share_ref[units:, :])
     for dz in range(len(out_refs)):
-        out_refs[dz][...] = result[dz * chunk_rows : (dz + 1) * chunk_rows]
+        first = dz * chunk_rows
+        out_refs[dz][...] = packed(result[first : first + rows_here])
 
 
 def add_kernel(near_ref, far_ref, out_ref):
@@ -446,7 +481,7 @@
 def last_kernel(count, *refs):
     near_ref, far_ref = refs[0], refs[1]
     arrived = refs[2 : 2 + count]
-    kept_ref, kept_other_ref, out_ref = refs[2 + count :]
+    kept_ref, kept_other_ref, out_ref, total_ref = refs[2 + count :]
     ci = place()[3]
     rows = out_ref.shape[0]
     half = kept_ref.shape[1]
@@ -455,8 +490,9 @@
     for ref in arrived:
         total = total + ref[...].astype(jnp.float32)
     low, high = jnp.where(ci == 0, kept, other), jnp.where(ci == 0, other, kept)
-    out_ref[:, :half] = (low + total[:, :half])[:rows].astype(jnp.bfloat16)
-    out_ref[:, half:] = (high + total[:, half:])[:rows].astype(jnp.bfloat16)
+    unpack(total, total_ref)
+    out_ref[:, :half] = (low[:rows] + total_ref[:, :half]).astype(jnp.bfloat16)
+    out_ref[:, half:] = (high[:rows] + total_ref[:, half:]).astype(jnp.bfloat16)
 
 
 def body(
@@ -478,7 +514,7 @@
     devices = lax.axis_size(AXIS)
     nz = devices // 4
     _, zi, yi, ci = place()
-    z_order = [k for k in (2, 1) if k < nz] + list(range(3, nz))
+    z_order = list(range(nz - 1, 0, -1))
 
     def along_z(value, k):
         return lax.ppermute(value, AXIS, [(i, i ^ (4 * k)) for i in range(devices)])
@@ -613,28 +649,29 @@
     came = across_core(send)
     kept_other = across_core(kept_send)
 
-    chunk = shape((chunk_rows, features), bf16)
+    chunk = shape((8, rows_here * features // 8), bf16)
     *far, hidden = kernel_call(
-        functools.partial(hidden_kernel, features),
+        functools.partial(hidden_kernel, features, chunk_rows, rows_here),
         (chunk,) * nz + (shape((slots, 2 * units), bf16),),
         [VMEM] * 4,
         name="hidden",
     )(keep, came, down_weight, share)
-    moved = {k: across_y(far[k]) for k in z_order + [0]}
+    moved = {k: across_y(far[k]) for k in [*range(1, nz), 0]}
     near = kernel_call(
-        down_kernel,
-        (shape((chunk_rows, features), f32),) * nz,
+        functools.partial(down_kernel, chunk_rows, rows_here),
+        (shape(chunk.shape, f32),) * nz,
         [VMEM] * 3,
         name="down",
     )(hidden, down_weight, share)
     arrived = []
-    for k in z_order:
+    for k in range(1, nz):
         part = kernel_call(add_kernel, chunk, [VMEM, VMEM], name="add")(near[k], moved[k])
         arrived.append(along_z(part, k))
     return kernel_call(
         functools.partial(last_kernel, len(arrived)),
         shape((rows_here, features), bf16),
         [VMEM] * (len(arrived) + 4),
+        [pltpu.VMEM((rows_here, features), f32)],
         name="last",
     )(near[0], moved[0], *arrived, kept, kept_other)
 

time: 99.6 us -> 97 us (0.974)
  waiting for transfers between devices: 54.3 us -> 52.7 us
  starting transfers between devices: 32.6 us -> 31.5 us
    ppermute x13, waiting for transfers between devices: 17.1 us -> 15.4 us  [across_y(): return lax.ppermute(value, AXIS, [(i, i ^ 2) for i in range(devices)])]
  transfers between devices with their start and end apart: 32 -> 32, of which waited for: 21 -> 22; matrix products, arithmetic and copies ran while one was open for 0% -> 0% of each run, Pallas kernels for 1% -> 1%
where the time goes in v5:
time: 97 us; the launch traced here: 96.8 us
  waiting for transfers between devices  52.7 us (54%)
  starting transfers between devices  31.5 us (32%)
  Pallas kernels  11.8 us (12%)
    ppermute x12, waiting for transfers between devices, along_z(): return lax.ppermute(value, AXIS, [(i, i ^ 4 * k) for i in range(devices)])  31.7 us
    ppermute x12, starting transfers between devices, along_z(): return lax.ppermute(value, AXIS, [(i, i ^ 4 * k) for i in range(devices)])  17.1 us
    ppermute x13, waiting for transfers between devices, across_y(): return lax.ppermute(value, AXIS, [(i, i ^ 2) for i in range(devices)])  15.4 us
    ppermute x13, starting transfers between devices, across_y(): return lax.ppermute(value, AXIS, [(i, i ^ 2) for i in range(devices)])  13.1 us
    ppermute x7, waiting for transfers between devices, across_core(): return lax.ppermute(value, AXIS, [(i, i ^ 1) for i in range(devices)])  5.58 us
    pallas_call x1, Pallas kernels, body(): kernel_call(fetch_kernel, shape((8, full * features + halved * half), bf1...  2.74 us
    pallas_call x1, Pallas kernels, body(): kernel_call(functools.partial(attention_kernel, query_rows, width), (shap...  2.1 us
    pallas_call x1, Pallas kernels, body(): kernel_call(functools.partial(projection_kernel, query_rows + CAP * BLK),...  1.98 us
  transfers between devices with their start and end apart: 32, of which 22 were waited for; matrix products, arithmetic and copies ran while one was open for 0% of the time, Pallas kernels for 1%

profile of v5, /device:TPU:0, one launch (start us, length us, event | category | flops | bytes accessed | tf_op | source)
XLA Modules:
  0.0 96.8 jit_solution(14244656710469116991)
XLA Ops:
  0.0 2.7 %fetch.1.piece_ref.refs_0_ = bf16[8,10240]{1,0:T(8,128)(2,1)} custom-call(s32[24]{0:T(128)} %bitcast.5, s32[24]{0:T(128)} %row_ref.1, bf16[64,4,4096]{2,1,0:T(4,128)(2,1)} %corpus_ref.1, bf16[8,4096]{1,0:T(8,128)(2,1)} %query_ref.1), custom_call_target="tpu_custom_call" | custom-call | flops 1000000000 | bytes 3000000 | tf_op jit(solution)/shard_map/fetch/pallas_call | solution.py:558
  2.8 0.1 stack.1
  2.9 0.5 collective-permute-start.7
  3.5 0.4 copy-done.7
  3.9 3.0 %collective-permute-start = (bf16[8,26624]{1,0:T(8,128)(2,1)S(1)}, bf16[8,26624]{1,0:T(8,128)(2,1)S(1)}, u32[]{:S(2)}, u32[]{:S(2)}) collective-permute-start(bf16[8,26624]{1,0:T(8,128)(2,1)S(1)} %across.1), channel_id=1, source_target_pairs={{0,2},{1,3},{2,0},{3,1},{4,6},{5,7},{6,4},{7,5},{8,10},{9,11},{10,... | collective-permute-start | bytes 1277960 | tf_op jit(solution)/shard_map/ppermute | solution.py:523
  6.9 1.6 %collective-permute-start.1 = (bf16[8,10240]{1,0:T(8,128)(2,1)S(1)}, bf16[8,10240]{1,0:T(8,128)(2,1)S(1)}, u32[]{:S(2)}, u32[]{:S(2)}) collective-permute-start(bf16[8,10240]{1,0:T(8,128)(2,1)S(1)} %copy-done.8), channel_id=1, source_target_pairs={{0,4},{1,5},{2,6},{3,7},{4,0},{5,1},{6,2},{7,3},{8,12},{9,13},{10,... | collective-permute-start | bytes 491528 | tf_op jit(solution)/shard_map/ppermute | solution.py:520
  8.5 2.5 %collective-permute-start.3 = (bf16[8,10240]{1,0:T(8,128)(2,1)S(1)}, bf16[8,10240]{1,0:T(8,128)(2,1)S(1)}, u32[]{:S(2)}, u32[]{:S(2)}) collective-permute-start(bf16[8,10240]{1,0:T(8,128)(2,1)S(1)} %copy-done.8), channel_id=1, source_target_pairs={{0,8},{1,9},{2,10},{3,11},{4,12},{5,13},{6,14},{7,15},{8,0},{9,1},... | collective-permute-start | bytes 491528 | tf_op jit(solution)/shard_map/ppermute | solution.py:520
  11.1 0.2 collective-permute-start.5
  11.3 3.5 %collective-permute-done.1.refs_2_ = bf16[8,10240]{1,0:T(8,128)(2,1)S(1)} collective-permute-done((bf16[8,10240]{1,0:T(8,128)(2,1)S(1)}, bf16[8,10240]{1,0:T(8,128)(2,1)S(1)}, u32[]{:S(2)}, u32[]{:S(2)}) %collective-permute-start.1) | collective-permute-done | bytes 163872 | tf_op jit(solution)/shard_map/ppermute | solution.py:520
  14.8 0.3 collective-permute-start.2
  15.2 8.4 %collective-permute-done.3.refs_4_ = bf16[8,10240]{1,0:T(8,128)(2,1)S(1)} collective-permute-done((bf16[8,10240]{1,0:T(8,128)(2,1)S(1)}, bf16[8,10240]{1,0:T(8,128)(2,1)S(1)}, u32[]{:S(2)}, u32[]{:S(2)}) %collective-permute-start.3) | collective-permute-done | bytes 163872 | tf_op jit(solution)/shard_map/ppermute | solution.py:520
  23.6 0.5 collective-permute-start.4
  24.1 1.5 %collective-permute-start.6 = (bf16[8,10240]{1,0:T(8,128)(2,1)S(1)}, bf16[8,10240]{1,0:T(8,128)(2,1)S(1)}, u32[]{:S(2)}, u32[]{:S(2)}) collective-permute-start(bf16[8,10240]{1,0:T(8,128)(2,1)S(1)} %collective-permute-done.5.refs_6_), channel_id=1, source_target_pairs={{0,2},{1,3},{2,0},{3,1},{4,6},{5,7},{6,4},{7,5},{8,10},{9,11},{10,... | collective-permute-start | bytes 491528 | tf_op jit(solution)/shard_map/ppermute | solution.py:523
  25.6 3.3 %collective-permute-done.4.refs_5_ = bf16[8,10240]{1,0:T(8,128)(2,1)S(1)} collective-permute-done((bf16[8,10240]{1,0:T(8,128)(2,1)S(1)}, bf16[8,10240]{1,0:T(8,128)(2,1)S(1)}, u32[]{:S(2)}, u32[]{:S(2)}) %collective-permute-start.4) | collective-permute-done | bytes 163872 | tf_op jit(solution)/shard_map/ppermute | solution.py:523
  28.9 1.8 %collective-permute-done.6.refs_7_ = bf16[8,10240]{1,0:T(8,128)(2,1)S(1)} collective-permute-done((bf16[8,10240]{1,0:T(8,128)(2,1)S(1)}, bf16[8,10240]{1,0:T(8,128)(2,1)S(1)}, u32[]{:S(2)}, u32[]{:S(2)}) %collective-permute-start.6) | collective-permute-done | bytes 163872 | tf_op jit(solution)/shard_map/ppermute | solution.py:523
  30.7 2.0 %project.1 = (bf16[160,512]{1,0:T(8,128)(2,1)S(1)}, bf16[160,512]{1,0:T(8,128)(2,1)S(1)}) custom-call(bf16[8,10240]{1,0:T(8,128)(2,1)S(1)} %copy-done.8, bf16[8,26624]{1,0:T(8,128)(2,1)S(1)} %collective-permute-done.refs_1_.far_ref, bf16[8,10240]{1,0:T(8,128)(2,1)S(1)} %collective-permute-done.1.refs_2_, ...), custom_call_target="tpu_custom_call" | custom-call | flops 10000000000 | bytes 30000000 | tf_op jit(solution)/shard_map/project/pallas_call | solution.py:591
  32.7 0.1 collective-permute-start.8
  32.8 1.4 %collective-permute-done.8.away_ref = bf16[160,512]{1,0:T(8,128)(2,1)S(1)} collective-permute-done((bf16[160,512]{1,0:T(8,128)(2,1)S(1)}, bf16[160,512]{1,0:T(8,128)(2,1)S(1)}, u32[]{:S(2)}, u32[]{:S(2)}) %collective-permute-start.8) | collective-permute-done | bytes 163872 | tf_op jit(solution)/shard_map/ppermute | solution.py:526
  34.2 2.1 %attend.1 = (bf16[112,128]{1,0:T(8,128)(2,1)S(1)}, bf16[224,256]{1,0:T(8,128)(2,1)S(1)}) custom-call(s32[24]{0:T(128)S(1)} %bitcast.6, s32[24]{0:T(128)S(1)} %copy-done.11, bf16[160,512]{1,0:T(8,128)(2,1)S(1)} %get-tuple-element.39.own_ref, bf16[160,512]{1,0:T(8,128)(2,1)S(1)} %collective-permute-done.8.away_ref), custom_call_target="tpu_custom_call" | custom-call | flops 1000000000 | bytes 3000000 | tf_op jit(solution)/shard_map/attend/pallas_call | solution.py:608
  36.3 0.2 share.1
  36.5 0.2 collective-permute-start.22
  36.7 0.1 pairs.1
  36.8 0.4 collective-permute-start.11
  37.2 0.5 collective-permute-start.9
  37.7 3.4 %collective-permute-done.9 = bf16[112,128]{1,0:T(8,128)(2,1)S(1)} collective-permute-done((bf16[112,128]{1,0:T(8,128)(2,1)S(1)}, bf16[112,128]{1,0:T(8,128)(2,1)S(1)}, u32[]{:S(2)}, u32[]{:S(2)}) %collective-permute-start.9) | collective-permute-done | bytes 28704 | tf_op jit(solution)/shard_map/ppermute | solution.py:523
  41.1 0.7 collective-permute-done.11.weight_other_ref
  41.8 0.5 collective-permute-done.10.other_ref
  42.3 0.4 out.1
  42.8 2.2 %collective-permute-start.12 = (bf16[224,256]{1,0:T(8,128)(2,1)S(1)}, bf16[224,256]{1,0:T(8,128)(2,1)S(1)}, u32[]{:S(2)}, u32[]{:S(2)}) collective-permute-start(bf16[224,256]{1,0:T(8,128)(2,1)S(1)} %get-tuple-element.46), channel_id=1, source_target_pairs={{0,12},{1,13},{2,14},{3,15},{4,8},{5,9},{6,10},{7,11},{8,4},{9,5},... | collective-permute-start | bytes 344072 | tf_op jit(solution)/shard_map/ppermute | solution.py:520
  45.0 0.4 collective-permute-start.13
  45.4 1.9 %collective-permute-start.14 = (bf16[224,256]{1,0:T(8,128)(2,1)S(1)}, bf16[224,256]{1,0:T(8,128)(2,1)S(1)}, u32[]{:S(2)}, u32[]{:S(2)}) collective-permute-start(bf16[224,256]{1,0:T(8,128)(2,1)S(1)} %get-tuple-element.48), channel_id=1, source_target_pairs={{0,4},{1,5},{2,6},{3,7},{4,0},{5,1},{6,2},{7,3},{8,12},{9,13},{10,... | collective-permute-start | bytes 344072 | tf_op jit(solution)/shard_map/ppermute | solution.py:520
  47.2 3.5 %collective-permute-done.12 = bf16[224,256]{1,0:T(8,128)(2,1)S(1)} collective-permute-done((bf16[224,256]{1,0:T(8,128)(2,1)S(1)}, bf16[224,256]{1,0:T(8,128)(2,1)S(1)}, u32[]{:S(2)}, u32[]{:S(2)}) %collective-permute-start.12) | collective-permute-done | bytes 114720 | tf_op jit(solution)/shard_map/ppermute | solution.py:520
  50.7 5.2 %collective-permute-done.13 = bf16[224,256]{1,0:T(8,128)(2,1)S(1)} collective-permute-done((bf16[224,256]{1,0:T(8,128)(2,1)S(1)}, bf16[224,256]{1,0:T(8,128)(2,1)S(1)}, u32[]{:S(2)}, u32[]{:S(2)}) %collective-permute-start.13) | collective-permute-done | bytes 114720 | tf_op jit(solution)/shard_map/ppermute | solution.py:520
  56.0 0.1 collective-permute-start.16
  56.1 2.5 %collective-permute-start.18 = (bf16[224,256]{1,0:T(8,128)(2,1)S(1)}, bf16[224,256]{1,0:T(8,128)(2,1)S(1)}, u32[]{:S(2)}, u32[]{:S(2)}) collective-permute-start(bf16[224,256]{1,0:T(8,128)(2,1)S(1)} %add_convert_fusion.refs_0_), channel_id=1, source_target_pairs={{0,8},{1,9},{2,10},{3,11},{4,12},{5,13},{6,14},{7,15},{8,0},{9,1},... | collective-permute-start | bytes 344072 | tf_op jit(solution)/shard_map/ppermute | solution.py:520
  58.6 1.8 %collective-permute-start.20 = (bf16[224,256]{1,0:T(8,128)(2,1)S(1)}, bf16[224,256]{1,0:T(8,128)(2,1)S(1)}, u32[]{:S(2)}, u32[]{:S(2)}) collective-permute-start(bf16[224,256]{1,0:T(8,128)(2,1)S(1)} %add_convert_fusion.refs_0_), channel_id=1, source_target_pairs={{0,12},{1,13},{2,14},{3,15},{4,8},{5,9},{6,10},{7,11},{8,4},{9,5},... | collective-permute-start | bytes 344072 | tf_op jit(solution)/shard_map/ppermute | solution.py:520
  60.4 0.5 collective-permute-start.15
  61.0 0.9 collective-permute-done.16.refs_2_
  61.9 0.6 collective-permute-start.17
  62.5 5.1 %collective-permute-done.18.refs_4_ = bf16[224,256]{1,0:T(8,128)(2,1)S(1)} collective-permute-done((bf16[224,256]{1,0:T(8,128)(2,1)S(1)}, bf16[224,256]{1,0:T(8,128)(2,1)S(1)}, u32[]{:S(2)}, u32[]{:S(2)}) %collective-permute-start.18) | collective-permute-done | bytes 114720 | tf_op jit(solution)/shard_map/ppermute | solution.py:520
  67.6 0.5 collective-permute-start.19
  68.1 1.5 %collective-permute-start.21 = (bf16[224,256]{1,0:T(8,128)(2,1)S(1)}, bf16[224,256]{1,0:T(8,128)(2,1)S(1)}, u32[]{:S(2)}, u32[]{:S(2)}) collective-permute-start(bf16[224,256]{1,0:T(8,128)(2,1)S(1)} %collective-permute-done.20.refs_6_), channel_id=1, source_target_pairs={{0,2},{1,3},{2,0},{3,1},{4,6},{5,7},{6,4},{7,5},{8,10},{9,11},{10,... | collective-permute-start | bytes 344072 | tf_op jit(solution)/shard_map/ppermute | solution.py:523
  69.6 2.8 %collective-permute-done.19.refs_5_ = bf16[224,256]{1,0:T(8,128)(2,1)S(1)} collective-permute-done((bf16[224,256]{1,0:T(8,128)(2,1)S(1)}, bf16[224,256]{1,0:T(8,128)(2,1)S(1)}, u32[]{:S(2)}, u32[]{:S(2)}) %collective-permute-start.19) | collective-permute-done | bytes 114720 | tf_op jit(solution)/shard_map/ppermute | solution.py:523
  72.4 1.2 %collective-permute-done.21.refs_7_ = bf16[224,256]{1,0:T(8,128)(2,1)S(1)} collective-permute-done((bf16[224,256]{1,0:T(8,128)(2,1)S(1)}, bf16[224,256]{1,0:T(8,128)(2,1)S(1)}, u32[]{:S(2)}, u32[]{:S(2)}) %collective-permute-start.21) | collective-permute-done | bytes 114720 | tf_op jit(solution)/shard_map/ppermute | solution.py:523
  73.6 1.9 %gate_up.1 = (f32[128,768]{1,0:T(8,128)S(1)}, f32[128,768]{1,0:T(8,128)S(1)}, bf16[16,2048]{1,0:T(8,128)(2,1)S(1)}, bf16[16,2048]{1,0:T(8,128)(2,1)S(1)}) custom-call(bf16[224,256]{1,0:T(8,128)(2,1)S(1)} %add_convert_fusion.refs_0_, bf16[224,256]{1,0:T(8,128)(2,1)S(1)} %collective-permute-done.15.refs_1_, ...), custom_call_target="tpu_custom_call" | custom-call | flops 1000000000 | bytes 3000000 | tf_op jit(solution)/shard_map/gate_up/pallas_call | solution.py:637
  75.5 0.1 collective-permute-start.23
  75.6 1.7 %collective-permute-done.23.came_ref = f32[128,768]{1,0:T(8,128)S(1)} collective-permute-done((f32[128,768]{1,0:T(8,128)S(1)}, f32[128,768]{1,0:T(8,128)S(1)}, u32[]{:S(2)}, u32[]{:S(2)}) %collective-permute-start.23) | collective-permute-done | bytes 393248 | tf_op jit(solution)/shard_map/ppermute | solution.py:526
  77.3 0.8 hidden.1
  78.1 0.8 collective-permute-start.29
  78.9 1.3 %collective-permute-start.27 = (bf16[8,7168]{1,0:T(8,128)(2,1)S(1)}, bf16[8,7168]{1,0:T(8,128)(2,1)S(1)}, u32[]{:S(2)}, u32[]{:S(2)}) collective-permute-start(bf16[8,7168]{1,0:T(8,128)(2,1)S(1)} %get-tuple-element.60), channel_id=1, source_target_pairs={{0,2},{1,3},{2,0},{3,1},{4,6},{5,7},{6,4},{7,5},{8,10},{9,11},{10,... | collective-permute-start | bytes 344072 | tf_op jit(solution)/shard_map/ppermute | solution.py:523
  80.2 0.8 collective-permute-start.25
  81.0 1.3 %collective-permute-start.24 = (bf16[8,7168]{1,0:T(8,128)(2,1)S(1)}, bf16[8,7168]{1,0:T(8,128)(2,1)S(1)}, u32[]{:S(2)}, u32[]{:S(2)}) collective-permute-start(bf16[8,7168]{1,0:T(8,128)(2,1)S(1)} %get-tuple-element.56), channel_id=1, source_target_pairs={{0,2},{1,3},{2,0},{3,1},{4,6},{5,7},{6,4},{7,5},{8,10},{9,11},{10,... | collective-permute-start | bytes 344072 | tf_op jit(solution)/shard_map/ppermute | solution.py:523
  82.2 0.6 down.1
  82.8 1.4 %collective-permute-done.29.far_ref = bf16[8,7168]{1,0:T(8,128)(2,1)S(1)} collective-permute-done((bf16[8,7168]{1,0:T(8,128)(2,1)S(1)}, bf16[8,7168]{1,0:T(8,128)(2,1)S(1)}, u32[]{:S(2)}, u32[]{:S(2)}) %collective-permute-start.29) | collective-permute-done | bytes 114720 | tf_op jit(solution)/shard_map/ppermute | solution.py:523
  84.2 2.1 %collective-permute-start.30 = (bf16[8,7168]{1,0:T(8,128)(2,1)S(1)}, bf16[8,7168]{1,0:T(8,128)(2,1)S(1)}, u32[]{:S(2)}, u32[]{:S(2)}) collective-permute-start(bf16[8,7168]{1,0:T(8,128)(2,1)S(1)} %add.25), channel_id=1, source_target_pairs={{0,12},{1,13},{2,14},{3,15},{4,8},{5,9},{6,10},{7,11},{8,4},{9,5},... | collective-permute-start | bytes 344072 | tf_op jit(solution)/shard_map/ppermute | solution.py:520
  86.2 0.4 collective-permute-done.27.far_ref
  86.7 1.2 %collective-permute-start.28 = (bf16[8,7168]{1,0:T(8,128)(2,1)S(1)}, bf16[8,7168]{1,0:T(8,128)(2,1)S(1)}, u32[]{:S(2)}, u32[]{:S(2)}) collective-permute-start(bf16[8,7168]{1,0:T(8,128)(2,1)S(1)} %add.24), channel_id=1, source_target_pairs={{0,8},{1,9},{2,10},{3,11},{4,12},{5,13},{6,14},{7,15},{8,0},{9,1},... | collective-permute-start | bytes 344072 | tf_op jit(solution)/shard_map/ppermute | solution.py:520
  87.8 1.2 %collective-permute-done.25.far_ref = bf16[8,7168]{1,0:T(8,128)(2,1)S(1)} collective-permute-done((bf16[8,7168]{1,0:T(8,128)(2,1)S(1)}, bf16[8,7168]{1,0:T(8,128)(2,1)S(1)}, u32[]{:S(2)}, u32[]{:S(2)}) %collective-permute-start.25) | collective-permute-done | bytes 114720 | tf_op jit(solution)/shard_map/ppermute | solution.py:523
  89.1 0.6 collective-permute-start.26
  89.7 1.3 %collective-permute-done.31.refs_6_ = bf16[16,2048]{1,0:T(8,128)(2,1)S(1)} collective-permute-done((bf16[16,2048]{1,0:T(8,128)(2,1)S(1)}, bf16[16,2048]{1,0:T(8,128)(2,1)S(1)}, u32[]{:S(2)}, u32[]{:S(2)}) %collective-permute-start.31) | collective-permute-done | bytes 65568 | tf_op jit(solution)/shard_map/ppermute | solution.py:526
  91.0 0.6 collective-permute-done.30.refs_4_
  91.6 4.2 %collective-permute-done.28.refs_3_ = bf16[8,7168]{1,0:T(8,128)(2,1)S(1)} collective-permute-done((bf16[8,7168]{1,0:T(8,128)(2,1)S(1)}, bf16[8,7168]{1,0:T(8,128)(2,1)S(1)}, u32[]{:S(2)}, u32[]{:S(2)}) %collective-permute-start.28) | collective-permute-done | bytes 114720 | tf_op jit(solution)/shard_map/ppermute | solution.py:520
  95.7 0.3 collective-permute-done.26.refs_2_
  96.0 0.8 last.1
  (42 shorter events, 0.3 us)
Async XLA Ops:
  0.0 2.8 %copy-start.4 = (bf16[64,4096]{1,0:T(8,128)(2,1)S(1)}, bf16[64,4096]{1,0:T(8,128)(2,1)}, u32[]{:S(2)}) copy-start(bf16[64,4096]{1,0:T(8,128)(2,1)} %refs_9_.2) | copy-start | bytes 1572868
  0.0 2.8 %copy-start.5 = (bf16[64,4096]{1,0:T(8,128)(2,1)S(1)}, bf16[64,4096]{1,0:T(8,128)(2,1)}, u32[]{:S(2)}) copy-start(bf16[64,4096]{1,0:T(8,128)(2,1)} %refs_10_.2) | copy-start | bytes 1572868
  0.0 2.8 %copy-start.6 = (bf16[64,4096]{1,0:T(8,128)(2,1)S(1)}, bf16[64,4096]{1,0:T(8,128)(2,1)}, u32[]{:S(2)}) copy-start(bf16[64,4096]{1,0:T(8,128)(2,1)} %refs_11_.1) | copy-start | bytes 1572868
  2.8 1.0 %copy-start.7 = (bf16[64,4096]{1,0:T(8,128)(2,1)S(1)}, bf16[64,4096]{1,0:T(8,128)(2,1)}, u32[]{:S(2)}) copy-start(bf16[64,4096]{1,0:T(8,128)(2,1)} %weight_ref.3) | copy-start | bytes 1572868
  2.8 1.1 %copy-start.8 = (bf16[8,10240]{1,0:T(8,128)(2,1)S(1)}, bf16[8,10240]{1,0:T(8,128)(2,1)}, u32[]{:S(2)}) copy-start(bf16[8,10240]{1,0:T(8,128)(2,1)} %fetch.1.piece_ref.refs_0_) | copy-start | bytes 491524
  2.9 27.8 %copy-start.9 = (f32[4096]{0:T(1024)S(1)}, f32[4096]{0:T(1024)}, u32[]{:S(2)}) copy-start(f32[4096]{0:T(1024)} %param.23) | copy-start | bytes 49156
  2.9 27.7 %collective-permute-start.7 = (bf16[192,4096]{1,0:T(8,128)(2,1)S(1)}, bf16[192,4096]{1,0:T(8,128)(2,1)S(1)}, u32[]{:S(2)}, u32[]{:S(2)}) collective-permute-start(bf16[192,4096]{1,0:T(8,128)(2,1)S(1)} %stack.1), channel_id=1, source_target_pairs={{0,1},{1,0},{2,3},{3,2},{4,5},{5,4},{6,7},{7,6},{8,9},{9,8},{10,11... | collective-permute-start | bytes 4718600 | tf_op jit(solution)/shard_map/ppermute | solution.py:526
  3.9 26.8 %collective-permute-start = (bf16[8,26624]{1,0:T(8,128)(2,1)S(1)}, bf16[8,26624]{1,0:T(8,128)(2,1)S(1)}, u32[]{:S(2)}, u32[]{:S(2)}) collective-permute-start(bf16[8,26624]{1,0:T(8,128)(2,1)S(1)} %across.1), channel_id=1, source_target_pairs={{0,2},{1,3},{2,0},{3,1},{4,6},{5,7},{6,4},{7,5},{8,10},{9,11},{10,... | collective-permute-start | bytes 1277960 | tf_op jit(solution)/shard_map/ppermute | solution.py:523
  6.9 7.9 %collective-permute-start.1 = (bf16[8,10240]{1,0:T(8,128)(2,1)S(1)}, bf16[8,10240]{1,0:T(8,128)(2,1)S(1)}, u32[]{:S(2)}, u32[]{:S(2)}) collective-permute-start(bf16[8,10240]{1,0:T(8,128)(2,1)S(1)} %copy-done.8), channel_id=1, source_target_pairs={{0,4},{1,5},{2,6},{3,7},{4,0},{5,1},{6,2},{7,3},{8,12},{9,13},{10,... | collective-permute-start | bytes 491528 | tf_op jit(solution)/shard_map/ppermute | solution.py:520
  8.5 15.1 %collective-permute-start.3 = (bf16[8,10240]{1,0:T(8,128)(2,1)S(1)}, bf16[8,10240]{1,0:T(8,128)(2,1)S(1)}, u32[]{:S(2)}, u32[]{:S(2)}) collective-permute-start(bf16[8,10240]{1,0:T(8,128)(2,1)S(1)} %copy-done.8), channel_id=1, source_target_pairs={{0,8},{1,9},{2,10},{3,11},{4,12},{5,13},{6,14},{7,15},{8,0},{9,1},... | collective-permute-start | bytes 491528 | tf_op jit(solution)/shard_map/ppermute | solution.py:520
  11.1 13.0 %collective-permute-start.5 = (bf16[8,10240]{1,0:T(8,128)(2,1)S(1)}, bf16[8,10240]{1,0:T(8,128)(2,1)S(1)}, u32[]{:S(2)}, u32[]{:S(2)}) collective-permute-start(bf16[8,10240]{1,0:T(8,128)(2,1)S(1)} %copy-done.8), channel_id=1, source_target_pairs={{0,12},{1,13},{2,14},{3,15},{4,8},{5,9},{6,10},{7,11},{8,4},{9,5},... | collective-permute-start | bytes 491528 | tf_op jit(solution)/shard_map/ppermute | solution.py:520
  14.8 10.8 %collective-permute-start.2 = (bf16[8,10240]{1,0:T(8,128)(2,1)S(1)}, bf16[8,10240]{1,0:T(8,128)(2,1)S(1)}, u32[]{:S(2)}, u32[]{:S(2)}) collective-permute-start(bf16[8,10240]{1,0:T(8,128)(2,1)S(1)} %collective-permute-done.1.refs_2_), channel_id=1, source_target_pairs={{0,2},{1,3},{2,0},{3,1},{4,6},{5,7},{6,4},{7,5},{8,10},{9,11},{10,... | collective-permute-start | bytes 491528 | tf_op jit(solution)/shard_map/ppermute | solution.py:523
  23.6 5.3 %collective-permute-start.4 = (bf16[8,10240]{1,0:T(8,128)(2,1)S(1)}, bf16[8,10240]{1,0:T(8,128)(2,1)S(1)}, u32[]{:S(2)}, u32[]{:S(2)}) collective-permute-start(bf16[8,10240]{1,0:T(8,128)(2,1)S(1)} %collective-permute-done.3.refs_4_), channel_id=1, source_target_pairs={{0,2},{1,3},{2,0},{3,1},{4,6},{5,7},{6,4},{7,5},{8,10},{9,11},{10,... | collective-permute-start | bytes 491528 | tf_op jit(solution)/shard_map/ppermute | solution.py:523
  24.1 6.6 %collective-permute-start.6 = (bf16[8,10240]{1,0:T(8,128)(2,1)S(1)}, bf16[8,10240]{1,0:T(8,128)(2,1)S(1)}, u32[]{:S(2)}, u32[]{:S(2)}) collective-permute-start(bf16[8,10240]{1,0:T(8,128)(2,1)S(1)} %collective-permute-done.5.refs_6_), channel_id=1, source_target_pairs={{0,2},{1,3},{2,0},{3,1},{4,6},{5,7},{6,4},{7,5},{8,10},{9,11},{10,... | collective-permute-start | bytes 491528 | tf_op jit(solution)/shard_map/ppermute | solution.py:523
  30.7 3.5 %copy-start.10 = (s32[24,1]{0,1:T(1,128)S(1)}, s32[24,1]{0,1:T(1,128)}, u32[]{:S(2)}) copy-start(s32[24,1]{0,1:T(1,128)} %param.16) | copy-start | bytes 292
  30.7 3.5 %copy-start.11 = (s32[24]{0:T(128)S(1)}, s32[24]{0:T(128)}, u32[]{:S(2)}) copy-start(s32[24]{0:T(128)} %segment_ref.1) | copy-start | bytes 292
  30.7 5.6 %copy-start.2 = (bf16[160,4096]{1,0:T(8,128)(2,1)S(1)}, bf16[160,4096]{1,0:T(8,128)(2,1)}, u32[]{:S(2)}) copy-start(bf16[160,4096]{1,0:T(8,128)(2,1)} %refs_10_.3) | copy-start | bytes 3932164
  32.7 1.5 %collective-permute-start.8 = (bf16[160,512]{1,0:T(8,128)(2,1)S(1)}, bf16[160,512]{1,0:T(8,128)(2,1)S(1)}, u32[]{:S(2)}, u32[]{:S(2)}) collective-permute-start(bf16[160,512]{1,0:T(8,128)(2,1)S(1)} %get-tuple-element.40), channel_id=1, source_target_pairs={{0,1},{1,0},{2,3},{3,2},{4,5},{5,4},{6,7},{7,6},{8,9},{9,8},{10,11... | collective-permute-start | bytes 491528 | tf_op jit(solution)/shard_map/ppermute | solution.py:526
  34.2 2.1 %copy-start = (bf16[160,4096]{1,0:T(8,128)(2,1)S(1)}, bf16[160,4096]{1,0:T(8,128)(2,1)}, u32[]{:S(2)}) copy-start(bf16[160,4096]{1,0:T(8,128)(2,1)} %down_ref.4) | copy-start | bytes 3932164
  34.2 2.1 %copy-start.1 = (bf16[160,4096]{1,0:T(8,128)(2,1)S(1)}, bf16[160,4096]{1,0:T(8,128)(2,1)}, u32[]{:S(2)}) copy-start(bf16[160,4096]{1,0:T(8,128)(2,1)} %refs_9_.3) | copy-start | bytes 3932164
  36.5 37.1 %collective-permute-start.22 = (bf16[320,4096]{1,0:T(8,128)(2,1)S(1)}, bf16[320,4096]{1,0:T(8,128)(2,1)S(1)}, u32[]{:S(2)}, u32[]{:S(2)}) collective-permute-start(bf16[320,4096]{1,0:T(8,128)(2,1)S(1)} %share.1), channel_id=1, source_target_pairs={{0,1},{1,0},{2,3},{3,2},{4,5},{5,4},{6,7},{7,6},{8,9},{9,8},{10,11... | collective-permute-start | bytes 7864328 | tf_op jit(solution)/shard_map/ppermute | solution.py:526
  36.8 5.1 %collective-permute-start.11 = (bf16[128,1024]{1,0:T(8,128)(2,1)S(1)}, bf16[128,1024]{1,0:T(8,128)(2,1)S(1)}, u32[]{:S(2)}, u32[]{:S(2)}) collective-permute-start(bf16[128,1024]{1,0:T(8,128)(2,1)S(1)} %get-tuple-element.44), channel_id=1, source_target_pairs={{0,1},{1,0},{2,3},{3,2},{4,5},{5,4},{6,7},{7,6},{8,9},{9,8},{10,11... | collective-permute-start | bytes 786440 | tf_op jit(solution)/shard_map/ppermute | solution.py:526
  37.2 3.9 %collective-permute-start.9 = (bf16[112,128]{1,0:T(8,128)(2,1)S(1)}, bf16[112,128]{1,0:T(8,128)(2,1)S(1)}, u32[]{:S(2)}, u32[]{:S(2)}) collective-permute-start(bf16[112,128]{1,0:T(8,128)(2,1)S(1)} %get-tuple-element.42), channel_id=1, source_target_pairs={{0,2},{1,3},{2,0},{3,1},{4,6},{5,7},{6,4},{7,5},{8,10},{9,11},{10,... | collective-permute-start | bytes 86024 | tf_op jit(solution)/shard_map/ppermute | solution.py:523
  41.1 1.2 %collective-permute-start.10 = (bf16[224,128]{1,0:T(8,128)(2,1)S(1)}, bf16[224,128]{1,0:T(8,128)(2,1)S(1)}, u32[]{:S(2)}, u32[]{:S(2)}) collective-permute-start(bf16[224,128]{1,0:T(8,128)(2,1)S(1)} %constant_dynamic-update-slice_fusion.own_ref), channel_id=1, source_target_pairs={{0,1},{1,0},{2,3},{3,2},{4,5},{5,4},{6,7},{7,6},{8,9},{9,8},{10,11... | collective-permute-start | bytes 172040 | tf_op jit(solution)/shard_map/ppermute | solution.py:526
  42.3 31.3 %copy-start.3 = (f32[4096]{0:T(1024)S(1)}, f32[4096]{0:T(1024)}, u32[]{:S(2)}) copy-start(f32[4096]{0:T(1024)} %param.24) | copy-start | bytes 49156
  42.8 8.0 %collective-permute-start.12 = (bf16[224,256]{1,0:T(8,128)(2,1)S(1)}, bf16[224,256]{1,0:T(8,128)(2,1)S(1)}, u32[]{:S(2)}, u32[]{:S(2)}) collective-permute-start(bf16[224,256]{1,0:T(8,128)(2,1)S(1)} %get-tuple-element.46), channel_id=1, source_target_pairs={{0,12},{1,13},{2,14},{3,15},{4,8},{5,9},{6,10},{7,11},{8,4},{9,5},... | collective-permute-start | bytes 344072 | tf_op jit(solution)/shard_map/ppermute | solution.py:520
  45.0 11.0 %collective-permute-start.13 = (bf16[224,256]{1,0:T(8,128)(2,1)S(1)}, bf16[224,256]{1,0:T(8,128)(2,1)S(1)}, u32[]{:S(2)}, u32[]{:S(2)}) collective-permute-start(bf16[224,256]{1,0:T(8,128)(2,1)S(1)} %get-tuple-element.47), channel_id=1, source_target_pairs={{0,8},{1,9},{2,10},{3,11},{4,12},{5,13},{6,14},{7,15},{8,0},{9,1},... | collective-permute-start | bytes 344072 | tf_op jit(solution)/shard_map/ppermute | solution.py:520
  45.4 10.6 %collective-permute-start.14 = (bf16[224,256]{1,0:T(8,128)(2,1)S(1)}, bf16[224,256]{1,0:T(8,128)(2,1)S(1)}, u32[]{:S(2)}, u32[]{:S(2)}) collective-permute-start(bf16[224,256]{1,0:T(8,128)(2,1)S(1)} %get-tuple-element.48), channel_id=1, source_target_pairs={{0,4},{1,5},{2,6},{3,7},{4,0},{5,1},{6,2},{7,3},{8,12},{9,13},{10,... | collective-permute-start | bytes 344072 | tf_op jit(solution)/shard_map/ppermute | solution.py:520
  56.0 5.9 %collective-permute-start.16 = (bf16[224,256]{1,0:T(8,128)(2,1)S(1)}, bf16[224,256]{1,0:T(8,128)(2,1)S(1)}, u32[]{:S(2)}, u32[]{:S(2)}) collective-permute-start(bf16[224,256]{1,0:T(8,128)(2,1)S(1)} %add_convert_fusion.refs_0_), channel_id=1, source_target_pairs={{0,4},{1,5},{2,6},{3,7},{4,0},{5,1},{6,2},{7,3},{8,12},{9,13},{10,... | collective-permute-start | bytes 344072 | tf_op jit(solution)/shard_map/ppermute | solution.py:520
  56.1 11.5 %collective-permute-start.18 = (bf16[224,256]{1,0:T(8,128)(2,1)S(1)}, bf16[224,256]{1,0:T(8,128)(2,1)S(1)}, u32[]{:S(2)}, u32[]{:S(2)}) collective-permute-start(bf16[224,256]{1,0:T(8,128)(2,1)S(1)} %add_convert_fusion.refs_0_), channel_id=1, source_target_pairs={{0,8},{1,9},{2,10},{3,11},{4,12},{5,13},{6,14},{7,15},{8,0},{9,1},... | collective-permute-start | bytes 344072 | tf_op jit(solution)/shard_map/ppermute | solution.py:520
  58.6 9.5 %collective-permute-start.20 = (bf16[224,256]{1,0:T(8,128)(2,1)S(1)}, bf16[224,256]{1,0:T(8,128)(2,1)S(1)}, u32[]{:S(2)}, u32[]{:S(2)}) collective-permute-start(bf16[224,256]{1,0:T(8,128)(2,1)S(1)} %add_convert_fusion.refs_0_), channel_id=1, source_target_pairs={{0,12},{1,13},{2,14},{3,15},{4,8},{5,9},{6,10},{7,11},{8,4},{9,5},... | collective-permute-start | bytes 344072 | tf_op jit(solution)/shard_map/ppermute | solution.py:520
  60.4 9.2 %collective-permute-start.15 = (bf16[224,256]{1,0:T(8,128)(2,1)S(1)}, bf16[224,256]{1,0:T(8,128)(2,1)S(1)}, u32[]{:S(2)}, u32[]{:S(2)}) collective-permute-start(bf16[224,256]{1,0:T(8,128)(2,1)S(1)} %add_convert_fusion.refs_0_), channel_id=1, source_target_pairs={{0,2},{1,3},{2,0},{3,1},{4,6},{5,7},{6,4},{7,5},{8,10},{9,11},{10,... | collective-permute-start | bytes 344072 | tf_op jit(solution)/shard_map/ppermute | solution.py:523
  61.9 7.7 %collective-permute-start.17 = (bf16[224,256]{1,0:T(8,128)(2,1)S(1)}, bf16[224,256]{1,0:T(8,128)(2,1)S(1)}, u32[]{:S(2)}, u32[]{:S(2)}) collective-permute-start(bf16[224,256]{1,0:T(8,128)(2,1)S(1)} %collective-permute-done.16.refs_2_), channel_id=1, source_target_pairs={{0,2},{1,3},{2,0},{3,1},{4,6},{5,7},{6,4},{7,5},{8,10},{9,11},{10,... | collective-permute-start | bytes 344072 | tf_op jit(solution)/shard_map/ppermute | solution.py:523
  67.6 4.8 %collective-permute-start.19 = (bf16[224,256]{1,0:T(8,128)(2,1)S(1)}, bf16[224,256]{1,0:T(8,128)(2,1)S(1)}, u32[]{:S(2)}, u32[]{:S(2)}) collective-permute-start(bf16[224,256]{1,0:T(8,128)(2,1)S(1)} %collective-permute-done.18.refs_4_), channel_id=1, source_target_pairs={{0,2},{1,3},{2,0},{3,1},{4,6},{5,7},{6,4},{7,5},{8,10},{9,11},{10,... | collective-permute-start | bytes 344072 | tf_op jit(solution)/shard_map/ppermute | solution.py:523
  68.1 5.5 %collective-permute-start.21 = (bf16[224,256]{1,0:T(8,128)(2,1)S(1)}, bf16[224,256]{1,0:T(8,128)(2,1)S(1)}, u32[]{:S(2)}, u32[]{:S(2)}) collective-permute-start(bf16[224,256]{1,0:T(8,128)(2,1)S(1)} %collective-permute-done.20.refs_6_), channel_id=1, source_target_pairs={{0,2},{1,3},{2,0},{3,1},{4,6},{5,7},{6,4},{7,5},{8,10},{9,11},{10,... | collective-permute-start | bytes 344072 | tf_op jit(solution)/shard_map/ppermute | solution.py:523
  75.5 1.8 %collective-permute-start.23 = (f32[128,768]{1,0:T(8,128)S(1)}, f32[128,768]{1,0:T(8,128)S(1)}, u32[]{:S(2)}, u32[]{:S(2)}) collective-permute-start(f32[128,768]{1,0:T(8,128)S(1)} %get-tuple-element.53), channel_id=1, source_target_pairs={{0,1},{1,0},{2,3},{3,2},{4,5},{5,4},{6,7},{7,6},{8,9},{9,8},{10,11... | collective-permute-start | bytes 1179656 | tf_op jit(solution)/shard_map/ppermute | solution.py:526
  78.1 6.1 %collective-permute-start.29 = (bf16[8,7168]{1,0:T(8,128)(2,1)S(1)}, bf16[8,7168]{1,0:T(8,128)(2,1)S(1)}, u32[]{:S(2)}, u32[]{:S(2)}) collective-permute-start(bf16[8,7168]{1,0:T(8,128)(2,1)S(1)} %get-tuple-element.62), channel_id=1, source_target_pairs={{0,2},{1,3},{2,0},{3,1},{4,6},{5,7},{6,4},{7,5},{8,10},{9,11},{10,... | collective-permute-start | bytes 344072 | tf_op jit(solution)/shard_map/ppermute | solution.py:523
  78.9 7.7 %collective-permute-start.27 = (bf16[8,7168]{1,0:T(8,128)(2,1)S(1)}, bf16[8,7168]{1,0:T(8,128)(2,1)S(1)}, u32[]{:S(2)}, u32[]{:S(2)}) collective-permute-start(bf16[8,7168]{1,0:T(8,128)(2,1)S(1)} %get-tuple-element.60), channel_id=1, source_target_pairs={{0,2},{1,3},{2,0},{3,1},{4,6},{5,7},{6,4},{7,5},{8,10},{9,11},{10,... | collective-permute-start | bytes 344072 | tf_op jit(solution)/shard_map/ppermute | solution.py:523
  80.2 8.9 %collective-permute-start.25 = (bf16[8,7168]{1,0:T(8,128)(2,1)S(1)}, bf16[8,7168]{1,0:T(8,128)(2,1)S(1)}, u32[]{:S(2)}, u32[]{:S(2)}) collective-permute-start(bf16[8,7168]{1,0:T(8,128)(2,1)S(1)} %get-tuple-element.58), channel_id=1, source_target_pairs={{0,2},{1,3},{2,0},{3,1},{4,6},{5,7},{6,4},{7,5},{8,10},{9,11},{10,... | collective-permute-start | bytes 344072 | tf_op jit(solution)/shard_map/ppermute | solution.py:523
  81.0 10.0 %collective-permute-start.24 = (bf16[8,7168]{1,0:T(8,128)(2,1)S(1)}, bf16[8,7168]{1,0:T(8,128)(2,1)S(1)}, u32[]{:S(2)}, u32[]{:S(2)}) collective-permute-start(bf16[8,7168]{1,0:T(8,128)(2,1)S(1)} %get-tuple-element.56), channel_id=1, source_target_pairs={{0,2},{1,3},{2,0},{3,1},{4,6},{5,7},{6,4},{7,5},{8,10},{9,11},{10,... | collective-permute-start | bytes 344072 | tf_op jit(solution)/shard_map/ppermute | solution.py:523
  84.2 7.4 %collective-permute-start.30 = (bf16[8,7168]{1,0:T(8,128)(2,1)S(1)}, bf16[8,7168]{1,0:T(8,128)(2,1)S(1)}, u32[]{:S(2)}, u32[]{:S(2)}) collective-permute-start(bf16[8,7168]{1,0:T(8,128)(2,1)S(1)} %add.25), channel_id=1, source_target_pairs={{0,12},{1,13},{2,14},{3,15},{4,8},{5,9},{6,10},{7,11},{8,4},{9,5},... | collective-permute-start | bytes 344072 | tf_op jit(solution)/shard_map/ppermute | solution.py:520
  86.7 9.1 %collective-permute-start.28 = (bf16[8,7168]{1,0:T(8,128)(2,1)S(1)}, bf16[8,7168]{1,0:T(8,128)(2,1)S(1)}, u32[]{:S(2)}, u32[]{:S(2)}) collective-permute-start(bf16[8,7168]{1,0:T(8,128)(2,1)S(1)} %add.24), channel_id=1, source_target_pairs={{0,8},{1,9},{2,10},{3,11},{4,12},{5,13},{6,14},{7,15},{8,0},{9,1},... | collective-permute-start | bytes 344072 | tf_op jit(solution)/shard_map/ppermute | solution.py:520
  89.1 6.9 %collective-permute-start.26 = (bf16[8,7168]{1,0:T(8,128)(2,1)S(1)}, bf16[8,7168]{1,0:T(8,128)(2,1)S(1)}, u32[]{:S(2)}, u32[]{:S(2)}) collective-permute-start(bf16[8,7168]{1,0:T(8,128)(2,1)S(1)} %add.23), channel_id=1, source_target_pairs={{0,4},{1,5},{2,6},{3,7},{4,0},{5,1},{6,2},{7,3},{8,12},{9,13},{10,... | collective-permute-start | bytes 344072 | tf_op jit(solution)/shard_map/ppermute | solution.py:520
  89.7 1.3 %collective-permute-start.31 = (bf16[16,2048]{1,0:T(8,128)(2,1)S(1)}, bf16[16,2048]{1,0:T(8,128)(2,1)S(1)}, u32[]{:S(2)}, u32[]{:S(2)}) collective-permute-start(bf16[16,2048]{1,0:T(8,128)(2,1)S(1)} %get-tuple-element.64), channel_id=1, source_target_pairs={{0,1},{1,0},{2,3},{3,2},{4,5},{5,4},{6,7},{7,6},{8,9},{9,8},{10,11... | collective-permute-start | bytes 196616 | tf_op jit(solution)/shard_map/ppermute | solution.py:526

commit v6 on v5

--- a/solution.py
+++ b/solution.py
@@ -175,12 +175,13 @@
     out_ref[units:, :] = down_ref[...]
 
 
-def out_kernel(own_ref, other_ref, weight_ref, weight_other_ref, mine_ref, *send_refs):
+def out_kernel(*refs):
+    near_ref, far_ref, other_ref, other_far_ref, weight_ref, weight_other_ref, mine_ref = refs[:7]
+    send_refs = refs[7:]
     width = mine_ref.shape[1]
-    half = own_ref.shape[0] // 2
-
-    def heads(ref):
-        near, far = ref[:half, :], ref[half:, :]
+
+    def heads(near_ref, far_ref):
+        near, far = near_ref[...], far_ref[...]
         return jnp.concatenate(
             [
                 jnp.concatenate([near[:, :HDIM], far[:, :HDIM]], axis=1),
@@ -189,7 +190,9 @@
             axis=0,
         )
 
-    attended = dot(heads(own_ref), weight_ref[...]) + dot(heads(other_ref), weight_other_ref[...])
+    attended = dot(heads(near_ref, far_ref), weight_ref[...]) + dot(
+        heads(other_ref, other_far_ref), weight_other_ref[...]
+    )
     mine_ref[...] = attended[:, :width]
     for d, ref in enumerate(send_refs, 1):
         ref[...] = attended[:, d * width : (d + 1) * width].astype(jnp.bfloat16)
@@ -272,7 +275,7 @@
         target[:, 0 : value.shape[1]] = value.astype(jnp.bfloat16)
 
 
-def attention_kernel(query_rows, width, owner_ref, segment_ref, own_ref, away_ref, ctx_ref, col_ref):
+def plan_kernel(query_rows, owner_ref, segment_ref, own_ref, away_ref, mask_ref):
     _, zi, yi, ci = place()
     nz = lax.axis_size(AXIS) // 4
     query_total = query_rows * 4 * nz
@@ -280,7 +283,7 @@
     tokens = query_total + blocks_total * BLK
     piece_rows = query_rows + CAP * BLK
     full, halved = piece_layout(piece_rows)
-    plane_rows = own_ref.shape[0]
+    plane_rows = own_ref.shape[1]
 
     def lay(shape, axis):
         token = lax.broadcasted_iota(jnp.int32, shape, axis)
@@ -322,15 +325,20 @@
         )
     spot = spot + ((owner % 2) ^ ci) * plane_rows
     lanes = lax.broadcasted_iota(jnp.int32, (tokens, plane_rows), 1)
-    pick_own = (lanes == spot).astype(jnp.bfloat16)
-    pick_away = (lanes == spot - plane_rows).astype(jnp.bfloat16)
-    packed = dot(pick_own, own_ref[...]) + dot(pick_away, away_ref[...])
+    own_ref[...] = (lanes == spot).astype(jnp.bfloat16)
+    away_ref[...] = (lanes == spot - plane_rows).astype(jnp.bfloat16)
+    mask_ref[...] = (pair == pair_row).astype(jnp.float32)
+
+
+def attention_kernel(width, pick_ref, pick_away_ref, mask_ref, own_ref, away_ref, ctx_ref, col_ref):
+    tokens = pick_ref.shape[0]
+    packed = dot(pick_ref[...], own_ref[...]) + dot(pick_away_ref[...], away_ref[...])
     col_ref[...] = packed[:, 256 : 256 + width].astype(jnp.bfloat16)
     query, key, value = (
         packed[:, i * HDIM : (i + 1) * HDIM].astype(jnp.bfloat16) for i in range(3)
     )
     scores = by_rows(query, key) * HDIM ** (-0.5)
-    scores = jnp.where(pair == pair_row, scores, -1e30)
+    scores = jnp.where(mask_ref[...] > 0.5, scores, -1e30)
     weights = jnp.exp(scores - jnp.max(scores, axis=-1, keepdims=True))
     probability = (weights / jnp.sum(weights, axis=-1, keepdims=True)).astype(jnp.bfloat16)
     context = dot(probability, value)
@@ -339,18 +347,16 @@
     ).astype(jnp.bfloat16)
 
 
-def gate_kernel(rows_here, chunk_rows, *refs):
-    count = len(refs) - 10
+def gate_kernel(rows_here, chunk_rows, own, *refs):
+    count = len(refs) - 8
     pieces = refs[:count]
     (
         gain_ref,
         gate_ref,
         up_ref,
         share_ref,
-        keep_ref,
-        send_ref,
+        out_ref,
         kept_ref,
-        kept_send_ref,
         order_ref,
         rows_ref,
     ) = refs[count:]
@@ -359,10 +365,9 @@
     tokens, width = pieces[0].shape
     half = 2 * nz * width
     total = order_ref.shape[0]
-    slots = total // 2
     row = lax.broadcasted_iota(jnp.int32, (total, 1), 0)
-    core = jnp.where(row < slots, ci, 1 - ci)
-    chunk = (row % slots) // chunk_rows
+    core = ci if own else 1 - ci
+    chunk = row // chunk_rows
     device = (zi ^ (chunk // 2)) * 4 + ((chunk % 2) ^ yi) * 2 + core
     wanted = device * rows_here + jnp.minimum(row % chunk_rows, rows_here - 1)
     lanes = lax.broadcasted_iota(jnp.int32, (total, tokens), 1)
@@ -379,9 +384,6 @@
         values = dot(order_ref[...], pair)
         squares = squares + jnp.sum(values * values, axis=-1, keepdims=True)
         kept_ref[:, pl.ds(start, 2 * width)] = values[0:chunk_rows].astype(jnp.bfloat16)
-        kept_send_ref[:, pl.ds(start, 2 * width)] = values[slots : slots + chunk_rows].astype(
-            jnp.bfloat16
-        )
         gain = gain_ref[:, pl.ds(pl.multiple_of(ci * half + start, 128), 2 * width)]
         rows_ref[:, pl.ds(start, 2 * width)] = (values * gain).astype(jnp.bfloat16)
     mine = pl.ds(pl.multiple_of(ci * half, 128), half)
@@ -391,14 +393,9 @@
     up = by_rows(rows, up_ref[:, mine])
     gate_other = by_rows(rows, share_ref[:units, :half])
     up_other = by_rows(rows, share_ref[:units, half:])
-    wide = keep_ref.shape[1] - 4 * units
-    spread = jnp.broadcast_to(squares, (total, wide))
-    keep_ref[...] = jnp.concatenate(
-        [gate[:slots], gate_other[:slots], up[:slots], up_other[:slots], spread[:slots]], axis=1
-    )
-    send_ref[...] = jnp.concatenate(
-        [gate_other[slots:], gate[slots:], up_other[slots:], up[slots:], spread[slots:]], axis=1
-    )
+    spread = jnp.broadcast_to(squares, (total, out_ref.shape[1] - 4 * units))
+    parts = (gate, gate_other, up, up_other) if own else (gate_other, gate, up_other, up)
+    out_ref[...] = jnp.concatenate([*parts, spread], axis=1)
 
 
 def packed(rows):
@@ -604,15 +601,42 @@
         name="pairs",
     )(out_weight, far[0])
     out_came = across_core(out_send)
-
+    own, out_came = lax.optimization_barrier((own, out_came))
+
+    plan = kernel_call(
+        functools.partial(plan_kernel, query_rows),
+        (
+            shape((tokens, plane_rows), bf16),
+            shape((tokens, plane_rows), bf16),
+            shape((tokens, tokens), f32),
+        ),
+        [SMEM, SMEM],
+        name="plan",
+    )(owners, segment)
     context, columns = kernel_call(
-        functools.partial(attention_kernel, query_rows, width),
+        functools.partial(attention_kernel, width),
         (shape((tokens // 2, 2 * HDIM), bf16), shape((tokens, width), bf16)),
-        [SMEM, SMEM, VMEM, VMEM],
+        [VMEM] * 5,
         name="attend",
-    )(owners, segment, own, across_core(away))
+    )(*plan, own, across_core(away))
+    contexts = [
+        context,
+        across_y(context),
+        across_core(context),
+        lax.ppermute(context, AXIS, [(i, i ^ 3) for i in range(devices)]),
+    ]
+    attended, *parts = kernel_call(
+        out_kernel,
+        (shape((tokens, width), f32),) + (shape((tokens, width), bf16),) * (nz - 1),
+        [VMEM] * 6,
+        name="out",
+    )(*contexts, out_keep, out_came)
+    middle = columns.astype(f32) + attended
+    for d in z_order:
+        middle = middle + along_z(parts[d - 1], d).astype(f32)
+    middle = middle.astype(bf16)
     share_gate, share_up, share_down, _ = lax.optimization_barrier(
-        (gate_weight, up_weight, down_weight, context)
+        (gate_weight, up_weight, down_weight, middle)
     )
     share = across_core(
         kernel_call(
@@ -620,32 +644,23 @@
         )(share_gate, share_up, share_down)
     )
 
-    contexts = jnp.concatenate([context, across_y(context)], axis=0)
-    attended, *parts = kernel_call(
-        out_kernel,
-        (shape((tokens, width), f32),) + (shape((tokens, width), bf16),) * (nz - 1),
-        [VMEM] * 4,
-        name="out",
-    )(contexts, across_core(contexts), out_keep, out_came)
-    middle = columns.astype(f32) + attended
-    for d in z_order:
-        middle = middle + along_z(parts[d - 1], d).astype(f32)
-    middle = middle.astype(bf16)
 
     slots = 2 * nz * chunk_rows
     lanes = -(-(4 * units + 1) // 128) * 128
-    keep, send, kept, kept_send = kernel_call(
-        functools.partial(gate_kernel, rows_here, chunk_rows),
-        (
-            shape((slots, lanes), f32),
-            shape((slots, lanes), f32),
-            shape((chunk_rows, half), bf16),
-            shape((chunk_rows, half), bf16),
-        ),
-        [VMEM] * (2 * nz + 4),
-        [pltpu.VMEM((2 * slots, tokens), bf16), pltpu.VMEM((2 * slots, half), bf16)],
-        name="gate_up",
-    )(*paired(*plane_gather(middle)), gain_ffn[None, :], gate_weight, up_weight, share)
+    blocks = paired(*plane_gather(middle))
+
+    def gate_up(own, blocks):
+        return kernel_call(
+            functools.partial(gate_kernel, rows_here, chunk_rows, own),
+            (shape((slots, lanes), f32), shape((chunk_rows, half), bf16)),
+            [VMEM] * (2 * nz + 4),
+            [pltpu.VMEM((slots, tokens), bf16), pltpu.VMEM((slots, half), bf16)],
+            name="gate_up_own" if own else "gate_up",
+        )(*blocks, gain_ffn[None, :], gate_weight, up_weight, share)
+
+    send, kept_send = gate_up(False, blocks)
+    first, _ = lax.optimization_barrier((blocks[0], send))
+    keep, kept = gate_up(True, [first, *blocks[1:]])
     came = across_core(send)
     kept_other = across_core(kept_send)
 

time: 97 us -> 94.6 us (0.975)
  waiting for transfers between devices: 52.7 us -> 45.8 us
  starting transfers between devices: 31.5 us -> 35 us
    ppermute x7, waiting for transfers between devices: 5.58 us -> 1.6 us  [across_core(): return lax.ppermute(value, AXIS, [(i, i ^ 1) for i in range(devices)])]
    ppermute x13, starting transfers between devices: 13.1 us -> 15.1 us  [across_y(): return lax.ppermute(value, AXIS, [(i, i ^ 2) for i in range(devices)])]
    ppermute x12, waiting for transfers between devices: 31.7 us -> 29.9 us  [along_z(): return lax.ppermute(value, AXIS, [(i, i ^ 4 * k) for i in range(devices)])]
    ppermute x0 -> x1, starting transfers between devices: none -> 1.48 us  [body(): lax.ppermute(context, AXIS, [(i, i ^ 3) for i in range(devices)])]
    ppermute x13, waiting for transfers between devices: 15.4 us -> 14.2 us  [across_y(): return lax.ppermute(value, AXIS, [(i, i ^ 2) for i in range(devices)])]
    pallas_call x2 -> x4, Pallas kernels: 3.97 us -> 4.93 us  [the longest x2 2.7 us: gate_up(): kernel_call(functools.partial(gate_kernel, rows_here, chunk_rows, own), (...]
  transfers between devices with their start and end apart: 32 -> 33, of which waited for: 22 -> 20; matrix products, arithmetic and copies ran while one was open for 0% -> 0% of each run, Pallas kernels for 1% -> 6%
where the time goes in v6:
time: 94.6 us; the launch traced here: 94.4 us
  waiting for transfers between devices  45.8 us (48%)
  starting transfers between devices  35 us (37%)
  Pallas kernels  12.7 us (13%)
    ppermute x12, waiting for transfers between devices, along_z(): return lax.ppermute(value, AXIS, [(i, i ^ 4 * k) for i in range(devices)])  29.9 us
    ppermute x12, starting transfers between devices, along_z(): return lax.ppermute(value, AXIS, [(i, i ^ 4 * k) for i in range(devices)])  17.4 us
    ppermute x13, starting transfers between devices, across_y(): return lax.ppermute(value, AXIS, [(i, i ^ 2) for i in range(devices)])  15.1 us
    ppermute x13, waiting for transfers between devices, across_y(): return lax.ppermute(value, AXIS, [(i, i ^ 2) for i in range(devices)])  14.2 us
    pallas_call x1, Pallas kernels, body(): kernel_call(fetch_kernel, shape((8, full * features + halved * half), bf1...  2.75 us
    pallas_call x2, Pallas kernels, gate_up(): kernel_call(functools.partial(gate_kernel, rows_here, chunk_rows, own), (...  2.7 us
    pallas_call x1, Pallas kernels, body(): kernel_call(functools.partial(projection_kernel, query_rows + CAP * BLK),...  1.98 us
  transfers between devices with their start and end apart: 33, of which 20 were waited for; matrix products, arithmetic and copies ran while one was open for 0% of the time, Pallas kernels for 6%

profile of v6, /device:TPU:0, one launch (start us, length us, event | category | flops | bytes accessed | tf_op | source)
XLA Modules:
  0.0 94.4 jit_solution(17563883051452135522)
XLA Ops:
  0.0 2.7 %fetch.1.piece_ref.refs_0_ = bf16[8,10240]{1,0:T(8,128)(2,1)} custom-call(s32[24]{0:T(128)} %bitcast.6, s32[24]{0:T(128)} %row_ref.1, bf16[64,4,4096]{2,1,0:T(4,128)(2,1)} %corpus_ref.1, bf16[8,4096]{1,0:T(8,128)(2,1)} %query_ref.1), custom_call_target="tpu_custom_call" | custom-call | flops 1000000000 | bytes 3000000 | tf_op jit(solution)/shard_map/fetch/pallas_call | solution.py:555
  2.8 0.1 stack.1
  2.9 0.5 collective-permute-start.7
  3.4 0.4 copy-done.4
  3.9 3.0 %collective-permute-start = (bf16[8,26624]{1,0:T(8,128)(2,1)S(1)}, bf16[8,26624]{1,0:T(8,128)(2,1)S(1)}, u32[]{:S(2)}, u32[]{:S(2)}) collective-permute-start(bf16[8,26624]{1,0:T(8,128)(2,1)S(1)} %across.1), channel_id=1, source_target_pairs={{0,2},{1,3},{2,0},{3,1},{4,6},{5,7},{6,4},{7,5},{8,10},{9,11},{10,... | collective-permute-start | bytes 1277960 | tf_op jit(solution)/shard_map/ppermute | solution.py:520
  6.9 1.6 %collective-permute-start.1 = (bf16[8,10240]{1,0:T(8,128)(2,1)S(1)}, bf16[8,10240]{1,0:T(8,128)(2,1)S(1)}, u32[]{:S(2)}, u32[]{:S(2)}) collective-permute-start(bf16[8,10240]{1,0:T(8,128)(2,1)S(1)} %copy-done.8), channel_id=1, source_target_pairs={{0,4},{1,5},{2,6},{3,7},{4,0},{5,1},{6,2},{7,3},{8,12},{9,13},{10,... | collective-permute-start | bytes 491528 | tf_op jit(solution)/shard_map/ppermute | solution.py:517
  8.6 2.5 %collective-permute-start.3 = (bf16[8,10240]{1,0:T(8,128)(2,1)S(1)}, bf16[8,10240]{1,0:T(8,128)(2,1)S(1)}, u32[]{:S(2)}, u32[]{:S(2)}) collective-permute-start(bf16[8,10240]{1,0:T(8,128)(2,1)S(1)} %copy-done.8), channel_id=1, source_target_pairs={{0,8},{1,9},{2,10},{3,11},{4,12},{5,13},{6,14},{7,15},{8,0},{9,1},... | collective-permute-start | bytes 491528 | tf_op jit(solution)/shard_map/ppermute | solution.py:517
  11.1 0.2 collective-permute-start.5
  11.3 3.4 %collective-permute-done.1.refs_2_ = bf16[8,10240]{1,0:T(8,128)(2,1)S(1)} collective-permute-done((bf16[8,10240]{1,0:T(8,128)(2,1)S(1)}, bf16[8,10240]{1,0:T(8,128)(2,1)S(1)}, u32[]{:S(2)}, u32[]{:S(2)}) %collective-permute-start.1) | collective-permute-done | bytes 163872 | tf_op jit(solution)/shard_map/ppermute | solution.py:517
  14.8 0.4 collective-permute-start.2
  15.2 8.4 %collective-permute-done.3.refs_4_ = bf16[8,10240]{1,0:T(8,128)(2,1)S(1)} collective-permute-done((bf16[8,10240]{1,0:T(8,128)(2,1)S(1)}, bf16[8,10240]{1,0:T(8,128)(2,1)S(1)}, u32[]{:S(2)}, u32[]{:S(2)}) %collective-permute-start.3) | collective-permute-done | bytes 163872 | tf_op jit(solution)/shard_map/ppermute | solution.py:517
  23.6 0.5 collective-permute-start.4
  24.1 1.6 %collective-permute-start.6 = (bf16[8,10240]{1,0:T(8,128)(2,1)S(1)}, bf16[8,10240]{1,0:T(8,128)(2,1)S(1)}, u32[]{:S(2)}, u32[]{:S(2)}) collective-permute-start(bf16[8,10240]{1,0:T(8,128)(2,1)S(1)} %collective-permute-done.5.refs_6_), channel_id=1, source_target_pairs={{0,2},{1,3},{2,0},{3,1},{4,6},{5,7},{6,4},{7,5},{8,10},{9,11},{10,... | collective-permute-start | bytes 491528 | tf_op jit(solution)/shard_map/ppermute | solution.py:520
  25.6 0.1 pairs.1
  25.7 0.1 collective-permute-start.8
  25.8 3.1 %collective-permute-done.4.refs_5_ = bf16[8,10240]{1,0:T(8,128)(2,1)S(1)} collective-permute-done((bf16[8,10240]{1,0:T(8,128)(2,1)S(1)}, bf16[8,10240]{1,0:T(8,128)(2,1)S(1)}, u32[]{:S(2)}, u32[]{:S(2)}) %collective-permute-start.4) | collective-permute-done | bytes 163872 | tf_op jit(solution)/shard_map/ppermute | solution.py:520
  28.9 1.8 %collective-permute-done.6.refs_7_ = bf16[8,10240]{1,0:T(8,128)(2,1)S(1)} collective-permute-done((bf16[8,10240]{1,0:T(8,128)(2,1)S(1)}, bf16[8,10240]{1,0:T(8,128)(2,1)S(1)}, u32[]{:S(2)}, u32[]{:S(2)}) %collective-permute-start.6) | collective-permute-done | bytes 163872 | tf_op jit(solution)/shard_map/ppermute | solution.py:520
  30.7 2.0 %project.1 = (bf16[160,512]{1,0:T(8,128)(2,1)S(1)}, bf16[160,512]{1,0:T(8,128)(2,1)S(1)}) custom-call(bf16[8,10240]{1,0:T(8,128)(2,1)S(1)} %copy-done.8, bf16[8,26624]{1,0:T(8,128)(2,1)S(1)} %collective-permute-done.refs_1_.far_ref, bf16[8,10240]{1,0:T(8,128)(2,1)S(1)} %collective-permute-done.1.refs_2_, ...), custom_call_target="tpu_custom_call" | custom-call | flops 10000000000 | bytes 30000000 | tf_op jit(solution)/shard_map/project/pallas_call | solution.py:588
  32.7 0.1 collective-permute-start.9
  32.8 1.3 %plan.1 = (bf16[224,160]{1,0:T(8,128)(2,1)S(1)}, bf16[224,160]{1,0:T(8,128)(2,1)S(1)}, f32[224,224]{1,0:T(8,128)S(1)}) custom-call(s32[24]{0:T(128)S(1)} %bitcast.7, s32[24]{0:T(128)S(1)} %copy-done.11), custom_call_target="tpu_custom_call" | custom-call | flops 1000000000 | bytes 3000000 | tf_op jit(solution)/shard_map/plan/pallas_call | solution.py:606
  34.2 0.9 attend.1
  35.1 0.5 collective-permute-start.10
  35.6 0.2 collective-permute-start.11
  35.8 1.5 %collective-permute-start.12 = (bf16[112,128]{1,0:T(8,128)(2,1)S(1)}, bf16[112,128]{1,0:T(8,128)(2,1)S(1)}, u32[]{:S(2)}, u32[]{:S(2)}) collective-permute-start(bf16[112,128]{1,0:T(8,128)(2,1)S(1)} %get-tuple-element.53.refs_0_), channel_id=1, source_target_pairs={{0,3},{1,2},{2,1},{3,0},{4,7},{5,6},{6,5},{7,4},{8,11},{9,10},{10,... | collective-permute-start | bytes 86024 | tf_op jit(solution)/shard_map/ppermute | solution.py:626
  37.2 1.9 %collective-permute-done.10.refs_1_ = bf16[112,128]{1,0:T(8,128)(2,1)S(1)} collective-permute-done((bf16[112,128]{1,0:T(8,128)(2,1)S(1)}, bf16[112,128]{1,0:T(8,128)(2,1)S(1)}, u32[]{:S(2)}, u32[]{:S(2)}) %collective-permute-start.10) | collective-permute-done | bytes 28704 | tf_op jit(solution)/shard_map/ppermute | solution.py:520
  39.2 0.1 collective-permute-done.12.refs_3_
  39.3 0.4 out.1
  39.8 2.2 %collective-permute-start.13 = (bf16[224,256]{1,0:T(8,128)(2,1)S(1)}, bf16[224,256]{1,0:T(8,128)(2,1)S(1)}, u32[]{:S(2)}, u32[]{:S(2)}) collective-permute-start(bf16[224,256]{1,0:T(8,128)(2,1)S(1)} %get-tuple-element.57), channel_id=1, source_target_pairs={{0,12},{1,13},{2,14},{3,15},{4,8},{5,9},{6,10},{7,11},{8,4},{9,5},... | collective-permute-start | bytes 344072 | tf_op jit(solution)/shard_map/ppermute | solution.py:517
  42.0 0.4 collective-permute-start.14
  42.4 1.9 %collective-permute-start.15 = (bf16[224,256]{1,0:T(8,128)(2,1)S(1)}, bf16[224,256]{1,0:T(8,128)(2,1)S(1)}, u32[]{:S(2)}, u32[]{:S(2)}) collective-permute-start(bf16[224,256]{1,0:T(8,128)(2,1)S(1)} %get-tuple-element.59), channel_id=1, source_target_pairs={{0,4},{1,5},{2,6},{3,7},{4,0},{5,1},{6,2},{7,3},{8,12},{9,13},{10,... | collective-permute-start | bytes 344072 | tf_op jit(solution)/shard_map/ppermute | solution.py:517
  44.2 3.5 %collective-permute-done.13 = bf16[224,256]{1,0:T(8,128)(2,1)S(1)} collective-permute-done((bf16[224,256]{1,0:T(8,128)(2,1)S(1)}, bf16[224,256]{1,0:T(8,128)(2,1)S(1)}, u32[]{:S(2)}, u32[]{:S(2)}) %collective-permute-start.13) | collective-permute-done | bytes 114720 | tf_op jit(solution)/shard_map/ppermute | solution.py:517
  47.7 5.2 %collective-permute-done.14 = bf16[224,256]{1,0:T(8,128)(2,1)S(1)} collective-permute-done((bf16[224,256]{1,0:T(8,128)(2,1)S(1)}, bf16[224,256]{1,0:T(8,128)(2,1)S(1)}, u32[]{:S(2)}, u32[]{:S(2)}) %collective-permute-start.14) | collective-permute-done | bytes 114720 | tf_op jit(solution)/shard_map/ppermute | solution.py:517
  53.0 0.2 share.1
  53.2 0.1 collective-permute-start.17
  53.3 2.5 %collective-permute-start.19 = (bf16[224,256]{1,0:T(8,128)(2,1)S(1)}, bf16[224,256]{1,0:T(8,128)(2,1)S(1)}, u32[]{:S(2)}, u32[]{:S(2)}) collective-permute-start(bf16[224,256]{1,0:T(8,128)(2,1)S(1)} %add_convert_fusion.refs_0_), channel_id=1, source_target_pairs={{0,8},{1,9},{2,10},{3,11},{4,12},{5,13},{6,14},{7,15},{8,0},{9,1},... | collective-permute-start | bytes 344072 | tf_op jit(solution)/shard_map/ppermute | solution.py:517
  55.8 1.9 %collective-permute-start.21 = (bf16[224,256]{1,0:T(8,128)(2,1)S(1)}, bf16[224,256]{1,0:T(8,128)(2,1)S(1)}, u32[]{:S(2)}, u32[]{:S(2)}) collective-permute-start(bf16[224,256]{1,0:T(8,128)(2,1)S(1)} %add_convert_fusion.refs_0_), channel_id=1, source_target_pairs={{0,12},{1,13},{2,14},{3,15},{4,8},{5,9},{6,10},{7,11},{8,4},{9,5},... | collective-permute-start | bytes 344072 | tf_op jit(solution)/shard_map/ppermute | solution.py:517
  57.7 1.5 %collective-permute-start.16 = (bf16[224,256]{1,0:T(8,128)(2,1)S(1)}, bf16[224,256]{1,0:T(8,128)(2,1)S(1)}, u32[]{:S(2)}, u32[]{:S(2)}) collective-permute-start(bf16[224,256]{1,0:T(8,128)(2,1)S(1)} %add_convert_fusion.refs_0_), channel_id=1, source_target_pairs={{0,2},{1,3},{2,0},{3,1},{4,6},{5,7},{6,4},{7,5},{8,10},{9,11},{10,... | collective-permute-start | bytes 344072 | tf_op jit(solution)/shard_map/ppermute | solution.py:520
  59.2 1.4 %collective-permute-done.17.refs_2_ = bf16[224,256]{1,0:T(8,128)(2,1)S(1)} collective-permute-done((bf16[224,256]{1,0:T(8,128)(2,1)S(1)}, bf16[224,256]{1,0:T(8,128)(2,1)S(1)}, u32[]{:S(2)}, u32[]{:S(2)}) %collective-permute-start.17) | collective-permute-done | bytes 114720 | tf_op jit(solution)/shard_map/ppermute | solution.py:517
  60.6 1.5 %collective-permute-start.18 = (bf16[224,256]{1,0:T(8,128)(2,1)S(1)}, bf16[224,256]{1,0:T(8,128)(2,1)S(1)}, u32[]{:S(2)}, u32[]{:S(2)}) collective-permute-start(bf16[224,256]{1,0:T(8,128)(2,1)S(1)} %collective-permute-done.17.refs_2_), channel_id=1, source_target_pairs={{0,2},{1,3},{2,0},{3,1},{4,6},{5,7},{6,4},{7,5},{8,10},{9,11},{10,... | collective-permute-start | bytes 344072 | tf_op jit(solution)/shard_map/ppermute | solution.py:520
  62.1 3.1 %collective-permute-done.19.refs_4_ = bf16[224,256]{1,0:T(8,128)(2,1)S(1)} collective-permute-done((bf16[224,256]{1,0:T(8,128)(2,1)S(1)}, bf16[224,256]{1,0:T(8,128)(2,1)S(1)}, u32[]{:S(2)}, u32[]{:S(2)}) %collective-permute-start.19) | collective-permute-done | bytes 114720 | tf_op jit(solution)/shard_map/ppermute | solution.py:517
  65.2 1.5 %collective-permute-start.20 = (bf16[224,256]{1,0:T(8,128)(2,1)S(1)}, bf16[224,256]{1,0:T(8,128)(2,1)S(1)}, u32[]{:S(2)}, u32[]{:S(2)}) collective-permute-start(bf16[224,256]{1,0:T(8,128)(2,1)S(1)} %collective-permute-done.19.refs_4_), channel_id=1, source_target_pairs={{0,2},{1,3},{2,0},{3,1},{4,6},{5,7},{6,4},{7,5},{8,10},{9,11},{10,... | collective-permute-start | bytes 344072 | tf_op jit(solution)/shard_map/ppermute | solution.py:520
  66.7 0.5 collective-permute-start.22
  67.2 3.3 %collective-permute-done.20.refs_5_ = bf16[224,256]{1,0:T(8,128)(2,1)S(1)} collective-permute-done((bf16[224,256]{1,0:T(8,128)(2,1)S(1)}, bf16[224,256]{1,0:T(8,128)(2,1)S(1)}, u32[]{:S(2)}, u32[]{:S(2)}) %collective-permute-start.20) | collective-permute-done | bytes 114720 | tf_op jit(solution)/shard_map/ppermute | solution.py:520
  70.5 1.2 %collective-permute-done.22.refs_7_ = bf16[224,256]{1,0:T(8,128)(2,1)S(1)} collective-permute-done((bf16[224,256]{1,0:T(8,128)(2,1)S(1)}, bf16[224,256]{1,0:T(8,128)(2,1)S(1)}, u32[]{:S(2)}, u32[]{:S(2)}) %collective-permute-start.22) | collective-permute-done | bytes 114720 | tf_op jit(solution)/shard_map/ppermute | solution.py:520
  71.7 1.3 %gate_up.1 = (f32[128,768]{1,0:T(8,128)S(1)}, bf16[16,2048]{1,0:T(8,128)(2,1)S(1)}) custom-call(bf16[224,256]{1,0:T(8,128)(2,1)S(1)} %add_convert_fusion.refs_0_, bf16[224,256]{1,0:T(8,128)(2,1)S(1)} %collective-permute-done.16.refs_1_, bf16[224,256]{1,0:T(8,128)(2,1)S(1)} %collective-permute-done.17.refs_2_, ...), custom_call_target="tpu_custom_call" | custom-call | flops 1000000000 | bytes 3000000 | tf_op jit(solution)/shard_map/gate_up/pallas_call | solution.py:653
  73.1 1.4 %gate_up_own.1 = (f32[128,768]{1,0:T(8,128)S(1)}, bf16[16,2048]{1,0:T(8,128)(2,1)S(1)}) custom-call(bf16[224,256]{1,0:T(8,128)(2,1)S(1)} %add_convert_fusion.refs_0_, bf16[224,256]{1,0:T(8,128)(2,1)S(1)} %collective-permute-done.16.refs_1_, bf16[224,256]{1,0:T(8,128)(2,1)S(1)} %collective-permute-done.17.refs_2_, ...), custom_call_target="tpu_custom_call" | custom-call | flops 1000000000 | bytes 3000000 | tf_op jit(solution)/shard_map/gate_up_own/pallas_call | solution.py:653
  74.5 0.3 collective-permute-done.24.came_ref
  74.9 0.8 hidden.1
  75.6 1.6 %collective-permute-start.30 = (bf16[8,7168]{1,0:T(8,128)(2,1)S(1)}, bf16[8,7168]{1,0:T(8,128)(2,1)S(1)}, u32[]{:S(2)}, u32[]{:S(2)}) collective-permute-start(bf16[8,7168]{1,0:T(8,128)(2,1)S(1)} %get-tuple-element.74), channel_id=1, source_target_pairs={{0,2},{1,3},{2,0},{3,1},{4,6},{5,7},{6,4},{7,5},{8,10},{9,11},{10,... | collective-permute-start | bytes 344072 | tf_op jit(solution)/shard_map/ppermute | solution.py:520
  77.2 0.5 collective-permute-start.28
  77.7 1.5 %collective-permute-start.26 = (bf16[8,7168]{1,0:T(8,128)(2,1)S(1)}, bf16[8,7168]{1,0:T(8,128)(2,1)S(1)}, u32[]{:S(2)}, u32[]{:S(2)}) collective-permute-start(bf16[8,7168]{1,0:T(8,128)(2,1)S(1)} %get-tuple-element.70), channel_id=1, source_target_pairs={{0,2},{1,3},{2,0},{3,1},{4,6},{5,7},{6,4},{7,5},{8,10},{9,11},{10,... | collective-permute-start | bytes 344072 | tf_op jit(solution)/shard_map/ppermute | solution.py:520
  79.2 0.5 collective-permute-start.25
  79.8 0.6 down.1
  80.3 1.4 %collective-permute-done.30.far_ref = bf16[8,7168]{1,0:T(8,128)(2,1)S(1)} collective-permute-done((bf16[8,7168]{1,0:T(8,128)(2,1)S(1)}, bf16[8,7168]{1,0:T(8,128)(2,1)S(1)}, u32[]{:S(2)}, u32[]{:S(2)}) %collective-permute-start.30) | collective-permute-done | bytes 114720 | tf_op jit(solution)/shard_map/ppermute | solution.py:520
  81.7 2.0 %collective-permute-start.31 = (bf16[8,7168]{1,0:T(8,128)(2,1)S(1)}, bf16[8,7168]{1,0:T(8,128)(2,1)S(1)}, u32[]{:S(2)}, u32[]{:S(2)}) collective-permute-start(bf16[8,7168]{1,0:T(8,128)(2,1)S(1)} %add.25), channel_id=1, source_target_pairs={{0,12},{1,13},{2,14},{3,15},{4,8},{5,9},{6,10},{7,11},{8,4},{9,5},... | collective-permute-start | bytes 344072 | tf_op jit(solution)/shard_map/ppermute | solution.py:517
  83.7 0.4 collective-permute-done.28.far_ref
  84.2 1.3 %collective-permute-start.29 = (bf16[8,7168]{1,0:T(8,128)(2,1)S(1)}, bf16[8,7168]{1,0:T(8,128)(2,1)S(1)}, u32[]{:S(2)}, u32[]{:S(2)}) collective-permute-start(bf16[8,7168]{1,0:T(8,128)(2,1)S(1)} %add.24), channel_id=1, source_target_pairs={{0,8},{1,9},{2,10},{3,11},{4,12},{5,13},{6,14},{7,15},{8,0},{9,1},... | collective-permute-start | bytes 344072 | tf_op jit(solution)/shard_map/ppermute | solution.py:517
  85.5 1.1 %collective-permute-done.26.far_ref = bf16[8,7168]{1,0:T(8,128)(2,1)S(1)} collective-permute-done((bf16[8,7168]{1,0:T(8,128)(2,1)S(1)}, bf16[8,7168]{1,0:T(8,128)(2,1)S(1)}, u32[]{:S(2)}, u32[]{:S(2)}) %collective-permute-start.26) | collective-permute-done | bytes 114720 | tf_op jit(solution)/shard_map/ppermute | solution.py:520
  86.6 0.8 collective-permute-start.27
  87.4 1.3 %collective-permute-done.32.refs_6_ = bf16[16,2048]{1,0:T(8,128)(2,1)S(1)} collective-permute-done((bf16[16,2048]{1,0:T(8,128)(2,1)S(1)}, bf16[16,2048]{1,0:T(8,128)(2,1)S(1)}, u32[]{:S(2)}, u32[]{:S(2)}) %collective-permute-start.32) | collective-permute-done | bytes 65568 | tf_op jit(solution)/shard_map/ppermute | solution.py:523
  88.7 0.7 collective-permute-done.31.refs_4_
  89.4 4.0 %collective-permute-done.29.refs_3_ = bf16[8,7168]{1,0:T(8,128)(2,1)S(1)} collective-permute-done((bf16[8,7168]{1,0:T(8,128)(2,1)S(1)}, bf16[8,7168]{1,0:T(8,128)(2,1)S(1)}, u32[]{:S(2)}, u32[]{:S(2)}) %collective-permute-start.29) | collective-permute-done | bytes 114720 | tf_op jit(solution)/shard_map/ppermute | solution.py:517
  93.4 0.1 collective-permute-done.27.refs_2_
  93.5 0.8 last.1
  (44 shorter events, 0.5 us)
Async XLA Ops:
  0.0 2.8 %copy-start.5 = (bf16[64,4096]{1,0:T(8,128)(2,1)S(1)}, bf16[64,4096]{1,0:T(8,128)(2,1)}, u32[]{:S(2)}) copy-start(bf16[64,4096]{1,0:T(8,128)(2,1)} %refs_9_.3) | copy-start | bytes 1572868
  0.0 2.8 %copy-start.6 = (bf16[64,4096]{1,0:T(8,128)(2,1)S(1)}, bf16[64,4096]{1,0:T(8,128)(2,1)}, u32[]{:S(2)}) copy-start(bf16[64,4096]{1,0:T(8,128)(2,1)} %refs_10_.3) | copy-start | bytes 1572868
  0.0 2.8 %copy-start.7 = (bf16[64,4096]{1,0:T(8,128)(2,1)S(1)}, bf16[64,4096]{1,0:T(8,128)(2,1)}, u32[]{:S(2)}) copy-start(bf16[64,4096]{1,0:T(8,128)(2,1)} %refs_11_.1) | copy-start | bytes 1572868
  2.8 1.0 %copy-start.4 = (bf16[64,4096]{1,0:T(8,128)(2,1)S(1)}, bf16[64,4096]{1,0:T(8,128)(2,1)}, u32[]{:S(2)}) copy-start(bf16[64,4096]{1,0:T(8,128)(2,1)} %weight_ref.3) | copy-start | bytes 1572868
  2.8 1.1 %copy-start.8 = (bf16[8,10240]{1,0:T(8,128)(2,1)S(1)}, bf16[8,10240]{1,0:T(8,128)(2,1)}, u32[]{:S(2)}) copy-start(bf16[8,10240]{1,0:T(8,128)(2,1)} %fetch.1.piece_ref.refs_0_) | copy-start | bytes 491524
  2.9 27.8 %collective-permute-start.7 = (bf16[192,4096]{1,0:T(8,128)(2,1)S(1)}, bf16[192,4096]{1,0:T(8,128)(2,1)S(1)}, u32[]{:S(2)}, u32[]{:S(2)}) collective-permute-start(bf16[192,4096]{1,0:T(8,128)(2,1)S(1)} %stack.1), channel_id=1, source_target_pairs={{0,1},{1,0},{2,3},{3,2},{4,5},{5,4},{6,7},{7,6},{8,9},{9,8},{10,11... | collective-permute-start | bytes 4718600 | tf_op jit(solution)/shard_map/ppermute | solution.py:523
  3.9 26.8 %copy-start.9 = (f32[4096]{0:T(1024)S(1)}, f32[4096]{0:T(1024)}, u32[]{:S(2)}) copy-start(f32[4096]{0:T(1024)} %param.23) | copy-start | bytes 49156
  3.9 21.7 %collective-permute-start = (bf16[8,26624]{1,0:T(8,128)(2,1)S(1)}, bf16[8,26624]{1,0:T(8,128)(2,1)S(1)}, u32[]{:S(2)}, u32[]{:S(2)}) collective-permute-start(bf16[8,26624]{1,0:T(8,128)(2,1)S(1)} %across.1), channel_id=1, source_target_pairs={{0,2},{1,3},{2,0},{3,1},{4,6},{5,7},{6,4},{7,5},{8,10},{9,11},{10,... | collective-permute-start | bytes 1277960 | tf_op jit(solution)/shard_map/ppermute | solution.py:520
  6.9 7.8 %collective-permute-start.1 = (bf16[8,10240]{1,0:T(8,128)(2,1)S(1)}, bf16[8,10240]{1,0:T(8,128)(2,1)S(1)}, u32[]{:S(2)}, u32[]{:S(2)}) collective-permute-start(bf16[8,10240]{1,0:T(8,128)(2,1)S(1)} %copy-done.8), channel_id=1, source_target_pairs={{0,4},{1,5},{2,6},{3,7},{4,0},{5,1},{6,2},{7,3},{8,12},{9,13},{10,... | collective-permute-start | bytes 491528 | tf_op jit(solution)/shard_map/ppermute | solution.py:517
  8.6 15.1 %collective-permute-start.3 = (bf16[8,10240]{1,0:T(8,128)(2,1)S(1)}, bf16[8,10240]{1,0:T(8,128)(2,1)S(1)}, u32[]{:S(2)}, u32[]{:S(2)}) collective-permute-start(bf16[8,10240]{1,0:T(8,128)(2,1)S(1)} %copy-done.8), channel_id=1, source_target_pairs={{0,8},{1,9},{2,10},{3,11},{4,12},{5,13},{6,14},{7,15},{8,0},{9,1},... | collective-permute-start | bytes 491528 | tf_op jit(solution)/shard_map/ppermute | solution.py:517
  11.1 13.0 %collective-permute-start.5 = (bf16[8,10240]{1,0:T(8,128)(2,1)S(1)}, bf16[8,10240]{1,0:T(8,128)(2,1)S(1)}, u32[]{:S(2)}, u32[]{:S(2)}) collective-permute-start(bf16[8,10240]{1,0:T(8,128)(2,1)S(1)} %copy-done.8), channel_id=1, source_target_pairs={{0,12},{1,13},{2,14},{3,15},{4,8},{5,9},{6,10},{7,11},{8,4},{9,5},... | collective-permute-start | bytes 491528 | tf_op jit(solution)/shard_map/ppermute | solution.py:517
  14.8 11.1 %collective-permute-start.2 = (bf16[8,10240]{1,0:T(8,128)(2,1)S(1)}, bf16[8,10240]{1,0:T(8,128)(2,1)S(1)}, u32[]{:S(2)}, u32[]{:S(2)}) collective-permute-start(bf16[8,10240]{1,0:T(8,128)(2,1)S(1)} %collective-permute-done.1.refs_2_), channel_id=1, source_target_pairs={{0,2},{1,3},{2,0},{3,1},{4,6},{5,7},{6,4},{7,5},{8,10},{9,11},{10,... | collective-permute-start | bytes 491528 | tf_op jit(solution)/shard_map/ppermute | solution.py:520
  23.6 5.3 %collective-permute-start.4 = (bf16[8,10240]{1,0:T(8,128)(2,1)S(1)}, bf16[8,10240]{1,0:T(8,128)(2,1)S(1)}, u32[]{:S(2)}, u32[]{:S(2)}) collective-permute-start(bf16[8,10240]{1,0:T(8,128)(2,1)S(1)} %collective-permute-done.3.refs_4_), channel_id=1, source_target_pairs={{0,2},{1,3},{2,0},{3,1},{4,6},{5,7},{6,4},{7,5},{8,10},{9,11},{10,... | collective-permute-start | bytes 491528 | tf_op jit(solution)/shard_map/ppermute | solution.py:520
  24.1 6.6 %collective-permute-start.6 = (bf16[8,10240]{1,0:T(8,128)(2,1)S(1)}, bf16[8,10240]{1,0:T(8,128)(2,1)S(1)}, u32[]{:S(2)}, u32[]{:S(2)}) collective-permute-start(bf16[8,10240]{1,0:T(8,128)(2,1)S(1)} %collective-permute-done.5.refs_6_), channel_id=1, source_target_pairs={{0,2},{1,3},{2,0},{3,1},{4,6},{5,7},{6,4},{7,5},{8,10},{9,11},{10,... | collective-permute-start | bytes 491528 | tf_op jit(solution)/shard_map/ppermute | solution.py:520
  25.7 8.4 %collective-permute-start.8 = (bf16[128,1024]{1,0:T(8,128)(2,1)S(1)}, bf16[128,1024]{1,0:T(8,128)(2,1)S(1)}, u32[]{:S(2)}, u32[]{:S(2)}) collective-permute-start(bf16[128,1024]{1,0:T(8,128)(2,1)S(1)} %get-tuple-element.49), channel_id=1, source_target_pairs={{0,1},{1,0},{2,3},{3,2},{4,5},{5,4},{6,7},{7,6},{8,9},{9,8},{10,11... | collective-permute-start | bytes 786440 | tf_op jit(solution)/shard_map/ppermute | solution.py:523
  30.7 2.1 %copy-start.10 = (s32[24,1]{0,1:T(1,128)S(1)}, s32[24,1]{0,1:T(1,128)}, u32[]{:S(2)}) copy-start(s32[24,1]{0,1:T(1,128)} %param.16) | copy-start | bytes 292
  30.7 2.1 %copy-start.11 = (s32[24]{0:T(128)S(1)}, s32[24]{0:T(128)}, u32[]{:S(2)}) copy-start(s32[24]{0:T(128)} %segment_ref.1) | copy-start | bytes 292
  32.7 1.5 %collective-permute-start.9 = (bf16[160,512]{1,0:T(8,128)(2,1)S(1)}, bf16[160,512]{1,0:T(8,128)(2,1)S(1)}, u32[]{:S(2)}, u32[]{:S(2)}) collective-permute-start(bf16[160,512]{1,0:T(8,128)(2,1)S(1)} %get-tuple-element.51), channel_id=1, source_target_pairs={{0,1},{1,0},{2,3},{3,2},{4,5},{5,4},{6,7},{7,6},{8,9},{9,8},{10,11... | collective-permute-start | bytes 491528 | tf_op jit(solution)/shard_map/ppermute | solution.py:523
  35.1 4.1 %collective-permute-start.10 = (bf16[112,128]{1,0:T(8,128)(2,1)S(1)}, bf16[112,128]{1,0:T(8,128)(2,1)S(1)}, u32[]{:S(2)}, u32[]{:S(2)}) collective-permute-start(bf16[112,128]{1,0:T(8,128)(2,1)S(1)} %get-tuple-element.53.refs_0_), channel_id=1, source_target_pairs={{0,2},{1,3},{2,0},{3,1},{4,6},{5,7},{6,4},{7,5},{8,10},{9,11},{10,... | collective-permute-start | bytes 86024 | tf_op jit(solution)/shard_map/ppermute | solution.py:520
  35.6 3.6 %collective-permute-start.11 = (bf16[112,128]{1,0:T(8,128)(2,1)S(1)}, bf16[112,128]{1,0:T(8,128)(2,1)S(1)}, u32[]{:S(2)}, u32[]{:S(2)}) collective-permute-start(bf16[112,128]{1,0:T(8,128)(2,1)S(1)} %get-tuple-element.53.refs_0_), channel_id=1, source_target_pairs={{0,1},{1,0},{2,3},{3,2},{4,5},{5,4},{6,7},{7,6},{8,9},{9,8},{10,11... | collective-permute-start | bytes 86024 | tf_op jit(solution)/shard_map/ppermute | solution.py:523
  35.8 3.6 %collective-permute-start.12 = (bf16[112,128]{1,0:T(8,128)(2,1)S(1)}, bf16[112,128]{1,0:T(8,128)(2,1)S(1)}, u32[]{:S(2)}, u32[]{:S(2)}) collective-permute-start(bf16[112,128]{1,0:T(8,128)(2,1)S(1)} %get-tuple-element.53.refs_0_), channel_id=1, source_target_pairs={{0,3},{1,2},{2,1},{3,0},{4,7},{5,6},{6,5},{7,4},{8,11},{9,10},{10,... | collective-permute-start | bytes 86024 | tf_op jit(solution)/shard_map/ppermute | solution.py:626
  39.3 13.6 %copy-start = (bf16[160,4096]{1,0:T(8,128)(2,1)S(1)}, bf16[160,4096]{1,0:T(8,128)(2,1)}, u32[]{:S(2)}) copy-start(bf16[160,4096]{1,0:T(8,128)(2,1)} %down_ref.4) | copy-start | bytes 3932164
  39.3 13.6 %copy-start.1 = (bf16[160,4096]{1,0:T(8,128)(2,1)S(1)}, bf16[160,4096]{1,0:T(8,128)(2,1)}, u32[]{:S(2)}) copy-start(bf16[160,4096]{1,0:T(8,128)(2,1)} %refs_9_.5) | copy-start | bytes 3932164
  39.3 13.6 %copy-start.2 = (bf16[160,4096]{1,0:T(8,128)(2,1)S(1)}, bf16[160,4096]{1,0:T(8,128)(2,1)}, u32[]{:S(2)}) copy-start(bf16[160,4096]{1,0:T(8,128)(2,1)} %refs_10_.5) | copy-start | bytes 3932164
  39.8 8.0 %collective-permute-start.13 = (bf16[224,256]{1,0:T(8,128)(2,1)S(1)}, bf16[224,256]{1,0:T(8,128)(2,1)S(1)}, u32[]{:S(2)}, u32[]{:S(2)}) collective-permute-start(bf16[224,256]{1,0:T(8,128)(2,1)S(1)} %get-tuple-element.57), channel_id=1, source_target_pairs={{0,12},{1,13},{2,14},{3,15},{4,8},{5,9},{6,10},{7,11},{8,4},{9,5},... | collective-permute-start | bytes 344072 | tf_op jit(solution)/shard_map/ppermute | solution.py:517
  42.0 10.9 %collective-permute-start.14 = (bf16[224,256]{1,0:T(8,128)(2,1)S(1)}, bf16[224,256]{1,0:T(8,128)(2,1)S(1)}, u32[]{:S(2)}, u32[]{:S(2)}) collective-permute-start(bf16[224,256]{1,0:T(8,128)(2,1)S(1)} %get-tuple-element.58), channel_id=1, source_target_pairs={{0,8},{1,9},{2,10},{3,11},{4,12},{5,13},{6,14},{7,15},{8,0},{9,1},... | collective-permute-start | bytes 344072 | tf_op jit(solution)/shard_map/ppermute | solution.py:517
  42.4 10.5 %collective-permute-start.15 = (bf16[224,256]{1,0:T(8,128)(2,1)S(1)}, bf16[224,256]{1,0:T(8,128)(2,1)S(1)}, u32[]{:S(2)}, u32[]{:S(2)}) collective-permute-start(bf16[224,256]{1,0:T(8,128)(2,1)S(1)} %get-tuple-element.59), channel_id=1, source_target_pairs={{0,4},{1,5},{2,6},{3,7},{4,0},{5,1},{6,2},{7,3},{8,12},{9,13},{10,... | collective-permute-start | bytes 344072 | tf_op jit(solution)/shard_map/ppermute | solution.py:517
  53.0 18.8 %copy-start.3 = (f32[4096]{0:T(1024)S(1)}, f32[4096]{0:T(1024)}, u32[]{:S(2)}) copy-start(f32[4096]{0:T(1024)} %param.24) | copy-start | bytes 49156
  53.2 18.6 %collective-permute-start.23 = (bf16[320,4096]{1,0:T(8,128)(2,1)S(1)}, bf16[320,4096]{1,0:T(8,128)(2,1)S(1)}, u32[]{:S(2)}, u32[]{:S(2)}) collective-permute-start(bf16[320,4096]{1,0:T(8,128)(2,1)S(1)} %share.1), channel_id=1, source_target_pairs={{0,1},{1,0},{2,3},{3,2},{4,5},{5,4},{6,7},{7,6},{8,9},{9,8},{10,11... | collective-permute-start | bytes 7864328 | tf_op jit(solution)/shard_map/ppermute | solution.py:523
  53.2 7.4 %collective-permute-start.17 = (bf16[224,256]{1,0:T(8,128)(2,1)S(1)}, bf16[224,256]{1,0:T(8,128)(2,1)S(1)}, u32[]{:S(2)}, u32[]{:S(2)}) collective-permute-start(bf16[224,256]{1,0:T(8,128)(2,1)S(1)} %add_convert_fusion.refs_0_), channel_id=1, source_target_pairs={{0,4},{1,5},{2,6},{3,7},{4,0},{5,1},{6,2},{7,3},{8,12},{9,13},{10,... | collective-permute-start | bytes 344072 | tf_op jit(solution)/shard_map/ppermute | solution.py:517
  53.3 11.9 %collective-permute-start.19 = (bf16[224,256]{1,0:T(8,128)(2,1)S(1)}, bf16[224,256]{1,0:T(8,128)(2,1)S(1)}, u32[]{:S(2)}, u32[]{:S(2)}) collective-permute-start(bf16[224,256]{1,0:T(8,128)(2,1)S(1)} %add_convert_fusion.refs_0_), channel_id=1, source_target_pairs={{0,8},{1,9},{2,10},{3,11},{4,12},{5,13},{6,14},{7,15},{8,0},{9,1},... | collective-permute-start | bytes 344072 | tf_op jit(solution)/shard_map/ppermute | solution.py:517
  55.8 10.9 %collective-permute-start.21 = (bf16[224,256]{1,0:T(8,128)(2,1)S(1)}, bf16[224,256]{1,0:T(8,128)(2,1)S(1)}, u32[]{:S(2)}, u32[]{:S(2)}) collective-permute-start(bf16[224,256]{1,0:T(8,128)(2,1)S(1)} %add_convert_fusion.refs_0_), channel_id=1, source_target_pairs={{0,12},{1,13},{2,14},{3,15},{4,8},{5,9},{6,10},{7,11},{8,4},{9,5},... | collective-permute-start | bytes 344072 | tf_op jit(solution)/shard_map/ppermute | solution.py:517
  57.7 9.5 %collective-permute-start.16 = (bf16[224,256]{1,0:T(8,128)(2,1)S(1)}, bf16[224,256]{1,0:T(8,128)(2,1)S(1)}, u32[]{:S(2)}, u32[]{:S(2)}) collective-permute-start(bf16[224,256]{1,0:T(8,128)(2,1)S(1)} %add_convert_fusion.refs_0_), channel_id=1, source_target_pairs={{0,2},{1,3},{2,0},{3,1},{4,6},{5,7},{6,4},{7,5},{8,10},{9,11},{10,... | collective-permute-start | bytes 344072 | tf_op jit(solution)/shard_map/ppermute | solution.py:520
  60.6 6.6 %collective-permute-start.18 = (bf16[224,256]{1,0:T(8,128)(2,1)S(1)}, bf16[224,256]{1,0:T(8,128)(2,1)S(1)}, u32[]{:S(2)}, u32[]{:S(2)}) collective-permute-start(bf16[224,256]{1,0:T(8,128)(2,1)S(1)} %collective-permute-done.17.refs_2_), channel_id=1, source_target_pairs={{0,2},{1,3},{2,0},{3,1},{4,6},{5,7},{6,4},{7,5},{8,10},{9,11},{10,... | collective-permute-start | bytes 344072 | tf_op jit(solution)/shard_map/ppermute | solution.py:520
  65.2 5.3 %collective-permute-start.20 = (bf16[224,256]{1,0:T(8,128)(2,1)S(1)}, bf16[224,256]{1,0:T(8,128)(2,1)S(1)}, u32[]{:S(2)}, u32[]{:S(2)}) collective-permute-start(bf16[224,256]{1,0:T(8,128)(2,1)S(1)} %collective-permute-done.19.refs_4_), channel_id=1, source_target_pairs={{0,2},{1,3},{2,0},{3,1},{4,6},{5,7},{6,4},{7,5},{8,10},{9,11},{10,... | collective-permute-start | bytes 344072 | tf_op jit(solution)/shard_map/ppermute | solution.py:520
  66.7 5.0 %collective-permute-start.22 = (bf16[224,256]{1,0:T(8,128)(2,1)S(1)}, bf16[224,256]{1,0:T(8,128)(2,1)S(1)}, u32[]{:S(2)}, u32[]{:S(2)}) collective-permute-start(bf16[224,256]{1,0:T(8,128)(2,1)S(1)} %collective-permute-done.21.refs_6_), channel_id=1, source_target_pairs={{0,2},{1,3},{2,0},{3,1},{4,6},{5,7},{6,4},{7,5},{8,10},{9,11},{10,... | collective-permute-start | bytes 344072 | tf_op jit(solution)/shard_map/ppermute | solution.py:520
  73.1 1.8 %collective-permute-start.24 = (f32[128,768]{1,0:T(8,128)S(1)}, f32[128,768]{1,0:T(8,128)S(1)}, u32[]{:S(2)}, u32[]{:S(2)}) collective-permute-start(f32[128,768]{1,0:T(8,128)S(1)} %get-tuple-element.63), channel_id=1, source_target_pairs={{0,1},{1,0},{2,3},{3,2},{4,5},{5,4},{6,7},{7,6},{8,9},{9,8},{10,11... | collective-permute-start | bytes 1179656 | tf_op jit(solution)/shard_map/ppermute | solution.py:523
  75.6 6.0 %collective-permute-start.30 = (bf16[8,7168]{1,0:T(8,128)(2,1)S(1)}, bf16[8,7168]{1,0:T(8,128)(2,1)S(1)}, u32[]{:S(2)}, u32[]{:S(2)}) collective-permute-start(bf16[8,7168]{1,0:T(8,128)(2,1)S(1)} %get-tuple-element.74), channel_id=1, source_target_pairs={{0,2},{1,3},{2,0},{3,1},{4,6},{5,7},{6,4},{7,5},{8,10},{9,11},{10,... | collective-permute-start | bytes 344072 | tf_op jit(solution)/shard_map/ppermute | solution.py:520
  77.2 6.9 %collective-permute-start.28 = (bf16[8,7168]{1,0:T(8,128)(2,1)S(1)}, bf16[8,7168]{1,0:T(8,128)(2,1)S(1)}, u32[]{:S(2)}, u32[]{:S(2)}) collective-permute-start(bf16[8,7168]{1,0:T(8,128)(2,1)S(1)} %get-tuple-element.72), channel_id=1, source_target_pairs={{0,2},{1,3},{2,0},{3,1},{4,6},{5,7},{6,4},{7,5},{8,10},{9,11},{10,... | collective-permute-start | bytes 344072 | tf_op jit(solution)/shard_map/ppermute | solution.py:520
  77.7 8.9 %collective-permute-start.26 = (bf16[8,7168]{1,0:T(8,128)(2,1)S(1)}, bf16[8,7168]{1,0:T(8,128)(2,1)S(1)}, u32[]{:S(2)}, u32[]{:S(2)}) collective-permute-start(bf16[8,7168]{1,0:T(8,128)(2,1)S(1)} %get-tuple-element.70), channel_id=1, source_target_pairs={{0,2},{1,3},{2,0},{3,1},{4,6},{5,7},{6,4},{7,5},{8,10},{9,11},{10,... | collective-permute-start | bytes 344072 | tf_op jit(solution)/shard_map/ppermute | solution.py:520
  79.2 9.4 %collective-permute-start.25 = (bf16[8,7168]{1,0:T(8,128)(2,1)S(1)}, bf16[8,7168]{1,0:T(8,128)(2,1)S(1)}, u32[]{:S(2)}, u32[]{:S(2)}) collective-permute-start(bf16[8,7168]{1,0:T(8,128)(2,1)S(1)} %get-tuple-element.68), channel_id=1, source_target_pairs={{0,2},{1,3},{2,0},{3,1},{4,6},{5,7},{6,4},{7,5},{8,10},{9,11},{10,... | collective-permute-start | bytes 344072 | tf_op jit(solution)/shard_map/ppermute | solution.py:520
  81.7 7.7 %collective-permute-start.31 = (bf16[8,7168]{1,0:T(8,128)(2,1)S(1)}, bf16[8,7168]{1,0:T(8,128)(2,1)S(1)}, u32[]{:S(2)}, u32[]{:S(2)}) collective-permute-start(bf16[8,7168]{1,0:T(8,128)(2,1)S(1)} %add.25), channel_id=1, source_target_pairs={{0,12},{1,13},{2,14},{3,15},{4,8},{5,9},{6,10},{7,11},{8,4},{9,5},... | collective-permute-start | bytes 344072 | tf_op jit(solution)/shard_map/ppermute | solution.py:517
  84.2 9.3 %collective-permute-start.29 = (bf16[8,7168]{1,0:T(8,128)(2,1)S(1)}, bf16[8,7168]{1,0:T(8,128)(2,1)S(1)}, u32[]{:S(2)}, u32[]{:S(2)}) collective-permute-start(bf16[8,7168]{1,0:T(8,128)(2,1)S(1)} %add.24), channel_id=1, source_target_pairs={{0,8},{1,9},{2,10},{3,11},{4,12},{5,13},{6,14},{7,15},{8,0},{9,1},... | collective-permute-start | bytes 344072 | tf_op jit(solution)/shard_map/ppermute | solution.py:517
  86.6 6.9 %collective-permute-start.27 = (bf16[8,7168]{1,0:T(8,128)(2,1)S(1)}, bf16[8,7168]{1,0:T(8,128)(2,1)S(1)}, u32[]{:S(2)}, u32[]{:S(2)}) collective-permute-start(bf16[8,7168]{1,0:T(8,128)(2,1)S(1)} %add.23), channel_id=1, source_target_pairs={{0,4},{1,5},{2,6},{3,7},{4,0},{5,1},{6,2},{7,3},{8,12},{9,13},{10,... | collective-permute-start | bytes 344072 | tf_op jit(solution)/shard_map/ppermute | solution.py:517
  87.4 1.3 %collective-permute-start.32 = (bf16[16,2048]{1,0:T(8,128)(2,1)S(1)}, bf16[16,2048]{1,0:T(8,128)(2,1)S(1)}, u32[]{:S(2)}, u32[]{:S(2)}) collective-permute-start(bf16[16,2048]{1,0:T(8,128)(2,1)S(1)} %get-tuple-element.76), channel_id=1, source_target_pairs={{0,1},{1,0},{2,3},{3,2},{4,5},{5,4},{6,7},{7,6},{8,9},{9,8},{10,11... | collective-permute-start | bytes 196616 | tf_op jit(solution)/shard_map/ppermute | solution.py:523

commit v7 on v6

--- a/solution.py
+++ b/solution.py
@@ -57,8 +57,10 @@
     return full + (rest > 0), False
 
 
-def fetch_kernel(owner_ref, row_ref, corpus_ref, query_ref, piece_ref, blocks, rows, sems):
+def fetch_kernel(owner_ref, row_ref, corpus_ref, query_ref, piece_ref, blocks, query, rows, sems):
     me = place()[0]
+    query_copy = pltpu.make_async_copy(query_ref, query, sems.at[CAP])
+    query_copy.start()
     features = query_ref.shape[1]
     query_rows = query_ref.shape[0]
 
@@ -80,7 +82,8 @@
         copy.start()
     total = query_rows + CAP * BLK
     full, halved = piece_layout(total)
-    rows[0:query_rows, :] = query_ref[...].astype(jnp.float32)
+    query_copy.wait()
+    rows[0:query_rows, :] = query[...].astype(jnp.float32)
     for k in range(CAP):
         copies[k].wait()
         first = query_rows + k * BLK
@@ -555,11 +558,12 @@
     piece = kernel_call(
         fetch_kernel,
         shape((8, full * features + halved * half), bf16),
-        [SMEM, SMEM, ANY, VMEM],
+        [SMEM, SMEM, ANY, ANY],
         [
             pltpu.VMEM((CAP, BLK, features), bf16),
+            pltpu.VMEM((query_rows, features), bf16),
             pltpu.VMEM((full * 8 + halved * 8, features), f32),
-            pltpu.SemaphoreType.DMA((CAP,)),
+            pltpu.SemaphoreType.DMA((CAP + 1,)),
         ],
         name="fetch",
         limit=60 * 1024 * 1024,

time: 94.6 us -> 94.4 us (level)
  no operation moved by 1% of the time
where the time goes in v7:
time: 94.4 us; the launch traced here: 94.2 us
  waiting for transfers between devices  45.7 us (48%)
  starting transfers between devices  35.1 us (37%)
  Pallas kernels  12.5 us (13%)
    ppermute x12, waiting for transfers between devices, along_z(): return lax.ppermute(value, AXIS, [(i, i ^ 4 * k) for i in range(devices)])  30 us
    ppermute x12, starting transfers between devices, along_z(): return lax.ppermute(value, AXIS, [(i, i ^ 4 * k) for i in range(devices)])  17.6 us
    ppermute x13, starting transfers between devices, across_y(): return lax.ppermute(value, AXIS, [(i, i ^ 2) for i in range(devices)])  15.1 us
    ppermute x13, waiting for transfers between devices, across_y(): return lax.ppermute(value, AXIS, [(i, i ^ 2) for i in range(devices)])  14 us
    pallas_call x2, Pallas kernels, gate_up(): kernel_call(functools.partial(gate_kernel, rows_here, chunk_rows, own), (...  2.72 us
    pallas_call x1, Pallas kernels, body(): kernel_call(fetch_kernel, shape((8, full * features + halved * half), bf1...  2.56 us
    pallas_call x1, Pallas kernels, body(): kernel_call(functools.partial(projection_kernel, query_rows + CAP * BLK),...  1.98 us
  transfers between devices with their start and end apart: 33, of which 20 were waited for; matrix products, arithmetic and copies ran while one was open for 0% of the time, Pallas kernels for 6%

profile of v7, /device:TPU:0, one launch (start us, length us, event | category | flops | bytes accessed | tf_op | source)
XLA Modules:
  0.0 94.2 jit_solution(15521396104278229297)
XLA Ops:
  0.0 2.6 %fetch.1.piece_ref.refs_0_ = bf16[8,10240]{1,0:T(8,128)(2,1)} custom-call(s32[24]{0:T(128)} %bitcast.6, s32[24]{0:T(128)} %row_ref.1, bf16[64,4,4096]{2,1,0:T(4,128)(2,1)} %corpus_ref.1, bf16[8,4096]{1,0:T(8,128)(2,1)} %query_ref.1), custom_call_target="tpu_custom_call" | custom-call | flops 1000000000 | bytes 3000000 | tf_op jit(solution)/shard_map/fetch/pallas_call | solution.py:558
  2.6 0.1 stack.1
  2.7 0.6 collective-permute-start.7
  3.3 0.3 copy-done.4
  3.7 3.1 %collective-permute-start = (bf16[8,26624]{1,0:T(8,128)(2,1)S(1)}, bf16[8,26624]{1,0:T(8,128)(2,1)S(1)}, u32[]{:S(2)}, u32[]{:S(2)}) collective-permute-start(bf16[8,26624]{1,0:T(8,128)(2,1)S(1)} %across.1), channel_id=1, source_target_pairs={{0,2},{1,3},{2,0},{3,1},{4,6},{5,7},{6,4},{7,5},{8,10},{9,11},{10,... | collective-permute-start | bytes 1277960 | tf_op jit(solution)/shard_map/ppermute | solution.py:523
  6.8 1.5 %collective-permute-start.1 = (bf16[8,10240]{1,0:T(8,128)(2,1)S(1)}, bf16[8,10240]{1,0:T(8,128)(2,1)S(1)}, u32[]{:S(2)}, u32[]{:S(2)}) collective-permute-start(bf16[8,10240]{1,0:T(8,128)(2,1)S(1)} %copy-done.8), channel_id=1, source_target_pairs={{0,4},{1,5},{2,6},{3,7},{4,0},{5,1},{6,2},{7,3},{8,12},{9,13},{10,... | collective-permute-start | bytes 491528 | tf_op jit(solution)/shard_map/ppermute | solution.py:520
  8.4 2.6 %collective-permute-start.3 = (bf16[8,10240]{1,0:T(8,128)(2,1)S(1)}, bf16[8,10240]{1,0:T(8,128)(2,1)S(1)}, u32[]{:S(2)}, u32[]{:S(2)}) collective-permute-start(bf16[8,10240]{1,0:T(8,128)(2,1)S(1)} %copy-done.8), channel_id=1, source_target_pairs={{0,8},{1,9},{2,10},{3,11},{4,12},{5,13},{6,14},{7,15},{8,0},{9,1},... | collective-permute-start | bytes 491528 | tf_op jit(solution)/shard_map/ppermute | solution.py:520
  11.0 0.3 collective-permute-start.5
  11.2 3.5 %collective-permute-done.1.refs_2_ = bf16[8,10240]{1,0:T(8,128)(2,1)S(1)} collective-permute-done((bf16[8,10240]{1,0:T(8,128)(2,1)S(1)}, bf16[8,10240]{1,0:T(8,128)(2,1)S(1)}, u32[]{:S(2)}, u32[]{:S(2)}) %collective-permute-start.1) | collective-permute-done | bytes 163872 | tf_op jit(solution)/shard_map/ppermute | solution.py:520
  14.8 0.3 collective-permute-start.2
  15.0 8.4 %collective-permute-done.3.refs_4_ = bf16[8,10240]{1,0:T(8,128)(2,1)S(1)} collective-permute-done((bf16[8,10240]{1,0:T(8,128)(2,1)S(1)}, bf16[8,10240]{1,0:T(8,128)(2,1)S(1)}, u32[]{:S(2)}, u32[]{:S(2)}) %collective-permute-start.3) | collective-permute-done | bytes 163872 | tf_op jit(solution)/shard_map/ppermute | solution.py:520
  23.4 0.5 collective-permute-start.4
  23.9 1.5 %collective-permute-start.6 = (bf16[8,10240]{1,0:T(8,128)(2,1)S(1)}, bf16[8,10240]{1,0:T(8,128)(2,1)S(1)}, u32[]{:S(2)}, u32[]{:S(2)}) collective-permute-start(bf16[8,10240]{1,0:T(8,128)(2,1)S(1)} %collective-permute-done.5.refs_6_), channel_id=1, source_target_pairs={{0,2},{1,3},{2,0},{3,1},{4,6},{5,7},{6,4},{7,5},{8,10},{9,11},{10,... | collective-permute-start | bytes 491528 | tf_op jit(solution)/shard_map/ppermute | solution.py:523
  25.5 0.1 pairs.1
  25.6 0.1 collective-permute-start.8
  25.6 3.1 %collective-permute-done.4.refs_5_ = bf16[8,10240]{1,0:T(8,128)(2,1)S(1)} collective-permute-done((bf16[8,10240]{1,0:T(8,128)(2,1)S(1)}, bf16[8,10240]{1,0:T(8,128)(2,1)S(1)}, u32[]{:S(2)}, u32[]{:S(2)}) %collective-permute-start.4) | collective-permute-done | bytes 163872 | tf_op jit(solution)/shard_map/ppermute | solution.py:523
  28.7 1.8 %collective-permute-done.6.refs_7_ = bf16[8,10240]{1,0:T(8,128)(2,1)S(1)} collective-permute-done((bf16[8,10240]{1,0:T(8,128)(2,1)S(1)}, bf16[8,10240]{1,0:T(8,128)(2,1)S(1)}, u32[]{:S(2)}, u32[]{:S(2)}) %collective-permute-start.6) | collective-permute-done | bytes 163872 | tf_op jit(solution)/shard_map/ppermute | solution.py:523
  30.5 2.0 %project.1 = (bf16[160,512]{1,0:T(8,128)(2,1)S(1)}, bf16[160,512]{1,0:T(8,128)(2,1)S(1)}) custom-call(bf16[8,10240]{1,0:T(8,128)(2,1)S(1)} %copy-done.8, bf16[8,26624]{1,0:T(8,128)(2,1)S(1)} %collective-permute-done.refs_1_.far_ref, bf16[8,10240]{1,0:T(8,128)(2,1)S(1)} %collective-permute-done.1.refs_2_, ...), custom_call_target="tpu_custom_call" | custom-call | flops 10000000000 | bytes 30000000 | tf_op jit(solution)/shard_map/project/pallas_call | solution.py:592
  32.6 1.3 %plan.1 = (bf16[224,160]{1,0:T(8,128)(2,1)S(1)}, bf16[224,160]{1,0:T(8,128)(2,1)S(1)}, f32[224,224]{1,0:T(8,128)S(1)}) custom-call(s32[24]{0:T(128)S(1)} %bitcast.7, s32[24]{0:T(128)S(1)} %copy-done.11), custom_call_target="tpu_custom_call" | custom-call | flops 1000000000 | bytes 3000000 | tf_op jit(solution)/shard_map/plan/pallas_call | solution.py:610
  34.0 0.9 attend.1
  34.9 0.5 collective-permute-start.10
  35.4 0.2 collective-permute-start.11
  35.6 1.4 %collective-permute-start.12 = (bf16[112,128]{1,0:T(8,128)(2,1)S(1)}, bf16[112,128]{1,0:T(8,128)(2,1)S(1)}, u32[]{:S(2)}, u32[]{:S(2)}) collective-permute-start(bf16[112,128]{1,0:T(8,128)(2,1)S(1)} %get-tuple-element.53.refs_0_), channel_id=1, source_target_pairs={{0,3},{1,2},{2,1},{3,0},{4,7},{5,6},{6,5},{7,4},{8,11},{9,10},{10,... | collective-permute-start | bytes 86024 | tf_op jit(solution)/shard_map/ppermute | solution.py:630
  37.0 1.9 %collective-permute-done.10.refs_1_ = bf16[112,128]{1,0:T(8,128)(2,1)S(1)} collective-permute-done((bf16[112,128]{1,0:T(8,128)(2,1)S(1)}, bf16[112,128]{1,0:T(8,128)(2,1)S(1)}, u32[]{:S(2)}, u32[]{:S(2)}) %collective-permute-start.10) | collective-permute-done | bytes 28704 | tf_op jit(solution)/shard_map/ppermute | solution.py:523
  39.0 0.1 collective-permute-done.12.refs_3_
  39.1 0.4 out.1
  39.5 2.2 %collective-permute-start.13 = (bf16[224,256]{1,0:T(8,128)(2,1)S(1)}, bf16[224,256]{1,0:T(8,128)(2,1)S(1)}, u32[]{:S(2)}, u32[]{:S(2)}) collective-permute-start(bf16[224,256]{1,0:T(8,128)(2,1)S(1)} %get-tuple-element.57), channel_id=1, source_target_pairs={{0,12},{1,13},{2,14},{3,15},{4,8},{5,9},{6,10},{7,11},{8,4},{9,5},... | collective-permute-start | bytes 344072 | tf_op jit(solution)/shard_map/ppermute | solution.py:520
  41.7 0.4 collective-permute-start.14
  42.1 1.8 %collective-permute-start.15 = (bf16[224,256]{1,0:T(8,128)(2,1)S(1)}, bf16[224,256]{1,0:T(8,128)(2,1)S(1)}, u32[]{:S(2)}, u32[]{:S(2)}) collective-permute-start(bf16[224,256]{1,0:T(8,128)(2,1)S(1)} %get-tuple-element.59), channel_id=1, source_target_pairs={{0,4},{1,5},{2,6},{3,7},{4,0},{5,1},{6,2},{7,3},{8,12},{9,13},{10,... | collective-permute-start | bytes 344072 | tf_op jit(solution)/shard_map/ppermute | solution.py:520
  44.0 3.5 %collective-permute-done.13 = bf16[224,256]{1,0:T(8,128)(2,1)S(1)} collective-permute-done((bf16[224,256]{1,0:T(8,128)(2,1)S(1)}, bf16[224,256]{1,0:T(8,128)(2,1)S(1)}, u32[]{:S(2)}, u32[]{:S(2)}) %collective-permute-start.13) | collective-permute-done | bytes 114720 | tf_op jit(solution)/shard_map/ppermute | solution.py:520
  47.5 5.2 %collective-permute-done.14 = bf16[224,256]{1,0:T(8,128)(2,1)S(1)} collective-permute-done((bf16[224,256]{1,0:T(8,128)(2,1)S(1)}, bf16[224,256]{1,0:T(8,128)(2,1)S(1)}, u32[]{:S(2)}, u32[]{:S(2)}) %collective-permute-start.14) | collective-permute-done | bytes 114720 | tf_op jit(solution)/shard_map/ppermute | solution.py:520
  52.8 0.2 share.1
  53.0 0.1 collective-permute-start.23
  53.2 2.6 %collective-permute-start.19 = (bf16[224,256]{1,0:T(8,128)(2,1)S(1)}, bf16[224,256]{1,0:T(8,128)(2,1)S(1)}, u32[]{:S(2)}, u32[]{:S(2)}) collective-permute-start(bf16[224,256]{1,0:T(8,128)(2,1)S(1)} %add_convert_fusion.refs_0_), channel_id=1, source_target_pairs={{0,8},{1,9},{2,10},{3,11},{4,12},{5,13},{6,14},{7,15},{8,0},{9,1},... | collective-permute-start | bytes 344072 | tf_op jit(solution)/shard_map/ppermute | solution.py:520
  55.7 1.8 %collective-permute-start.21 = (bf16[224,256]{1,0:T(8,128)(2,1)S(1)}, bf16[224,256]{1,0:T(8,128)(2,1)S(1)}, u32[]{:S(2)}, u32[]{:S(2)}) collective-permute-start(bf16[224,256]{1,0:T(8,128)(2,1)S(1)} %add_convert_fusion.refs_0_), channel_id=1, source_target_pairs={{0,12},{1,13},{2,14},{3,15},{4,8},{5,9},{6,10},{7,11},{8,4},{9,5},... | collective-permute-start | bytes 344072 | tf_op jit(solution)/shard_map/ppermute | solution.py:520
  57.5 1.5 %collective-permute-start.16 = (bf16[224,256]{1,0:T(8,128)(2,1)S(1)}, bf16[224,256]{1,0:T(8,128)(2,1)S(1)}, u32[]{:S(2)}, u32[]{:S(2)}) collective-permute-start(bf16[224,256]{1,0:T(8,128)(2,1)S(1)} %add_convert_fusion.refs_0_), channel_id=1, source_target_pairs={{0,2},{1,3},{2,0},{3,1},{4,6},{5,7},{6,4},{7,5},{8,10},{9,11},{10,... | collective-permute-start | bytes 344072 | tf_op jit(solution)/shard_map/ppermute | solution.py:523
  59.0 1.5 %collective-permute-done.17.refs_2_ = bf16[224,256]{1,0:T(8,128)(2,1)S(1)} collective-permute-done((bf16[224,256]{1,0:T(8,128)(2,1)S(1)}, bf16[224,256]{1,0:T(8,128)(2,1)S(1)}, u32[]{:S(2)}, u32[]{:S(2)}) %collective-permute-start.17) | collective-permute-done | bytes 114720 | tf_op jit(solution)/shard_map/ppermute | solution.py:520
  60.5 1.5 %collective-permute-start.18 = (bf16[224,256]{1,0:T(8,128)(2,1)S(1)}, bf16[224,256]{1,0:T(8,128)(2,1)S(1)}, u32[]{:S(2)}, u32[]{:S(2)}) collective-permute-start(bf16[224,256]{1,0:T(8,128)(2,1)S(1)} %collective-permute-done.17.refs_2_), channel_id=1, source_target_pairs={{0,2},{1,3},{2,0},{3,1},{4,6},{5,7},{6,4},{7,5},{8,10},{9,11},{10,... | collective-permute-start | bytes 344072 | tf_op jit(solution)/shard_map/ppermute | solution.py:523
  62.0 3.0 %collective-permute-done.19.refs_4_ = bf16[224,256]{1,0:T(8,128)(2,1)S(1)} collective-permute-done((bf16[224,256]{1,0:T(8,128)(2,1)S(1)}, bf16[224,256]{1,0:T(8,128)(2,1)S(1)}, u32[]{:S(2)}, u32[]{:S(2)}) %collective-permute-start.19) | collective-permute-done | bytes 114720 | tf_op jit(solution)/shard_map/ppermute | solution.py:520
  65.0 1.5 %collective-permute-start.20 = (bf16[224,256]{1,0:T(8,128)(2,1)S(1)}, bf16[224,256]{1,0:T(8,128)(2,1)S(1)}, u32[]{:S(2)}, u32[]{:S(2)}) collective-permute-start(bf16[224,256]{1,0:T(8,128)(2,1)S(1)} %collective-permute-done.19.refs_4_), channel_id=1, source_target_pairs={{0,2},{1,3},{2,0},{3,1},{4,6},{5,7},{6,4},{7,5},{8,10},{9,11},{10,... | collective-permute-start | bytes 344072 | tf_op jit(solution)/shard_map/ppermute | solution.py:523
  66.5 0.5 collective-permute-start.22
  67.1 3.2 %collective-permute-done.20.refs_5_ = bf16[224,256]{1,0:T(8,128)(2,1)S(1)} collective-permute-done((bf16[224,256]{1,0:T(8,128)(2,1)S(1)}, bf16[224,256]{1,0:T(8,128)(2,1)S(1)}, u32[]{:S(2)}, u32[]{:S(2)}) %collective-permute-start.20) | collective-permute-done | bytes 114720 | tf_op jit(solution)/shard_map/ppermute | solution.py:523
  70.3 1.2 %collective-permute-done.22.refs_7_ = bf16[224,256]{1,0:T(8,128)(2,1)S(1)} collective-permute-done((bf16[224,256]{1,0:T(8,128)(2,1)S(1)}, bf16[224,256]{1,0:T(8,128)(2,1)S(1)}, u32[]{:S(2)}, u32[]{:S(2)}) %collective-permute-start.22) | collective-permute-done | bytes 114720 | tf_op jit(solution)/shard_map/ppermute | solution.py:523
  71.6 1.3 %gate_up.1 = (f32[128,768]{1,0:T(8,128)S(1)}, bf16[16,2048]{1,0:T(8,128)(2,1)S(1)}) custom-call(bf16[224,256]{1,0:T(8,128)(2,1)S(1)} %add_convert_fusion.refs_0_, bf16[224,256]{1,0:T(8,128)(2,1)S(1)} %collective-permute-done.16.refs_1_, bf16[224,256]{1,0:T(8,128)(2,1)S(1)} %collective-permute-done.17.refs_2_, ...), custom_call_target="tpu_custom_call" | custom-call | flops 1000000000 | bytes 3000000 | tf_op jit(solution)/shard_map/gate_up/pallas_call | solution.py:657
  72.9 0.1 collective-permute-start.24
  73.0 1.4 %gate_up_own.1 = (f32[128,768]{1,0:T(8,128)S(1)}, bf16[16,2048]{1,0:T(8,128)(2,1)S(1)}) custom-call(bf16[224,256]{1,0:T(8,128)(2,1)S(1)} %add_convert_fusion.refs_0_, bf16[224,256]{1,0:T(8,128)(2,1)S(1)} %collective-permute-done.16.refs_1_, bf16[224,256]{1,0:T(8,128)(2,1)S(1)} %collective-permute-done.17.refs_2_, ...), custom_call_target="tpu_custom_call" | custom-call | flops 1000000000 | bytes 3000000 | tf_op jit(solution)/shard_map/gate_up_own/pallas_call | solution.py:657
  74.4 0.3 collective-permute-done.24.came_ref
  74.7 0.8 hidden.1
  75.5 1.1 %collective-permute-start.30 = (bf16[8,7168]{1,0:T(8,128)(2,1)S(1)}, bf16[8,7168]{1,0:T(8,128)(2,1)S(1)}, u32[]{:S(2)}, u32[]{:S(2)}) collective-permute-start(bf16[8,7168]{1,0:T(8,128)(2,1)S(1)} %get-tuple-element.74), channel_id=1, source_target_pairs={{0,2},{1,3},{2,0},{3,1},{4,6},{5,7},{6,4},{7,5},{8,10},{9,11},{10,... | collective-permute-start | bytes 344072 | tf_op jit(solution)/shard_map/ppermute | solution.py:523
  76.5 1.0 %collective-permute-start.28 = (bf16[8,7168]{1,0:T(8,128)(2,1)S(1)}, bf16[8,7168]{1,0:T(8,128)(2,1)S(1)}, u32[]{:S(2)}, u32[]{:S(2)}) collective-permute-start(bf16[8,7168]{1,0:T(8,128)(2,1)S(1)} %get-tuple-element.72), channel_id=1, source_target_pairs={{0,2},{1,3},{2,0},{3,1},{4,6},{5,7},{6,4},{7,5},{8,10},{9,11},{10,... | collective-permute-start | bytes 344072 | tf_op jit(solution)/shard_map/ppermute | solution.py:523
  77.6 1.0 %collective-permute-start.26 = (bf16[8,7168]{1,0:T(8,128)(2,1)S(1)}, bf16[8,7168]{1,0:T(8,128)(2,1)S(1)}, u32[]{:S(2)}, u32[]{:S(2)}) collective-permute-start(bf16[8,7168]{1,0:T(8,128)(2,1)S(1)} %get-tuple-element.70), channel_id=1, source_target_pairs={{0,2},{1,3},{2,0},{3,1},{4,6},{5,7},{6,4},{7,5},{8,10},{9,11},{10,... | collective-permute-start | bytes 344072 | tf_op jit(solution)/shard_map/ppermute | solution.py:523
  78.6 1.0 %collective-permute-start.25 = (bf16[8,7168]{1,0:T(8,128)(2,1)S(1)}, bf16[8,7168]{1,0:T(8,128)(2,1)S(1)}, u32[]{:S(2)}, u32[]{:S(2)}) collective-permute-start(bf16[8,7168]{1,0:T(8,128)(2,1)S(1)} %get-tuple-element.68), channel_id=1, source_target_pairs={{0,2},{1,3},{2,0},{3,1},{4,6},{5,7},{6,4},{7,5},{8,10},{9,11},{10,... | collective-permute-start | bytes 344072 | tf_op jit(solution)/shard_map/ppermute | solution.py:523
  79.6 0.6 down.1
  80.2 1.4 %collective-permute-done.30.far_ref = bf16[8,7168]{1,0:T(8,128)(2,1)S(1)} collective-permute-done((bf16[8,7168]{1,0:T(8,128)(2,1)S(1)}, bf16[8,7168]{1,0:T(8,128)(2,1)S(1)}, u32[]{:S(2)}, u32[]{:S(2)}) %collective-permute-start.30) | collective-permute-done | bytes 114720 | tf_op jit(solution)/shard_map/ppermute | solution.py:523
  81.6 2.1 %collective-permute-start.31 = (bf16[8,7168]{1,0:T(8,128)(2,1)S(1)}, bf16[8,7168]{1,0:T(8,128)(2,1)S(1)}, u32[]{:S(2)}, u32[]{:S(2)}) collective-permute-start(bf16[8,7168]{1,0:T(8,128)(2,1)S(1)} %add.25), channel_id=1, source_target_pairs={{0,12},{1,13},{2,14},{3,15},{4,8},{5,9},{6,10},{7,11},{8,4},{9,5},... | collective-permute-start | bytes 344072 | tf_op jit(solution)/shard_map/ppermute | solution.py:520
  83.6 0.4 collective-permute-done.28.far_ref
  84.0 1.4 %collective-permute-start.29 = (bf16[8,7168]{1,0:T(8,128)(2,1)S(1)}, bf16[8,7168]{1,0:T(8,128)(2,1)S(1)}, u32[]{:S(2)}, u32[]{:S(2)}) collective-permute-start(bf16[8,7168]{1,0:T(8,128)(2,1)S(1)} %add.24), channel_id=1, source_target_pairs={{0,8},{1,9},{2,10},{3,11},{4,12},{5,13},{6,14},{7,15},{8,0},{9,1},... | collective-permute-start | bytes 344072 | tf_op jit(solution)/shard_map/ppermute | solution.py:520
  85.4 1.1 %collective-permute-done.26.far_ref = bf16[8,7168]{1,0:T(8,128)(2,1)S(1)} collective-permute-done((bf16[8,7168]{1,0:T(8,128)(2,1)S(1)}, bf16[8,7168]{1,0:T(8,128)(2,1)S(1)}, u32[]{:S(2)}, u32[]{:S(2)}) %collective-permute-start.26) | collective-permute-done | bytes 114720 | tf_op jit(solution)/shard_map/ppermute | solution.py:523
  86.5 0.8 collective-permute-start.27
  87.3 1.3 %collective-permute-done.32.refs_6_ = bf16[16,2048]{1,0:T(8,128)(2,1)S(1)} collective-permute-done((bf16[16,2048]{1,0:T(8,128)(2,1)S(1)}, bf16[16,2048]{1,0:T(8,128)(2,1)S(1)}, u32[]{:S(2)}, u32[]{:S(2)}) %collective-permute-start.32) | collective-permute-done | bytes 65568 | tf_op jit(solution)/shard_map/ppermute | solution.py:526
  88.6 0.6 collective-permute-done.31.refs_4_
  89.2 4.1 %collective-permute-done.29.refs_3_ = bf16[8,7168]{1,0:T(8,128)(2,1)S(1)} collective-permute-done((bf16[8,7168]{1,0:T(8,128)(2,1)S(1)}, bf16[8,7168]{1,0:T(8,128)(2,1)S(1)}, u32[]{:S(2)}, u32[]{:S(2)}) %collective-permute-start.29) | collective-permute-done | bytes 114720 | tf_op jit(solution)/shard_map/ppermute | solution.py:520
  93.3 0.1 collective-permute-done.27.refs_2_
  93.4 0.8 last.1
  (44 shorter events, 0.5 us)
Async XLA Ops:
  0.0 2.6 %copy-start.5 = (bf16[64,4096]{1,0:T(8,128)(2,1)S(1)}, bf16[64,4096]{1,0:T(8,128)(2,1)}, u32[]{:S(2)}) copy-start(bf16[64,4096]{1,0:T(8,128)(2,1)} %refs_9_.3) | copy-start | bytes 1572868
  0.0 2.6 %copy-start.6 = (bf16[64,4096]{1,0:T(8,128)(2,1)S(1)}, bf16[64,4096]{1,0:T(8,128)(2,1)}, u32[]{:S(2)}) copy-start(bf16[64,4096]{1,0:T(8,128)(2,1)} %refs_10_.3) | copy-start | bytes 1572868
  0.0 2.6 %copy-start.7 = (bf16[64,4096]{1,0:T(8,128)(2,1)S(1)}, bf16[64,4096]{1,0:T(8,128)(2,1)}, u32[]{:S(2)}) copy-start(bf16[64,4096]{1,0:T(8,128)(2,1)} %refs_11_.1) | copy-start | bytes 1572868
  2.6 1.0 %copy-start.4 = (bf16[64,4096]{1,0:T(8,128)(2,1)S(1)}, bf16[64,4096]{1,0:T(8,128)(2,1)}, u32[]{:S(2)}) copy-start(bf16[64,4096]{1,0:T(8,128)(2,1)} %weight_ref.3) | copy-start | bytes 1572868
  2.6 1.1 %copy-start.8 = (bf16[8,10240]{1,0:T(8,128)(2,1)S(1)}, bf16[8,10240]{1,0:T(8,128)(2,1)}, u32[]{:S(2)}) copy-start(bf16[8,10240]{1,0:T(8,128)(2,1)} %fetch.1.piece_ref.refs_0_) | copy-start | bytes 491524
  2.7 27.8 %collective-permute-start.7 = (bf16[192,4096]{1,0:T(8,128)(2,1)S(1)}, bf16[192,4096]{1,0:T(8,128)(2,1)S(1)}, u32[]{:S(2)}, u32[]{:S(2)}) collective-permute-start(bf16[192,4096]{1,0:T(8,128)(2,1)S(1)} %stack.1), channel_id=1, source_target_pairs={{0,1},{1,0},{2,3},{3,2},{4,5},{5,4},{6,7},{7,6},{8,9},{9,8},{10,11... | collective-permute-start | bytes 4718600 | tf_op jit(solution)/shard_map/ppermute | solution.py:526
  3.7 26.8 %copy-start.9 = (f32[4096]{0:T(1024)S(1)}, f32[4096]{0:T(1024)}, u32[]{:S(2)}) copy-start(f32[4096]{0:T(1024)} %param.23) | copy-start | bytes 49156
  3.7 21.7 %collective-permute-start = (bf16[8,26624]{1,0:T(8,128)(2,1)S(1)}, bf16[8,26624]{1,0:T(8,128)(2,1)S(1)}, u32[]{:S(2)}, u32[]{:S(2)}) collective-permute-start(bf16[8,26624]{1,0:T(8,128)(2,1)S(1)} %across.1), channel_id=1, source_target_pairs={{0,2},{1,3},{2,0},{3,1},{4,6},{5,7},{6,4},{7,5},{8,10},{9,11},{10,... | collective-permute-start | bytes 1277960 | tf_op jit(solution)/shard_map/ppermute | solution.py:523
  6.8 7.9 %collective-permute-start.1 = (bf16[8,10240]{1,0:T(8,128)(2,1)S(1)}, bf16[8,10240]{1,0:T(8,128)(2,1)S(1)}, u32[]{:S(2)}, u32[]{:S(2)}) collective-permute-start(bf16[8,10240]{1,0:T(8,128)(2,1)S(1)} %copy-done.8), channel_id=1, source_target_pairs={{0,4},{1,5},{2,6},{3,7},{4,0},{5,1},{6,2},{7,3},{8,12},{9,13},{10,... | collective-permute-start | bytes 491528 | tf_op jit(solution)/shard_map/ppermute | solution.py:520
  8.4 15.1 %collective-permute-start.3 = (bf16[8,10240]{1,0:T(8,128)(2,1)S(1)}, bf16[8,10240]{1,0:T(8,128)(2,1)S(1)}, u32[]{:S(2)}, u32[]{:S(2)}) collective-permute-start(bf16[8,10240]{1,0:T(8,128)(2,1)S(1)} %copy-done.8), channel_id=1, source_target_pairs={{0,8},{1,9},{2,10},{3,11},{4,12},{5,13},{6,14},{7,15},{8,0},{9,1},... | collective-permute-start | bytes 491528 | tf_op jit(solution)/shard_map/ppermute | solution.py:520
  11.0 13.0 %collective-permute-start.5 = (bf16[8,10240]{1,0:T(8,128)(2,1)S(1)}, bf16[8,10240]{1,0:T(8,128)(2,1)S(1)}, u32[]{:S(2)}, u32[]{:S(2)}) collective-permute-start(bf16[8,10240]{1,0:T(8,128)(2,1)S(1)} %copy-done.8), channel_id=1, source_target_pairs={{0,12},{1,13},{2,14},{3,15},{4,8},{5,9},{6,10},{7,11},{8,4},{9,5},... | collective-permute-start | bytes 491528 | tf_op jit(solution)/shard_map/ppermute | solution.py:520
  14.8 10.9 %collective-permute-start.2 = (bf16[8,10240]{1,0:T(8,128)(2,1)S(1)}, bf16[8,10240]{1,0:T(8,128)(2,1)S(1)}, u32[]{:S(2)}, u32[]{:S(2)}) collective-permute-start(bf16[8,10240]{1,0:T(8,128)(2,1)S(1)} %collective-permute-done.1.refs_2_), channel_id=1, source_target_pairs={{0,2},{1,3},{2,0},{3,1},{4,6},{5,7},{6,4},{7,5},{8,10},{9,11},{10,... | collective-permute-start | bytes 491528 | tf_op jit(solution)/shard_map/ppermute | solution.py:523
  23.4 5.3 %collective-permute-start.4 = (bf16[8,10240]{1,0:T(8,128)(2,1)S(1)}, bf16[8,10240]{1,0:T(8,128)(2,1)S(1)}, u32[]{:S(2)}, u32[]{:S(2)}) collective-permute-start(bf16[8,10240]{1,0:T(8,128)(2,1)S(1)} %collective-permute-done.3.refs_4_), channel_id=1, source_target_pairs={{0,2},{1,3},{2,0},{3,1},{4,6},{5,7},{6,4},{7,5},{8,10},{9,11},{10,... | collective-permute-start | bytes 491528 | tf_op jit(solution)/shard_map/ppermute | solution.py:523
  23.9 6.6 %collective-permute-start.6 = (bf16[8,10240]{1,0:T(8,128)(2,1)S(1)}, bf16[8,10240]{1,0:T(8,128)(2,1)S(1)}, u32[]{:S(2)}, u32[]{:S(2)}) collective-permute-start(bf16[8,10240]{1,0:T(8,128)(2,1)S(1)} %collective-permute-done.5.refs_6_), channel_id=1, source_target_pairs={{0,2},{1,3},{2,0},{3,1},{4,6},{5,7},{6,4},{7,5},{8,10},{9,11},{10,... | collective-permute-start | bytes 491528 | tf_op jit(solution)/shard_map/ppermute | solution.py:523
  25.6 8.4 %collective-permute-start.8 = (bf16[128,1024]{1,0:T(8,128)(2,1)S(1)}, bf16[128,1024]{1,0:T(8,128)(2,1)S(1)}, u32[]{:S(2)}, u32[]{:S(2)}) collective-permute-start(bf16[128,1024]{1,0:T(8,128)(2,1)S(1)} %get-tuple-element.49), channel_id=1, source_target_pairs={{0,1},{1,0},{2,3},{3,2},{4,5},{5,4},{6,7},{7,6},{8,9},{9,8},{10,11... | collective-permute-start | bytes 786440 | tf_op jit(solution)/shard_map/ppermute | solution.py:526
  30.5 2.1 %copy-start.10 = (s32[24,1]{0,1:T(1,128)S(1)}, s32[24,1]{0,1:T(1,128)}, u32[]{:S(2)}) copy-start(s32[24,1]{0,1:T(1,128)} %param.16) | copy-start | bytes 292
  30.5 2.1 %copy-start.11 = (s32[24]{0:T(128)S(1)}, s32[24]{0:T(128)}, u32[]{:S(2)}) copy-start(s32[24]{0:T(128)} %segment_ref.1) | copy-start | bytes 292
  32.5 1.5 %collective-permute-start.9 = (bf16[160,512]{1,0:T(8,128)(2,1)S(1)}, bf16[160,512]{1,0:T(8,128)(2,1)S(1)}, u32[]{:S(2)}, u32[]{:S(2)}) collective-permute-start(bf16[160,512]{1,0:T(8,128)(2,1)S(1)} %get-tuple-element.51), channel_id=1, source_target_pairs={{0,1},{1,0},{2,3},{3,2},{4,5},{5,4},{6,7},{7,6},{8,9},{9,8},{10,11... | collective-permute-start | bytes 491528 | tf_op jit(solution)/shard_map/ppermute | solution.py:526
  34.9 4.1 %collective-permute-start.10 = (bf16[112,128]{1,0:T(8,128)(2,1)S(1)}, bf16[112,128]{1,0:T(8,128)(2,1)S(1)}, u32[]{:S(2)}, u32[]{:S(2)}) collective-permute-start(bf16[112,128]{1,0:T(8,128)(2,1)S(1)} %get-tuple-element.53.refs_0_), channel_id=1, source_target_pairs={{0,2},{1,3},{2,0},{3,1},{4,6},{5,7},{6,4},{7,5},{8,10},{9,11},{10,... | collective-permute-start | bytes 86024 | tf_op jit(solution)/shard_map/ppermute | solution.py:523
  35.4 3.5 %collective-permute-start.11 = (bf16[112,128]{1,0:T(8,128)(2,1)S(1)}, bf16[112,128]{1,0:T(8,128)(2,1)S(1)}, u32[]{:S(2)}, u32[]{:S(2)}) collective-permute-start(bf16[112,128]{1,0:T(8,128)(2,1)S(1)} %get-tuple-element.53.refs_0_), channel_id=1, source_target_pairs={{0,1},{1,0},{2,3},{3,2},{4,5},{5,4},{6,7},{7,6},{8,9},{9,8},{10,11... | collective-permute-start | bytes 86024 | tf_op jit(solution)/shard_map/ppermute | solution.py:526
  35.6 3.5 %collective-permute-start.12 = (bf16[112,128]{1,0:T(8,128)(2,1)S(1)}, bf16[112,128]{1,0:T(8,128)(2,1)S(1)}, u32[]{:S(2)}, u32[]{:S(2)}) collective-permute-start(bf16[112,128]{1,0:T(8,128)(2,1)S(1)} %get-tuple-element.53.refs_0_), channel_id=1, source_target_pairs={{0,3},{1,2},{2,1},{3,0},{4,7},{5,6},{6,5},{7,4},{8,11},{9,10},{10,... | collective-permute-start | bytes 86024 | tf_op jit(solution)/shard_map/ppermute | solution.py:630
  39.1 13.7 %copy-start = (bf16[160,4096]{1,0:T(8,128)(2,1)S(1)}, bf16[160,4096]{1,0:T(8,128)(2,1)}, u32[]{:S(2)}) copy-start(bf16[160,4096]{1,0:T(8,128)(2,1)} %down_ref.4) | copy-start | bytes 3932164
  39.1 13.7 %copy-start.1 = (bf16[160,4096]{1,0:T(8,128)(2,1)S(1)}, bf16[160,4096]{1,0:T(8,128)(2,1)}, u32[]{:S(2)}) copy-start(bf16[160,4096]{1,0:T(8,128)(2,1)} %refs_9_.5) | copy-start | bytes 3932164
  39.1 13.7 %copy-start.2 = (bf16[160,4096]{1,0:T(8,128)(2,1)S(1)}, bf16[160,4096]{1,0:T(8,128)(2,1)}, u32[]{:S(2)}) copy-start(bf16[160,4096]{1,0:T(8,128)(2,1)} %refs_10_.5) | copy-start | bytes 3932164
  39.5 8.0 %collective-permute-start.13 = (bf16[224,256]{1,0:T(8,128)(2,1)S(1)}, bf16[224,256]{1,0:T(8,128)(2,1)S(1)}, u32[]{:S(2)}, u32[]{:S(2)}) collective-permute-start(bf16[224,256]{1,0:T(8,128)(2,1)S(1)} %get-tuple-element.57), channel_id=1, source_target_pairs={{0,12},{1,13},{2,14},{3,15},{4,8},{5,9},{6,10},{7,11},{8,4},{9,5},... | collective-permute-start | bytes 344072 | tf_op jit(solution)/shard_map/ppermute | solution.py:520
  41.7 11.0 %collective-permute-start.14 = (bf16[224,256]{1,0:T(8,128)(2,1)S(1)}, bf16[224,256]{1,0:T(8,128)(2,1)S(1)}, u32[]{:S(2)}, u32[]{:S(2)}) collective-permute-start(bf16[224,256]{1,0:T(8,128)(2,1)S(1)} %get-tuple-element.58), channel_id=1, source_target_pairs={{0,8},{1,9},{2,10},{3,11},{4,12},{5,13},{6,14},{7,15},{8,0},{9,1},... | collective-permute-start | bytes 344072 | tf_op jit(solution)/shard_map/ppermute | solution.py:520
  42.1 10.6 %collective-permute-start.15 = (bf16[224,256]{1,0:T(8,128)(2,1)S(1)}, bf16[224,256]{1,0:T(8,128)(2,1)S(1)}, u32[]{:S(2)}, u32[]{:S(2)}) collective-permute-start(bf16[224,256]{1,0:T(8,128)(2,1)S(1)} %get-tuple-element.59), channel_id=1, source_target_pairs={{0,4},{1,5},{2,6},{3,7},{4,0},{5,1},{6,2},{7,3},{8,12},{9,13},{10,... | collective-permute-start | bytes 344072 | tf_op jit(solution)/shard_map/ppermute | solution.py:520
  52.8 18.8 %copy-start.3 = (f32[4096]{0:T(1024)S(1)}, f32[4096]{0:T(1024)}, u32[]{:S(2)}) copy-start(f32[4096]{0:T(1024)} %param.24) | copy-start | bytes 49156
  53.0 18.6 %collective-permute-start.23 = (bf16[320,4096]{1,0:T(8,128)(2,1)S(1)}, bf16[320,4096]{1,0:T(8,128)(2,1)S(1)}, u32[]{:S(2)}, u32[]{:S(2)}) collective-permute-start(bf16[320,4096]{1,0:T(8,128)(2,1)S(1)} %share.1), channel_id=1, source_target_pairs={{0,1},{1,0},{2,3},{3,2},{4,5},{5,4},{6,7},{7,6},{8,9},{9,8},{10,11... | collective-permute-start | bytes 7864328 | tf_op jit(solution)/shard_map/ppermute | solution.py:526
  53.1 7.4 %collective-permute-start.17 = (bf16[224,256]{1,0:T(8,128)(2,1)S(1)}, bf16[224,256]{1,0:T(8,128)(2,1)S(1)}, u32[]{:S(2)}, u32[]{:S(2)}) collective-permute-start(bf16[224,256]{1,0:T(8,128)(2,1)S(1)} %add_convert_fusion.refs_0_), channel_id=1, source_target_pairs={{0,4},{1,5},{2,6},{3,7},{4,0},{5,1},{6,2},{7,3},{8,12},{9,13},{10,... | collective-permute-start | bytes 344072 | tf_op jit(solution)/shard_map/ppermute | solution.py:520
  53.2 11.9 %collective-permute-start.19 = (bf16[224,256]{1,0:T(8,128)(2,1)S(1)}, bf16[224,256]{1,0:T(8,128)(2,1)S(1)}, u32[]{:S(2)}, u32[]{:S(2)}) collective-permute-start(bf16[224,256]{1,0:T(8,128)(2,1)S(1)} %add_convert_fusion.refs_0_), channel_id=1, source_target_pairs={{0,8},{1,9},{2,10},{3,11},{4,12},{5,13},{6,14},{7,15},{8,0},{9,1},... | collective-permute-start | bytes 344072 | tf_op jit(solution)/shard_map/ppermute | solution.py:520
  55.7 10.8 %collective-permute-start.21 = (bf16[224,256]{1,0:T(8,128)(2,1)S(1)}, bf16[224,256]{1,0:T(8,128)(2,1)S(1)}, u32[]{:S(2)}, u32[]{:S(2)}) collective-permute-start(bf16[224,256]{1,0:T(8,128)(2,1)S(1)} %add_convert_fusion.refs_0_), channel_id=1, source_target_pairs={{0,12},{1,13},{2,14},{3,15},{4,8},{5,9},{6,10},{7,11},{8,4},{9,5},... | collective-permute-start | bytes 344072 | tf_op jit(solution)/shard_map/ppermute | solution.py:520
  57.5 9.5 %collective-permute-start.16 = (bf16[224,256]{1,0:T(8,128)(2,1)S(1)}, bf16[224,256]{1,0:T(8,128)(2,1)S(1)}, u32[]{:S(2)}, u32[]{:S(2)}) collective-permute-start(bf16[224,256]{1,0:T(8,128)(2,1)S(1)} %add_convert_fusion.refs_0_), channel_id=1, source_target_pairs={{0,2},{1,3},{2,0},{3,1},{4,6},{5,7},{6,4},{7,5},{8,10},{9,11},{10,... | collective-permute-start | bytes 344072 | tf_op jit(solution)/shard_map/ppermute | solution.py:523
  60.5 6.6 %collective-permute-start.18 = (bf16[224,256]{1,0:T(8,128)(2,1)S(1)}, bf16[224,256]{1,0:T(8,128)(2,1)S(1)}, u32[]{:S(2)}, u32[]{:S(2)}) collective-permute-start(bf16[224,256]{1,0:T(8,128)(2,1)S(1)} %collective-permute-done.17.refs_2_), channel_id=1, source_target_pairs={{0,2},{1,3},{2,0},{3,1},{4,6},{5,7},{6,4},{7,5},{8,10},{9,11},{10,... | collective-permute-start | bytes 344072 | tf_op jit(solution)/shard_map/ppermute | solution.py:523
  65.0 5.3 %collective-permute-start.20 = (bf16[224,256]{1,0:T(8,128)(2,1)S(1)}, bf16[224,256]{1,0:T(8,128)(2,1)S(1)}, u32[]{:S(2)}, u32[]{:S(2)}) collective-permute-start(bf16[224,256]{1,0:T(8,128)(2,1)S(1)} %collective-permute-done.19.refs_4_), channel_id=1, source_target_pairs={{0,2},{1,3},{2,0},{3,1},{4,6},{5,7},{6,4},{7,5},{8,10},{9,11},{10,... | collective-permute-start | bytes 344072 | tf_op jit(solution)/shard_map/ppermute | solution.py:523
  66.5 5.0 %collective-permute-start.22 = (bf16[224,256]{1,0:T(8,128)(2,1)S(1)}, bf16[224,256]{1,0:T(8,128)(2,1)S(1)}, u32[]{:S(2)}, u32[]{:S(2)}) collective-permute-start(bf16[224,256]{1,0:T(8,128)(2,1)S(1)} %collective-permute-done.21.refs_6_), channel_id=1, source_target_pairs={{0,2},{1,3},{2,0},{3,1},{4,6},{5,7},{6,4},{7,5},{8,10},{9,11},{10,... | collective-permute-start | bytes 344072 | tf_op jit(solution)/shard_map/ppermute | solution.py:523
  72.9 1.8 %collective-permute-start.24 = (f32[128,768]{1,0:T(8,128)S(1)}, f32[128,768]{1,0:T(8,128)S(1)}, u32[]{:S(2)}, u32[]{:S(2)}) collective-permute-start(f32[128,768]{1,0:T(8,128)S(1)} %get-tuple-element.63), channel_id=1, source_target_pairs={{0,1},{1,0},{2,3},{3,2},{4,5},{5,4},{6,7},{7,6},{8,9},{9,8},{10,11... | collective-permute-start | bytes 1179656 | tf_op jit(solution)/shard_map/ppermute | solution.py:526
  75.5 6.1 %collective-permute-start.30 = (bf16[8,7168]{1,0:T(8,128)(2,1)S(1)}, bf16[8,7168]{1,0:T(8,128)(2,1)S(1)}, u32[]{:S(2)}, u32[]{:S(2)}) collective-permute-start(bf16[8,7168]{1,0:T(8,128)(2,1)S(1)} %get-tuple-element.74), channel_id=1, source_target_pairs={{0,2},{1,3},{2,0},{3,1},{4,6},{5,7},{6,4},{7,5},{8,10},{9,11},{10,... | collective-permute-start | bytes 344072 | tf_op jit(solution)/shard_map/ppermute | solution.py:523
  76.5 7.5 %collective-permute-start.28 = (bf16[8,7168]{1,0:T(8,128)(2,1)S(1)}, bf16[8,7168]{1,0:T(8,128)(2,1)S(1)}, u32[]{:S(2)}, u32[]{:S(2)}) collective-permute-start(bf16[8,7168]{1,0:T(8,128)(2,1)S(1)} %get-tuple-element.72), channel_id=1, source_target_pairs={{0,2},{1,3},{2,0},{3,1},{4,6},{5,7},{6,4},{7,5},{8,10},{9,11},{10,... | collective-permute-start | bytes 344072 | tf_op jit(solution)/shard_map/ppermute | solution.py:523
  77.6 8.9 %collective-permute-start.26 = (bf16[8,7168]{1,0:T(8,128)(2,1)S(1)}, bf16[8,7168]{1,0:T(8,128)(2,1)S(1)}, u32[]{:S(2)}, u32[]{:S(2)}) collective-permute-start(bf16[8,7168]{1,0:T(8,128)(2,1)S(1)} %get-tuple-element.70), channel_id=1, source_target_pairs={{0,2},{1,3},{2,0},{3,1},{4,6},{5,7},{6,4},{7,5},{8,10},{9,11},{10,... | collective-permute-start | bytes 344072 | tf_op jit(solution)/shard_map/ppermute | solution.py:523
  78.6 10.0 %collective-permute-start.25 = (bf16[8,7168]{1,0:T(8,128)(2,1)S(1)}, bf16[8,7168]{1,0:T(8,128)(2,1)S(1)}, u32[]{:S(2)}, u32[]{:S(2)}) collective-permute-start(bf16[8,7168]{1,0:T(8,128)(2,1)S(1)} %get-tuple-element.68), channel_id=1, source_target_pairs={{0,2},{1,3},{2,0},{3,1},{4,6},{5,7},{6,4},{7,5},{8,10},{9,11},{10,... | collective-permute-start | bytes 344072 | tf_op jit(solution)/shard_map/ppermute | solution.py:523
  81.6 7.6 %collective-permute-start.31 = (bf16[8,7168]{1,0:T(8,128)(2,1)S(1)}, bf16[8,7168]{1,0:T(8,128)(2,1)S(1)}, u32[]{:S(2)}, u32[]{:S(2)}) collective-permute-start(bf16[8,7168]{1,0:T(8,128)(2,1)S(1)} %add.25), channel_id=1, source_target_pairs={{0,12},{1,13},{2,14},{3,15},{4,8},{5,9},{6,10},{7,11},{8,4},{9,5},... | collective-permute-start | bytes 344072 | tf_op jit(solution)/shard_map/ppermute | solution.py:520
  84.0 9.3 %collective-permute-start.29 = (bf16[8,7168]{1,0:T(8,128)(2,1)S(1)}, bf16[8,7168]{1,0:T(8,128)(2,1)S(1)}, u32[]{:S(2)}, u32[]{:S(2)}) collective-permute-start(bf16[8,7168]{1,0:T(8,128)(2,1)S(1)} %add.24), channel_id=1, source_target_pairs={{0,8},{1,9},{2,10},{3,11},{4,12},{5,13},{6,14},{7,15},{8,0},{9,1},... | collective-permute-start | bytes 344072 | tf_op jit(solution)/shard_map/ppermute | solution.py:520
  86.5 6.9 %collective-permute-start.27 = (bf16[8,7168]{1,0:T(8,128)(2,1)S(1)}, bf16[8,7168]{1,0:T(8,128)(2,1)S(1)}, u32[]{:S(2)}, u32[]{:S(2)}) collective-permute-start(bf16[8,7168]{1,0:T(8,128)(2,1)S(1)} %add.23), channel_id=1, source_target_pairs={{0,4},{1,5},{2,6},{3,7},{4,0},{5,1},{6,2},{7,3},{8,12},{9,13},{10,... | collective-permute-start | bytes 344072 | tf_op jit(solution)/shard_map/ppermute | solution.py:520
  87.3 1.3 %collective-permute-start.32 = (bf16[16,2048]{1,0:T(8,128)(2,1)S(1)}, bf16[16,2048]{1,0:T(8,128)(2,1)S(1)}, u32[]{:S(2)}, u32[]{:S(2)}) collective-permute-start(bf16[16,2048]{1,0:T(8,128)(2,1)S(1)} %get-tuple-element.76), channel_id=1, source_target_pairs={{0,1},{1,0},{2,3},{3,2},{4,5},{5,4},{6,7},{7,6},{8,9},{9,8},{10,11... | collective-permute-start | bytes 196616 | tf_op jit(solution)/shard_map/ppermute | solution.py:526

commit v8 on v7

--- a/solution.py
+++ b/solution.py
@@ -478,21 +478,24 @@
     out_ref[...] = (near_ref[...] + far_ref[...].astype(jnp.float32)).astype(jnp.bfloat16)
 
 
-def last_kernel(count, *refs):
-    near_ref, far_ref = refs[0], refs[1]
-    arrived = refs[2 : 2 + count]
-    kept_ref, kept_other_ref, out_ref, total_ref = refs[2 + count :]
+def base_kernel(near_ref, far_ref, kept_ref, kept_other_ref, out_ref):
     ci = place()[3]
     rows = out_ref.shape[0]
     half = kept_ref.shape[1]
     kept, other = kept_ref[...].astype(jnp.float32), kept_other_ref[...].astype(jnp.float32)
-    total = near_ref[...] + far_ref[...].astype(jnp.float32)
-    for ref in arrived:
+    low, high = jnp.where(ci == 0, kept, other), jnp.where(ci == 0, other, kept)
+    unpack(near_ref[...] + far_ref[...].astype(jnp.float32), out_ref)
+    out_ref[:, :half] = low[:rows] + out_ref[:, :half]
+    out_ref[:, half:] = high[:rows] + out_ref[:, half:]
+
+
+def last_kernel(base_ref, *refs):
+    arrived, (out_ref, total_ref) = refs[:-2], refs[-2:]
+    total = arrived[0][...].astype(jnp.float32)
+    for ref in arrived[1:]:
         total = total + ref[...].astype(jnp.float32)
-    low, high = jnp.where(ci == 0, kept, other), jnp.where(ci == 0, other, kept)
     unpack(total, total_ref)
-    out_ref[:, :half] = (low[:rows] + total_ref[:, :half]).astype(jnp.bfloat16)
-    out_ref[:, half:] = (high[:rows] + total_ref[:, half:]).astype(jnp.bfloat16)
+    out_ref[...] = (base_ref[...] + total_ref[...]).astype(jnp.bfloat16)
 
 
 def body(
@@ -686,13 +689,16 @@
     for k in range(1, nz):
         part = kernel_call(add_kernel, chunk, [VMEM, VMEM], name="add")(near[k], moved[k])
         arrived.append(along_z(part, k))
+    base = kernel_call(
+        base_kernel, shape((rows_here, features), f32), [VMEM] * 4, name="base"
+    )(near[0], moved[0], kept, kept_other)
     return kernel_call(
-        functools.partial(last_kernel, len(arrived)),
+        last_kernel,
         shape((rows_here, features), bf16),
-        [VMEM] * (len(arrived) + 4),
+        [VMEM] * (len(arrived) + 1),
         [pltpu.VMEM((rows_here, features), f32)],
         name="last",
-    )(near[0], moved[0], *arrived, kept, kept_other)
+    )(base, *arrived)
 
 
 def solution(mesh):

time: 94.4 us -> 94.1 us (level)
    ppermute x7, waiting for transfers between devices: 1.6 us -> 0.35 us  [across_core(): return lax.ppermute(value, AXIS, [(i, i ^ 1) for i in range(devices)])]
  transfers between devices with their start and end apart: 33 -> 33, of which waited for: 20 -> 19; matrix products, arithmetic and copies ran while one was open for 0% -> 0% of each run, Pallas kernels for 6% -> 6%
where the time goes in v8:
time: 94.1 us; the launch traced here: 93.8 us
  waiting for transfers between devices  44.8 us (48%)
  starting transfers between devices  35.4 us (38%)
  Pallas kernels  12.6 us (13%)
    ppermute x12, waiting for transfers between devices, along_z(): return lax.ppermute(value, AXIS, [(i, i ^ 4 * k) for i in range(devices)])  30.1 us
    ppermute x12, starting transfers between devices, along_z(): return lax.ppermute(value, AXIS, [(i, i ^ 4 * k) for i in range(devices)])  18 us
    ppermute x13, starting transfers between devices, across_y(): return lax.ppermute(value, AXIS, [(i, i ^ 2) for i in range(devices)])  15 us
    ppermute x13, waiting for transfers between devices, across_y(): return lax.ppermute(value, AXIS, [(i, i ^ 2) for i in range(devices)])  14.3 us
    pallas_call x2, Pallas kernels, gate_up(): kernel_call(functools.partial(gate_kernel, rows_here, chunk_rows, own), (...  2.71 us
    pallas_call x1, Pallas kernels, body(): kernel_call(fetch_kernel, shape((8, full * features + halved * half), bf1...  2.6 us
    pallas_call x1, Pallas kernels, body(): kernel_call(functools.partial(projection_kernel, query_rows + CAP * BLK),...  1.98 us
  transfers between devices with their start and end apart: 33, of which 19 were waited for; matrix products, arithmetic and copies ran while one was open for 0% of the time, Pallas kernels for 6%

profile of v8, /device:TPU:0, one launch (start us, length us, event | category | flops | bytes accessed | tf_op | source)
XLA Modules:
  0.0 93.8 jit_solution(8428411212836143381)
XLA Ops:
  0.0 2.6 %fetch.1.piece_ref.refs_0_ = bf16[8,10240]{1,0:T(8,128)(2,1)} custom-call(s32[24]{0:T(128)} %bitcast.6, s32[24]{0:T(128)} %row_ref.1, bf16[64,4,4096]{2,1,0:T(4,128)(2,1)} %corpus_ref.1, bf16[8,4096]{1,0:T(8,128)(2,1)} %query_ref.1), custom_call_target="tpu_custom_call" | custom-call | flops 1000000000 | bytes 3000000 | tf_op jit(solution)/shard_map/fetch/pallas_call | solution.py:561
  2.7 0.1 stack.1
  2.8 0.5 collective-permute-start.7
  3.3 0.4 copy-done.4
  3.8 3.0 %collective-permute-start = (bf16[8,26624]{1,0:T(8,128)(2,1)S(1)}, bf16[8,26624]{1,0:T(8,128)(2,1)S(1)}, u32[]{:S(2)}, u32[]{:S(2)}) collective-permute-start(bf16[8,26624]{1,0:T(8,128)(2,1)S(1)} %across.1), channel_id=1, source_target_pairs={{0,2},{1,3},{2,0},{3,1},{4,6},{5,7},{6,4},{7,5},{8,10},{9,11},{10,... | collective-permute-start | bytes 1277960 | tf_op jit(solution)/shard_map/ppermute | solution.py:526
  6.8 1.6 %collective-permute-start.1 = (bf16[8,10240]{1,0:T(8,128)(2,1)S(1)}, bf16[8,10240]{1,0:T(8,128)(2,1)S(1)}, u32[]{:S(2)}, u32[]{:S(2)}) collective-permute-start(bf16[8,10240]{1,0:T(8,128)(2,1)S(1)} %copy-done.8), channel_id=1, source_target_pairs={{0,4},{1,5},{2,6},{3,7},{4,0},{5,1},{6,2},{7,3},{8,12},{9,13},{10,... | collective-permute-start | bytes 491528 | tf_op jit(solution)/shard_map/ppermute | solution.py:523
  8.4 2.5 %collective-permute-start.3 = (bf16[8,10240]{1,0:T(8,128)(2,1)S(1)}, bf16[8,10240]{1,0:T(8,128)(2,1)S(1)}, u32[]{:S(2)}, u32[]{:S(2)}) collective-permute-start(bf16[8,10240]{1,0:T(8,128)(2,1)S(1)} %copy-done.8), channel_id=1, source_target_pairs={{0,8},{1,9},{2,10},{3,11},{4,12},{5,13},{6,14},{7,15},{8,0},{9,1},... | collective-permute-start | bytes 491528 | tf_op jit(solution)/shard_map/ppermute | solution.py:523
  11.0 0.3 collective-permute-start.5
  11.2 3.5 %collective-permute-done.1.refs_2_ = bf16[8,10240]{1,0:T(8,128)(2,1)S(1)} collective-permute-done((bf16[8,10240]{1,0:T(8,128)(2,1)S(1)}, bf16[8,10240]{1,0:T(8,128)(2,1)S(1)}, u32[]{:S(2)}, u32[]{:S(2)}) %collective-permute-start.1) | collective-permute-done | bytes 163872 | tf_op jit(solution)/shard_map/ppermute | solution.py:523
  14.7 0.3 collective-permute-start.2
  15.0 8.5 %collective-permute-done.3.refs_4_ = bf16[8,10240]{1,0:T(8,128)(2,1)S(1)} collective-permute-done((bf16[8,10240]{1,0:T(8,128)(2,1)S(1)}, bf16[8,10240]{1,0:T(8,128)(2,1)S(1)}, u32[]{:S(2)}, u32[]{:S(2)}) %collective-permute-start.3) | collective-permute-done | bytes 163872 | tf_op jit(solution)/shard_map/ppermute | solution.py:523
  23.5 0.5 collective-permute-start.4
  24.0 1.6 %collective-permute-start.6 = (bf16[8,10240]{1,0:T(8,128)(2,1)S(1)}, bf16[8,10240]{1,0:T(8,128)(2,1)S(1)}, u32[]{:S(2)}, u32[]{:S(2)}) collective-permute-start(bf16[8,10240]{1,0:T(8,128)(2,1)S(1)} %collective-permute-done.5.refs_6_), channel_id=1, source_target_pairs={{0,2},{1,3},{2,0},{3,1},{4,6},{5,7},{6,4},{7,5},{8,10},{9,11},{10,... | collective-permute-start | bytes 491528 | tf_op jit(solution)/shard_map/ppermute | solution.py:526
  25.5 0.1 pairs.1
  25.6 0.1 collective-permute-start.8
  25.7 3.1 %collective-permute-done.4.refs_5_ = bf16[8,10240]{1,0:T(8,128)(2,1)S(1)} collective-permute-done((bf16[8,10240]{1,0:T(8,128)(2,1)S(1)}, bf16[8,10240]{1,0:T(8,128)(2,1)S(1)}, u32[]{:S(2)}, u32[]{:S(2)}) %collective-permute-start.4) | collective-permute-done | bytes 163872 | tf_op jit(solution)/shard_map/ppermute | solution.py:526
  28.8 1.8 %collective-permute-done.6.refs_7_ = bf16[8,10240]{1,0:T(8,128)(2,1)S(1)} collective-permute-done((bf16[8,10240]{1,0:T(8,128)(2,1)S(1)}, bf16[8,10240]{1,0:T(8,128)(2,1)S(1)}, u32[]{:S(2)}, u32[]{:S(2)}) %collective-permute-start.6) | collective-permute-done | bytes 163872 | tf_op jit(solution)/shard_map/ppermute | solution.py:526
  30.6 2.0 %project.1 = (bf16[160,512]{1,0:T(8,128)(2,1)S(1)}, bf16[160,512]{1,0:T(8,128)(2,1)S(1)}) custom-call(bf16[8,10240]{1,0:T(8,128)(2,1)S(1)} %copy-done.8, bf16[8,26624]{1,0:T(8,128)(2,1)S(1)} %collective-permute-done.refs_1_.far_ref, bf16[8,10240]{1,0:T(8,128)(2,1)S(1)} %collective-permute-done.1.refs_2_, ...), custom_call_target="tpu_custom_call" | custom-call | flops 10000000000 | bytes 30000000 | tf_op jit(solution)/shard_map/project/pallas_call | solution.py:595
  32.7 1.3 %plan.1 = (bf16[224,160]{1,0:T(8,128)(2,1)S(1)}, bf16[224,160]{1,0:T(8,128)(2,1)S(1)}, f32[224,224]{1,0:T(8,128)S(1)}) custom-call(s32[24]{0:T(128)S(1)} %bitcast.7, s32[24]{0:T(128)S(1)} %copy-done.11), custom_call_target="tpu_custom_call" | custom-call | flops 1000000000 | bytes 3000000 | tf_op jit(solution)/shard_map/plan/pallas_call | solution.py:613
  34.0 0.9 attend.1
  34.9 0.5 collective-permute-start.10
  35.5 0.2 collective-permute-start.11
  35.7 1.5 %collective-permute-start.12 = (bf16[112,128]{1,0:T(8,128)(2,1)S(1)}, bf16[112,128]{1,0:T(8,128)(2,1)S(1)}, u32[]{:S(2)}, u32[]{:S(2)}) collective-permute-start(bf16[112,128]{1,0:T(8,128)(2,1)S(1)} %get-tuple-element.53.refs_0_), channel_id=1, source_target_pairs={{0,3},{1,2},{2,1},{3,0},{4,7},{5,6},{6,5},{7,4},{8,11},{9,10},{10,... | collective-permute-start | bytes 86024 | tf_op jit(solution)/shard_map/ppermute | solution.py:633
  37.1 1.9 %collective-permute-done.10.refs_1_ = bf16[112,128]{1,0:T(8,128)(2,1)S(1)} collective-permute-done((bf16[112,128]{1,0:T(8,128)(2,1)S(1)}, bf16[112,128]{1,0:T(8,128)(2,1)S(1)}, u32[]{:S(2)}, u32[]{:S(2)}) %collective-permute-start.10) | collective-permute-done | bytes 28704 | tf_op jit(solution)/shard_map/ppermute | solution.py:526
  39.1 0.1 collective-permute-done.12.refs_3_
  39.2 0.4 out.1
  39.6 2.1 %collective-permute-start.13 = (bf16[224,256]{1,0:T(8,128)(2,1)S(1)}, bf16[224,256]{1,0:T(8,128)(2,1)S(1)}, u32[]{:S(2)}, u32[]{:S(2)}) collective-permute-start(bf16[224,256]{1,0:T(8,128)(2,1)S(1)} %get-tuple-element.57), channel_id=1, source_target_pairs={{0,12},{1,13},{2,14},{3,15},{4,8},{5,9},{6,10},{7,11},{8,4},{9,5},... | collective-permute-start | bytes 344072 | tf_op jit(solution)/shard_map/ppermute | solution.py:523
  41.7 0.4 collective-permute-start.14
  42.1 2.0 %collective-permute-start.15 = (bf16[224,256]{1,0:T(8,128)(2,1)S(1)}, bf16[224,256]{1,0:T(8,128)(2,1)S(1)}, u32[]{:S(2)}, u32[]{:S(2)}) collective-permute-start(bf16[224,256]{1,0:T(8,128)(2,1)S(1)} %get-tuple-element.59), channel_id=1, source_target_pairs={{0,4},{1,5},{2,6},{3,7},{4,0},{5,1},{6,2},{7,3},{8,12},{9,13},{10,... | collective-permute-start | bytes 344072 | tf_op jit(solution)/shard_map/ppermute | solution.py:523
  44.1 3.5 %collective-permute-done.13 = bf16[224,256]{1,0:T(8,128)(2,1)S(1)} collective-permute-done((bf16[224,256]{1,0:T(8,128)(2,1)S(1)}, bf16[224,256]{1,0:T(8,128)(2,1)S(1)}, u32[]{:S(2)}, u32[]{:S(2)}) %collective-permute-start.13) | collective-permute-done | bytes 114720 | tf_op jit(solution)/shard_map/ppermute | solution.py:523
  47.6 5.1 %collective-permute-done.14 = bf16[224,256]{1,0:T(8,128)(2,1)S(1)} collective-permute-done((bf16[224,256]{1,0:T(8,128)(2,1)S(1)}, bf16[224,256]{1,0:T(8,128)(2,1)S(1)}, u32[]{:S(2)}, u32[]{:S(2)}) %collective-permute-start.14) | collective-permute-done | bytes 114720 | tf_op jit(solution)/shard_map/ppermute | solution.py:523
  52.8 0.2 share.1
  53.0 0.1 collective-permute-start.23
  53.0 0.1 collective-permute-start.17
  53.1 2.6 %collective-permute-start.19 = (bf16[224,256]{1,0:T(8,128)(2,1)S(1)}, bf16[224,256]{1,0:T(8,128)(2,1)S(1)}, u32[]{:S(2)}, u32[]{:S(2)}) collective-permute-start(bf16[224,256]{1,0:T(8,128)(2,1)S(1)} %add_convert_fusion.refs_0_), channel_id=1, source_target_pairs={{0,8},{1,9},{2,10},{3,11},{4,12},{5,13},{6,14},{7,15},{8,0},{9,1},... | collective-permute-start | bytes 344072 | tf_op jit(solution)/shard_map/ppermute | solution.py:523
  55.7 1.8 %collective-permute-start.21 = (bf16[224,256]{1,0:T(8,128)(2,1)S(1)}, bf16[224,256]{1,0:T(8,128)(2,1)S(1)}, u32[]{:S(2)}, u32[]{:S(2)}) collective-permute-start(bf16[224,256]{1,0:T(8,128)(2,1)S(1)} %add_convert_fusion.refs_0_), channel_id=1, source_target_pairs={{0,12},{1,13},{2,14},{3,15},{4,8},{5,9},{6,10},{7,11},{8,4},{9,5},... | collective-permute-start | bytes 344072 | tf_op jit(solution)/shard_map/ppermute | solution.py:523
  57.5 1.5 %collective-permute-start.16 = (bf16[224,256]{1,0:T(8,128)(2,1)S(1)}, bf16[224,256]{1,0:T(8,128)(2,1)S(1)}, u32[]{:S(2)}, u32[]{:S(2)}) collective-permute-start(bf16[224,256]{1,0:T(8,128)(2,1)S(1)} %add_convert_fusion.refs_0_), channel_id=1, source_target_pairs={{0,2},{1,3},{2,0},{3,1},{4,6},{5,7},{6,4},{7,5},{8,10},{9,11},{10,... | collective-permute-start | bytes 344072 | tf_op jit(solution)/shard_map/ppermute | solution.py:526
  59.0 1.5 %collective-permute-done.17.refs_2_ = bf16[224,256]{1,0:T(8,128)(2,1)S(1)} collective-permute-done((bf16[224,256]{1,0:T(8,128)(2,1)S(1)}, bf16[224,256]{1,0:T(8,128)(2,1)S(1)}, u32[]{:S(2)}, u32[]{:S(2)}) %collective-permute-start.17) | collective-permute-done | bytes 114720 | tf_op jit(solution)/shard_map/ppermute | solution.py:523
  60.5 1.5 %collective-permute-start.18 = (bf16[224,256]{1,0:T(8,128)(2,1)S(1)}, bf16[224,256]{1,0:T(8,128)(2,1)S(1)}, u32[]{:S(2)}, u32[]{:S(2)}) collective-permute-start(bf16[224,256]{1,0:T(8,128)(2,1)S(1)} %collective-permute-done.17.refs_2_), channel_id=1, source_target_pairs={{0,2},{1,3},{2,0},{3,1},{4,6},{5,7},{6,4},{7,5},{8,10},{9,11},{10,... | collective-permute-start | bytes 344072 | tf_op jit(solution)/shard_map/ppermute | solution.py:526
  62.0 3.0 %collective-permute-done.19.refs_4_ = bf16[224,256]{1,0:T(8,128)(2,1)S(1)} collective-permute-done((bf16[224,256]{1,0:T(8,128)(2,1)S(1)}, bf16[224,256]{1,0:T(8,128)(2,1)S(1)}, u32[]{:S(2)}, u32[]{:S(2)}) %collective-permute-start.19) | collective-permute-done | bytes 114720 | tf_op jit(solution)/shard_map/ppermute | solution.py:523
  65.0 1.5 %collective-permute-start.20 = (bf16[224,256]{1,0:T(8,128)(2,1)S(1)}, bf16[224,256]{1,0:T(8,128)(2,1)S(1)}, u32[]{:S(2)}, u32[]{:S(2)}) collective-permute-start(bf16[224,256]{1,0:T(8,128)(2,1)S(1)} %collective-permute-done.19.refs_4_), channel_id=1, source_target_pairs={{0,2},{1,3},{2,0},{3,1},{4,6},{5,7},{6,4},{7,5},{8,10},{9,11},{10,... | collective-permute-start | bytes 344072 | tf_op jit(solution)/shard_map/ppermute | solution.py:526
  66.5 0.5 collective-permute-start.22
  67.0 2.8 %collective-permute-done.20.refs_5_ = bf16[224,256]{1,0:T(8,128)(2,1)S(1)} collective-permute-done((bf16[224,256]{1,0:T(8,128)(2,1)S(1)}, bf16[224,256]{1,0:T(8,128)(2,1)S(1)}, u32[]{:S(2)}, u32[]{:S(2)}) %collective-permute-start.20) | collective-permute-done | bytes 114720 | tf_op jit(solution)/shard_map/ppermute | solution.py:526
  69.8 1.5 %collective-permute-done.22.refs_7_ = bf16[224,256]{1,0:T(8,128)(2,1)S(1)} collective-permute-done((bf16[224,256]{1,0:T(8,128)(2,1)S(1)}, bf16[224,256]{1,0:T(8,128)(2,1)S(1)}, u32[]{:S(2)}, u32[]{:S(2)}) %collective-permute-start.22) | collective-permute-done | bytes 114720 | tf_op jit(solution)/shard_map/ppermute | solution.py:526
  71.3 1.3 %gate_up.1 = (f32[128,768]{1,0:T(8,128)S(1)}, bf16[16,2048]{1,0:T(8,128)(2,1)S(1)}) custom-call(bf16[224,256]{1,0:T(8,128)(2,1)S(1)} %add_convert_fusion.refs_0_, bf16[224,256]{1,0:T(8,128)(2,1)S(1)} %collective-permute-done.16.refs_1_, bf16[224,256]{1,0:T(8,128)(2,1)S(1)} %collective-permute-done.17.refs_2_, ...), custom_call_target="tpu_custom_call" | custom-call | flops 1000000000 | bytes 3000000 | tf_op jit(solution)/shard_map/gate_up/pallas_call | solution.py:660
  72.7 1.4 %gate_up_own.1 = (f32[128,768]{1,0:T(8,128)S(1)}, bf16[16,2048]{1,0:T(8,128)(2,1)S(1)}) custom-call(bf16[224,256]{1,0:T(8,128)(2,1)S(1)} %add_convert_fusion.refs_0_, bf16[224,256]{1,0:T(8,128)(2,1)S(1)} %collective-permute-done.16.refs_1_, bf16[224,256]{1,0:T(8,128)(2,1)S(1)} %collective-permute-done.17.refs_2_, ...), custom_call_target="tpu_custom_call" | custom-call | flops 1000000000 | bytes 3000000 | tf_op jit(solution)/shard_map/gate_up_own/pallas_call | solution.py:660
  74.1 0.3 collective-permute-done.24.came_ref
  74.4 0.8 hidden.1
  75.2 1.3 %collective-permute-start.31 = (bf16[8,7168]{1,0:T(8,128)(2,1)S(1)}, bf16[8,7168]{1,0:T(8,128)(2,1)S(1)}, u32[]{:S(2)}, u32[]{:S(2)}) collective-permute-start(bf16[8,7168]{1,0:T(8,128)(2,1)S(1)} %get-tuple-element.76), channel_id=1, source_target_pairs={{0,2},{1,3},{2,0},{3,1},{4,6},{5,7},{6,4},{7,5},{8,10},{9,11},{10,... | collective-permute-start | bytes 344072 | tf_op jit(solution)/shard_map/ppermute | solution.py:526
  76.5 0.8 collective-permute-start.29
  77.3 1.3 %collective-permute-start.27 = (bf16[8,7168]{1,0:T(8,128)(2,1)S(1)}, bf16[8,7168]{1,0:T(8,128)(2,1)S(1)}, u32[]{:S(2)}, u32[]{:S(2)}) collective-permute-start(bf16[8,7168]{1,0:T(8,128)(2,1)S(1)} %get-tuple-element.72), channel_id=1, source_target_pairs={{0,2},{1,3},{2,0},{3,1},{4,6},{5,7},{6,4},{7,5},{8,10},{9,11},{10,... | collective-permute-start | bytes 344072 | tf_op jit(solution)/shard_map/ppermute | solution.py:526
  78.6 0.8 collective-permute-start.25
  79.3 0.6 down.1
  79.9 1.3 %collective-permute-done.31.far_ref = bf16[8,7168]{1,0:T(8,128)(2,1)S(1)} collective-permute-done((bf16[8,7168]{1,0:T(8,128)(2,1)S(1)}, bf16[8,7168]{1,0:T(8,128)(2,1)S(1)}, u32[]{:S(2)}, u32[]{:S(2)}) %collective-permute-start.31) | collective-permute-done | bytes 114720 | tf_op jit(solution)/shard_map/ppermute | solution.py:526
  81.3 2.2 %collective-permute-start.32 = (bf16[8,7168]{1,0:T(8,128)(2,1)S(1)}, bf16[8,7168]{1,0:T(8,128)(2,1)S(1)}, u32[]{:S(2)}, u32[]{:S(2)}) collective-permute-start(bf16[8,7168]{1,0:T(8,128)(2,1)S(1)} %add.25), channel_id=1, source_target_pairs={{0,12},{1,13},{2,14},{3,15},{4,8},{5,9},{6,10},{7,11},{8,4},{9,5},... | collective-permute-start | bytes 344072 | tf_op jit(solution)/shard_map/ppermute | solution.py:523
  83.5 0.2 collective-permute-done.29.far_ref
  83.8 1.6 %collective-permute-start.30 = (bf16[8,7168]{1,0:T(8,128)(2,1)S(1)}, bf16[8,7168]{1,0:T(8,128)(2,1)S(1)}, u32[]{:S(2)}, u32[]{:S(2)}) collective-permute-start(bf16[8,7168]{1,0:T(8,128)(2,1)S(1)} %add.24), channel_id=1, source_target_pairs={{0,8},{1,9},{2,10},{3,11},{4,12},{5,13},{6,14},{7,15},{8,0},{9,1},... | collective-permute-start | bytes 344072 | tf_op jit(solution)/shard_map/ppermute | solution.py:523
  85.3 0.9 collective-permute-done.27.far_ref
  86.2 0.9 collective-permute-start.28
  87.1 0.8 collective-permute-done.25.far_ref
  87.9 0.1 base.1.base_ref
  88.0 1.2 %collective-permute-done.32.refs_2_ = bf16[8,7168]{1,0:T(8,128)(2,1)S(1)} collective-permute-done((bf16[8,7168]{1,0:T(8,128)(2,1)S(1)}, bf16[8,7168]{1,0:T(8,128)(2,1)S(1)}, u32[]{:S(2)}, u32[]{:S(2)}) %collective-permute-start.32) | collective-permute-done | bytes 114720 | tf_op jit(solution)/shard_map/ppermute | solution.py:523
  89.2 3.8 %collective-permute-done.30.refs_1_ = bf16[8,7168]{1,0:T(8,128)(2,1)S(1)} collective-permute-done((bf16[8,7168]{1,0:T(8,128)(2,1)S(1)}, bf16[8,7168]{1,0:T(8,128)(2,1)S(1)}, u32[]{:S(2)}, u32[]{:S(2)}) %collective-permute-start.30) | collective-permute-done | bytes 114720 | tf_op jit(solution)/shard_map/ppermute | solution.py:523
  93.0 0.7 last.1
  (45 shorter events, 0.5 us)
Async XLA Ops:
  0.0 2.6 %copy-start.5 = (bf16[64,4096]{1,0:T(8,128)(2,1)S(1)}, bf16[64,4096]{1,0:T(8,128)(2,1)}, u32[]{:S(2)}) copy-start(bf16[64,4096]{1,0:T(8,128)(2,1)} %refs_9_.3) | copy-start | bytes 1572868
  0.0 2.6 %copy-start.6 = (bf16[64,4096]{1,0:T(8,128)(2,1)S(1)}, bf16[64,4096]{1,0:T(8,128)(2,1)}, u32[]{:S(2)}) copy-start(bf16[64,4096]{1,0:T(8,128)(2,1)} %refs_10_.3) | copy-start | bytes 1572868
  0.0 2.6 %copy-start.7 = (bf16[64,4096]{1,0:T(8,128)(2,1)S(1)}, bf16[64,4096]{1,0:T(8,128)(2,1)}, u32[]{:S(2)}) copy-start(bf16[64,4096]{1,0:T(8,128)(2,1)} %refs_11_.1) | copy-start | bytes 1572868
  2.6 1.0 %copy-start.4 = (bf16[64,4096]{1,0:T(8,128)(2,1)S(1)}, bf16[64,4096]{1,0:T(8,128)(2,1)}, u32[]{:S(2)}) copy-start(bf16[64,4096]{1,0:T(8,128)(2,1)} %weight_ref.3) | copy-start | bytes 1572868
  2.7 1.1 %copy-start.8 = (bf16[8,10240]{1,0:T(8,128)(2,1)S(1)}, bf16[8,10240]{1,0:T(8,128)(2,1)}, u32[]{:S(2)}) copy-start(bf16[8,10240]{1,0:T(8,128)(2,1)} %fetch.1.piece_ref.refs_0_) | copy-start | bytes 491524
  2.8 27.8 %collective-permute-start.7 = (bf16[192,4096]{1,0:T(8,128)(2,1)S(1)}, bf16[192,4096]{1,0:T(8,128)(2,1)S(1)}, u32[]{:S(2)}, u32[]{:S(2)}) collective-permute-start(bf16[192,4096]{1,0:T(8,128)(2,1)S(1)} %stack.1), channel_id=1, source_target_pairs={{0,1},{1,0},{2,3},{3,2},{4,5},{5,4},{6,7},{7,6},{8,9},{9,8},{10,11... | collective-permute-start | bytes 4718600 | tf_op jit(solution)/shard_map/ppermute | solution.py:529
  3.8 26.8 %copy-start.9 = (f32[4096]{0:T(1024)S(1)}, f32[4096]{0:T(1024)}, u32[]{:S(2)}) copy-start(f32[4096]{0:T(1024)} %param.23) | copy-start | bytes 49156
  3.8 21.7 %collective-permute-start = (bf16[8,26624]{1,0:T(8,128)(2,1)S(1)}, bf16[8,26624]{1,0:T(8,128)(2,1)S(1)}, u32[]{:S(2)}, u32[]{:S(2)}) collective-permute-start(bf16[8,26624]{1,0:T(8,128)(2,1)S(1)} %across.1), channel_id=1, source_target_pairs={{0,2},{1,3},{2,0},{3,1},{4,6},{5,7},{6,4},{7,5},{8,10},{9,11},{10,... | collective-permute-start | bytes 1277960 | tf_op jit(solution)/shard_map/ppermute | solution.py:526
  6.8 7.9 %collective-permute-start.1 = (bf16[8,10240]{1,0:T(8,128)(2,1)S(1)}, bf16[8,10240]{1,0:T(8,128)(2,1)S(1)}, u32[]{:S(2)}, u32[]{:S(2)}) collective-permute-start(bf16[8,10240]{1,0:T(8,128)(2,1)S(1)} %copy-done.8), channel_id=1, source_target_pairs={{0,4},{1,5},{2,6},{3,7},{4,0},{5,1},{6,2},{7,3},{8,12},{9,13},{10,... | collective-permute-start | bytes 491528 | tf_op jit(solution)/shard_map/ppermute | solution.py:523
  8.4 15.1 %collective-permute-start.3 = (bf16[8,10240]{1,0:T(8,128)(2,1)S(1)}, bf16[8,10240]{1,0:T(8,128)(2,1)S(1)}, u32[]{:S(2)}, u32[]{:S(2)}) collective-permute-start(bf16[8,10240]{1,0:T(8,128)(2,1)S(1)} %copy-done.8), channel_id=1, source_target_pairs={{0,8},{1,9},{2,10},{3,11},{4,12},{5,13},{6,14},{7,15},{8,0},{9,1},... | collective-permute-start | bytes 491528 | tf_op jit(solution)/shard_map/ppermute | solution.py:523
  11.0 13.0 %collective-permute-start.5 = (bf16[8,10240]{1,0:T(8,128)(2,1)S(1)}, bf16[8,10240]{1,0:T(8,128)(2,1)S(1)}, u32[]{:S(2)}, u32[]{:S(2)}) collective-permute-start(bf16[8,10240]{1,0:T(8,128)(2,1)S(1)} %copy-done.8), channel_id=1, source_target_pairs={{0,12},{1,13},{2,14},{3,15},{4,8},{5,9},{6,10},{7,11},{8,4},{9,5},... | collective-permute-start | bytes 491528 | tf_op jit(solution)/shard_map/ppermute | solution.py:523
  14.7 11.0 %collective-permute-start.2 = (bf16[8,10240]{1,0:T(8,128)(2,1)S(1)}, bf16[8,10240]{1,0:T(8,128)(2,1)S(1)}, u32[]{:S(2)}, u32[]{:S(2)}) collective-permute-start(bf16[8,10240]{1,0:T(8,128)(2,1)S(1)} %collective-permute-done.1.refs_2_), channel_id=1, source_target_pairs={{0,2},{1,3},{2,0},{3,1},{4,6},{5,7},{6,4},{7,5},{8,10},{9,11},{10,... | collective-permute-start | bytes 491528 | tf_op jit(solution)/shard_map/ppermute | solution.py:526
  23.5 5.3 %collective-permute-start.4 = (bf16[8,10240]{1,0:T(8,128)(2,1)S(1)}, bf16[8,10240]{1,0:T(8,128)(2,1)S(1)}, u32[]{:S(2)}, u32[]{:S(2)}) collective-permute-start(bf16[8,10240]{1,0:T(8,128)(2,1)S(1)} %collective-permute-done.3.refs_4_), channel_id=1, source_target_pairs={{0,2},{1,3},{2,0},{3,1},{4,6},{5,7},{6,4},{7,5},{8,10},{9,11},{10,... | collective-permute-start | bytes 491528 | tf_op jit(solution)/shard_map/ppermute | solution.py:526
  24.0 6.6 %collective-permute-start.6 = (bf16[8,10240]{1,0:T(8,128)(2,1)S(1)}, bf16[8,10240]{1,0:T(8,128)(2,1)S(1)}, u32[]{:S(2)}, u32[]{:S(2)}) collective-permute-start(bf16[8,10240]{1,0:T(8,128)(2,1)S(1)} %collective-permute-done.5.refs_6_), channel_id=1, source_target_pairs={{0,2},{1,3},{2,0},{3,1},{4,6},{5,7},{6,4},{7,5},{8,10},{9,11},{10,... | collective-permute-start | bytes 491528 | tf_op jit(solution)/shard_map/ppermute | solution.py:526
  25.6 8.4 %collective-permute-start.8 = (bf16[128,1024]{1,0:T(8,128)(2,1)S(1)}, bf16[128,1024]{1,0:T(8,128)(2,1)S(1)}, u32[]{:S(2)}, u32[]{:S(2)}) collective-permute-start(bf16[128,1024]{1,0:T(8,128)(2,1)S(1)} %get-tuple-element.49), channel_id=1, source_target_pairs={{0,1},{1,0},{2,3},{3,2},{4,5},{5,4},{6,7},{7,6},{8,9},{9,8},{10,11... | collective-permute-start | bytes 786440 | tf_op jit(solution)/shard_map/ppermute | solution.py:529
  30.6 2.1 %copy-start.10 = (s32[24,1]{0,1:T(1,128)S(1)}, s32[24,1]{0,1:T(1,128)}, u32[]{:S(2)}) copy-start(s32[24,1]{0,1:T(1,128)} %param.16) | copy-start | bytes 292
  30.6 2.1 %copy-start.11 = (s32[24]{0:T(128)S(1)}, s32[24]{0:T(128)}, u32[]{:S(2)}) copy-start(s32[24]{0:T(128)} %segment_ref.1) | copy-start | bytes 292
  32.6 1.5 %collective-permute-start.9 = (bf16[160,512]{1,0:T(8,128)(2,1)S(1)}, bf16[160,512]{1,0:T(8,128)(2,1)S(1)}, u32[]{:S(2)}, u32[]{:S(2)}) collective-permute-start(bf16[160,512]{1,0:T(8,128)(2,1)S(1)} %get-tuple-element.51), channel_id=1, source_target_pairs={{0,1},{1,0},{2,3},{3,2},{4,5},{5,4},{6,7},{7,6},{8,9},{9,8},{10,11... | collective-permute-start | bytes 491528 | tf_op jit(solution)/shard_map/ppermute | solution.py:529
  34.9 4.1 %collective-permute-start.10 = (bf16[112,128]{1,0:T(8,128)(2,1)S(1)}, bf16[112,128]{1,0:T(8,128)(2,1)S(1)}, u32[]{:S(2)}, u32[]{:S(2)}) collective-permute-start(bf16[112,128]{1,0:T(8,128)(2,1)S(1)} %get-tuple-element.53.refs_0_), channel_id=1, source_target_pairs={{0,2},{1,3},{2,0},{3,1},{4,6},{5,7},{6,4},{7,5},{8,10},{9,11},{10,... | collective-permute-start | bytes 86024 | tf_op jit(solution)/shard_map/ppermute | solution.py:526
  35.5 3.6 %collective-permute-start.11 = (bf16[112,128]{1,0:T(8,128)(2,1)S(1)}, bf16[112,128]{1,0:T(8,128)(2,1)S(1)}, u32[]{:S(2)}, u32[]{:S(2)}) collective-permute-start(bf16[112,128]{1,0:T(8,128)(2,1)S(1)} %get-tuple-element.53.refs_0_), channel_id=1, source_target_pairs={{0,1},{1,0},{2,3},{3,2},{4,5},{5,4},{6,7},{7,6},{8,9},{9,8},{10,11... | collective-permute-start | bytes 86024 | tf_op jit(solution)/shard_map/ppermute | solution.py:529
  35.7 3.5 %collective-permute-start.12 = (bf16[112,128]{1,0:T(8,128)(2,1)S(1)}, bf16[112,128]{1,0:T(8,128)(2,1)S(1)}, u32[]{:S(2)}, u32[]{:S(2)}) collective-permute-start(bf16[112,128]{1,0:T(8,128)(2,1)S(1)} %get-tuple-element.53.refs_0_), channel_id=1, source_target_pairs={{0,3},{1,2},{2,1},{3,0},{4,7},{5,6},{6,5},{7,4},{8,11},{9,10},{10,... | collective-permute-start | bytes 86024 | tf_op jit(solution)/shard_map/ppermute | solution.py:633
  39.2 13.6 %copy-start = (bf16[160,4096]{1,0:T(8,128)(2,1)S(1)}, bf16[160,4096]{1,0:T(8,128)(2,1)}, u32[]{:S(2)}) copy-start(bf16[160,4096]{1,0:T(8,128)(2,1)} %down_ref.4) | copy-start | bytes 3932164
  39.2 13.6 %copy-start.1 = (bf16[160,4096]{1,0:T(8,128)(2,1)S(1)}, bf16[160,4096]{1,0:T(8,128)(2,1)}, u32[]{:S(2)}) copy-start(bf16[160,4096]{1,0:T(8,128)(2,1)} %refs_9_.5) | copy-start | bytes 3932164
  39.2 13.6 %copy-start.2 = (bf16[160,4096]{1,0:T(8,128)(2,1)S(1)}, bf16[160,4096]{1,0:T(8,128)(2,1)}, u32[]{:S(2)}) copy-start(bf16[160,4096]{1,0:T(8,128)(2,1)} %refs_10_.5) | copy-start | bytes 3932164
  39.6 8.0 %collective-permute-start.13 = (bf16[224,256]{1,0:T(8,128)(2,1)S(1)}, bf16[224,256]{1,0:T(8,128)(2,1)S(1)}, u32[]{:S(2)}, u32[]{:S(2)}) collective-permute-start(bf16[224,256]{1,0:T(8,128)(2,1)S(1)} %get-tuple-element.57), channel_id=1, source_target_pairs={{0,12},{1,13},{2,14},{3,15},{4,8},{5,9},{6,10},{7,11},{8,4},{9,5},... | collective-permute-start | bytes 344072 | tf_op jit(solution)/shard_map/ppermute | solution.py:523
  41.7 11.0 %collective-permute-start.14 = (bf16[224,256]{1,0:T(8,128)(2,1)S(1)}, bf16[224,256]{1,0:T(8,128)(2,1)S(1)}, u32[]{:S(2)}, u32[]{:S(2)}) collective-permute-start(bf16[224,256]{1,0:T(8,128)(2,1)S(1)} %get-tuple-element.58), channel_id=1, source_target_pairs={{0,8},{1,9},{2,10},{3,11},{4,12},{5,13},{6,14},{7,15},{8,0},{9,1},... | collective-permute-start | bytes 344072 | tf_op jit(solution)/shard_map/ppermute | solution.py:523
  42.1 10.6 %collective-permute-start.15 = (bf16[224,256]{1,0:T(8,128)(2,1)S(1)}, bf16[224,256]{1,0:T(8,128)(2,1)S(1)}, u32[]{:S(2)}, u32[]{:S(2)}) collective-permute-start(bf16[224,256]{1,0:T(8,128)(2,1)S(1)} %get-tuple-element.59), channel_id=1, source_target_pairs={{0,4},{1,5},{2,6},{3,7},{4,0},{5,1},{6,2},{7,3},{8,12},{9,13},{10,... | collective-permute-start | bytes 344072 | tf_op jit(solution)/shard_map/ppermute | solution.py:523
  52.8 18.5 %copy-start.3 = (f32[4096]{0:T(1024)S(1)}, f32[4096]{0:T(1024)}, u32[]{:S(2)}) copy-start(f32[4096]{0:T(1024)} %param.24) | copy-start | bytes 49156
  53.0 18.3 %collective-permute-start.23 = (bf16[320,4096]{1,0:T(8,128)(2,1)S(1)}, bf16[320,4096]{1,0:T(8,128)(2,1)S(1)}, u32[]{:S(2)}, u32[]{:S(2)}) collective-permute-start(bf16[320,4096]{1,0:T(8,128)(2,1)S(1)} %share.1), channel_id=1, source_target_pairs={{0,1},{1,0},{2,3},{3,2},{4,5},{5,4},{6,7},{7,6},{8,9},{9,8},{10,11... | collective-permute-start | bytes 7864328 | tf_op jit(solution)/shard_map/ppermute | solution.py:529
  53.0 7.5 %collective-permute-start.17 = (bf16[224,256]{1,0:T(8,128)(2,1)S(1)}, bf16[224,256]{1,0:T(8,128)(2,1)S(1)}, u32[]{:S(2)}, u32[]{:S(2)}) collective-permute-start(bf16[224,256]{1,0:T(8,128)(2,1)S(1)} %add_convert_fusion.refs_0_), channel_id=1, source_target_pairs={{0,4},{1,5},{2,6},{3,7},{4,0},{5,1},{6,2},{7,3},{8,12},{9,13},{10,... | collective-permute-start | bytes 344072 | tf_op jit(solution)/shard_map/ppermute | solution.py:523
  53.1 11.9 %collective-permute-start.19 = (bf16[224,256]{1,0:T(8,128)(2,1)S(1)}, bf16[224,256]{1,0:T(8,128)(2,1)S(1)}, u32[]{:S(2)}, u32[]{:S(2)}) collective-permute-start(bf16[224,256]{1,0:T(8,128)(2,1)S(1)} %add_convert_fusion.refs_0_), channel_id=1, source_target_pairs={{0,8},{1,9},{2,10},{3,11},{4,12},{5,13},{6,14},{7,15},{8,0},{9,1},... | collective-permute-start | bytes 344072 | tf_op jit(solution)/shard_map/ppermute | solution.py:523
  55.7 10.8 %collective-permute-start.21 = (bf16[224,256]{1,0:T(8,128)(2,1)S(1)}, bf16[224,256]{1,0:T(8,128)(2,1)S(1)}, u32[]{:S(2)}, u32[]{:S(2)}) collective-permute-start(bf16[224,256]{1,0:T(8,128)(2,1)S(1)} %add_convert_fusion.refs_0_), channel_id=1, source_target_pairs={{0,12},{1,13},{2,14},{3,15},{4,8},{5,9},{6,10},{7,11},{8,4},{9,5},... | collective-permute-start | bytes 344072 | tf_op jit(solution)/shard_map/ppermute | solution.py:523
  57.5 9.5 %collective-permute-start.16 = (bf16[224,256]{1,0:T(8,128)(2,1)S(1)}, bf16[224,256]{1,0:T(8,128)(2,1)S(1)}, u32[]{:S(2)}, u32[]{:S(2)}) collective-permute-start(bf16[224,256]{1,0:T(8,128)(2,1)S(1)} %add_convert_fusion.refs_0_), channel_id=1, source_target_pairs={{0,2},{1,3},{2,0},{3,1},{4,6},{5,7},{6,4},{7,5},{8,10},{9,11},{10,... | collective-permute-start | bytes 344072 | tf_op jit(solution)/shard_map/ppermute | solution.py:526
  60.5 6.5 %collective-permute-start.18 = (bf16[224,256]{1,0:T(8,128)(2,1)S(1)}, bf16[224,256]{1,0:T(8,128)(2,1)S(1)}, u32[]{:S(2)}, u32[]{:S(2)}) collective-permute-start(bf16[224,256]{1,0:T(8,128)(2,1)S(1)} %collective-permute-done.17.refs_2_), channel_id=1, source_target_pairs={{0,2},{1,3},{2,0},{3,1},{4,6},{5,7},{6,4},{7,5},{8,10},{9,11},{10,... | collective-permute-start | bytes 344072 | tf_op jit(solution)/shard_map/ppermute | solution.py:526
  65.0 4.8 %collective-permute-start.20 = (bf16[224,256]{1,0:T(8,128)(2,1)S(1)}, bf16[224,256]{1,0:T(8,128)(2,1)S(1)}, u32[]{:S(2)}, u32[]{:S(2)}) collective-permute-start(bf16[224,256]{1,0:T(8,128)(2,1)S(1)} %collective-permute-done.19.refs_4_), channel_id=1, source_target_pairs={{0,2},{1,3},{2,0},{3,1},{4,6},{5,7},{6,4},{7,5},{8,10},{9,11},{10,... | collective-permute-start | bytes 344072 | tf_op jit(solution)/shard_map/ppermute | solution.py:526
  66.5 4.8 %collective-permute-start.22 = (bf16[224,256]{1,0:T(8,128)(2,1)S(1)}, bf16[224,256]{1,0:T(8,128)(2,1)S(1)}, u32[]{:S(2)}, u32[]{:S(2)}) collective-permute-start(bf16[224,256]{1,0:T(8,128)(2,1)S(1)} %collective-permute-done.21.refs_6_), channel_id=1, source_target_pairs={{0,2},{1,3},{2,0},{3,1},{4,6},{5,7},{6,4},{7,5},{8,10},{9,11},{10,... | collective-permute-start | bytes 344072 | tf_op jit(solution)/shard_map/ppermute | solution.py:526
  72.6 1.8 %collective-permute-start.24 = (f32[128,768]{1,0:T(8,128)S(1)}, f32[128,768]{1,0:T(8,128)S(1)}, u32[]{:S(2)}, u32[]{:S(2)}) collective-permute-start(f32[128,768]{1,0:T(8,128)S(1)} %get-tuple-element.63), channel_id=1, source_target_pairs={{0,1},{1,0},{2,3},{3,2},{4,5},{5,4},{6,7},{7,6},{8,9},{9,8},{10,11... | collective-permute-start | bytes 1179656 | tf_op jit(solution)/shard_map/ppermute | solution.py:529
  75.2 6.0 %collective-permute-start.31 = (bf16[8,7168]{1,0:T(8,128)(2,1)S(1)}, bf16[8,7168]{1,0:T(8,128)(2,1)S(1)}, u32[]{:S(2)}, u32[]{:S(2)}) collective-permute-start(bf16[8,7168]{1,0:T(8,128)(2,1)S(1)} %get-tuple-element.76), channel_id=1, source_target_pairs={{0,2},{1,3},{2,0},{3,1},{4,6},{5,7},{6,4},{7,5},{8,10},{9,11},{10,... | collective-permute-start | bytes 344072 | tf_op jit(solution)/shard_map/ppermute | solution.py:526
  76.5 10.6 %collective-permute-start.26 = (bf16[16,2048]{1,0:T(8,128)(2,1)S(1)}, bf16[16,2048]{1,0:T(8,128)(2,1)S(1)}, u32[]{:S(2)}, u32[]{:S(2)}) collective-permute-start(bf16[16,2048]{1,0:T(8,128)(2,1)S(1)} %get-tuple-element.70), channel_id=1, source_target_pairs={{0,1},{1,0},{2,3},{3,2},{4,5},{5,4},{6,7},{7,6},{8,9},{9,8},{10,11... | collective-permute-start | bytes 196616 | tf_op jit(solution)/shard_map/ppermute | solution.py:529
  76.5 7.2 %collective-permute-start.29 = (bf16[8,7168]{1,0:T(8,128)(2,1)S(1)}, bf16[8,7168]{1,0:T(8,128)(2,1)S(1)}, u32[]{:S(2)}, u32[]{:S(2)}) collective-permute-start(bf16[8,7168]{1,0:T(8,128)(2,1)S(1)} %get-tuple-element.74), channel_id=1, source_target_pairs={{0,2},{1,3},{2,0},{3,1},{4,6},{5,7},{6,4},{7,5},{8,10},{9,11},{10,... | collective-permute-start | bytes 344072 | tf_op jit(solution)/shard_map/ppermute | solution.py:526
  77.3 8.9 %collective-permute-start.27 = (bf16[8,7168]{1,0:T(8,128)(2,1)S(1)}, bf16[8,7168]{1,0:T(8,128)(2,1)S(1)}, u32[]{:S(2)}, u32[]{:S(2)}) collective-permute-start(bf16[8,7168]{1,0:T(8,128)(2,1)S(1)} %get-tuple-element.72), channel_id=1, source_target_pairs={{0,2},{1,3},{2,0},{3,1},{4,6},{5,7},{6,4},{7,5},{8,10},{9,11},{10,... | collective-permute-start | bytes 344072 | tf_op jit(solution)/shard_map/ppermute | solution.py:526
  78.6 9.3 %collective-permute-start.25 = (bf16[8,7168]{1,0:T(8,128)(2,1)S(1)}, bf16[8,7168]{1,0:T(8,128)(2,1)S(1)}, u32[]{:S(2)}, u32[]{:S(2)}) collective-permute-start(bf16[8,7168]{1,0:T(8,128)(2,1)S(1)} %get-tuple-element.68), channel_id=1, source_target_pairs={{0,2},{1,3},{2,0},{3,1},{4,6},{5,7},{6,4},{7,5},{8,10},{9,11},{10,... | collective-permute-start | bytes 344072 | tf_op jit(solution)/shard_map/ppermute | solution.py:526
  81.3 7.9 %collective-permute-start.32 = (bf16[8,7168]{1,0:T(8,128)(2,1)S(1)}, bf16[8,7168]{1,0:T(8,128)(2,1)S(1)}, u32[]{:S(2)}, u32[]{:S(2)}) collective-permute-start(bf16[8,7168]{1,0:T(8,128)(2,1)S(1)} %add.25), channel_id=1, source_target_pairs={{0,12},{1,13},{2,14},{3,15},{4,8},{5,9},{6,10},{7,11},{8,4},{9,5},... | collective-permute-start | bytes 344072 | tf_op jit(solution)/shard_map/ppermute | solution.py:523
  83.8 9.3 %collective-permute-start.30 = (bf16[8,7168]{1,0:T(8,128)(2,1)S(1)}, bf16[8,7168]{1,0:T(8,128)(2,1)S(1)}, u32[]{:S(2)}, u32[]{:S(2)}) collective-permute-start(bf16[8,7168]{1,0:T(8,128)(2,1)S(1)} %add.24), channel_id=1, source_target_pairs={{0,8},{1,9},{2,10},{3,11},{4,12},{5,13},{6,14},{7,15},{8,0},{9,1},... | collective-permute-start | bytes 344072 | tf_op jit(solution)/shard_map/ppermute | solution.py:523
  86.2 6.8 %collective-permute-start.28 = (bf16[8,7168]{1,0:T(8,128)(2,1)S(1)}, bf16[8,7168]{1,0:T(8,128)(2,1)S(1)}, u32[]{:S(2)}, u32[]{:S(2)}) collective-permute-start(bf16[8,7168]{1,0:T(8,128)(2,1)S(1)} %add.23), channel_id=1, source_target_pairs={{0,4},{1,5},{2,6},{3,7},{4,0},{5,1},{6,2},{7,3},{8,12},{9,13},{10,... | collective-permute-start | bytes 344072 | tf_op jit(solution)/shard_map/ppermute | solution.py:523

commit v9 on v7

--- a/solution.py
+++ b/solution.py
@@ -527,7 +527,7 @@
 
     def plane_gather(value, value_across=None, fence=None):
         near = {0: value}
-        for k in z_order:
+        for k in range(1, nz):
             near[k] = along_z(value, k)
         if fence is not None:
             for k in near:
@@ -535,7 +535,7 @@
         if value_across is None:
             value_across = near[0]
         return near, {
-            k: across_y(near[k] if k else value_across) for k in [0] + z_order
+            k: across_y(near[k] if k else value_across) for k in range(nz)
         }
 
     def paired(near, far):

time: 94.4 us -> 94.4 us (level)
  no operation moved by 1% of the time
where the time goes in v9:
time: 94.4 us; the launch traced here: 94.2 us
  waiting for transfers between devices  45.7 us (48%)
  starting transfers between devices  35 us (37%)
  Pallas kernels  12.6 us (13%)
    ppermute x12, waiting for transfers between devices, along_z(): return lax.ppermute(value, AXIS, [(i, i ^ 4 * k) for i in range(devices)])  30 us
    ppermute x12, starting transfers between devices, along_z(): return lax.ppermute(value, AXIS, [(i, i ^ 4 * k) for i in range(devices)])  17.6 us
    ppermute x13, starting transfers between devices, across_y(): return lax.ppermute(value, AXIS, [(i, i ^ 2) for i in range(devices)])  15 us
    ppermute x13, waiting for transfers between devices, across_y(): return lax.ppermute(value, AXIS, [(i, i ^ 2) for i in range(devices)])  14 us
    pallas_call x2, Pallas kernels, gate_up(): kernel_call(functools.partial(gate_kernel, rows_here, chunk_rows, own), (...  2.72 us
    pallas_call x1, Pallas kernels, body(): kernel_call(fetch_kernel, shape((8, full * features + halved * half), bf1...  2.6 us
    pallas_call x1, Pallas kernels, body(): kernel_call(functools.partial(projection_kernel, query_rows + CAP * BLK),...  1.98 us
  transfers between devices with their start and end apart: 33, of which 20 were waited for; matrix products, arithmetic and copies ran while one was open for 0% of the time, Pallas kernels for 6%

profile of v9, /device:TPU:0, one launch (start us, length us, event | category | flops | bytes accessed | tf_op | source)
XLA Modules:
  0.0 94.2 jit_solution(15521396104278229297)
XLA Ops:
  0.0 2.6 %fetch.1.piece_ref.refs_0_ = bf16[8,10240]{1,0:T(8,128)(2,1)} custom-call(s32[24]{0:T(128)} %bitcast.6, s32[24]{0:T(128)} %row_ref.1, bf16[64,4,4096]{2,1,0:T(4,128)(2,1)} %corpus_ref.1, bf16[8,4096]{1,0:T(8,128)(2,1)} %query_ref.1), custom_call_target="tpu_custom_call" | custom-call | flops 1000000000 | bytes 3000000 | tf_op jit(solution)/shard_map/fetch/pallas_call | solution.py:558
  2.7 0.1 stack.1
  2.8 0.5 collective-permute-start.7
  3.3 0.4 copy-done.4
  3.8 3.0 %collective-permute-start = (bf16[8,26624]{1,0:T(8,128)(2,1)S(1)}, bf16[8,26624]{1,0:T(8,128)(2,1)S(1)}, u32[]{:S(2)}, u32[]{:S(2)}) collective-permute-start(bf16[8,26624]{1,0:T(8,128)(2,1)S(1)} %across.1), channel_id=1, source_target_pairs={{0,2},{1,3},{2,0},{3,1},{4,6},{5,7},{6,4},{7,5},{8,10},{9,11},{10,... | collective-permute-start | bytes 1277960 | tf_op jit(solution)/shard_map/ppermute | solution.py:523
  6.8 1.6 %collective-permute-start.1 = (bf16[8,10240]{1,0:T(8,128)(2,1)S(1)}, bf16[8,10240]{1,0:T(8,128)(2,1)S(1)}, u32[]{:S(2)}, u32[]{:S(2)}) collective-permute-start(bf16[8,10240]{1,0:T(8,128)(2,1)S(1)} %copy-done.8), channel_id=1, source_target_pairs={{0,4},{1,5},{2,6},{3,7},{4,0},{5,1},{6,2},{7,3},{8,12},{9,13},{10,... | collective-permute-start | bytes 491528 | tf_op jit(solution)/shard_map/ppermute | solution.py:520
  8.4 2.5 %collective-permute-start.3 = (bf16[8,10240]{1,0:T(8,128)(2,1)S(1)}, bf16[8,10240]{1,0:T(8,128)(2,1)S(1)}, u32[]{:S(2)}, u32[]{:S(2)}) collective-permute-start(bf16[8,10240]{1,0:T(8,128)(2,1)S(1)} %copy-done.8), channel_id=1, source_target_pairs={{0,8},{1,9},{2,10},{3,11},{4,12},{5,13},{6,14},{7,15},{8,0},{9,1},... | collective-permute-start | bytes 491528 | tf_op jit(solution)/shard_map/ppermute | solution.py:520
  11.0 0.2 collective-permute-start.5
  11.2 3.5 %collective-permute-done.1.refs_2_ = bf16[8,10240]{1,0:T(8,128)(2,1)S(1)} collective-permute-done((bf16[8,10240]{1,0:T(8,128)(2,1)S(1)}, bf16[8,10240]{1,0:T(8,128)(2,1)S(1)}, u32[]{:S(2)}, u32[]{:S(2)}) %collective-permute-start.1) | collective-permute-done | bytes 163872 | tf_op jit(solution)/shard_map/ppermute | solution.py:520
  14.7 0.3 collective-permute-start.2
  15.0 8.5 %collective-permute-done.3.refs_4_ = bf16[8,10240]{1,0:T(8,128)(2,1)S(1)} collective-permute-done((bf16[8,10240]{1,0:T(8,128)(2,1)S(1)}, bf16[8,10240]{1,0:T(8,128)(2,1)S(1)}, u32[]{:S(2)}, u32[]{:S(2)}) %collective-permute-start.3) | collective-permute-done | bytes 163872 | tf_op jit(solution)/shard_map/ppermute | solution.py:520
  23.5 0.5 collective-permute-start.4
  24.0 1.5 %collective-permute-start.6 = (bf16[8,10240]{1,0:T(8,128)(2,1)S(1)}, bf16[8,10240]{1,0:T(8,128)(2,1)S(1)}, u32[]{:S(2)}, u32[]{:S(2)}) collective-permute-start(bf16[8,10240]{1,0:T(8,128)(2,1)S(1)} %collective-permute-done.5.refs_6_), channel_id=1, source_target_pairs={{0,2},{1,3},{2,0},{3,1},{4,6},{5,7},{6,4},{7,5},{8,10},{9,11},{10,... | collective-permute-start | bytes 491528 | tf_op jit(solution)/shard_map/ppermute | solution.py:523
  25.5 0.1 pairs.1
  25.7 3.1 %collective-permute-done.4.refs_5_ = bf16[8,10240]{1,0:T(8,128)(2,1)S(1)} collective-permute-done((bf16[8,10240]{1,0:T(8,128)(2,1)S(1)}, bf16[8,10240]{1,0:T(8,128)(2,1)S(1)}, u32[]{:S(2)}, u32[]{:S(2)}) %collective-permute-start.4) | collective-permute-done | bytes 163872 | tf_op jit(solution)/shard_map/ppermute | solution.py:523
  28.8 1.8 %collective-permute-done.6.refs_7_ = bf16[8,10240]{1,0:T(8,128)(2,1)S(1)} collective-permute-done((bf16[8,10240]{1,0:T(8,128)(2,1)S(1)}, bf16[8,10240]{1,0:T(8,128)(2,1)S(1)}, u32[]{:S(2)}, u32[]{:S(2)}) %collective-permute-start.6) | collective-permute-done | bytes 163872 | tf_op jit(solution)/shard_map/ppermute | solution.py:523
  30.6 2.0 %project.1 = (bf16[160,512]{1,0:T(8,128)(2,1)S(1)}, bf16[160,512]{1,0:T(8,128)(2,1)S(1)}) custom-call(bf16[8,10240]{1,0:T(8,128)(2,1)S(1)} %copy-done.8, bf16[8,26624]{1,0:T(8,128)(2,1)S(1)} %collective-permute-done.refs_1_.far_ref, bf16[8,10240]{1,0:T(8,128)(2,1)S(1)} %collective-permute-done.1.refs_2_, ...), custom_call_target="tpu_custom_call" | custom-call | flops 10000000000 | bytes 30000000 | tf_op jit(solution)/shard_map/project/pallas_call | solution.py:592
  32.5 0.1 collective-permute-start.9
  32.6 1.3 %plan.1 = (bf16[224,160]{1,0:T(8,128)(2,1)S(1)}, bf16[224,160]{1,0:T(8,128)(2,1)S(1)}, f32[224,224]{1,0:T(8,128)S(1)}) custom-call(s32[24]{0:T(128)S(1)} %bitcast.7, s32[24]{0:T(128)S(1)} %copy-done.11), custom_call_target="tpu_custom_call" | custom-call | flops 1000000000 | bytes 3000000 | tf_op jit(solution)/shard_map/plan/pallas_call | solution.py:610
  34.0 0.9 attend.1
  34.9 0.5 collective-permute-start.10
  35.5 0.2 collective-permute-start.11
  35.7 1.4 %collective-permute-start.12 = (bf16[112,128]{1,0:T(8,128)(2,1)S(1)}, bf16[112,128]{1,0:T(8,128)(2,1)S(1)}, u32[]{:S(2)}, u32[]{:S(2)}) collective-permute-start(bf16[112,128]{1,0:T(8,128)(2,1)S(1)} %get-tuple-element.53.refs_0_), channel_id=1, source_target_pairs={{0,3},{1,2},{2,1},{3,0},{4,7},{5,6},{6,5},{7,4},{8,11},{9,10},{10,... | collective-permute-start | bytes 86024 | tf_op jit(solution)/shard_map/ppermute | solution.py:630
  37.1 1.9 %collective-permute-done.10.refs_1_ = bf16[112,128]{1,0:T(8,128)(2,1)S(1)} collective-permute-done((bf16[112,128]{1,0:T(8,128)(2,1)S(1)}, bf16[112,128]{1,0:T(8,128)(2,1)S(1)}, u32[]{:S(2)}, u32[]{:S(2)}) %collective-permute-start.10) | collective-permute-done | bytes 28704 | tf_op jit(solution)/shard_map/ppermute | solution.py:523
  39.0 0.1 collective-permute-done.12.refs_3_
  39.1 0.4 out.1
  39.6 2.1 %collective-permute-start.13 = (bf16[224,256]{1,0:T(8,128)(2,1)S(1)}, bf16[224,256]{1,0:T(8,128)(2,1)S(1)}, u32[]{:S(2)}, u32[]{:S(2)}) collective-permute-start(bf16[224,256]{1,0:T(8,128)(2,1)S(1)} %get-tuple-element.57), channel_id=1, source_target_pairs={{0,12},{1,13},{2,14},{3,15},{4,8},{5,9},{6,10},{7,11},{8,4},{9,5},... | collective-permute-start | bytes 344072 | tf_op jit(solution)/shard_map/ppermute | solution.py:520
  41.7 0.4 collective-permute-start.14
  42.1 1.9 %collective-permute-start.15 = (bf16[224,256]{1,0:T(8,128)(2,1)S(1)}, bf16[224,256]{1,0:T(8,128)(2,1)S(1)}, u32[]{:S(2)}, u32[]{:S(2)}) collective-permute-start(bf16[224,256]{1,0:T(8,128)(2,1)S(1)} %get-tuple-element.59), channel_id=1, source_target_pairs={{0,4},{1,5},{2,6},{3,7},{4,0},{5,1},{6,2},{7,3},{8,12},{9,13},{10,... | collective-permute-start | bytes 344072 | tf_op jit(solution)/shard_map/ppermute | solution.py:520
  44.0 3.5 %collective-permute-done.13 = bf16[224,256]{1,0:T(8,128)(2,1)S(1)} collective-permute-done((bf16[224,256]{1,0:T(8,128)(2,1)S(1)}, bf16[224,256]{1,0:T(8,128)(2,1)S(1)}, u32[]{:S(2)}, u32[]{:S(2)}) %collective-permute-start.13) | collective-permute-done | bytes 114720 | tf_op jit(solution)/shard_map/ppermute | solution.py:520
  47.5 5.2 %collective-permute-done.14 = bf16[224,256]{1,0:T(8,128)(2,1)S(1)} collective-permute-done((bf16[224,256]{1,0:T(8,128)(2,1)S(1)}, bf16[224,256]{1,0:T(8,128)(2,1)S(1)}, u32[]{:S(2)}, u32[]{:S(2)}) %collective-permute-start.14) | collective-permute-done | bytes 114720 | tf_op jit(solution)/shard_map/ppermute | solution.py:520
  52.8 0.2 share.1
  53.0 0.1 collective-permute-start.23
  53.1 0.1 collective-permute-start.17
  53.2 2.6 %collective-permute-start.19 = (bf16[224,256]{1,0:T(8,128)(2,1)S(1)}, bf16[224,256]{1,0:T(8,128)(2,1)S(1)}, u32[]{:S(2)}, u32[]{:S(2)}) collective-permute-start(bf16[224,256]{1,0:T(8,128)(2,1)S(1)} %add_convert_fusion.refs_0_), channel_id=1, source_target_pairs={{0,8},{1,9},{2,10},{3,11},{4,12},{5,13},{6,14},{7,15},{8,0},{9,1},... | collective-permute-start | bytes 344072 | tf_op jit(solution)/shard_map/ppermute | solution.py:520
  55.7 1.8 %collective-permute-start.21 = (bf16[224,256]{1,0:T(8,128)(2,1)S(1)}, bf16[224,256]{1,0:T(8,128)(2,1)S(1)}, u32[]{:S(2)}, u32[]{:S(2)}) collective-permute-start(bf16[224,256]{1,0:T(8,128)(2,1)S(1)} %add_convert_fusion.refs_0_), channel_id=1, source_target_pairs={{0,12},{1,13},{2,14},{3,15},{4,8},{5,9},{6,10},{7,11},{8,4},{9,5},... | collective-permute-start | bytes 344072 | tf_op jit(solution)/shard_map/ppermute | solution.py:520
  57.5 1.5 %collective-permute-start.16 = (bf16[224,256]{1,0:T(8,128)(2,1)S(1)}, bf16[224,256]{1,0:T(8,128)(2,1)S(1)}, u32[]{:S(2)}, u32[]{:S(2)}) collective-permute-start(bf16[224,256]{1,0:T(8,128)(2,1)S(1)} %add_convert_fusion.refs_0_), channel_id=1, source_target_pairs={{0,2},{1,3},{2,0},{3,1},{4,6},{5,7},{6,4},{7,5},{8,10},{9,11},{10,... | collective-permute-start | bytes 344072 | tf_op jit(solution)/shard_map/ppermute | solution.py:523
  59.0 1.5 %collective-permute-done.17.refs_2_ = bf16[224,256]{1,0:T(8,128)(2,1)S(1)} collective-permute-done((bf16[224,256]{1,0:T(8,128)(2,1)S(1)}, bf16[224,256]{1,0:T(8,128)(2,1)S(1)}, u32[]{:S(2)}, u32[]{:S(2)}) %collective-permute-start.17) | collective-permute-done | bytes 114720 | tf_op jit(solution)/shard_map/ppermute | solution.py:520
  60.5 1.5 %collective-permute-start.18 = (bf16[224,256]{1,0:T(8,128)(2,1)S(1)}, bf16[224,256]{1,0:T(8,128)(2,1)S(1)}, u32[]{:S(2)}, u32[]{:S(2)}) collective-permute-start(bf16[224,256]{1,0:T(8,128)(2,1)S(1)} %collective-permute-done.17.refs_2_), channel_id=1, source_target_pairs={{0,2},{1,3},{2,0},{3,1},{4,6},{5,7},{6,4},{7,5},{8,10},{9,11},{10,... | collective-permute-start | bytes 344072 | tf_op jit(solution)/shard_map/ppermute | solution.py:523
  62.0 3.0 %collective-permute-done.19.refs_4_ = bf16[224,256]{1,0:T(8,128)(2,1)S(1)} collective-permute-done((bf16[224,256]{1,0:T(8,128)(2,1)S(1)}, bf16[224,256]{1,0:T(8,128)(2,1)S(1)}, u32[]{:S(2)}, u32[]{:S(2)}) %collective-permute-start.19) | collective-permute-done | bytes 114720 | tf_op jit(solution)/shard_map/ppermute | solution.py:520
  65.0 1.5 %collective-permute-start.20 = (bf16[224,256]{1,0:T(8,128)(2,1)S(1)}, bf16[224,256]{1,0:T(8,128)(2,1)S(1)}, u32[]{:S(2)}, u32[]{:S(2)}) collective-permute-start(bf16[224,256]{1,0:T(8,128)(2,1)S(1)} %collective-permute-done.19.refs_4_), channel_id=1, source_target_pairs={{0,2},{1,3},{2,0},{3,1},{4,6},{5,7},{6,4},{7,5},{8,10},{9,11},{10,... | collective-permute-start | bytes 344072 | tf_op jit(solution)/shard_map/ppermute | solution.py:523
  66.5 0.6 collective-permute-start.22
  67.1 3.2 %collective-permute-done.20.refs_5_ = bf16[224,256]{1,0:T(8,128)(2,1)S(1)} collective-permute-done((bf16[224,256]{1,0:T(8,128)(2,1)S(1)}, bf16[224,256]{1,0:T(8,128)(2,1)S(1)}, u32[]{:S(2)}, u32[]{:S(2)}) %collective-permute-start.20) | collective-permute-done | bytes 114720 | tf_op jit(solution)/shard_map/ppermute | solution.py:523
  70.3 1.2 %collective-permute-done.22.refs_7_ = bf16[224,256]{1,0:T(8,128)(2,1)S(1)} collective-permute-done((bf16[224,256]{1,0:T(8,128)(2,1)S(1)}, bf16[224,256]{1,0:T(8,128)(2,1)S(1)}, u32[]{:S(2)}, u32[]{:S(2)}) %collective-permute-start.22) | collective-permute-done | bytes 114720 | tf_op jit(solution)/shard_map/ppermute | solution.py:523
  71.6 1.3 %gate_up.1 = (f32[128,768]{1,0:T(8,128)S(1)}, bf16[16,2048]{1,0:T(8,128)(2,1)S(1)}) custom-call(bf16[224,256]{1,0:T(8,128)(2,1)S(1)} %add_convert_fusion.refs_0_, bf16[224,256]{1,0:T(8,128)(2,1)S(1)} %collective-permute-done.16.refs_1_, bf16[224,256]{1,0:T(8,128)(2,1)S(1)} %collective-permute-done.17.refs_2_, ...), custom_call_target="tpu_custom_call" | custom-call | flops 1000000000 | bytes 3000000 | tf_op jit(solution)/shard_map/gate_up/pallas_call | solution.py:657
  73.0 1.4 %gate_up_own.1 = (f32[128,768]{1,0:T(8,128)S(1)}, bf16[16,2048]{1,0:T(8,128)(2,1)S(1)}) custom-call(bf16[224,256]{1,0:T(8,128)(2,1)S(1)} %add_convert_fusion.refs_0_, bf16[224,256]{1,0:T(8,128)(2,1)S(1)} %collective-permute-done.16.refs_1_, bf16[224,256]{1,0:T(8,128)(2,1)S(1)} %collective-permute-done.17.refs_2_, ...), custom_call_target="tpu_custom_call" | custom-call | flops 1000000000 | bytes 3000000 | tf_op jit(solution)/shard_map/gate_up_own/pallas_call | solution.py:657
  74.4 0.3 collective-permute-done.24.came_ref
  74.7 0.8 hidden.1
  75.5 1.1 %collective-permute-start.30 = (bf16[8,7168]{1,0:T(8,128)(2,1)S(1)}, bf16[8,7168]{1,0:T(8,128)(2,1)S(1)}, u32[]{:S(2)}, u32[]{:S(2)}) collective-permute-start(bf16[8,7168]{1,0:T(8,128)(2,1)S(1)} %get-tuple-element.74), channel_id=1, source_target_pairs={{0,2},{1,3},{2,0},{3,1},{4,6},{5,7},{6,4},{7,5},{8,10},{9,11},{10,... | collective-permute-start | bytes 344072 | tf_op jit(solution)/shard_map/ppermute | solution.py:523
  76.6 1.0 %collective-permute-start.28 = (bf16[8,7168]{1,0:T(8,128)(2,1)S(1)}, bf16[8,7168]{1,0:T(8,128)(2,1)S(1)}, u32[]{:S(2)}, u32[]{:S(2)}) collective-permute-start(bf16[8,7168]{1,0:T(8,128)(2,1)S(1)} %get-tuple-element.72), channel_id=1, source_target_pairs={{0,2},{1,3},{2,0},{3,1},{4,6},{5,7},{6,4},{7,5},{8,10},{9,11},{10,... | collective-permute-start | bytes 344072 | tf_op jit(solution)/shard_map/ppermute | solution.py:523
  77.6 1.0 %collective-permute-start.26 = (bf16[8,7168]{1,0:T(8,128)(2,1)S(1)}, bf16[8,7168]{1,0:T(8,128)(2,1)S(1)}, u32[]{:S(2)}, u32[]{:S(2)}) collective-permute-start(bf16[8,7168]{1,0:T(8,128)(2,1)S(1)} %get-tuple-element.70), channel_id=1, source_target_pairs={{0,2},{1,3},{2,0},{3,1},{4,6},{5,7},{6,4},{7,5},{8,10},{9,11},{10,... | collective-permute-start | bytes 344072 | tf_op jit(solution)/shard_map/ppermute | solution.py:523
  78.6 1.0 %collective-permute-start.25 = (bf16[8,7168]{1,0:T(8,128)(2,1)S(1)}, bf16[8,7168]{1,0:T(8,128)(2,1)S(1)}, u32[]{:S(2)}, u32[]{:S(2)}) collective-permute-start(bf16[8,7168]{1,0:T(8,128)(2,1)S(1)} %get-tuple-element.68), channel_id=1, source_target_pairs={{0,2},{1,3},{2,0},{3,1},{4,6},{5,7},{6,4},{7,5},{8,10},{9,11},{10,... | collective-permute-start | bytes 344072 | tf_op jit(solution)/shard_map/ppermute | solution.py:523
  79.6 0.6 down.1
  80.2 1.4 %collective-permute-done.30.far_ref = bf16[8,7168]{1,0:T(8,128)(2,1)S(1)} collective-permute-done((bf16[8,7168]{1,0:T(8,128)(2,1)S(1)}, bf16[8,7168]{1,0:T(8,128)(2,1)S(1)}, u32[]{:S(2)}, u32[]{:S(2)}) %collective-permute-start.30) | collective-permute-done | bytes 114720 | tf_op jit(solution)/shard_map/ppermute | solution.py:523
  81.6 2.1 %collective-permute-start.31 = (bf16[8,7168]{1,0:T(8,128)(2,1)S(1)}, bf16[8,7168]{1,0:T(8,128)(2,1)S(1)}, u32[]{:S(2)}, u32[]{:S(2)}) collective-permute-start(bf16[8,7168]{1,0:T(8,128)(2,1)S(1)} %add.25), channel_id=1, source_target_pairs={{0,12},{1,13},{2,14},{3,15},{4,8},{5,9},{6,10},{7,11},{8,4},{9,5},... | collective-permute-start | bytes 344072 | tf_op jit(solution)/shard_map/ppermute | solution.py:520
  83.6 0.4 collective-permute-done.28.far_ref
  84.0 1.4 %collective-permute-start.29 = (bf16[8,7168]{1,0:T(8,128)(2,1)S(1)}, bf16[8,7168]{1,0:T(8,128)(2,1)S(1)}, u32[]{:S(2)}, u32[]{:S(2)}) collective-permute-start(bf16[8,7168]{1,0:T(8,128)(2,1)S(1)} %add.24), channel_id=1, source_target_pairs={{0,8},{1,9},{2,10},{3,11},{4,12},{5,13},{6,14},{7,15},{8,0},{9,1},... | collective-permute-start | bytes 344072 | tf_op jit(solution)/shard_map/ppermute | solution.py:520
  85.4 1.1 %collective-permute-done.26.far_ref = bf16[8,7168]{1,0:T(8,128)(2,1)S(1)} collective-permute-done((bf16[8,7168]{1,0:T(8,128)(2,1)S(1)}, bf16[8,7168]{1,0:T(8,128)(2,1)S(1)}, u32[]{:S(2)}, u32[]{:S(2)}) %collective-permute-start.26) | collective-permute-done | bytes 114720 | tf_op jit(solution)/shard_map/ppermute | solution.py:523
  86.5 0.8 collective-permute-start.27
  87.3 1.3 %collective-permute-done.32.refs_6_ = bf16[16,2048]{1,0:T(8,128)(2,1)S(1)} collective-permute-done((bf16[16,2048]{1,0:T(8,128)(2,1)S(1)}, bf16[16,2048]{1,0:T(8,128)(2,1)S(1)}, u32[]{:S(2)}, u32[]{:S(2)}) %collective-permute-start.32) | collective-permute-done | bytes 65568 | tf_op jit(solution)/shard_map/ppermute | solution.py:526
  88.6 0.6 collective-permute-done.31.refs_4_
  89.2 4.1 %collective-permute-done.29.refs_3_ = bf16[8,7168]{1,0:T(8,128)(2,1)S(1)} collective-permute-done((bf16[8,7168]{1,0:T(8,128)(2,1)S(1)}, bf16[8,7168]{1,0:T(8,128)(2,1)S(1)}, u32[]{:S(2)}, u32[]{:S(2)}) %collective-permute-start.29) | collective-permute-done | bytes 114720 | tf_op jit(solution)/shard_map/ppermute | solution.py:520
  93.3 0.1 collective-permute-done.27.refs_2_
  93.4 0.8 last.1
  (44 shorter events, 0.5 us)
Async XLA Ops:
  0.0 2.6 %copy-start.5 = (bf16[64,4096]{1,0:T(8,128)(2,1)S(1)}, bf16[64,4096]{1,0:T(8,128)(2,1)}, u32[]{:S(2)}) copy-start(bf16[64,4096]{1,0:T(8,128)(2,1)} %refs_9_.3) | copy-start | bytes 1572868
  0.0 2.6 %copy-start.6 = (bf16[64,4096]{1,0:T(8,128)(2,1)S(1)}, bf16[64,4096]{1,0:T(8,128)(2,1)}, u32[]{:S(2)}) copy-start(bf16[64,4096]{1,0:T(8,128)(2,1)} %refs_10_.3) | copy-start | bytes 1572868
  0.0 2.6 %copy-start.7 = (bf16[64,4096]{1,0:T(8,128)(2,1)S(1)}, bf16[64,4096]{1,0:T(8,128)(2,1)}, u32[]{:S(2)}) copy-start(bf16[64,4096]{1,0:T(8,128)(2,1)} %refs_11_.1) | copy-start | bytes 1572868
  2.6 1.0 %copy-start.4 = (bf16[64,4096]{1,0:T(8,128)(2,1)S(1)}, bf16[64,4096]{1,0:T(8,128)(2,1)}, u32[]{:S(2)}) copy-start(bf16[64,4096]{1,0:T(8,128)(2,1)} %weight_ref.3) | copy-start | bytes 1572868
  2.7 1.1 %copy-start.8 = (bf16[8,10240]{1,0:T(8,128)(2,1)S(1)}, bf16[8,10240]{1,0:T(8,128)(2,1)}, u32[]{:S(2)}) copy-start(bf16[8,10240]{1,0:T(8,128)(2,1)} %fetch.1.piece_ref.refs_0_) | copy-start | bytes 491524
  2.8 27.8 %collective-permute-start.7 = (bf16[192,4096]{1,0:T(8,128)(2,1)S(1)}, bf16[192,4096]{1,0:T(8,128)(2,1)S(1)}, u32[]{:S(2)}, u32[]{:S(2)}) collective-permute-start(bf16[192,4096]{1,0:T(8,128)(2,1)S(1)} %stack.1), channel_id=1, source_target_pairs={{0,1},{1,0},{2,3},{3,2},{4,5},{5,4},{6,7},{7,6},{8,9},{9,8},{10,11... | collective-permute-start | bytes 4718600 | tf_op jit(solution)/shard_map/ppermute | solution.py:526
  3.8 26.8 %copy-start.9 = (f32[4096]{0:T(1024)S(1)}, f32[4096]{0:T(1024)}, u32[]{:S(2)}) copy-start(f32[4096]{0:T(1024)} %param.23) | copy-start | bytes 49156
  3.8 21.7 %collective-permute-start = (bf16[8,26624]{1,0:T(8,128)(2,1)S(1)}, bf16[8,26624]{1,0:T(8,128)(2,1)S(1)}, u32[]{:S(2)}, u32[]{:S(2)}) collective-permute-start(bf16[8,26624]{1,0:T(8,128)(2,1)S(1)} %across.1), channel_id=1, source_target_pairs={{0,2},{1,3},{2,0},{3,1},{4,6},{5,7},{6,4},{7,5},{8,10},{9,11},{10,... | collective-permute-start | bytes 1277960 | tf_op jit(solution)/shard_map/ppermute | solution.py:523
  6.8 7.9 %collective-permute-start.1 = (bf16[8,10240]{1,0:T(8,128)(2,1)S(1)}, bf16[8,10240]{1,0:T(8,128)(2,1)S(1)}, u32[]{:S(2)}, u32[]{:S(2)}) collective-permute-start(bf16[8,10240]{1,0:T(8,128)(2,1)S(1)} %copy-done.8), channel_id=1, source_target_pairs={{0,4},{1,5},{2,6},{3,7},{4,0},{5,1},{6,2},{7,3},{8,12},{9,13},{10,... | collective-permute-start | bytes 491528 | tf_op jit(solution)/shard_map/ppermute | solution.py:520
  8.4 15.1 %collective-permute-start.3 = (bf16[8,10240]{1,0:T(8,128)(2,1)S(1)}, bf16[8,10240]{1,0:T(8,128)(2,1)S(1)}, u32[]{:S(2)}, u32[]{:S(2)}) collective-permute-start(bf16[8,10240]{1,0:T(8,128)(2,1)S(1)} %copy-done.8), channel_id=1, source_target_pairs={{0,8},{1,9},{2,10},{3,11},{4,12},{5,13},{6,14},{7,15},{8,0},{9,1},... | collective-permute-start | bytes 491528 | tf_op jit(solution)/shard_map/ppermute | solution.py:520
  11.0 13.0 %collective-permute-start.5 = (bf16[8,10240]{1,0:T(8,128)(2,1)S(1)}, bf16[8,10240]{1,0:T(8,128)(2,1)S(1)}, u32[]{:S(2)}, u32[]{:S(2)}) collective-permute-start(bf16[8,10240]{1,0:T(8,128)(2,1)S(1)} %copy-done.8), channel_id=1, source_target_pairs={{0,12},{1,13},{2,14},{3,15},{4,8},{5,9},{6,10},{7,11},{8,4},{9,5},... | collective-permute-start | bytes 491528 | tf_op jit(solution)/shard_map/ppermute | solution.py:520
  14.7 11.0 %collective-permute-start.2 = (bf16[8,10240]{1,0:T(8,128)(2,1)S(1)}, bf16[8,10240]{1,0:T(8,128)(2,1)S(1)}, u32[]{:S(2)}, u32[]{:S(2)}) collective-permute-start(bf16[8,10240]{1,0:T(8,128)(2,1)S(1)} %collective-permute-done.1.refs_2_), channel_id=1, source_target_pairs={{0,2},{1,3},{2,0},{3,1},{4,6},{5,7},{6,4},{7,5},{8,10},{9,11},{10,... | collective-permute-start | bytes 491528 | tf_op jit(solution)/shard_map/ppermute | solution.py:523
  23.5 5.3 %collective-permute-start.4 = (bf16[8,10240]{1,0:T(8,128)(2,1)S(1)}, bf16[8,10240]{1,0:T(8,128)(2,1)S(1)}, u32[]{:S(2)}, u32[]{:S(2)}) collective-permute-start(bf16[8,10240]{1,0:T(8,128)(2,1)S(1)} %collective-permute-done.3.refs_4_), channel_id=1, source_target_pairs={{0,2},{1,3},{2,0},{3,1},{4,6},{5,7},{6,4},{7,5},{8,10},{9,11},{10,... | collective-permute-start | bytes 491528 | tf_op jit(solution)/shard_map/ppermute | solution.py:523
  24.0 6.6 %collective-permute-start.6 = (bf16[8,10240]{1,0:T(8,128)(2,1)S(1)}, bf16[8,10240]{1,0:T(8,128)(2,1)S(1)}, u32[]{:S(2)}, u32[]{:S(2)}) collective-permute-start(bf16[8,10240]{1,0:T(8,128)(2,1)S(1)} %collective-permute-done.5.refs_6_), channel_id=1, source_target_pairs={{0,2},{1,3},{2,0},{3,1},{4,6},{5,7},{6,4},{7,5},{8,10},{9,11},{10,... | collective-permute-start | bytes 491528 | tf_op jit(solution)/shard_map/ppermute | solution.py:523
  25.6 8.4 %collective-permute-start.8 = (bf16[128,1024]{1,0:T(8,128)(2,1)S(1)}, bf16[128,1024]{1,0:T(8,128)(2,1)S(1)}, u32[]{:S(2)}, u32[]{:S(2)}) collective-permute-start(bf16[128,1024]{1,0:T(8,128)(2,1)S(1)} %get-tuple-element.49), channel_id=1, source_target_pairs={{0,1},{1,0},{2,3},{3,2},{4,5},{5,4},{6,7},{7,6},{8,9},{9,8},{10,11... | collective-permute-start | bytes 786440 | tf_op jit(solution)/shard_map/ppermute | solution.py:526
  30.5 2.1 %copy-start.10 = (s32[24,1]{0,1:T(1,128)S(1)}, s32[24,1]{0,1:T(1,128)}, u32[]{:S(2)}) copy-start(s32[24,1]{0,1:T(1,128)} %param.16) | copy-start | bytes 292
  30.6 2.1 %copy-start.11 = (s32[24]{0:T(128)S(1)}, s32[24]{0:T(128)}, u32[]{:S(2)}) copy-start(s32[24]{0:T(128)} %segment_ref.1) | copy-start | bytes 292
  32.5 1.5 %collective-permute-start.9 = (bf16[160,512]{1,0:T(8,128)(2,1)S(1)}, bf16[160,512]{1,0:T(8,128)(2,1)S(1)}, u32[]{:S(2)}, u32[]{:S(2)}) collective-permute-start(bf16[160,512]{1,0:T(8,128)(2,1)S(1)} %get-tuple-element.51), channel_id=1, source_target_pairs={{0,1},{1,0},{2,3},{3,2},{4,5},{5,4},{6,7},{7,6},{8,9},{9,8},{10,11... | collective-permute-start | bytes 491528 | tf_op jit(solution)/shard_map/ppermute | solution.py:526
  34.9 4.1 %collective-permute-start.10 = (bf16[112,128]{1,0:T(8,128)(2,1)S(1)}, bf16[112,128]{1,0:T(8,128)(2,1)S(1)}, u32[]{:S(2)}, u32[]{:S(2)}) collective-permute-start(bf16[112,128]{1,0:T(8,128)(2,1)S(1)} %get-tuple-element.53.refs_0_), channel_id=1, source_target_pairs={{0,2},{1,3},{2,0},{3,1},{4,6},{5,7},{6,4},{7,5},{8,10},{9,11},{10,... | collective-permute-start | bytes 86024 | tf_op jit(solution)/shard_map/ppermute | solution.py:523
  35.5 3.5 %collective-permute-start.11 = (bf16[112,128]{1,0:T(8,128)(2,1)S(1)}, bf16[112,128]{1,0:T(8,128)(2,1)S(1)}, u32[]{:S(2)}, u32[]{:S(2)}) collective-permute-start(bf16[112,128]{1,0:T(8,128)(2,1)S(1)} %get-tuple-element.53.refs_0_), channel_id=1, source_target_pairs={{0,1},{1,0},{2,3},{3,2},{4,5},{5,4},{6,7},{7,6},{8,9},{9,8},{10,11... | collective-permute-start | bytes 86024 | tf_op jit(solution)/shard_map/ppermute | solution.py:526
  35.7 3.5 %collective-permute-start.12 = (bf16[112,128]{1,0:T(8,128)(2,1)S(1)}, bf16[112,128]{1,0:T(8,128)(2,1)S(1)}, u32[]{:S(2)}, u32[]{:S(2)}) collective-permute-start(bf16[112,128]{1,0:T(8,128)(2,1)S(1)} %get-tuple-element.53.refs_0_), channel_id=1, source_target_pairs={{0,3},{1,2},{2,1},{3,0},{4,7},{5,6},{6,5},{7,4},{8,11},{9,10},{10,... | collective-permute-start | bytes 86024 | tf_op jit(solution)/shard_map/ppermute | solution.py:630
  39.1 13.7 %copy-start = (bf16[160,4096]{1,0:T(8,128)(2,1)S(1)}, bf16[160,4096]{1,0:T(8,128)(2,1)}, u32[]{:S(2)}) copy-start(bf16[160,4096]{1,0:T(8,128)(2,1)} %down_ref.4) | copy-start | bytes 3932164
  39.1 13.7 %copy-start.1 = (bf16[160,4096]{1,0:T(8,128)(2,1)S(1)}, bf16[160,4096]{1,0:T(8,128)(2,1)}, u32[]{:S(2)}) copy-start(bf16[160,4096]{1,0:T(8,128)(2,1)} %refs_9_.5) | copy-start | bytes 3932164
  39.1 13.7 %copy-start.2 = (bf16[160,4096]{1,0:T(8,128)(2,1)S(1)}, bf16[160,4096]{1,0:T(8,128)(2,1)}, u32[]{:S(2)}) copy-start(bf16[160,4096]{1,0:T(8,128)(2,1)} %refs_10_.5) | copy-start | bytes 3932164
  39.6 8.0 %collective-permute-start.13 = (bf16[224,256]{1,0:T(8,128)(2,1)S(1)}, bf16[224,256]{1,0:T(8,128)(2,1)S(1)}, u32[]{:S(2)}, u32[]{:S(2)}) collective-permute-start(bf16[224,256]{1,0:T(8,128)(2,1)S(1)} %get-tuple-element.57), channel_id=1, source_target_pairs={{0,12},{1,13},{2,14},{3,15},{4,8},{5,9},{6,10},{7,11},{8,4},{9,5},... | collective-permute-start | bytes 344072 | tf_op jit(solution)/shard_map/ppermute | solution.py:520
  41.7 11.0 %collective-permute-start.14 = (bf16[224,256]{1,0:T(8,128)(2,1)S(1)}, bf16[224,256]{1,0:T(8,128)(2,1)S(1)}, u32[]{:S(2)}, u32[]{:S(2)}) collective-permute-start(bf16[224,256]{1,0:T(8,128)(2,1)S(1)} %get-tuple-element.58), channel_id=1, source_target_pairs={{0,8},{1,9},{2,10},{3,11},{4,12},{5,13},{6,14},{7,15},{8,0},{9,1},... | collective-permute-start | bytes 344072 | tf_op jit(solution)/shard_map/ppermute | solution.py:520
  42.1 10.6 %collective-permute-start.15 = (bf16[224,256]{1,0:T(8,128)(2,1)S(1)}, bf16[224,256]{1,0:T(8,128)(2,1)S(1)}, u32[]{:S(2)}, u32[]{:S(2)}) collective-permute-start(bf16[224,256]{1,0:T(8,128)(2,1)S(1)} %get-tuple-element.59), channel_id=1, source_target_pairs={{0,4},{1,5},{2,6},{3,7},{4,0},{5,1},{6,2},{7,3},{8,12},{9,13},{10,... | collective-permute-start | bytes 344072 | tf_op jit(solution)/shard_map/ppermute | solution.py:520
  52.8 18.8 %copy-start.3 = (f32[4096]{0:T(1024)S(1)}, f32[4096]{0:T(1024)}, u32[]{:S(2)}) copy-start(f32[4096]{0:T(1024)} %param.24) | copy-start | bytes 49156
  53.0 18.6 %collective-permute-start.23 = (bf16[320,4096]{1,0:T(8,128)(2,1)S(1)}, bf16[320,4096]{1,0:T(8,128)(2,1)S(1)}, u32[]{:S(2)}, u32[]{:S(2)}) collective-permute-start(bf16[320,4096]{1,0:T(8,128)(2,1)S(1)} %share.1), channel_id=1, source_target_pairs={{0,1},{1,0},{2,3},{3,2},{4,5},{5,4},{6,7},{7,6},{8,9},{9,8},{10,11... | collective-permute-start | bytes 7864328 | tf_op jit(solution)/shard_map/ppermute | solution.py:526
  53.1 7.4 %collective-permute-start.17 = (bf16[224,256]{1,0:T(8,128)(2,1)S(1)}, bf16[224,256]{1,0:T(8,128)(2,1)S(1)}, u32[]{:S(2)}, u32[]{:S(2)}) collective-permute-start(bf16[224,256]{1,0:T(8,128)(2,1)S(1)} %add_convert_fusion.refs_0_), channel_id=1, source_target_pairs={{0,4},{1,5},{2,6},{3,7},{4,0},{5,1},{6,2},{7,3},{8,12},{9,13},{10,... | collective-permute-start | bytes 344072 | tf_op jit(solution)/shard_map/ppermute | solution.py:520
  53.2 11.9 %collective-permute-start.19 = (bf16[224,256]{1,0:T(8,128)(2,1)S(1)}, bf16[224,256]{1,0:T(8,128)(2,1)S(1)}, u32[]{:S(2)}, u32[]{:S(2)}) collective-permute-start(bf16[224,256]{1,0:T(8,128)(2,1)S(1)} %add_convert_fusion.refs_0_), channel_id=1, source_target_pairs={{0,8},{1,9},{2,10},{3,11},{4,12},{5,13},{6,14},{7,15},{8,0},{9,1},... | collective-permute-start | bytes 344072 | tf_op jit(solution)/shard_map/ppermute | solution.py:520
  55.7 10.8 %collective-permute-start.21 = (bf16[224,256]{1,0:T(8,128)(2,1)S(1)}, bf16[224,256]{1,0:T(8,128)(2,1)S(1)}, u32[]{:S(2)}, u32[]{:S(2)}) collective-permute-start(bf16[224,256]{1,0:T(8,128)(2,1)S(1)} %add_convert_fusion.refs_0_), channel_id=1, source_target_pairs={{0,12},{1,13},{2,14},{3,15},{4,8},{5,9},{6,10},{7,11},{8,4},{9,5},... | collective-permute-start | bytes 344072 | tf_op jit(solution)/shard_map/ppermute | solution.py:520
  57.5 9.5 %collective-permute-start.16 = (bf16[224,256]{1,0:T(8,128)(2,1)S(1)}, bf16[224,256]{1,0:T(8,128)(2,1)S(1)}, u32[]{:S(2)}, u32[]{:S(2)}) collective-permute-start(bf16[224,256]{1,0:T(8,128)(2,1)S(1)} %add_convert_fusion.refs_0_), channel_id=1, source_target_pairs={{0,2},{1,3},{2,0},{3,1},{4,6},{5,7},{6,4},{7,5},{8,10},{9,11},{10,... | collective-permute-start | bytes 344072 | tf_op jit(solution)/shard_map/ppermute | solution.py:523
  60.5 6.6 %collective-permute-start.18 = (bf16[224,256]{1,0:T(8,128)(2,1)S(1)}, bf16[224,256]{1,0:T(8,128)(2,1)S(1)}, u32[]{:S(2)}, u32[]{:S(2)}) collective-permute-start(bf16[224,256]{1,0:T(8,128)(2,1)S(1)} %collective-permute-done.17.refs_2_), channel_id=1, source_target_pairs={{0,2},{1,3},{2,0},{3,1},{4,6},{5,7},{6,4},{7,5},{8,10},{9,11},{10,... | collective-permute-start | bytes 344072 | tf_op jit(solution)/shard_map/ppermute | solution.py:523
  65.0 5.3 %collective-permute-start.20 = (bf16[224,256]{1,0:T(8,128)(2,1)S(1)}, bf16[224,256]{1,0:T(8,128)(2,1)S(1)}, u32[]{:S(2)}, u32[]{:S(2)}) collective-permute-start(bf16[224,256]{1,0:T(8,128)(2,1)S(1)} %collective-permute-done.19.refs_4_), channel_id=1, source_target_pairs={{0,2},{1,3},{2,0},{3,1},{4,6},{5,7},{6,4},{7,5},{8,10},{9,11},{10,... | collective-permute-start | bytes 344072 | tf_op jit(solution)/shard_map/ppermute | solution.py:523
  66.5 5.0 %collective-permute-start.22 = (bf16[224,256]{1,0:T(8,128)(2,1)S(1)}, bf16[224,256]{1,0:T(8,128)(2,1)S(1)}, u32[]{:S(2)}, u32[]{:S(2)}) collective-permute-start(bf16[224,256]{1,0:T(8,128)(2,1)S(1)} %collective-permute-done.21.refs_6_), channel_id=1, source_target_pairs={{0,2},{1,3},{2,0},{3,1},{4,6},{5,7},{6,4},{7,5},{8,10},{9,11},{10,... | collective-permute-start | bytes 344072 | tf_op jit(solution)/shard_map/ppermute | solution.py:523
  72.9 1.8 %collective-permute-start.24 = (f32[128,768]{1,0:T(8,128)S(1)}, f32[128,768]{1,0:T(8,128)S(1)}, u32[]{:S(2)}, u32[]{:S(2)}) collective-permute-start(f32[128,768]{1,0:T(8,128)S(1)} %get-tuple-element.63), channel_id=1, source_target_pairs={{0,1},{1,0},{2,3},{3,2},{4,5},{5,4},{6,7},{7,6},{8,9},{9,8},{10,11... | collective-permute-start | bytes 1179656 | tf_op jit(solution)/shard_map/ppermute | solution.py:526
  75.5 6.1 %collective-permute-start.30 = (bf16[8,7168]{1,0:T(8,128)(2,1)S(1)}, bf16[8,7168]{1,0:T(8,128)(2,1)S(1)}, u32[]{:S(2)}, u32[]{:S(2)}) collective-permute-start(bf16[8,7168]{1,0:T(8,128)(2,1)S(1)} %get-tuple-element.74), channel_id=1, source_target_pairs={{0,2},{1,3},{2,0},{3,1},{4,6},{5,7},{6,4},{7,5},{8,10},{9,11},{10,... | collective-permute-start | bytes 344072 | tf_op jit(solution)/shard_map/ppermute | solution.py:523
  76.6 7.4 %collective-permute-start.28 = (bf16[8,7168]{1,0:T(8,128)(2,1)S(1)}, bf16[8,7168]{1,0:T(8,128)(2,1)S(1)}, u32[]{:S(2)}, u32[]{:S(2)}) collective-permute-start(bf16[8,7168]{1,0:T(8,128)(2,1)S(1)} %get-tuple-element.72), channel_id=1, source_target_pairs={{0,2},{1,3},{2,0},{3,1},{4,6},{5,7},{6,4},{7,5},{8,10},{9,11},{10,... | collective-permute-start | bytes 344072 | tf_op jit(solution)/shard_map/ppermute | solution.py:523
  77.6 8.9 %collective-permute-start.26 = (bf16[8,7168]{1,0:T(8,128)(2,1)S(1)}, bf16[8,7168]{1,0:T(8,128)(2,1)S(1)}, u32[]{:S(2)}, u32[]{:S(2)}) collective-permute-start(bf16[8,7168]{1,0:T(8,128)(2,1)S(1)} %get-tuple-element.70), channel_id=1, source_target_pairs={{0,2},{1,3},{2,0},{3,1},{4,6},{5,7},{6,4},{7,5},{8,10},{9,11},{10,... | collective-permute-start | bytes 344072 | tf_op jit(solution)/shard_map/ppermute | solution.py:523
  78.6 10.0 %collective-permute-start.25 = (bf16[8,7168]{1,0:T(8,128)(2,1)S(1)}, bf16[8,7168]{1,0:T(8,128)(2,1)S(1)}, u32[]{:S(2)}, u32[]{:S(2)}) collective-permute-start(bf16[8,7168]{1,0:T(8,128)(2,1)S(1)} %get-tuple-element.68), channel_id=1, source_target_pairs={{0,2},{1,3},{2,0},{3,1},{4,6},{5,7},{6,4},{7,5},{8,10},{9,11},{10,... | collective-permute-start | bytes 344072 | tf_op jit(solution)/shard_map/ppermute | solution.py:523
  81.6 7.6 %collective-permute-start.31 = (bf16[8,7168]{1,0:T(8,128)(2,1)S(1)}, bf16[8,7168]{1,0:T(8,128)(2,1)S(1)}, u32[]{:S(2)}, u32[]{:S(2)}) collective-permute-start(bf16[8,7168]{1,0:T(8,128)(2,1)S(1)} %add.25), channel_id=1, source_target_pairs={{0,12},{1,13},{2,14},{3,15},{4,8},{5,9},{6,10},{7,11},{8,4},{9,5},... | collective-permute-start | bytes 344072 | tf_op jit(solution)/shard_map/ppermute | solution.py:520
  84.0 9.3 %collective-permute-start.29 = (bf16[8,7168]{1,0:T(8,128)(2,1)S(1)}, bf16[8,7168]{1,0:T(8,128)(2,1)S(1)}, u32[]{:S(2)}, u32[]{:S(2)}) collective-permute-start(bf16[8,7168]{1,0:T(8,128)(2,1)S(1)} %add.24), channel_id=1, source_target_pairs={{0,8},{1,9},{2,10},{3,11},{4,12},{5,13},{6,14},{7,15},{8,0},{9,1},... | collective-permute-start | bytes 344072 | tf_op jit(solution)/shard_map/ppermute | solution.py:520
  86.5 6.9 %collective-permute-start.27 = (bf16[8,7168]{1,0:T(8,128)(2,1)S(1)}, bf16[8,7168]{1,0:T(8,128)(2,1)S(1)}, u32[]{:S(2)}, u32[]{:S(2)}) collective-permute-start(bf16[8,7168]{1,0:T(8,128)(2,1)S(1)} %add.23), channel_id=1, source_target_pairs={{0,4},{1,5},{2,6},{3,7},{4,0},{5,1},{6,2},{7,3},{8,12},{9,13},{10,... | collective-permute-start | bytes 344072 | tf_op jit(solution)/shard_map/ppermute | solution.py:520
  87.3 1.3 %collective-permute-start.32 = (bf16[16,2048]{1,0:T(8,128)(2,1)S(1)}, bf16[16,2048]{1,0:T(8,128)(2,1)S(1)}, u32[]{:S(2)}, u32[]{:S(2)}) collective-permute-start(bf16[16,2048]{1,0:T(8,128)(2,1)S(1)} %get-tuple-element.76), channel_id=1, source_target_pairs={{0,1},{1,0},{2,3},{3,2},{4,5},{5,4},{6,7},{7,6},{8,9},{9,8},{10,11... | collective-permute-start | bytes 196616 | tf_op jit(solution)/shard_map/ppermute | solution.py:526
